TPU v7x, 32 devices: a whole 2x2x4 slice. The times are simulated.
32 devices in a mesh: feat: 8 (over z, x), dp: 4 (over y, core).
Axes of the slice: x: 2, y: 2, z: 4, core: 2. Of those that a mesh axis runs over, the one named last changes fastest.
Arguments:
- node_feats: bfloat16 [1024, 131072], P('feat'), may hold values from -6 to 6
- first_layer: bfloat16 [2, 1024, 256], P(None, 'feat'), may hold values from -0.125 to 0.125
- second_layer: bfloat16 [2, 256, 172], replicated, may hold values from -0.375 to 0.375
- seed_ids: int32 [32, 64], P('dp'), may hold values from 0 to 131071
- hop1_ids: int32 [32, 640], P('dp'), may hold values from 0 to 131071
- hop1_count: int32 [32, 64], P('dp'), may hold values from 1 to 10, 352 in all within a row
- hop2_ids: int32 [32, 7040], P('dp'), may hold values from 0 to 131071
- hop2_count: int32 [32, 704], P('dp'), may hold values from 1 to 10, 3872 in all within a row
- batch_sizes: int32 [32], replicated, may hold values from 1 to 64, 1536 in all
- label_ids: int32 [32, 64], P('dp'), may hold values from 0 to 171
Outputs:
- grad_first: float32 [2, 1024, 256], P(None, 'feat')
- grad_second: float32 [2, 256, 172], replicated
Inputs may be any that keep to these rules, and one draw needn't show every extreme that they name: The first hop1_count entries of a seed's list are used; the counts of one mini-batch sum to 352. The first hop2_count entries of a row's list are used; the counts of one mini-batch sum to 3872. Seeds at positions batch_sizes[o] and beyond are padding; the sizes sum to 1536.
All inputs are finite; a program needn't handle non-finite values.
Results may differ from a plain program's by a relative error of at most 0.0035.
The roundings to bfloat16 on the way count: a program that leaves them out, or rounds other values in their place, can miss the bound.
Values may be sent and summed in bfloat16 or wider, within the bound.
No kernel may reach another device: no remote copies, remote signals or barrier semaphores. Data moves between devices by JAX's collectives and lax.ppermute only.
A program may use at most 512 MiB of HBM per device.

v0:
```python
import jax
import jax.numpy as jnp
from jax import lax
from jax.sharding import PartitionSpec as P


def upper_layers(preact, second_layer, hop1_count, label_ids, batch_size):
    seed_total = hop1_count.shape[0]
    hidden_width = preact.shape[1]
    fanout = (preact.shape[0] - seed_total) // seed_total
    hidden = jnp.maximum(preact, 0.0).astype(jnp.bfloat16)
    seed_hidden = hidden[:seed_total]
    neighbour_hidden = (
        hidden[seed_total:].reshape(seed_total, fanout, hidden_width).astype(jnp.float32)
    )
    keep_one = jnp.arange(fanout)[None, :] < hop1_count[:, None]
    counts = hop1_count.astype(jnp.float32)[:, None]
    near_mean = (
        jnp.sum(jnp.where(keep_one[:, :, None], neighbour_hidden, 0.0), axis=1) / counts
    ).astype(jnp.bfloat16)
    logits = jnp.dot(seed_hidden, second_layer[0], preferred_element_type=jnp.float32)
    logits = logits + jnp.dot(near_mean, second_layer[1], preferred_element_type=jnp.float32)
    shifted = logits - jnp.max(logits, axis=1, keepdims=True)
    exponent = jnp.exp(shifted)
    probabilities = exponent / jnp.sum(exponent, axis=1, keepdims=True)
    onehot = (label_ids[:, None] == jnp.arange(logits.shape[1])[None, :]).astype(jnp.float32)
    valid_rows = (jnp.arange(seed_total) < batch_size).astype(jnp.float32)
    dlogits = (
        (probabilities - onehot) * valid_rows[:, None] / batch_size.astype(jnp.float32)
    ).astype(jnp.bfloat16)
    grad_second = jnp.stack(
        [
            jnp.dot(seed_hidden.T, dlogits, preferred_element_type=jnp.float32),
            jnp.dot(near_mean.T, dlogits, preferred_element_type=jnp.float32),
        ]
    )
    back_seed = jnp.dot(dlogits, second_layer[0].T, preferred_element_type=jnp.float32)
    back_near = jnp.dot(dlogits, second_layer[1].T, preferred_element_type=jnp.float32)
    spread = jnp.where(keep_one[:, :, None], (back_near / counts)[:, None, :], 0.0)
    back_hidden = jnp.concatenate([back_seed, spread.reshape(-1, hidden_width)], axis=0)
    dpreact = jnp.where(preact > 0, back_hidden, 0.0).astype(jnp.bfloat16)
    return (dpreact, grad_second)


def add_batches(local_inputs, block_grads):
    return jnp.einsum("fbr,brh->fh", local_inputs, block_grads, preferred_element_type=jnp.float32)


def shards(
    node_feats,
    first_layer,
    second_layer,
    seed_ids,
    hop1_ids,
    hop1_count,
    hop2_ids,
    hop2_count,
    batch_sizes,
    label_ids,
):
    groups = seed_ids.shape[0]
    column_rank = lax.axis_index("feat")
    owner_index = lax.axis_index("dp") * groups + column_rank
    slice_width = node_feats.shape[0]
    hidden_width = first_layer.shape[2]
    node_list = jnp.concatenate([seed_ids, hop1_ids], axis=1)
    row_total = node_list.shape[1]
    node_table = node_feats.T
    own_rows = node_table[node_list]
    neighbours = node_table[hop2_ids].reshape(groups, row_total, -1, slice_width)
    keep_two = jnp.arange(neighbours.shape[2])[None, None, :] < hop2_count[:, :, None]
    summed = jnp.sum(
        jnp.where(keep_two[:, :, :, None], neighbours.astype(jnp.float32), 0.0), axis=2
    )
    averaged = (summed / hop2_count[:, :, None].astype(jnp.float32)).astype(jnp.bfloat16)
    local_inputs = jnp.transpose(jnp.concatenate([own_rows, averaged], axis=2), (2, 0, 1))
    local_weights = first_layer.reshape(2 * slice_width, hidden_width)
    own_count = lax.dynamic_index_in_dim(hop1_count, column_rank, 0, keepdims=False)
    own_labels = lax.dynamic_index_in_dim(label_ids, column_rank, 0, keepdims=False)
    own_size = lax.dynamic_index_in_dim(batch_sizes, owner_index, 0, keepdims=False)
    preact = lax.psum_scatter(
        jnp.einsum("fbr,fh->brh", local_inputs, local_weights, preferred_element_type=jnp.float32),
        "feat",
        scatter_dimension=0,
        tiled=True,
    )[0]
    dpreact, grad_second = upper_layers(preact, second_layer, own_count, own_labels, own_size)
    grad_slice = add_batches(
        local_inputs, lax.all_gather(dpreact[None], "feat", axis=0, tiled=True)
    )
    grad_slice = grad_slice.reshape(2, slice_width, hidden_width)
    grad_first = lax.psum(grad_slice, "dp")
    grad_second = lax.psum(grad_second, ("feat", "dp"))
    return (grad_first, grad_second)


def solution(mesh):
    return jax.shard_map(
        shards,
        mesh=mesh,
        in_specs=(
            P("feat", None),
            P(None, "feat", None),
            P(),
            P("dp", None),
            P("dp", None),
            P("dp", None),
            P("dp", None),
            P("dp", None),
            P(),
            P("dp", None),
        ),
        out_specs=(P(None, "feat", None), P()),
        check_vma=False,
    )
```

profile of v0, /device:TPU:0, one launch (start us, length us, event | category | flops | bytes accessed | tf_op | source)
XLA Modules:
  0.0 1343.0 jit_solution(2675133303224575427)
XLA Ops:
  7.2 0.8 convert_element_type.56
  8.0 2.2 iota_compare_fusion
  10.2 0.8 compare_select_fusion.1
  11.1 1.0 compare_select_fusion
  12.2 43.9 %copy.18 = bf16[128,131072]{0,1:T(8,128)(2,1)} copy(bf16[128,131072]{1,0:T(8,128)(2,1)} %param.10) | data formatting | bytes 67108864 | tf_op args[0]
  56.1 28.0 %gather_fusion = bf16[5632,128]{1,0:T(8,128)(2,1)S(1)} fusion(bf16[131072,128]{1,0:T(8,128)(2,1)} %bitcast.49, s32[6144]{0:T(1024)S(1)} %pad_clamp_fusion), kind=kCustom, calls=%fused_computation | custom fusion | bytes 2906112 | tf_op jit(solution)/shard_map/gather | solution.py:69
  84.1 835.8 %gather_fusion.1 = bf16[56320,128]{1,0:T(8,128)(2,1)} fusion(bf16[131072,128]{1,0:T(8,128)(2,1)} %bitcast.50, s32[56320]{0:T(1024)S(1)} %broadcast_clamp_fusion), kind=kCustom, calls=%fused_computation.1 | custom fusion | bytes 29061120 | tf_op jit(solution)/shard_map/gather | solution.py:70
  919.8 28.7 %reshape.182 = f32[8,704,10,128]{3,2,1,0:T(8,128)} reshape(bf16[56320,128]{1,0:T(8,128)(2,1)} %gather_fusion.1) | data formatting | bytes 43253760 | tf_op jit(solution)/shard_map/convert_element_type | solution.py:73
  948.6 33.4 %select_reduce_fusion = f32[8,704,128]{2,1,0:T(8,128)S(1)} fusion(f32[8,704,10,128]{3,2,1,0:T(8,128)} %reshape.182, pred[8,704,10]{2,1,0:T(8,128)(4,1)S(1)} %iota_compare_fusion), kind=kLoop, calls=%fused_computation.2 | loop fusion | flops 13697024 | bytes 31775744 | tf_op jit(solution)/shard_map/reduce_sum | solution.py:72
  982.0 0.9 divide_convert_fusion
  983.0 3.4 fusion.1
  987.0 0.6 dynamic_slice.13
  988.3 1.3 fusion.7
  989.7 1.2 compare_convert_fusion
  991.2 108.4 %reduce-scatter.2.cloned.1.call-done = f32[1,704,256]{2,1,0:T(8,128)} async-done(((f32[8,704,256]{2,1,0:T(8,128)}), f32[1,704,256]{2,1,0:T(8,128)}) %reduce-scatter.2.cloned.1.call-update) | async-done | bytes 720912 | tf_op jit(solution)/shard_map/reduce_scatter | solution.py:81
  1099.6 1.2 maximum_convert_fusion
  1100.8 1.0 slice_convert_fusion
  1101.9 2.2 reshape.183
  1104.1 1.6 select_reduce_fusion.1
  1106.9 0.8 convolution_bitcast_fusion.2
  1107.7 0.8 broadcast_in_dim.75
  1108.5 1.1 broadcast_select_fusion
  1109.6 2.0 fusion.2
  1111.7 1.0 convolution_bitcast_fusion.1
  1112.7 1.1 convolution_bitcast_fusion
  1113.8 0.7 pad_maximum_fusion
  1114.6 54.7 %all-gather.2.cloned.1.call-done = bf16[8,704,256]{2,1,0:T(8,128)(2,1)} async-done(((bf16[1,704,256]{2,1,0:T(8,128)(2,1)}), bf16[8,704,256]{2,1,0:T(8,128)(2,1)}) %all-gather.2.cloned.1.call-update) | async-done | bytes 2883600 | tf_op jit(solution)/shard_map/all_gather | solution.py:89
  1169.3 3.5 fusion
  1172.7 126.9 %all-reduce.5.cloned.1.call-done = f32[2,256,172]{1,2,0:T(8,128)} async-done(((f32[2,256,172]{1,2,0:T(8,128)}), f32[2,256,172]{1,2,0:T(8,128)}) %all-reduce.5.cloned.1.call-update) | async-done | bytes 352272 | tf_op jit(solution)/shard_map/psum | solution.py:93
  1299.6 2.0 copy.21
  1301.6 33.1 %all-reduce.3.cloned.1.call-done = f32[2,128,256]{2,1,0:T(8,128)} async-done(((f32[2,128,256]{2,1,0:T(8,128)}), f32[2,128,256]{2,1,0:T(8,128)}) %all-reduce.3.cloned.1.call-update) | async-done | bytes 262160 | tf_op jit(solution)/shard_map/psum | solution.py:92
  1334.7 1.7 copy.34
  (39 shorter events, 2.8 us)
Async XLA Ops:
  7.2 975.8 %copy-start = (bf16[2,128,256]{2,1,0:T(8,128)(2,1)S(1)}, bf16[2,128,256]{2,1,0:T(8,128)(2,1)}, u32[]{:S(2)}) copy-start(bf16[2,128,256]{2,1,0:T(8,128)(2,1)} %param.11) | copy-start | bytes 393220
  7.2 1092.4 %reduce-scatter.2.cloned.1.call-start = ((), (), s32[]{:S(2)}) async-start(), calls=%async_computation.1 | async-start | bytes 6488064 | tf_op jit(solution)/shard_map/reduce_scatter | solution.py:81
  986.4 0.7 copy-start.8
  986.4 4.6 copy-start.2
  986.4 182.9 %all-gather.2.cloned.1.call-start = ((), (), s32[]{:S(2)}) async-start(), calls=%async_computation.2 | async-start | bytes 3244032 | tf_op jit(solution)/shard_map/all_gather | solution.py:89
  991.2 114.4 %copy-start.5 = (f32[64]{0:T(128)S(1)}, f32[64]{0:T(128)}, u32[]{:S(2)}) copy-start(f32[64]{0:T(128)} %get-tuple-element.8) | copy-start | bytes 772
  991.2 114.9 %copy-start.6 = (s32[64]{0:T(128)S(1)}, s32[64]{0:T(128)}, u32[]{:S(2)}) copy-start(s32[64]{0:T(128)} %get-tuple-element.14) | copy-start | bytes 772
  991.2 114.9 %copy-start.7 = (f32[64]{0:T(128)S(1)}, f32[64]{0:T(128)}, u32[]{:S(2)}) copy-start(f32[64]{0:T(128)} %compare_convert_fusion) | copy-start | bytes 772
  1100.8 1.0 copy-start.1
  1105.6 2.0 copy-start.4
  1106.3 0.6 copy-start.3
  1111.6 188.0 %all-reduce.5.cloned.1.call-start = ((), (), s32[]{:S(2)}) async-start(), calls=%async_computation.4 | async-start | bytes 720896 | tf_op jit(solution)/shard_map/psum | solution.py:93
  1114.5 220.2 %all-reduce.3.cloned.1.call-start = ((), (), s32[]{:S(2)}) async-start(), calls=%async_computation.3 | async-start | bytes 524288 | tf_op jit(solution)/shard_map/psum | solution.py:92
Sparse Core Ops, SparseCore 0:
  986.5 113.0 reduce-scatter.1
  1111.7 57.4 all-gather.1
  1174.6 124.9 all-reduce.4
  1302.5 32.1 all-reduce.2
where the time goes:
time: 1350 us; the launch traced here: 1340 us
  local copies, waits for them, and re-layouts  945 us (70%)
  waiting for transfers between devices  323 us (24%)
  other arithmetic  49.5 us (4%)
  between operations  14.6 us (1%)
    gather x1, local copies, waits for them, and re-layouts, shards(): node_table[hop2_ids].reshape(groups, row_total, -1, slice_width)  836 us
    psum x1, waiting for transfers between devices, shards(): grad_second = lax.psum(grad_second, ('feat', 'dp'))  127 us
    reduce_scatter x1, waiting for transfers between devices, shards(): lax.psum_scatter(jnp.einsum('fbr,fh->brh', local_inputs, local_weights, p...  108 us
    all_gather x1, waiting for transfers between devices, shards(): lax.all_gather(dpreact[None], 'feat', axis=0, tiled=True)  54.7 us
    unnamed x21, local copies, waits for them, and re-layouts  48.6 us
    reduce_sum x1, other arithmetic, shards(): jnp.sum(jnp.where(keep_two[:, :, :, None], neighbours.astype(jnp.float32)...  33.4 us
    psum x1, waiting for transfers between devices, shards(): grad_first = lax.psum(grad_slice, 'dp')  33.1 us
    convert_element_type x1, local copies, waits for them, and re-layouts, shards(): neighbours.astype(jnp.float32)  28.7 us
  transfers between devices with their start and end apart: 4, of which 4 were waited for; matrix products, arithmetic and copies ran while one was open for 1% of the time, Pallas kernels for 0%

commit v1 on v0

v1 whole, which is shorter than its diff:
```python
import functools

import jax
import jax.numpy as jnp
from jax import lax
from jax.experimental import pallas as pl
from jax.experimental.pallas import tpu as pltpu
from jax.sharding import PartitionSpec as P

LANES = 128
TILE = 16
CODE_BITS = 5
CODES = 1 << CODE_BITS
UNROLL = 4
BLOCK = 256


def round_up(value, step):
    return (value + step - 1) // step * step


def plan_rows(hop1_count, hop2_count, sizes, kept):
    groups, seed_total = hop1_count.shape
    row_total = hop2_count.shape[1]
    fanout = (row_total - seed_total) // seed_total
    live = jnp.arange(seed_total)[None, :] < sizes[:, None]
    near = jnp.arange(fanout)[None, None, :] < jnp.where(live, hop1_count, 0)[:, :, None]
    used = jnp.concatenate([live, near.reshape(groups, -1)], axis=1)
    count = jnp.where(used, hop2_count, 0)
    row = jnp.arange(row_total)[None, :]
    mixed = count * row_total + (row_total - 1 - row)
    place = jnp.sum((mixed[:, None, :] > mixed[:, :, None]).astype(jnp.int32), axis=2)
    packed = row * 16 + count
    order = jnp.sum(
        jnp.where(place[:, None, :] == jnp.arange(kept)[None, :, None], packed[:, None, :], 0), axis=2
    )
    enough = jnp.sum(
        (count[:, None, :] >= jnp.arange(16)[None, :, None]).astype(jnp.int32), axis=2
    )
    return order, enough


def slot_codes(ids, live):
    return (ids // TILE) * CODES + jnp.where(live, ids % TILE, TILE)


def gather_kernel(
    loads, fanout, capacity, enough_ref, order_ref, own_ref, near_ref, count_ref, feats_ref, weights_ref,
    inputs_ref, preact_ref, table_ref, mask_ref, own_sum_ref, near_sum_ref,
):
    step = pl.program_id(0)
    width, chunk = feats_ref.shape
    padded = table_ref.shape[1]

    @pl.when(step == 0)
    def _():
        shape = mask_ref.shape
        code = lax.broadcasted_iota(jnp.int32, shape, 0)
        line = lax.broadcasted_iota(jnp.int32, shape, 1)
        mask_ref[...] = jnp.where(code == line, 1.0, 0.0).astype(jnp.bfloat16)
        own_sum_ref[...] = jnp.zeros_like(own_sum_ref)
        near_sum_ref[...] = jnp.zeros_like(near_sum_ref)

    @pl.when(step < loads)
    def _():
        down = lax.broadcasted_iota(jnp.int32, (BLOCK, BLOCK), 0)
        across = lax.broadcasted_iota(jnp.int32, (BLOCK, BLOCK), 1)
        identity = jnp.where(down == across, 1.0, 0.0).astype(jnp.bfloat16)
        for part in range(chunk // BLOCK):
            piece = feats_ref[:, part * BLOCK : (part + 1) * BLOCK]
            if padded > width:
                piece = jnp.concatenate([piece, jnp.zeros((padded - width, BLOCK), piece.dtype)], axis=0)
            turned = lax.dot_general(
                identity, piece, (((1,), (1,)), ((), ())), preferred_element_type=jnp.float32
            )
            start = pl.multiple_of(step * chunk + part * BLOCK, BLOCK)
            table_ref[pl.ds(start, BLOCK), :] = turned.astype(jnp.bfloat16)

    @pl.when(step >= loads)
    def _():
        tiles = table_ref.reshape(table_ref.shape[0] // TILE, TILE, padded)

        def fetch(code):
            return (tiles[code >> CODE_BITS] * mask_ref[code & (CODES - 1)]).astype(jnp.float32)

        def fold(value):
            return value[: TILE // 2] + value[TILE // 2 :]

        def gather_rows(slots, number, carry):
            first = number * UNROLL
            rows = [order_ref[0, 0, first + i] >> 4 for i in range(UNROLL)]
            for i, row in enumerate(rows):
                start = pl.multiple_of((first + i) * 8, 8)
                own_sum_ref[pl.ds(start, 8), :] = fold(fetch(own_ref[0, 0, row]))
                total = fetch(near_ref[0, 0, row * fanout])
                for slot in range(1, slots):
                    total = total + fetch(near_ref[0, 0, row * fanout + slot])
                near_sum_ref[pl.ds(start, 8), :] = fold(total)
            return carry

        begin = 0
        for slots in range(fanout, 0, -1):
            end = lax.div(enough_ref[0, 0, slots] + UNROLL - 1, UNROLL)
            lax.fori_loop(begin, end, functools.partial(gather_rows, slots), 0)
            begin = end

        def collect(ref):
            total = ref[pl.ds(0, capacity, stride=8), :]
            for line in range(1, 8):
                total = total + ref[pl.ds(line, capacity, stride=8), :]
            return total

        counts = jnp.transpose(jnp.broadcast_to(count_ref[0], (padded, count_ref.shape[2])))[:capacity]
        own = collect(own_sum_ref).astype(jnp.bfloat16)[:, :width]
        near = (collect(near_sum_ref) / counts).astype(jnp.bfloat16)[:, :width]
        inputs_ref[0] = jnp.concatenate([own, near], axis=1)
        preact_ref[0] = jnp.dot(own, weights_ref[0], preferred_element_type=jnp.float32) + jnp.dot(
            near, weights_ref[1], preferred_element_type=jnp.float32
        )


def gather_layer(node_feats, first_layer, enough, order, own_codes, near_codes, capacity):
    width, nodes = node_feats.shape
    groups, kept = order.shape
    hidden_width = first_layer.shape[2]
    row_total = own_codes.shape[1]
    fanout = near_codes.shape[1] // row_total
    padded = max(width, LANES)
    chunk = min(nodes, 8192)
    loads = nodes // chunk
    counts = jnp.maximum(order % 16, 1).astype(jnp.float32)

    def per_group(length):
        return pl.BlockSpec(
            (1, 1, length), lambda step: (jnp.maximum(step - loads, 0), 0, 0), memory_space=pltpu.SMEM
        )

    return pl.pallas_call(
        functools.partial(gather_kernel, loads, fanout, capacity),
        grid=(loads + groups,),
        in_specs=[
            per_group(16),
            per_group(kept),
            per_group(row_total),
            per_group(row_total * fanout),
            pl.BlockSpec((1, 1, kept), lambda step: (jnp.maximum(step - loads, 0), 0, 0)),
            pl.BlockSpec((width, chunk), lambda step: (0, jnp.minimum(step, loads - 1))),
            pl.BlockSpec((2, width, hidden_width), lambda step: (0, 0, 0)),
        ],
        out_specs=[
            pl.BlockSpec((1, capacity, 2 * width), lambda step: (jnp.maximum(step - loads, 0), 0, 0)),
            pl.BlockSpec((1, capacity, hidden_width), lambda step: (jnp.maximum(step - loads, 0), 0, 0)),
        ],
        out_shape=[
            jax.ShapeDtypeStruct((groups, capacity, 2 * width), jnp.bfloat16),
            jax.ShapeDtypeStruct((groups, capacity, hidden_width), jnp.float32),
        ],
        scratch_shapes=[
            pltpu.VMEM((nodes, padded), jnp.bfloat16),
            pltpu.VMEM((CODES, TILE, padded), jnp.bfloat16),
            pltpu.VMEM((capacity * 8, padded), jnp.float32),
            pltpu.VMEM((capacity * 8, padded), jnp.float32),
        ],
        compiler_params=pltpu.CompilerParams(vmem_limit_bytes=52 * 2**20),
        name="gather_layer",
    )(
        enough[:, None, :], order[:, None, :], own_codes[:, None, :], near_codes[:, None, :],
        counts[:, None, :], node_feats, first_layer,
    )


def upper_kernel(fanout, size_ref, preact_ref, layer_ref, row_ref, count_ref, label_ref, out_ref):
    seed_total = count_ref.shape[0]
    capacity, hidden_width = preact_ref.shape
    classes = layer_ref.shape[2]
    size = size_ref[0]
    seed = lax.broadcasted_iota(jnp.int32, (seed_total, capacity), 0)
    row = jnp.broadcast_to(row_ref[...], (seed_total, capacity))
    first = seed_total + seed * fanout
    is_seed = jnp.where(row == seed, 1.0, 0.0).astype(jnp.bfloat16)
    is_near = jnp.where((row >= first) & (row < first + fanout), 1.0, 0.0).astype(jnp.bfloat16)
    preact = preact_ref[...]
    hidden = jnp.maximum(preact, 0.0).astype(jnp.bfloat16)
    counts = count_ref[...]
    seed_hidden = jnp.dot(is_seed, hidden, preferred_element_type=jnp.float32).astype(jnp.bfloat16)
    near_mean = (jnp.dot(is_near, hidden, preferred_element_type=jnp.float32) / counts).astype(jnp.bfloat16)
    logits = jnp.dot(seed_hidden, layer_ref[0], preferred_element_type=jnp.float32) + jnp.dot(
        near_mean, layer_ref[1], preferred_element_type=jnp.float32
    )
    exponent = jnp.exp(logits - jnp.max(logits, axis=1, keepdims=True))
    probabilities = exponent / jnp.sum(exponent, axis=1, keepdims=True)
    label = jnp.broadcast_to(label_ref[...], (seed_total, classes))
    onehot = jnp.where(label == lax.broadcasted_iota(jnp.int32, (seed_total, classes), 1), 1.0, 0.0)
    valid = lax.broadcasted_iota(jnp.int32, (seed_total, classes), 0) < size
    dlogits = jnp.where(valid, (probabilities - onehot) / size.astype(jnp.float32), 0.0).astype(jnp.bfloat16)
    last = (((1,), (1,)), ((), ()))
    back_seed = lax.dot_general(dlogits, layer_ref[0], last, preferred_element_type=jnp.float32)
    back_near = lax.dot_general(dlogits, layer_ref[1], last, preferred_element_type=jnp.float32) / counts
    rows = (((0,), (0,)), ((), ()))
    spread = lax.dot_general(is_seed, back_seed.astype(jnp.bfloat16), rows, preferred_element_type=jnp.float32)
    spread = spread + lax.dot_general(
        is_near, back_near.astype(jnp.bfloat16), rows, preferred_element_type=jnp.float32
    )
    out_ref[:capacity] = jnp.where(preact > 0, spread, 0.0).astype(jnp.bfloat16)
    out_ref[capacity : capacity + seed_total] = seed_hidden
    out_ref[capacity + seed_total : capacity + 2 * seed_total] = near_mean
    out_ref[capacity + 2 * seed_total :] = jnp.zeros((seed_total, hidden_width), jnp.bfloat16)
    out_ref[capacity + 2 * seed_total :, :classes] = dlogits


def upper_layers(preact, second_layer, order, hop1_count, label_ids, size, fanout):
    seed_total = hop1_count.shape[0]
    capacity, hidden_width = preact.shape
    row = jnp.where(order % 16 > 0, order // 16, -1)[None, :]
    vmem = pl.BlockSpec(memory_space=pltpu.VMEM)
    return pl.pallas_call(
        functools.partial(upper_kernel, fanout),
        in_specs=[pl.BlockSpec(memory_space=pltpu.SMEM)] + [vmem] * 5,
        out_specs=vmem,
        out_shape=jax.ShapeDtypeStruct((capacity + 3 * seed_total, hidden_width), jnp.bfloat16),
        compiler_params=pltpu.CompilerParams(vmem_limit_bytes=24 * 2**20),
        name="upper_layers",
    )(
        size[None], preact, second_layer, row, hop1_count.astype(jnp.float32)[:, None], label_ids[:, None]
    )


def shards(
    node_feats,
    first_layer,
    second_layer,
    seed_ids,
    hop1_ids,
    hop1_count,
    hop2_ids,
    hop2_count,
    batch_sizes,
    label_ids,
):
    groups, seed_total = seed_ids.shape
    row_total = hop2_count.shape[1]
    fanout = hop1_ids.shape[1] // seed_total
    slots = hop2_ids.shape[1] // row_total
    slice_width = node_feats.shape[0]
    hidden_width = first_layer.shape[2]
    classes = second_layer.shape[2]
    capacity = round_up(seed_total + row_total // 2, 16)
    kept = round_up(capacity, LANES)
    column_rank = lax.axis_index("feat")
    group_start = lax.axis_index("dp") * groups
    sizes = lax.dynamic_slice_in_dim(batch_sizes, group_start, groups)
    order, enough = plan_rows(hop1_count, hop2_count, sizes, kept)
    own_codes = slot_codes(jnp.concatenate([seed_ids, hop1_ids], axis=1), True)
    near_codes = slot_codes(
        hop2_ids.reshape(groups, row_total, slots),
        jnp.arange(slots)[None, None, :] < hop2_count[:, :, None],
    ).reshape(groups, row_total * slots)
    inputs, partial = gather_layer(
        node_feats, first_layer, enough, order, own_codes, near_codes, capacity
    )
    preact = lax.psum_scatter(partial, "feat", scatter_dimension=0, tiled=True)[0]

    def own(array):
        return lax.dynamic_index_in_dim(array, column_rank, 0, keepdims=False)

    sent = upper_layers(
        preact, second_layer, own(order)[:capacity], own(hop1_count), own(label_ids), own(sizes), fanout
    )
    every = lax.all_gather(sent[None], "feat", axis=0, tiled=True)
    grad_first = jnp.einsum(
        "brf,brh->fh", inputs, every[:, :capacity], preferred_element_type=jnp.float32
    )
    units = every[:, capacity : capacity + 2 * seed_total].reshape(groups, 2, seed_total, hidden_width)
    dlogits = every[:, capacity + 2 * seed_total :, :classes]
    grad_second = jnp.einsum("blsh,bsc->lhc", units, dlogits, preferred_element_type=jnp.float32)
    grad_first = lax.psum(grad_first.reshape(2, slice_width, hidden_width), "dp")
    grad_second = lax.psum(grad_second, "dp")
    return (grad_first, grad_second)


def solution(mesh):
    return jax.shard_map(
        shards,
        mesh=mesh,
        in_specs=(
            P("feat", None),
            P(None, "feat", None),
            P(),
            P("dp", None),
            P("dp", None),
            P("dp", None),
            P("dp", None),
            P("dp", None),
            P(),
            P("dp", None),
        ),
        out_specs=(P(None, "feat", None), P()),
        check_vma=False,
    )
```

time: 1350 us -> 285 us (0.21)
  local copies, waits for them, and re-layouts: 945 us -> 13.1 us
  waiting for transfers between devices: 323 us -> 162 us
  Pallas kernels: 0 us -> 79.4 us
  other arithmetic: 49.5 us -> 7.78 us
    gather x2 -> x0, local copies, waits for them, and re-layouts: 864 us -> none  [the longest x1 836 us: shards(): node_table[hop2_ids].reshape(groups, row_total, -1, slice_width)]
    psum x2 -> x1, waiting for transfers between devices: 160 us -> 32.5 us  [shards(): lax.psum(grad_first.reshape(2, slice_width, hidden_width), 'dp')]
    pallas_call x0 -> x2, Pallas kernels: none -> 79.4 us  [the longest x1 77.1 us: gather_layer(): pl.pallas_call(functools.partial(gather_kernel, loads, fanout, capacity),...]
    unnamed x21 -> x17, local copies, waits for them, and re-layouts: 48.6 us -> 5.42 us
    reduce_scatter x1, waiting for transfers between devices: 108 us -> 77.1 us  [shards(): lax.psum_scatter(partial, 'feat', scatter_dimension=0, tiled=True)[0]]
    convert_element_type x2 -> x1, local copies, waits for them, and re-layouts: 30.9 us -> 0.1 us  [upper_layers(): hop1_count.astype(jnp.float32)[:, None]]
    reduce_sum x3, other arithmetic: 35.2 us -> 4.83 us  [the longest x1 2.46 us: plan_rows(): jnp.sum((mixed[:, None, :] > mixed[:, :, None]).astype(jnp.int32), axis=2)]
  transfers between devices with their start and end apart: 4 -> 3, of which waited for: 4 -> 3; matrix products, arithmetic and copies ran while one was open for 1% -> 1% of each run, Pallas kernels for 0% -> 0%
where the time goes in v1:
time: 285 us; the launch traced here: 282 us
  waiting for transfers between devices  162 us (57%)
  Pallas kernels  79.4 us (28%)
  between operations  14 us (5%)
  local copies, waits for them, and re-layouts  13.1 us (5%)
  other arithmetic  7.78 us (3%)
  matrix products  4.8 us (2%)
    reduce_scatter x1, waiting for transfers between devices, shards(): lax.psum_scatter(partial, 'feat', scatter_dimension=0, tiled=True)[0]  77.1 us
    pallas_call x1, Pallas kernels, gather_layer(): pl.pallas_call(functools.partial(gather_kernel, loads, fanout, capacity),...  77.1 us
    all_gather x1, waiting for transfers between devices, shards(): every = lax.all_gather(sent[None], 'feat', axis=0, tiled=True)  52.8 us
    psum x1, waiting for transfers between devices, shards(): lax.psum(grad_first.reshape(2, slice_width, hidden_width), 'dp')  32.5 us
  transfers between devices with their start and end apart: 3, of which 3 were waited for; matrix products, arithmetic and copies ran while one was open for 1% of the time, Pallas kernels for 0%

profile of v1, /device:TPU:0, one launch (start us, length us, event | category | flops | bytes accessed | tf_op | source)
XLA Modules:
  0.0 281.5 jit_solution(10964260899611268668)
XLA Ops:
  7.2 0.7 dynamic_slice.20
  8.0 0.8 broadcast_select_fusion
  8.8 0.1 lt.97
  8.9 0.2 lt.98
  9.1 0.1 lt.95
  9.3 0.8 multiply_add_fusion
  10.1 0.2 convert_reduce_fusion.1
  10.3 2.5 convert_reduce_fusion
  12.8 2.1 select_reduce_fusion
  15.0 0.7 concatenate.43
  15.8 1.6 lt.104
  17.4 1.9 lt.105
  19.3 0.3 lt.102
  19.6 0.2 fusion.3
  19.8 0.2 add.115.near_ref
  20.0 0.2 fusion.9.own_ref
  20.3 77.1 %gather_layer.1 = (bf16[8,416,256]{2,1,0:T(8,128)(2,1)}, f32[8,416,256]{2,1,0:T(8,128)}) custom-call(s32[8,1,16]{2,1,0:T(1,128)S(1)} %bitcast.24, s32[8,1,512]{2,1,0:T(1,128)S(1)} %broadcast_in_dim.39.order_ref, s32[8,1,704]{2,1,0:T(1,128)S(1)} %fusion.9.own_ref, s32[8,1,7040]{2,1,0:T(1,128)S(1)} %add.115.near_ref, f32[8,1,512]{2,1,0:T(1,128)S(1)} %fusion.11.count_ref, ...), custom_call_target="tpu_custom_call" | custom-call | tf_op jit(solution)/shard_map/gather_layer/pallas_call | solution.py:138
  97.4 0.5 copy-done.6
  98.0 0.6 dynamic_slice.22.size_ref
  98.6 0.2 copy.29.layer_ref
  98.8 0.7 fusion.13
  99.5 0.1 copy.30.count_ref
  99.7 77.1 %reduce-scatter.2.cloned.1.call-done = f32[1,416,256]{2,1,0:T(8,128)} async-done(((f32[8,416,256]{2,1,0:T(8,128)}), f32[1,416,256]{2,1,0:T(8,128)}) %reduce-scatter.2.cloned.1.call-update) | async-done | bytes 426000 | tf_op jit(solution)/shard_map/reduce_scatter | solution.py:261
  176.8 1.0 copy-done
  177.8 2.3 upper_layers.1
  180.2 52.8 %all-gather.3.cloned.1.call-done = bf16[4864,256]{1,0:T(8,128)(2,1)} async-done(((bf16[608,256]{1,0:T(8,128)(2,1)}), bf16[4864,256]{1,0:T(8,128)(2,1)}) %all-gather.3.cloned.1.call-update) | async-done | bytes 2490384 | tf_op jit(solution)/shard_map/all_gather | solution.py:269
  232.9 1.1 slice.18
  234.0 2.8 %fusion = f32[256,256,1]{1,0,2:T(8,128)} fusion(bf16[8,416,256]{2,1,0:T(8,128)(2,1)S(1)} %copy-done.5, bf16[8,608,256]{2,1,0:T(8,128)(2,1)} %bitcast.28), kind=kOutput, calls=%fused_computation.3 | convolution fusion | flops 436207616 | bytes 3670016 | tf_op jit(solution)/shard_map/brf,brh->fh/dot_general | solution.py:270
  236.8 2.0 convolution_bitcast_fusion
  238.8 32.5 %all-reduce.3.cloned.1.call-done = (f32[2,128,256]{2,1,0:T(8,128)}, f32[2,256,172]{1,2,0:T(8,128)}) async-done(((f32[2,128,256]{2,1,0:T(8,128)}, f32[2,256,172]{1,2,0:T(8,128)}), (f32[2,128,256]{2,1,0:T(8,128)}, f32[2,256,172]{1,2,0:T(8,128)})) %all-reduce.3.cloned.1.call-update) | async-done | bytes 614416 | tf_op jit(solution)/shard_map/psum | solution.py:276
  271.3 2.0 copy.32
  273.3 1.7 copy.36
  (29 shorter events, 0.5 us)
Async XLA Ops:
  7.2 169.6 %reduce-scatter.2.cloned.1.call-start = ((), (), s32[]{:S(2)}) async-start(), calls=%async_computation.1 | async-start | bytes 3833856 | tf_op jit(solution)/shard_map/reduce_scatter | solution.py:261
  15.8 3.8 %copy-start.2 = (s32[8,7040]{1,0:T(8,128)S(1)}, s32[8,7040]{1,0:T(8,128)}, u32[]{:S(2)}) copy-start(s32[8,7040]{1,0:T(8,128)} %param.16) | copy-start | bytes 675844
  17.4 2.6 copy-start.4
  17.4 2.9 %copy-start.1 = (bf16[2,128,256]{2,1,0:T(8,128)(2,1)S(1)}, bf16[2,128,256]{2,1,0:T(8,128)(2,1)}, u32[]{:S(2)}) copy-start(bf16[2,128,256]{2,1,0:T(8,128)(2,1)} %weights_ref.1) | copy-start | bytes 393220
  97.3 0.7 copy-start.6
  97.3 1.2 copy-start.3
  97.3 136.7 %copy-start.5 = (bf16[8,416,256]{2,1,0:T(8,128)(2,1)S(1)}, bf16[8,416,256]{2,1,0:T(8,128)(2,1)}, u32[]{:S(2)}) copy-start(bf16[8,416,256]{2,1,0:T(8,128)(2,1)} %get-tuple-element.4) | copy-start | bytes 5111812
  97.4 135.6 %all-gather.3.cloned.1.call-start = ((), (), s32[]{:S(2)}) async-start(), calls=%async_computation.2 | async-start | bytes 2801664 | tf_op jit(solution)/shard_map/all_gather | solution.py:269
  176.8 1.0 copy-start
  180.1 91.2 %all-reduce.3.cloned.1.call-start = ((), (), s32[]{:S(2)}) async-start(), calls=%async_computation.3 | async-start | bytes 1245184 | tf_op jit(solution)/shard_map/psum | solution.py:276
Sparse Core Ops, SparseCore 0:
  97.5 79.2 reduce-scatter.1
  180.2 52.6 all-gather.2
  239.0 32.3 all-reduce.2

commit v2 on v1

--- a/solution.py
+++ b/solution.py
@@ -45,9 +45,9 @@
 
 
 def gather_kernel(
-    loads, fanout, capacity, enough_ref, order_ref, own_ref, near_ref, count_ref, feats_ref, weights_ref,
-    inputs_ref, preact_ref, table_ref, mask_ref, own_sum_ref, near_sum_ref,
+    loads, fanout, capacity, turn_ref, enough_ref, order_ref, own_ref, near_ref, count_ref, feats_ref, *rest
 ):
+    *inputs_refs, table_ref, mask_ref, own_sum_ref, near_sum_ref = rest
     step = pl.program_id(0)
     width, chunk = feats_ref.shape
     padded = table_ref.shape[1]
@@ -113,16 +113,17 @@
         counts = jnp.transpose(jnp.broadcast_to(count_ref[0], (padded, count_ref.shape[2])))[:capacity]
         own = collect(own_sum_ref).astype(jnp.bfloat16)[:, :width]
         near = (collect(near_sum_ref) / counts).astype(jnp.bfloat16)[:, :width]
-        inputs_ref[0] = jnp.concatenate([own, near], axis=1)
-        preact_ref[0] = jnp.dot(own, weights_ref[0], preferred_element_type=jnp.float32) + jnp.dot(
-            near, weights_ref[1], preferred_element_type=jnp.float32
-        )
-
-
-def gather_layer(node_feats, first_layer, enough, order, own_codes, near_codes, capacity):
+        both = jnp.concatenate([own, near], axis=1)
+        for place, inputs_ref in enumerate(inputs_refs):
+
+            @pl.when(step == loads + place)
+            def _():
+                inputs_ref[...] = both
+
+
+def gather_layer(node_feats, turn, enough, order, own_codes, near_codes, capacity):
     width, nodes = node_feats.shape
     groups, kept = order.shape
-    hidden_width = first_layer.shape[2]
     row_total = own_codes.shape[1]
     fanout = near_codes.shape[1] // row_total
     padded = max(width, LANES)
@@ -130,56 +131,59 @@
     loads = nodes // chunk
     counts = jnp.maximum(order % 16, 1).astype(jnp.float32)
 
+    def group_of(step, turn_ref):
+        return (turn_ref[jnp.maximum(step - loads, 0)], 0, 0)
+
     def per_group(length):
-        return pl.BlockSpec(
-            (1, 1, length), lambda step: (jnp.maximum(step - loads, 0), 0, 0), memory_space=pltpu.SMEM
-        )
+        return pl.BlockSpec((1, 1, length), group_of, memory_space=pltpu.SMEM)
 
     return pl.pallas_call(
         functools.partial(gather_kernel, loads, fanout, capacity),
-        grid=(loads + groups,),
-        in_specs=[
-            per_group(16),
-            per_group(kept),
-            per_group(row_total),
-            per_group(row_total * fanout),
-            pl.BlockSpec((1, 1, kept), lambda step: (jnp.maximum(step - loads, 0), 0, 0)),
-            pl.BlockSpec((width, chunk), lambda step: (0, jnp.minimum(step, loads - 1))),
-            pl.BlockSpec((2, width, hidden_width), lambda step: (0, 0, 0)),
-        ],
-        out_specs=[
-            pl.BlockSpec((1, capacity, 2 * width), lambda step: (jnp.maximum(step - loads, 0), 0, 0)),
-            pl.BlockSpec((1, capacity, hidden_width), lambda step: (jnp.maximum(step - loads, 0), 0, 0)),
-        ],
-        out_shape=[
-            jax.ShapeDtypeStruct((groups, capacity, 2 * width), jnp.bfloat16),
-            jax.ShapeDtypeStruct((groups, capacity, hidden_width), jnp.float32),
-        ],
-        scratch_shapes=[
-            pltpu.VMEM((nodes, padded), jnp.bfloat16),
-            pltpu.VMEM((CODES, TILE, padded), jnp.bfloat16),
-            pltpu.VMEM((capacity * 8, padded), jnp.float32),
-            pltpu.VMEM((capacity * 8, padded), jnp.float32),
-        ],
+        grid_spec=pltpu.PrefetchScalarGridSpec(
+            num_scalar_prefetch=1,
+            grid=(loads + groups,),
+            in_specs=[
+                per_group(16),
+                per_group(kept),
+                per_group(row_total),
+                per_group(row_total * fanout),
+                pl.BlockSpec((1, 1, kept), group_of),
+                pl.BlockSpec((width, chunk), lambda step, turn_ref: (0, jnp.minimum(step, loads - 1))),
+            ],
+            out_specs=[pl.BlockSpec((capacity, 2 * width), lambda step, turn_ref: (0, 0))] * groups,
+            scratch_shapes=[
+                pltpu.VMEM((nodes, padded), jnp.bfloat16),
+                pltpu.VMEM((CODES, TILE, padded), jnp.bfloat16),
+                pltpu.VMEM((capacity * 8, padded), jnp.float32),
+                pltpu.VMEM((capacity * 8, padded), jnp.float32),
+            ],
+        ),
+        out_shape=[jax.ShapeDtypeStruct((capacity, 2 * width), jnp.bfloat16)] * groups,
         compiler_params=pltpu.CompilerParams(vmem_limit_bytes=52 * 2**20),
         name="gather_layer",
     )(
-        enough[:, None, :], order[:, None, :], own_codes[:, None, :], near_codes[:, None, :],
-        counts[:, None, :], node_feats, first_layer,
-    )
-
-
-def upper_kernel(fanout, size_ref, preact_ref, layer_ref, row_ref, count_ref, label_ref, out_ref):
+        turn, enough[:, None, :], order[:, None, :], own_codes[:, None, :], near_codes[:, None, :],
+        counts[:, None, :], node_feats,
+    )
+
+
+def upper_kernel(fanout, own_ref, weights_ref, layer_ref, row_ref, count_ref, label_ref, *rest):
+    *inputs_refs, out_ref = rest
     seed_total = count_ref.shape[0]
-    capacity, hidden_width = preact_ref.shape
+    capacity = inputs_refs[0].shape[0]
+    hidden_width = weights_ref.shape[2]
     classes = layer_ref.shape[2]
-    size = size_ref[0]
+    size = own_ref[0]
     seed = lax.broadcasted_iota(jnp.int32, (seed_total, capacity), 0)
     row = jnp.broadcast_to(row_ref[...], (seed_total, capacity))
     first = seed_total + seed * fanout
     is_seed = jnp.where(row == seed, 1.0, 0.0).astype(jnp.bfloat16)
     is_near = jnp.where((row >= first) & (row < first + fanout), 1.0, 0.0).astype(jnp.bfloat16)
-    preact = preact_ref[...]
+    preact = jnp.dot(inputs_refs[0][...], weights_ref[own_ref[1]], preferred_element_type=jnp.float32)
+    for place in range(1, len(inputs_refs)):
+        preact = preact + jnp.dot(
+            inputs_refs[place][...], weights_ref[own_ref[1 + place]], preferred_element_type=jnp.float32
+        )
     hidden = jnp.maximum(preact, 0.0).astype(jnp.bfloat16)
     counts = count_ref[...]
     seed_hidden = jnp.dot(is_seed, hidden, preferred_element_type=jnp.float32).astype(jnp.bfloat16)
@@ -208,21 +212,123 @@
     out_ref[capacity + 2 * seed_total :, :classes] = dlogits
 
 
-def upper_layers(preact, second_layer, order, hop1_count, label_ids, size, fanout):
+def upper_layers(inputs, sources, weights, second_layer, order, hop1_count, label_ids, size, fanout):
     seed_total = hop1_count.shape[0]
-    capacity, hidden_width = preact.shape
+    capacity = inputs[0].shape[0]
+    hidden_width = weights.shape[2]
     row = jnp.where(order % 16 > 0, order // 16, -1)[None, :]
     vmem = pl.BlockSpec(memory_space=pltpu.VMEM)
     return pl.pallas_call(
         functools.partial(upper_kernel, fanout),
-        in_specs=[pl.BlockSpec(memory_space=pltpu.SMEM)] + [vmem] * 5,
+        in_specs=[pl.BlockSpec(memory_space=pltpu.SMEM)] + [vmem] * (5 + len(inputs)),
         out_specs=vmem,
         out_shape=jax.ShapeDtypeStruct((capacity + 3 * seed_total, hidden_width), jnp.bfloat16),
-        compiler_params=pltpu.CompilerParams(vmem_limit_bytes=24 * 2**20),
+        compiler_params=pltpu.CompilerParams(vmem_limit_bytes=32 * 2**20),
         name="upper_layers",
     )(
-        size[None], preact, second_layer, row, hop1_count.astype(jnp.float32)[:, None], label_ids[:, None]
-    )
+        jnp.concatenate([size[None], sources]), weights, second_layer, row,
+        hop1_count.astype(jnp.float32)[:, None], label_ids[:, None], *inputs,
+    )
+
+
+def grad_kernel(seed_total, classes, source_ref, *rest):
+    count = (len(rest) - 2) // 2
+    inputs_refs, sent_refs = rest[:count], rest[count : 2 * count]
+    out_ref, units_ref = rest[2 * count :]
+    capacity, double = inputs_refs[0].shape
+    hidden_width = out_ref.shape[1]
+    rows = (((0,), (0,)), ((), ()))
+    first = jnp.zeros((double, hidden_width), jnp.float32)
+    for place in range(count):
+        first = first + lax.dot_general(
+            inputs_refs[place][...], sent_refs[place][:capacity], rows, preferred_element_type=jnp.float32
+        )
+        start = pl.multiple_of(source_ref[place] * seed_total, seed_total)
+        for part in range(3):
+            units_ref[part, pl.ds(start, seed_total), :] = sent_refs[place][
+                capacity + part * seed_total : capacity + (part + 1) * seed_total
+            ]
+    out_ref[:double] = first
+    for layer in range(2):
+        second = lax.dot_general(units_ref[2], units_ref[layer], rows, preferred_element_type=jnp.float32)
+        start = double + layer * round_up(classes, 8)
+        out_ref[start : start + round_up(classes, 8)] = second[: round_up(classes, 8)]
+
+
+def grad_layer(inputs, sent, sources, seed_total, classes):
+    capacity, double = inputs[0].shape
+    hidden_width = sent[0].shape[1]
+    vmem = pl.BlockSpec(memory_space=pltpu.VMEM)
+    return pl.pallas_call(
+        functools.partial(grad_kernel, seed_total, classes),
+        in_specs=[pl.BlockSpec(memory_space=pltpu.SMEM)] + [vmem] * (2 * len(inputs)),
+        out_specs=vmem,
+        out_shape=jax.ShapeDtypeStruct((double + 2 * round_up(classes, 8), hidden_width), jnp.float32),
+        scratch_shapes=[pltpu.VMEM((3, len(inputs) * seed_total, hidden_width), jnp.bfloat16)],
+        compiler_params=pltpu.CompilerParams(vmem_limit_bytes=40 * 2**20),
+        name="grad_layer",
+    )(sources, *inputs, *sent)
+
+
+def final_kernel(mine_ref, other_ref, first_ref, second_ref):
+    width = first_ref.shape[1]
+    classes = second_ref.shape[2]
+    total = mine_ref[...].astype(jnp.float32) + other_ref[...].astype(jnp.float32)
+    for layer in range(2):
+        first_ref[layer] = total[layer * width : (layer + 1) * width]
+        start = 2 * width + layer * round_up(classes, 8)
+        second_ref[layer] = jnp.transpose(total[start : start + round_up(classes, 8)])[:, :classes]
+
+
+def final_sum(mine, other, width, classes):
+    hidden_width = mine.shape[1]
+    return pl.pallas_call(
+        final_kernel,
+        out_shape=[
+            jax.ShapeDtypeStruct((2, width, hidden_width), jnp.float32),
+            jax.ShapeDtypeStruct((2, hidden_width, classes), jnp.float32),
+        ],
+        name="final_sum",
+    )(mine, other)
+
+
+def ring_of(count):
+    if count % 2:
+        return list(range(count))
+    return list(range(0, count, 2)) + list(range(count - 1, 0, -2))
+
+
+def send_along(array, ring, shift):
+    count = len(ring)
+    return lax.ppermute(array, "feat", [(ring[i], ring[(i + shift) % count]) for i in range(count)])
+
+
+def ring_gather(array, ring):
+    count = len(ring)
+    result = [array] + [None] * (count - 1)
+    ahead = behind = array
+    for hop in range(1, count // 2 + 1):
+        behind = send_along(behind, ring, 1)
+        result[count - hop] = behind
+        if 2 * hop < count:
+            ahead = send_along(ahead, ring, -1)
+            result[hop] = ahead
+    return result
+
+
+def group_sum(grads, width, classes):
+    count = lax.axis_size("dp")
+    mine = grads
+    stride = 1
+    while 2 * stride < count:
+        mine = mine + lax.ppermute(mine, "dp", [(i, i ^ stride) for i in range(count)])
+        stride *= 2
+    mine = mine.astype(jnp.bfloat16)
+    if count > 1:
+        other = lax.ppermute(mine, "dp", [(i, i ^ stride) for i in range(count)])
+    else:
+        other = jnp.zeros_like(mine)
+    return final_sum(mine, other, width, classes)
 
 
 def shards(
@@ -255,27 +361,24 @@
         hop2_ids.reshape(groups, row_total, slots),
         jnp.arange(slots)[None, None, :] < hop2_count[:, :, None],
     ).reshape(groups, row_total * slots)
-    inputs, partial = gather_layer(
-        node_feats, first_layer, enough, order, own_codes, near_codes, capacity
-    )
-    preact = lax.psum_scatter(partial, "feat", scatter_dimension=0, tiled=True)[0]
+    count = lax.axis_size("feat")
+    ring = ring_of(count)
+    turns = jnp.array([[ring[(ring.index(i) + t) % count] for t in range(count)] for i in range(count)], jnp.int32)
+    turn = lax.dynamic_index_in_dim(turns, column_rank, 0, keepdims=False)
+    weights = lax.all_gather(first_layer.reshape(2 * slice_width, hidden_width), "feat", axis=0)
+    inputs = gather_layer(node_feats, turn, enough, order, own_codes, near_codes, capacity)
+    received = [inputs[0]] + [send_along(inputs[t], ring, t) for t in range(1, count)]
+    behind = jnp.concatenate([turn[:1], turn[:0:-1]])
 
     def own(array):
         return lax.dynamic_index_in_dim(array, column_rank, 0, keepdims=False)
 
     sent = upper_layers(
-        preact, second_layer, own(order)[:capacity], own(hop1_count), own(label_ids), own(sizes), fanout
-    )
-    every = lax.all_gather(sent[None], "feat", axis=0, tiled=True)
-    grad_first = jnp.einsum(
-        "brf,brh->fh", inputs, every[:, :capacity], preferred_element_type=jnp.float32
-    )
-    units = every[:, capacity : capacity + 2 * seed_total].reshape(groups, 2, seed_total, hidden_width)
-    dlogits = every[:, capacity + 2 * seed_total :, :classes]
-    grad_second = jnp.einsum("blsh,bsc->lhc", units, dlogits, preferred_element_type=jnp.float32)
-    grad_first = lax.psum(grad_first.reshape(2, slice_width, hidden_width), "dp")
-    grad_second = lax.psum(grad_second, "dp")
-    return (grad_first, grad_second)
+        received, behind, weights, second_layer, own(order)[:capacity], own(hop1_count), own(label_ids),
+        own(sizes), fanout,
+    )
+    grads = grad_layer(inputs, ring_gather(sent, ring), turn, seed_total, classes)
+    return tuple(group_sum(grads, slice_width, classes))
 
 
 def solution(mesh):

time: 285 us -> 206 us (0.72)
  waiting for transfers between devices: 162 us -> 51.7 us
  starting transfers between devices: 0.12 us -> 38.5 us
  matrix products: 4.8 us -> 0 us
  Pallas kernels: 79.4 us -> 75.9 us
  other arithmetic: 7.78 us -> 10.9 us
    reduce_scatter x1 -> x0, waiting for transfers between devices: 77.1 us -> none  [shards(): lax.psum_scatter(partial, 'feat', scatter_dimension=0, tiled=True)[0]]
    all_gather x1, waiting for transfers between devices: 52.8 us -> 0.01 us  [shards(): lax.all_gather(first_layer.reshape(2 * slice_width, hidden_width), 'feat'...]
    ppermute x0 -> x16, waiting for transfers between devices: none -> 51 us  [the longest x14 41.3 us: send_along(): lax.ppermute(array, 'feat', [(ring[i], ring[(i + shift) % count]) for i i...]
    ppermute x0 -> x16, starting transfers between devices: none -> 38.5 us  [the longest x14 35.5 us: send_along(): lax.ppermute(array, 'feat', [(ring[i], ring[(i + shift) % count]) for i i...]
    psum x1 -> x0, waiting for transfers between devices: 32.5 us -> none  [shards(): lax.psum(grad_first.reshape(2, slice_width, hidden_width), 'dp')]
    pallas_call x1, Pallas kernels: 77.1 us -> 69.8 us  [gather_layer(): pl.pallas_call(functools.partial(gather_kernel, loads, fanout, capacity),...]
    dot_general x2 -> x0, matrix products: 4.8 us -> none  [the longest x1 2.82 us: shards(): jnp.einsum('brf,brh->fh', inputs, every[:, :capacity], preferred_element_...]
    pallas_call x0 -> x2, Pallas kernels: none -> 3.59 us  [the longest x1 2.11 us: final_sum(): pl.pallas_call(final_kernel, out_shape=[jax.ShapeDtypeStruct((2, width, h...]
  transfers between devices with their start and end apart: 3 -> 17, of which waited for: 3 -> 9; matrix products, arithmetic and copies ran while one was open for 1% -> 9% of each run, Pallas kernels for 0% -> 34%
where the time goes in v2:
time: 206 us; the launch traced here: 203 us
  Pallas kernels  75.9 us (37%)
  waiting for transfers between devices  51.7 us (25%)
  starting transfers between devices  38.5 us (19%)
  between operations  14.2 us (7%)
  local copies, waits for them, and re-layouts  12 us (6%)
  other arithmetic  10.9 us (5%)
    pallas_call x1, Pallas kernels, gather_layer(): pl.pallas_call(functools.partial(gather_kernel, loads, fanout, capacity),...  69.8 us
    ppermute x14, waiting for transfers between devices, send_along(): lax.ppermute(array, 'feat', [(ring[i], ring[(i + shift) % count]) for i i...  41.3 us
    ppermute x14, starting transfers between devices, send_along(): lax.ppermute(array, 'feat', [(ring[i], ring[(i + shift) % count]) for i i...  35.5 us
    ppermute x1, waiting for transfers between devices, group_sum(): other = lax.ppermute(mine, 'dp', [(i, i ^ stride) for i in range(count)])  7.66 us
  transfers between devices with their start and end apart: 17, of which 9 were waited for; matrix products, arithmetic and copies ran while one was open for 9% of the time, Pallas kernels for 34%

profile of v2, /device:TPU:0, one launch (start us, length us, event | category | flops | bytes accessed | tf_op | source)
XLA Modules:
  0.0 203.3 jit_solution(11033546599930887353)
XLA Ops:
  11.5 2.5 %convert_reduce_fusion = s32[8,704]{1,0:T(8,128)S(1)} fusion(s32[8,704]{1,0:T(8,128)S(1)} %get-tuple-element.26), kind=kLoop, calls=%fused_computation | loop fusion | flops 11889152 | bytes 45056 | tf_op jit(solution)/shard_map/reduce_sum | solution.py:32
  14.0 2.1 %select_reduce_fusion = s32[8,512]{1,0:T(8,128)S(1)} fusion(s32[8,704]{1,0:T(8,128)S(1)} %broadcast_add_fusion, s32[8,704]{1,0:T(8,128)S(1)} %convert_reduce_fusion), kind=kLoop, calls=%fused_computation.1 | loop fusion | flops 8646656 | bytes 61440 | tf_op jit(solution)/shard_map/reduce_sum | solution.py:34
  16.5 1.5 lt.107
  18.0 1.9 lt.108
  19.9 1.2 fusion.1
  23.2 69.8 %gather_layer.1 = (bf16[416,256]{1,0:T(8,128)(2,1)S(1)}, bf16[416,256]{1,0:T(8,128)(2,1)S(1)}, bf16[416,256]{1,0:T(8,128)(2,1)S(1)}, bf16[416,256]{1,0:T(8,128)(...) custom-call(s32[8]{0:T(128)S(1)} %get-tuple-element.29.turn_ref.sour, ...), custom_call_target="tpu_custom_call" | custom-call | tf_op jit(solution)/shard_map/gather_layer/pallas_call | solution.py:140
  93.0 3.1 %collective-permute-start = (bf16[416,256]{1,0:T(8,128)(2,1)S(1)}, bf16[416,256]{1,0:T(8,128)(2,1)S(1)}, u32[]{:S(2)}, u32[]{:S(2)}) collective-permute-start(bf16[416,256]{1,0:T(8,128)(2,1)S(1)} %get-tuple-element.11.rest_1_), channel_id=1, source_target_pairs={{0,8},{8,16},{16,24},{24,28},{28,20},{20,12},{12,4},{4,0},{1,9},{9... | collective-permute-start | bytes 638984 | tf_op jit(solution)/shard_map/ppermute | solution.py:303
  96.2 2.5 %collective-permute-start.1 = (bf16[416,256]{1,0:T(8,128)(2,1)S(1)}, bf16[416,256]{1,0:T(8,128)(2,1)S(1)}, u32[]{:S(2)}, u32[]{:S(2)}) collective-permute-start(bf16[416,256]{1,0:T(8,128)(2,1)S(1)} %get-tuple-element.12.rest_2_), channel_id=1, source_target_pairs={{0,16},{8,24},{16,28},{24,20},{28,12},{20,4},{12,0},{4,8},{1,17},{... | collective-permute-start | bytes 638984 | tf_op jit(solution)/shard_map/ppermute | solution.py:303
  98.7 1.3 collective-permute-start.2
  100.0 2.4 %collective-permute-start.3 = (bf16[416,256]{1,0:T(8,128)(2,1)S(1)}, bf16[416,256]{1,0:T(8,128)(2,1)S(1)}, u32[]{:S(2)}, u32[]{:S(2)}) collective-permute-start(bf16[416,256]{1,0:T(8,128)(2,1)S(1)} %get-tuple-element.14.rest_4_), channel_id=1, source_target_pairs={{0,28},{8,20},{16,12},{24,4},{28,0},{20,8},{12,16},{4,24},{1,29},{... | collective-permute-start | bytes 638984 | tf_op jit(solution)/shard_map/ppermute | solution.py:303
  105.2 3.5 %collective-permute-start.5 = (bf16[416,256]{1,0:T(8,128)(2,1)S(1)}, bf16[416,256]{1,0:T(8,128)(2,1)S(1)}, u32[]{:S(2)}, u32[]{:S(2)}) collective-permute-start(bf16[416,256]{1,0:T(8,128)(2,1)S(1)} %get-tuple-element.16.rest_6_), channel_id=1, source_target_pairs={{0,12},{8,4},{16,0},{24,8},{28,16},{20,24},{12,28},{4,20},{1,13},{... | collective-permute-start | bytes 638984 | tf_op jit(solution)/shard_map/ppermute | solution.py:303
  108.7 11.9 %collective-permute-start.6 = (bf16[416,256]{1,0:T(8,128)(2,1)S(1)}, bf16[416,256]{1,0:T(8,128)(2,1)S(1)}, u32[]{:S(2)}, u32[]{:S(2)}) collective-permute-start(bf16[416,256]{1,0:T(8,128)(2,1)S(1)} %get-tuple-element.17.rest_7_), channel_id=1, source_target_pairs={{0,4},{8,0},{16,8},{24,16},{28,24},{20,28},{12,20},{4,12},{1,5},{9... | collective-permute-start | bytes 638984 | tf_op jit(solution)/shard_map/ppermute | solution.py:303
  120.6 1.4 pad_add_fusion.1.own_ref
  122.0 6.6 %collective-permute-done.2.rest_3_ = bf16[416,256]{1,0:T(8,128)(2,1)S(1)} collective-permute-done((bf16[416,256]{1,0:T(8,128)(2,1)S(1)}, bf16[416,256]{1,0:T(8,128)(2,1)S(1)}, u32[]{:S(2)}, u32[]{:S(2)}) %collective-permute-start.2) | collective-permute-done | bytes 213024 | tf_op jit(solution)/shard_map/ppermute | solution.py:303
  128.7 6.0 %collective-permute-done.5.rest_6_ = bf16[416,256]{1,0:T(8,128)(2,1)S(1)} collective-permute-done((bf16[416,256]{1,0:T(8,128)(2,1)S(1)}, bf16[416,256]{1,0:T(8,128)(2,1)S(1)}, u32[]{:S(2)}, u32[]{:S(2)}) %collective-permute-start.5) | collective-permute-done | bytes 213024 | tf_op jit(solution)/shard_map/ppermute | solution.py:303
  134.7 1.9 collective-permute-done.6.rest_7_
  136.5 1.2 copy-done
  137.8 2.5 %upper_layers.1.rest_8_ = bf16[608,256]{1,0:T(8,128)(2,1)S(1)} custom-call(s32[9]{0:T(128)S(1)} %pad_add_fusion.1.own_ref, bf16[8,256,256]{2,1,0:T(8,128)(2,1)S(1)} %copy-done, bf16[2,256,172]{2,1,0:T(8,128)(2,1)S(1)} %copy.35.layer_ref, s32[1,416]{1,0:T(1,128)S(1)} %compare_select_fusion.5.row_ref, f32[64,1]{1,0:T(8,128)S(1)} %copy.36.count_ref, ...), custom_call_target="tpu_custom_call" | custom-call | tf_op jit(solution)/shard_map/upper_layers/pallas_call | solution.py:221
  140.3 3.3 %collective-permute-start.10 = (bf16[608,256]{1,0:T(8,128)(2,1)S(1)}, bf16[608,256]{1,0:T(8,128)(2,1)S(1)}, u32[]{:S(2)}, u32[]{:S(2)}) collective-permute-start(bf16[608,256]{1,0:T(8,128)(2,1)S(1)} %upper_layers.1.rest_8_), channel_id=1, source_target_pairs={{0,8},{8,16},{16,24},{24,28},{28,20},{20,12},{12,4},{4,0},{1,9},{9... | collective-permute-start | bytes 933896 | tf_op jit(solution)/shard_map/ppermute | solution.py:303
  143.5 7.6 %collective-permute-done.10.rest_15_ = bf16[608,256]{1,0:T(8,128)(2,1)S(1)} collective-permute-done((bf16[608,256]{1,0:T(8,128)(2,1)S(1)}, bf16[608,256]{1,0:T(8,128)(2,1)S(1)}, u32[]{:S(2)}, u32[]{:S(2)}) %collective-permute-start.10) | collective-permute-done | bytes 311328 | tf_op jit(solution)/shard_map/ppermute | solution.py:303
  151.1 2.5 %collective-permute-start.11 = (bf16[608,256]{1,0:T(8,128)(2,1)S(1)}, bf16[608,256]{1,0:T(8,128)(2,1)S(1)}, u32[]{:S(2)}, u32[]{:S(2)}) collective-permute-start(bf16[608,256]{1,0:T(8,128)(2,1)S(1)} %collective-permute-done.10.rest_15_), channel_id=1, source_target_pairs={{0,8},{8,16},{16,24},{24,28},{28,20},{20,12},{12,4},{4,0},{1,9},{9... | collective-permute-start | bytes 933896 | tf_op jit(solution)/shard_map/ppermute | solution.py:303
  153.6 7.1 %collective-permute-done.11.rest_14_ = bf16[608,256]{1,0:T(8,128)(2,1)S(1)} collective-permute-done((bf16[608,256]{1,0:T(8,128)(2,1)S(1)}, bf16[608,256]{1,0:T(8,128)(2,1)S(1)}, u32[]{:S(2)}, u32[]{:S(2)}) %collective-permute-start.11) | collective-permute-done | bytes 311328 | tf_op jit(solution)/shard_map/ppermute | solution.py:303
  160.7 2.3 %collective-permute-start.12 = (bf16[608,256]{1,0:T(8,128)(2,1)S(1)}, bf16[608,256]{1,0:T(8,128)(2,1)S(1)}, u32[]{:S(2)}, u32[]{:S(2)}) collective-permute-start(bf16[608,256]{1,0:T(8,128)(2,1)S(1)} %collective-permute-done.11.rest_14_), channel_id=1, source_target_pairs={{0,8},{8,16},{16,24},{24,28},{28,20},{20,12},{12,4},{4,0},{1,9},{9... | collective-permute-start | bytes 933896 | tf_op jit(solution)/shard_map/ppermute | solution.py:303
  163.2 6.4 %collective-permute-done.12.rest_13_ = bf16[608,256]{1,0:T(8,128)(2,1)S(1)} collective-permute-done((bf16[608,256]{1,0:T(8,128)(2,1)S(1)}, bf16[608,256]{1,0:T(8,128)(2,1)S(1)}, u32[]{:S(2)}, u32[]{:S(2)}) %collective-permute-start.12) | collective-permute-done | bytes 311328 | tf_op jit(solution)/shard_map/ppermute | solution.py:303
  169.5 2.2 %collective-permute-start.13 = (bf16[608,256]{1,0:T(8,128)(2,1)S(1)}, bf16[608,256]{1,0:T(8,128)(2,1)S(1)}, u32[]{:S(2)}, u32[]{:S(2)}) collective-permute-start(bf16[608,256]{1,0:T(8,128)(2,1)S(1)} %collective-permute-done.12.rest_13_), channel_id=1, source_target_pairs={{0,8},{8,16},{16,24},{24,28},{28,20},{20,12},{12,4},{4,0},{1,9},{9... | collective-permute-start | bytes 933896 | tf_op jit(solution)/shard_map/ppermute | solution.py:303
  171.7 5.7 %collective-permute-done.13.rest_12_ = bf16[608,256]{1,0:T(8,128)(2,1)S(1)} collective-permute-done((bf16[608,256]{1,0:T(8,128)(2,1)S(1)}, bf16[608,256]{1,0:T(8,128)(2,1)S(1)}, u32[]{:S(2)}, u32[]{:S(2)}) %collective-permute-start.13) | collective-permute-done | bytes 311328 | tf_op jit(solution)/shard_map/ppermute | solution.py:303
  177.4 1.5 grad_layer.1
  179.0 2.0 %collective-permute-done.14 = f32[608,256]{1,0:T(8,128)S(1)} collective-permute-done((f32[608,256]{1,0:T(8,128)S(1)}, f32[608,256]{1,0:T(8,128)S(1)}, u32[]{:S(2)}, u32[]{:S(2)}) %collective-permute-start.14) | collective-permute-done | bytes 622624 | tf_op jit(solution)/shard_map/ppermute | solution.py:324
  181.1 2.9 %collective-permute-start.15 = (bf16[608,256]{1,0:T(8,128)(2,1)S(1)}, bf16[608,256]{1,0:T(8,128)(2,1)S(1)}, u32[]{:S(2)}, u32[]{:S(2)}) collective-permute-start(bf16[608,256]{1,0:T(8,128)(2,1)S(1)} %add_convert_fusion.mine_ref), channel_id=1, source_target_pairs={{0,2},{1,3},{2,0},{3,1},{4,6},{5,7},{6,4},{7,5},{8,10},{9,11},{10,... | collective-permute-start | bytes 933896 | tf_op jit(solution)/shard_map/ppermute | solution.py:328
  184.0 7.7 %collective-permute-done.15.other_ref = bf16[608,256]{1,0:T(8,128)(2,1)S(1)} collective-permute-done((bf16[608,256]{1,0:T(8,128)(2,1)S(1)}, bf16[608,256]{1,0:T(8,128)(2,1)S(1)}, u32[]{:S(2)}, u32[]{:S(2)}) %collective-permute-start.15) | collective-permute-done | bytes 311328 | tf_op jit(solution)/shard_map/ppermute | solution.py:328
  192.4 2.1 %final_sum.1 = (f32[2,128,256]{2,1,0:T(8,128)}, f32[2,256,172]{2,1,0:T(8,128)}) custom-call(bf16[608,256]{1,0:T(8,128)(2,1)} %copy-done.1, bf16[608,256]{1,0:T(8,128)(2,1)} %copy-done.2), custom_call_target="tpu_custom_call" | custom-call | tf_op jit(solution)/shard_map/final_sum/pallas_call | solution.py:285
  194.5 2.0 copy.38
  (54 shorter events, 10.5 us)
Async XLA Ops:
  7.2 129.4 %all-gather.2.cloned.1.call-start = ((), (), s32[]{:S(2)}) async-start(), calls=%async_computation | async-start | bytes 1179648 | tf_op jit(solution)/shard_map/all_gather | solution.py:368
  23.2 79.8 %copy-start.4 = (s32[32]{0:T(128)S(1)}, s32[32]{0:T(128)}, u32[]{:S(2)}) copy-start(s32[32]{0:T(128)} %param.19) | copy-start | bytes 388
  23.2 81.8 %copy-start.3 = (bf16[2,256,172]{1,0,2:T(2,128)(2,1)S(1)}, bf16[2,256,172]{1,0,2:T(2,128)(2,1)}, u32[]{:S(2)}) copy-start(bf16[2,256,172]{1,0,2:T(2,128)(2,1)} %param.13) | copy-start | bytes 528388
  93.0 12.2 %collective-permute-start = (bf16[416,256]{1,0:T(8,128)(2,1)S(1)}, bf16[416,256]{1,0:T(8,128)(2,1)S(1)}, u32[]{:S(2)}, u32[]{:S(2)}) collective-permute-start(bf16[416,256]{1,0:T(8,128)(2,1)S(1)} %get-tuple-element.11.rest_1_), channel_id=1, source_target_pairs={{0,8},{8,16},{16,24},{24,28},{28,20},{20,12},{12,4},{4,0},{1,9},{9... | collective-permute-start | bytes 638984 | tf_op jit(solution)/shard_map/ppermute | solution.py:303
  96.2 12.5 %collective-permute-start.1 = (bf16[416,256]{1,0:T(8,128)(2,1)S(1)}, bf16[416,256]{1,0:T(8,128)(2,1)S(1)}, u32[]{:S(2)}, u32[]{:S(2)}) collective-permute-start(bf16[416,256]{1,0:T(8,128)(2,1)S(1)} %get-tuple-element.12.rest_2_), channel_id=1, source_target_pairs={{0,16},{8,24},{16,28},{24,20},{28,12},{20,4},{12,0},{4,8},{1,17},{... | collective-permute-start | bytes 638984 | tf_op jit(solution)/shard_map/ppermute | solution.py:303
  98.7 30.0 %collective-permute-start.2 = (bf16[416,256]{1,0:T(8,128)(2,1)S(1)}, bf16[416,256]{1,0:T(8,128)(2,1)S(1)}, u32[]{:S(2)}, u32[]{:S(2)}) collective-permute-start(bf16[416,256]{1,0:T(8,128)(2,1)S(1)} %get-tuple-element.13.rest_3_), channel_id=1, source_target_pairs={{0,24},{8,28},{16,20},{24,12},{28,4},{20,0},{12,8},{4,16},{1,25},{... | collective-permute-start | bytes 638984 | tf_op jit(solution)/shard_map/ppermute | solution.py:303
  100.0 28.6 %collective-permute-start.3 = (bf16[416,256]{1,0:T(8,128)(2,1)S(1)}, bf16[416,256]{1,0:T(8,128)(2,1)S(1)}, u32[]{:S(2)}, u32[]{:S(2)}) collective-permute-start(bf16[416,256]{1,0:T(8,128)(2,1)S(1)} %get-tuple-element.14.rest_4_), channel_id=1, source_target_pairs={{0,28},{8,20},{16,12},{24,4},{28,0},{20,8},{12,16},{4,24},{1,29},{... | collective-permute-start | bytes 638984 | tf_op jit(solution)/shard_map/ppermute | solution.py:303
  102.4 26.2 %collective-permute-start.4 = (bf16[416,256]{1,0:T(8,128)(2,1)S(1)}, bf16[416,256]{1,0:T(8,128)(2,1)S(1)}, u32[]{:S(2)}, u32[]{:S(2)}) collective-permute-start(bf16[416,256]{1,0:T(8,128)(2,1)S(1)} %get-tuple-element.15.rest_5_), channel_id=1, source_target_pairs={{0,20},{8,12},{16,4},{24,0},{28,8},{20,16},{12,24},{4,28},{1,21},{... | collective-permute-start | bytes 638984 | tf_op jit(solution)/shard_map/ppermute | solution.py:303
  105.2 29.5 %collective-permute-start.5 = (bf16[416,256]{1,0:T(8,128)(2,1)S(1)}, bf16[416,256]{1,0:T(8,128)(2,1)S(1)}, u32[]{:S(2)}, u32[]{:S(2)}) collective-permute-start(bf16[416,256]{1,0:T(8,128)(2,1)S(1)} %get-tuple-element.16.rest_6_), channel_id=1, source_target_pairs={{0,12},{8,4},{16,0},{24,8},{28,16},{20,24},{12,28},{4,20},{1,13},{... | collective-permute-start | bytes 638984 | tf_op jit(solution)/shard_map/ppermute | solution.py:303
  108.7 27.8 %collective-permute-start.6 = (bf16[416,256]{1,0:T(8,128)(2,1)S(1)}, bf16[416,256]{1,0:T(8,128)(2,1)S(1)}, u32[]{:S(2)}, u32[]{:S(2)}) collective-permute-start(bf16[416,256]{1,0:T(8,128)(2,1)S(1)} %get-tuple-element.17.rest_7_), channel_id=1, source_target_pairs={{0,4},{8,0},{16,8},{24,16},{28,24},{20,28},{12,20},{4,12},{1,5},{9... | collective-permute-start | bytes 638984 | tf_op jit(solution)/shard_map/ppermute | solution.py:303
  136.5 1.2 copy-start
  140.3 10.9 %collective-permute-start.10 = (bf16[608,256]{1,0:T(8,128)(2,1)S(1)}, bf16[608,256]{1,0:T(8,128)(2,1)S(1)}, u32[]{:S(2)}, u32[]{:S(2)}) collective-permute-start(bf16[608,256]{1,0:T(8,128)(2,1)S(1)} %upper_layers.1.rest_8_), channel_id=1, source_target_pairs={{0,8},{8,16},{16,24},{24,28},{28,20},{20,12},{12,4},{4,0},{1,9},{9... | collective-permute-start | bytes 933896 | tf_op jit(solution)/shard_map/ppermute | solution.py:303
  143.5 10.1 %collective-permute-start.7 = (bf16[608,256]{1,0:T(8,128)(2,1)S(1)}, bf16[608,256]{1,0:T(8,128)(2,1)S(1)}, u32[]{:S(2)}, u32[]{:S(2)}) collective-permute-start(bf16[608,256]{1,0:T(8,128)(2,1)S(1)} %upper_layers.1.rest_8_), channel_id=1, source_target_pairs={{0,4},{8,0},{16,8},{24,16},{28,24},{20,28},{12,20},{4,12},{1,5},{9... | collective-permute-start | bytes 933896 | tf_op jit(solution)/shard_map/ppermute | solution.py:303
  151.1 9.6 %collective-permute-start.11 = (bf16[608,256]{1,0:T(8,128)(2,1)S(1)}, bf16[608,256]{1,0:T(8,128)(2,1)S(1)}, u32[]{:S(2)}, u32[]{:S(2)}) collective-permute-start(bf16[608,256]{1,0:T(8,128)(2,1)S(1)} %collective-permute-done.10.rest_15_), channel_id=1, source_target_pairs={{0,8},{8,16},{16,24},{24,28},{28,20},{20,12},{12,4},{4,0},{1,9},{9... | collective-permute-start | bytes 933896 | tf_op jit(solution)/shard_map/ppermute | solution.py:303
  153.6 9.4 %collective-permute-start.8 = (bf16[608,256]{1,0:T(8,128)(2,1)S(1)}, bf16[608,256]{1,0:T(8,128)(2,1)S(1)}, u32[]{:S(2)}, u32[]{:S(2)}) collective-permute-start(bf16[608,256]{1,0:T(8,128)(2,1)S(1)} %collective-permute-done.7.rest_9_), channel_id=1, source_target_pairs={{0,4},{8,0},{16,8},{24,16},{28,24},{20,28},{12,20},{4,12},{1,5},{9... | collective-permute-start | bytes 933896 | tf_op jit(solution)/shard_map/ppermute | solution.py:303
  160.7 8.8 %collective-permute-start.12 = (bf16[608,256]{1,0:T(8,128)(2,1)S(1)}, bf16[608,256]{1,0:T(8,128)(2,1)S(1)}, u32[]{:S(2)}, u32[]{:S(2)}) collective-permute-start(bf16[608,256]{1,0:T(8,128)(2,1)S(1)} %collective-permute-done.11.rest_14_), channel_id=1, source_target_pairs={{0,8},{8,16},{16,24},{24,28},{28,20},{20,12},{12,4},{4,0},{1,9},{9... | collective-permute-start | bytes 933896 | tf_op jit(solution)/shard_map/ppermute | solution.py:303
  163.1 8.6 %collective-permute-start.9 = (bf16[608,256]{1,0:T(8,128)(2,1)S(1)}, bf16[608,256]{1,0:T(8,128)(2,1)S(1)}, u32[]{:S(2)}, u32[]{:S(2)}) collective-permute-start(bf16[608,256]{1,0:T(8,128)(2,1)S(1)} %collective-permute-done.8.rest_10_), channel_id=1, source_target_pairs={{0,4},{8,0},{16,8},{24,16},{28,24},{20,28},{12,20},{4,12},{1,5},{9... | collective-permute-start | bytes 933896 | tf_op jit(solution)/shard_map/ppermute | solution.py:303
  169.5 7.9 %collective-permute-start.13 = (bf16[608,256]{1,0:T(8,128)(2,1)S(1)}, bf16[608,256]{1,0:T(8,128)(2,1)S(1)}, u32[]{:S(2)}, u32[]{:S(2)}) collective-permute-start(bf16[608,256]{1,0:T(8,128)(2,1)S(1)} %collective-permute-done.12.rest_13_), channel_id=1, source_target_pairs={{0,8},{8,16},{16,24},{24,28},{28,20},{20,12},{12,4},{4,0},{1,9},{9... | collective-permute-start | bytes 933896 | tf_op jit(solution)/shard_map/ppermute | solution.py:303
  178.9 2.1 %collective-permute-start.14 = (f32[608,256]{1,0:T(8,128)S(1)}, f32[608,256]{1,0:T(8,128)S(1)}, u32[]{:S(2)}, u32[]{:S(2)}) collective-permute-start(f32[608,256]{1,0:T(8,128)S(1)} %grad_layer.1), channel_id=1, source_target_pairs={{0,1},{1,0},{2,3},{3,2},{4,5},{5,4},{6,7},{7,6},{8,9},{9,8},{10,11... | collective-permute-start | bytes 1867784 | tf_op jit(solution)/shard_map/ppermute | solution.py:324
  181.1 10.6 %copy-start.1 = (bf16[608,256]{1,0:T(8,128)(2,1)}, bf16[608,256]{1,0:T(8,128)(2,1)S(1)}, u32[]{:S(2)}) copy-start(bf16[608,256]{1,0:T(8,128)(2,1)S(1)} %add_convert_fusion.mine_ref) | copy-start | bytes 933892
  181.1 10.6 %collective-permute-start.15 = (bf16[608,256]{1,0:T(8,128)(2,1)S(1)}, bf16[608,256]{1,0:T(8,128)(2,1)S(1)}, u32[]{:S(2)}, u32[]{:S(2)}) collective-permute-start(bf16[608,256]{1,0:T(8,128)(2,1)S(1)} %add_convert_fusion.mine_ref), channel_id=1, source_target_pairs={{0,2},{1,3},{2,0},{3,1},{4,6},{5,7},{6,4},{7,5},{8,10},{9,11},{10,... | collective-permute-start | bytes 933896 | tf_op jit(solution)/shard_map/ppermute | solution.py:328
  191.7 0.7 copy-start.2
Sparse Core Ops, SparseCore 0:
  10.1 42.8 all-gather.1

commit v3 on v2

v3 whole, which is shorter than its diff:
```python
import functools

import jax
import jax.numpy as jnp
from jax import lax
from jax.experimental import pallas as pl
from jax.experimental.pallas import tpu as pltpu
from jax.sharding import PartitionSpec as P

LANES = 128
TILE = 16
TILE_BITS = 4
UNROLL = 4
CALLS = 3
BLOCK = 256


def round_up(value, step):
    return (value + step - 1) // step * step


def plan_rows(hop1_count, hop2_count, sizes, kept):
    groups, seed_total = hop1_count.shape
    row_total = hop2_count.shape[1]
    fanout = (row_total - seed_total) // seed_total
    live = jnp.arange(seed_total)[None, :] < sizes[:, None]
    near = jnp.arange(fanout)[None, None, :] < jnp.where(live, hop1_count, 0)[:, :, None]
    used = jnp.concatenate([live, near.reshape(groups, -1)], axis=1)
    count = jnp.where(used, hop2_count, 0)
    row = jnp.arange(row_total)[None, :]
    mixed = count * row_total + (row_total - 1 - row)
    place = jnp.sum((mixed[:, None, :] > mixed[:, :, None]).astype(jnp.int32), axis=2)
    packed = row * 16 + count
    order = jnp.sum(
        jnp.where(place[:, None, :] == jnp.arange(kept)[None, :, None], packed[:, None, :], 0), axis=2
    )
    enough = jnp.sum(
        (count[:, None, :] >= jnp.arange(16)[None, :, None]).astype(jnp.int32), axis=2
    )
    return order, enough


def table_kernel(feats_ref, table_ref):
    step = pl.program_id(0)
    width, chunk = feats_ref.shape
    padded = table_ref.shape[1]
    down = lax.broadcasted_iota(jnp.int32, (BLOCK, BLOCK), 0)
    across = lax.broadcasted_iota(jnp.int32, (BLOCK, BLOCK), 1)
    identity = jnp.where(down == across, 1.0, 0.0).astype(jnp.bfloat16)
    for part in range(chunk // BLOCK):
        piece = feats_ref[:, part * BLOCK : (part + 1) * BLOCK]
        if padded > width:
            piece = jnp.concatenate([piece, jnp.zeros((padded - width, BLOCK), piece.dtype)], axis=0)
        turned = lax.dot_general(
            identity, piece, (((1,), (1,)), ((), ())), preferred_element_type=jnp.float32
        )
        start = pl.multiple_of(step * chunk + part * BLOCK, BLOCK)
        table_ref[pl.ds(start, BLOCK), :] = turned.astype(jnp.bfloat16)


def build_table(node_feats):
    width, nodes = node_feats.shape
    padded = max(width, LANES)
    chunk = min(nodes, 8192)
    return pl.pallas_call(
        table_kernel,
        grid=(nodes // chunk,),
        in_specs=[pl.BlockSpec((width, chunk), lambda step: (0, step))],
        out_specs=pl.BlockSpec(memory_space=pltpu.VMEM),
        out_shape=pltpu.VMEM((nodes, padded), jnp.bfloat16),
        compiler_params=pltpu.CompilerParams(vmem_limit_bytes=8 * 2**20),
        name="build_table",
    )(node_feats)


def gather_kernel(
    fanout, capacity, turn_ref, enough_ref, order_ref, own_ref, near_ref, count_ref, table_ref, *rest
):
    *inputs_refs, _, mask_ref, own_sum_ref, near_sum_ref = rest
    step = pl.program_id(0)
    width = inputs_refs[0].shape[1] // 2
    padded = table_ref.shape[1]

    @pl.when(step == 0)
    def _():
        shape = mask_ref.shape
        code = lax.broadcasted_iota(jnp.int32, shape, 0)
        line = lax.broadcasted_iota(jnp.int32, shape, 1)
        mask_ref[...] = jnp.where(code == line, 1.0, 0.0).astype(jnp.bfloat16)

    tiles = table_ref.reshape(table_ref.shape[0] // TILE, TILE, padded)

    def fetch(node):
        return (tiles[node >> TILE_BITS] * mask_ref[node & (TILE - 1)]).astype(jnp.float32)

    def fold(value):
        return value[: TILE // 2] + value[TILE // 2 :]

    def gather_rows(slots, first, number):
        owns, nears = [], []
        for i in range(number):
            row = order_ref[0, 0, first + i] >> 4
            owns.append(fold(fetch(own_ref[0, 0, row])))
            totals = [fetch(near_ref[0, 0, row * fanout + slot]) for slot in range(slots)]
            while len(totals) > 1:
                totals = [sum(totals[at + 1 : at + 2], totals[at]) for at in range(0, len(totals), 2)]
            nears.append(fold(totals[0]))
        for i in range(number):
            start = pl.multiple_of((first + i) * 8, 8)
            own_sum_ref[pl.ds(start, 8), :] = owns[i]
            near_sum_ref[pl.ds(start, 8), :] = nears[i]

    begin = 0
    for slots in range(fanout, 0, -1):
        end = enough_ref[0, 0, slots]
        whole = end - begin >= UNROLL

        def chunk_of(number, carry, slots=slots, begin=begin, end=end):
            gather_rows(slots, jnp.minimum(begin + number * UNROLL, end - UNROLL), UNROLL)
            return carry

        def one_of(at, carry, slots=slots):
            gather_rows(slots, at, 1)
            return carry

        lax.fori_loop(0, jnp.where(whole, lax.div(end - begin + UNROLL - 1, UNROLL), 0), chunk_of, 0)
        lax.fori_loop(begin, jnp.where(whole, begin, end), one_of, 0)
        begin = end

    def clear(at, carry):
        start = pl.multiple_of(at * 8, 8)
        own_sum_ref[pl.ds(start, 8), :] = jnp.zeros((8, padded), jnp.float32)
        near_sum_ref[pl.ds(start, 8), :] = jnp.zeros((8, padded), jnp.float32)
        return carry

    lax.fori_loop(begin, capacity, clear, 0)

    def collect(ref):
        total = ref[pl.ds(0, capacity, stride=8), :]
        for line in range(1, 8):
            total = total + ref[pl.ds(line, capacity, stride=8), :]
        return total

    counts = jnp.transpose(jnp.broadcast_to(count_ref[0], (padded, count_ref.shape[2])))[:capacity]
    own = collect(own_sum_ref).astype(jnp.bfloat16)[:, :width]
    near = (collect(near_sum_ref) / counts).astype(jnp.bfloat16)[:, :width]
    both = jnp.concatenate([own, near], axis=1)
    for place, inputs_ref in enumerate(inputs_refs):

        @pl.when(step == place)
        def _():
            inputs_ref[...] = both


def gather_layer(table, turn, begin, end, enough, order, counts, own_ids, near_ids, width, capacity):
    nodes, padded = table.shape
    groups = end - begin
    kept = order.shape[2]
    row_total = own_ids.shape[2]
    fanout = near_ids.shape[2] // row_total

    def group_of(step, turn_ref):
        return (turn_ref[begin + step], 0, 0)

    def per_group(length):
        return pl.BlockSpec((1, 1, length), group_of, memory_space=pltpu.SMEM)

    return pl.pallas_call(
        functools.partial(gather_kernel, fanout, capacity),
        grid_spec=pltpu.PrefetchScalarGridSpec(
            num_scalar_prefetch=1,
            grid=(groups,),
            in_specs=[
                per_group(16),
                per_group(kept),
                per_group(row_total),
                per_group(row_total * fanout),
                pl.BlockSpec((1, 1, kept), group_of),
                pl.BlockSpec(memory_space=pltpu.VMEM),
            ],
            out_specs=[pl.BlockSpec((capacity, 2 * width), lambda step, turn_ref: (0, 0))] * groups
            + [pl.BlockSpec(memory_space=pltpu.VMEM)],
            scratch_shapes=[
                pltpu.VMEM((TILE, TILE, padded), jnp.bfloat16),
                pltpu.VMEM((capacity * 8, padded), jnp.float32),
                pltpu.VMEM((capacity * 8, padded), jnp.float32),
            ],
        ),
        out_shape=[jax.ShapeDtypeStruct((capacity, 2 * width), jnp.bfloat16)] * groups
        + [pltpu.VMEM((nodes, padded), jnp.bfloat16)],
        input_output_aliases={6: groups},
        cost_estimate=pl.CostEstimate(
            flops=0, bytes_accessed=groups * capacity * fanout * TILE * padded * 2, transcendentals=0
        ),
        compiler_params=pltpu.CompilerParams(vmem_limit_bytes=14 * 2**20),
        name="gather_layer",
    )(
        turn, enough, order, own_ids, near_ids, counts,
        pltpu.with_memory_space_constraint(table, pltpu.VMEM),
    )


def upper_kernel(fanout, size_ref, turn_ref, weights_ref, layer_ref, row_ref, seed_ref, *rest):
    *inputs_refs, out_ref = rest
    seed_total = seed_ref.shape[1]
    capacity = inputs_refs[0].shape[0]
    hidden_width = weights_ref.shape[2]
    classes = layer_ref.shape[1]
    size = size_ref[0]
    seed = lax.broadcasted_iota(jnp.int32, (seed_total, capacity), 0)
    row = jnp.broadcast_to(row_ref[...], (seed_total, capacity))
    first = seed_total + seed * fanout
    is_seed = jnp.where(row == seed, 1.0, 0.0).astype(jnp.bfloat16)
    is_near = jnp.where((row >= first) & (row < first + fanout), 1.0, 0.0).astype(jnp.bfloat16)
    preact = jnp.zeros((capacity, hidden_width), jnp.float32)
    for place, inputs_ref in enumerate(inputs_refs):
        source = turn_ref[len(inputs_refs) + place]
        preact = preact + jnp.dot(inputs_ref[...], weights_ref[source], preferred_element_type=jnp.float32)
    hidden = jnp.maximum(preact, 0.0).astype(jnp.bfloat16)
    counts = seed_ref[0][:, :1].astype(jnp.float32)
    last = (((1,), (1,)), ((), ()))
    seed_hidden = jnp.dot(is_seed, hidden, preferred_element_type=jnp.float32).astype(jnp.bfloat16)
    near_mean = (jnp.dot(is_near, hidden, preferred_element_type=jnp.float32) / counts).astype(jnp.bfloat16)
    logits = lax.dot_general(seed_hidden, layer_ref[0], last, preferred_element_type=jnp.float32)
    logits = logits + lax.dot_general(near_mean, layer_ref[1], last, preferred_element_type=jnp.float32)
    exponent = jnp.exp(logits - jnp.max(logits, axis=1, keepdims=True))
    probabilities = exponent / jnp.sum(exponent, axis=1, keepdims=True)
    label = jnp.broadcast_to(seed_ref[1][:, :1], (seed_total, classes))
    onehot = jnp.where(label == lax.broadcasted_iota(jnp.int32, (seed_total, classes), 1), 1.0, 0.0)
    valid = lax.broadcasted_iota(jnp.int32, (seed_total, classes), 0) < size
    dlogits = jnp.where(valid, (probabilities - onehot) / size.astype(jnp.float32), 0.0).astype(jnp.bfloat16)
    back_seed = jnp.dot(dlogits, layer_ref[0], preferred_element_type=jnp.float32)
    back_near = jnp.dot(dlogits, layer_ref[1], preferred_element_type=jnp.float32) / counts
    rows = (((0,), (0,)), ((), ()))
    spread = lax.dot_general(is_seed, back_seed.astype(jnp.bfloat16), rows, preferred_element_type=jnp.float32)
    spread = spread + lax.dot_general(
        is_near, back_near.astype(jnp.bfloat16), rows, preferred_element_type=jnp.float32
    )
    out_ref[:capacity] = jnp.where(preact > 0, spread, 0.0).astype(jnp.bfloat16)
    out_ref[capacity : capacity + seed_total] = seed_hidden
    out_ref[capacity + seed_total : capacity + 2 * seed_total] = near_mean
    out_ref[capacity + 2 * seed_total :] = jnp.zeros((seed_total, hidden_width), jnp.bfloat16)
    out_ref[capacity + 2 * seed_total :, :classes] = dlogits


def upper_layers(inputs, size, turn, weights, layer, row, seeds, fanout):
    seed_total = seeds.shape[1]
    capacity = inputs[0].shape[0]
    hidden_width = weights.shape[2]
    smem = pl.BlockSpec(memory_space=pltpu.SMEM)
    vmem = pl.BlockSpec(memory_space=pltpu.VMEM)
    return pl.pallas_call(
        functools.partial(upper_kernel, fanout),
        in_specs=[smem] * 2 + [vmem] * (4 + len(inputs)),
        out_specs=vmem,
        out_shape=jax.ShapeDtypeStruct((capacity + 3 * seed_total, hidden_width), jnp.bfloat16),
        compiler_params=pltpu.CompilerParams(vmem_limit_bytes=32 * 2**20),
        name="upper_layers",
    )(size, turn, weights, layer, row, seeds, *inputs)


def grad_kernel(seed_total, classes, source_ref, *rest):
    count = (len(rest) - 2) // 2
    inputs_refs, sent_refs = rest[:count], rest[count : 2 * count]
    out_ref, units_ref = rest[2 * count :]
    capacity, double = inputs_refs[0].shape
    hidden_width = out_ref.shape[1]
    rows = (((0,), (0,)), ((), ()))
    first = jnp.zeros((double, hidden_width), jnp.float32)
    for place in range(count):
        first = first + lax.dot_general(
            inputs_refs[place][...], sent_refs[place][:capacity], rows, preferred_element_type=jnp.float32
        )
        start = pl.multiple_of(source_ref[place] * seed_total, seed_total)
        for part in range(3):
            units_ref[part, pl.ds(start, seed_total), :] = sent_refs[place][
                capacity + part * seed_total : capacity + (part + 1) * seed_total
            ]
    out_ref[:double] = first
    for layer in range(2):
        second = lax.dot_general(units_ref[2], units_ref[layer], rows, preferred_element_type=jnp.float32)
        start = double + layer * round_up(classes, 8)
        out_ref[start : start + round_up(classes, 8)] = second[: round_up(classes, 8)]


def grad_layer(inputs, sent, sources, seed_total, classes):
    capacity, double = inputs[0].shape
    hidden_width = sent[0].shape[1]
    vmem = pl.BlockSpec(memory_space=pltpu.VMEM)
    return pl.pallas_call(
        functools.partial(grad_kernel, seed_total, classes),
        in_specs=[pl.BlockSpec(memory_space=pltpu.SMEM)] + [vmem] * (2 * len(inputs)),
        out_specs=vmem,
        out_shape=jax.ShapeDtypeStruct((double + 2 * round_up(classes, 8), hidden_width), jnp.float32),
        scratch_shapes=[pltpu.VMEM((3, len(inputs) * seed_total, hidden_width), jnp.bfloat16)],
        compiler_params=pltpu.CompilerParams(vmem_limit_bytes=40 * 2**20),
        name="grad_layer",
    )(sources, *inputs, *sent)


def final_kernel(mine_ref, other_ref, first_ref, second_ref):
    width = first_ref.shape[1]
    classes = second_ref.shape[0]
    total = mine_ref[...].astype(jnp.float32) + other_ref[...].astype(jnp.float32)
    for layer in range(2):
        first_ref[layer] = total[layer * width : (layer + 1) * width]
        start = 2 * width + layer * round_up(classes, 8)
        second_ref[:, layer, :] = total[start : start + classes]


def final_sum(mine, other, width, classes):
    hidden_width = mine.shape[1]
    first, second = pl.pallas_call(
        final_kernel,
        out_shape=[
            jax.ShapeDtypeStruct((2, width, hidden_width), jnp.float32),
            jax.ShapeDtypeStruct((classes, 2, hidden_width), jnp.float32),
        ],
        name="final_sum",
    )(mine, other)
    return first, jnp.transpose(second, (1, 2, 0))


def ring_of(count):
    if count % 2:
        return list(range(count))
    return list(range(0, count, 2)) + list(range(count - 1, 0, -2))


def send_along(array, ring, shift):
    count = len(ring)
    return lax.ppermute(array, "feat", [(ring[i], ring[(i + shift) % count]) for i in range(count)])


def ring_gather(array, ring):
    count = len(ring)
    result = [array] + [None] * (count - 1)
    ahead = behind = array
    for hop in range(1, count // 2 + 1):
        behind = send_along(behind, ring, 1)
        result[count - hop] = behind
        if 2 * hop < count:
            ahead = send_along(ahead, ring, -1)
            result[hop] = ahead
    return result


def group_sum(grads, width, classes):
    count = lax.axis_size("dp")
    mine = grads
    stride = 1
    while 2 * stride < count:
        mine = mine + lax.ppermute(mine, "dp", [(i, i ^ stride) for i in range(count)])
        stride *= 2
    mine = mine.astype(jnp.bfloat16)
    if count > 1:
        other = lax.ppermute(mine, "dp", [(i, i ^ stride) for i in range(count)])
    else:
        other = jnp.zeros_like(mine)
    return final_sum(mine, other, width, classes)


def shards(
    node_feats,
    first_layer,
    second_layer,
    seed_ids,
    hop1_ids,
    hop1_count,
    hop2_ids,
    hop2_count,
    batch_sizes,
    label_ids,
):
    groups, seed_total = seed_ids.shape
    row_total = hop2_count.shape[1]
    fanout = hop1_ids.shape[1] // seed_total
    slice_width = node_feats.shape[0]
    hidden_width = first_layer.shape[2]
    classes = second_layer.shape[2]
    capacity = round_up(seed_total + row_total // 2, 16)
    kept = round_up(capacity, LANES)
    column_rank = lax.axis_index("feat")
    group_start = lax.axis_index("dp") * groups
    sizes = lax.dynamic_slice_in_dim(batch_sizes, group_start, groups)
    order, enough = plan_rows(hop1_count, hop2_count, sizes, kept)
    count = lax.axis_size("feat")
    ring = ring_of(count)
    places = sorted(range(count), key=lambda t: -min(t, count - t))
    turns = [
        [ring[(ring.index(i) + sign * t) % count] for sign in (1, -1) for t in places] for i in range(count)
    ]
    turn = lax.dynamic_index_in_dim(jnp.array(turns, jnp.int32), column_rank, 0, keepdims=False)
    weights = lax.all_gather(first_layer.reshape(2 * slice_width, hidden_width), "feat", axis=0)
    lists = [
        enough[:, None, :],
        order[:, None, :],
        jnp.maximum(order % 16, 1).astype(jnp.float32)[:, None, :],
        jnp.concatenate([seed_ids, hop1_ids], axis=1)[:, None, :],
        hop2_ids[:, None, :],
    ]

    def own(array):
        return lax.dynamic_index_in_dim(array, column_rank, 0, keepdims=False)

    own_order = own(order)[None, :capacity]
    row = jnp.where(own_order % 16 > 0, own_order // 16, -1)
    seeds = jnp.stack([own(hop1_count), own(label_ids)])
    seeds = jnp.broadcast_to(seeds[:, :, None], (2, seed_total, LANES))
    size = lax.dynamic_slice_in_dim(sizes, column_rank, 1)
    layer = jnp.transpose(second_layer, (0, 2, 1))
    node_feats, turn, size, layer, row, seeds, *lists = lax.optimization_barrier(
        (node_feats, turn, size, layer, row, seeds, *lists)
    )
    table = build_table(node_feats)
    inputs, received, arrived = [], [], []
    for call in range(CALLS):
        begin, end = -(-call * count // CALLS), -(-(call + 1) * count // CALLS)
        *blocks, table = gather_layer(table, turn, begin, end, *lists, slice_width, capacity)
        table, blocks, arrived = lax.optimization_barrier((table, blocks, arrived))
        inputs += blocks
        received += arrived
        arrived = [send_along(block, ring, t) if t else block for t, block in zip(places[begin:end], blocks)]
    received += arrived

    sent = upper_layers(received, size, turn, weights, layer, row, seeds, fanout)
    every = ring_gather(sent, ring)
    grads = grad_layer(inputs, [every[t] for t in places], turn, seed_total, classes)
    return tuple(group_sum(grads, slice_width, classes))


def solution(mesh):
    return jax.shard_map(
        shards,
        mesh=mesh,
        in_specs=(
            P("feat", None),
            P(None, "feat", None),
            P(),
            P("dp", None),
            P("dp", None),
            P("dp", None),
            P("dp", None),
            P("dp", None),
            P(),
            P("dp", None),
        ),
        out_specs=(P(None, "feat", None), P()),
        check_vma=False,
    )
```

time: 206 us -> 199 us (0.966); the launches traced: 203 us -> 200 us
  Pallas kernels: 75.9 us -> 102 us
  starting transfers between devices: 38.5 us -> 22.2 us
  waiting for transfers between devices: 51.7 us -> 45.6 us
  local copies, waits for them, and re-layouts: 12 us -> 7.9 us
  other arithmetic: 10.9 us -> 7.49 us
    pallas_call x2 -> x5, Pallas kernels: 72.3 us -> 98.7 us  [the longest x3 71.1 us: gather_layer(): pl.pallas_call(functools.partial(gather_kernel, fanout, capacity), grid_s...]
    ppermute x14, starting transfers between devices: 35.5 us -> 22 us  [send_along(): lax.ppermute(array, 'feat', [(ring[i], ring[(i + shift) % count]) for i i...]
    ppermute x14, waiting for transfers between devices: 41.3 us -> 33.5 us  [send_along(): lax.ppermute(array, 'feat', [(ring[i], ring[(i + shift) % count]) for i i...]
    lt x4 -> x0, local copies, waits for them, and re-layouts: 3.72 us -> none  [shards(): jnp.arange(slots)[None, None, :] < hop2_count[:, :, None]]
    ppermute x1, starting transfers between devices: 2.91 us -> 0.07 us  [group_sum(): other = lax.ppermute(mine, 'dp', [(i, i ^ stride) for i in range(count)])]
    add x2 -> x0, other arithmetic: 2.11 us -> none  [slot_codes(): return ids // TILE * CODES + jnp.where(live, ids % TILE, TILE)]
  transfers between devices with their start and end apart: 17 -> 17, of which waited for: 9 -> 7; matrix products, arithmetic and copies ran while one was open for 9% -> 7% of each run, Pallas kernels for 34% -> 48%
where the time goes in v3:
time: 199 us; the launch traced here: 200 us
  Pallas kernels  102 us (51%)
  waiting for transfers between devices  45.6 us (23%)
  starting transfers between devices  22.2 us (11%)
  between operations  14.3 us (7%)
  local copies, waits for them, and re-layouts  7.9 us (4%)
  other arithmetic  7.49 us (4%)
    pallas_call x3, Pallas kernels, gather_layer(): pl.pallas_call(functools.partial(gather_kernel, fanout, capacity), grid_s...  71.1 us
    ppermute x14, waiting for transfers between devices, send_along(): lax.ppermute(array, 'feat', [(ring[i], ring[(i + shift) % count]) for i i...  33.5 us
    pallas_call x1, Pallas kernels, build_table(): pl.pallas_call(table_kernel, grid=(nodes // chunk,), in_specs=[pl.BlockSp...  24.6 us
    ppermute x14, starting transfers between devices, send_along(): lax.ppermute(array, 'feat', [(ring[i], ring[(i + shift) % count]) for i i...  22 us
    ppermute x1, waiting for transfers between devices, group_sum(): other = lax.ppermute(mine, 'dp', [(i, i ^ stride) for i in range(count)])  9.39 us
  transfers between devices with their start and end apart: 17, of which 7 were waited for; matrix products, arithmetic and copies ran while one was open for 7% of the time, Pallas kernels for 48%

profile of v3, /device:TPU:0, one launch (start us, length us, event | category | flops | bytes accessed | tf_op | source)
XLA Modules:
  0.0 199.6 jit_solution(6482196717981664119)
XLA Ops:
  10.0 0.8 multiply_add_fusion
  10.8 2.5 %convert_reduce_fusion = s32[8,704]{1,0:T(8,128)S(1)} fusion(s32[8,704]{1,0:T(8,128)S(1)} %get-tuple-element.80), kind=kLoop, calls=%fused_computation | loop fusion | flops 11889152 | bytes 45056 | tf_op jit(solution)/shard_map/reduce_sum | solution.py:32
  13.3 2.1 %select_reduce_fusion = s32[8,512]{1,0:T(8,128)S(1)} fusion(s32[8,704]{1,0:T(8,128)S(1)} %broadcast_add_fusion, s32[8,704]{1,0:T(8,128)S(1)} %convert_reduce_fusion), kind=kLoop, calls=%fused_computation.1 | loop fusion | flops 8646656 | bytes 61440 | tf_op jit(solution)/shard_map/reduce_sum | solution.py:34
  15.4 1.2 dynamic_slice.25.size_ref
  16.7 1.1 broadcast_in_dim.62.near_ref
  17.8 0.9 copy.51
  18.7 0.8 pad_add_fusion
  21.4 24.6 %build_table.1.table_ref = bf16[131072,128]{1,0:T(8,128)(2,1)S(1)} custom-call(bf16[128,131072]{1,0:T(8,128)(2,1)} %feats_ref), custom_call_target="tpu_custom_call" | custom-call | tf_op jit(solution)/shard_map/build_table/pallas_call | solution.py:65
  46.0 28.6 %gather_layer.3 = (bf16[416,256]{1,0:T(8,128)(2,1)S(1)}, bf16[416,256]{1,0:T(8,128)(2,1)S(1)}, bf16[416,256]{1,0:T(8,128)(2,1)S(1)}, bf16[131072,128]{1,0:T(8,128)(2,1)S(1)}) custom-call(s32[16]{0:T(128)S(1)} %fusion.3.turn_ref.source_ref, s32[8,1,16]{2,1,0:T(1,128)S(1)} %bitcast.10, ...), custom_call_target="tpu_custom_call", output_to_operand_aliasing={{3}: (6, {})} | custom-call | bytes 51118080 | tf_op jit(solution)/shard_map/gather_layer/pallas_call | solution.py:168
  74.5 3.7 %collective-permute-start = (bf16[416,256]{1,0:T(8,128)(2,1)S(1)}, bf16[416,256]{1,0:T(8,128)(2,1)S(1)}, u32[]{:S(2)}, u32[]{:S(2)}) collective-permute-start(bf16[416,256]{1,0:T(8,128)(2,1)S(1)} %get-tuple-element.52.rest_0_), channel_id=1, source_target_pairs={{0,28},{8,20},{16,12},{24,4},{28,0},{20,8},{12,16},{4,24},{1,29},{... | collective-permute-start | bytes 638984 | tf_op jit(solution)/shard_map/ppermute | solution.py:332
  78.2 3.8 %collective-permute-start.2 = (bf16[416,256]{1,0:T(8,128)(2,1)S(1)}, bf16[416,256]{1,0:T(8,128)(2,1)S(1)}, u32[]{:S(2)}, u32[]{:S(2)}) collective-permute-start(bf16[416,256]{1,0:T(8,128)(2,1)S(1)} %get-tuple-element.54.rest_2_), channel_id=1, source_target_pairs={{0,20},{8,12},{16,4},{24,0},{28,8},{20,16},{12,24},{4,28},{1,21},{... | collective-permute-start | bytes 638984 | tf_op jit(solution)/shard_map/ppermute | solution.py:332
  82.0 25.2 %gather_layer.4 = (bf16[416,256]{1,0:T(8,128)(2,1)S(1)}, bf16[416,256]{1,0:T(8,128)(2,1)S(1)}, bf16[416,256]{1,0:T(8,128)(2,1)S(1)}, bf16[131072,128]{1,0:T(8,128)(2,1)S(1)}) custom-call(s32[16]{0:T(128)S(1)} %fusion.3.turn_ref.source_ref, s32[8,1,16]{2,1,0:T(1,128)S(1)} %bitcast.11, ...), custom_call_target="tpu_custom_call", output_to_operand_aliasing={{3}: (6, {})} | custom-call | bytes 51118080 | tf_op jit(solution)/shard_map/gather_layer/pallas_call | solution.py:168
  107.3 2.4 %collective-permute-start.3 = (bf16[416,256]{1,0:T(8,128)(2,1)S(1)}, bf16[416,256]{1,0:T(8,128)(2,1)S(1)}, u32[]{:S(2)}, u32[]{:S(2)}) collective-permute-start(bf16[416,256]{1,0:T(8,128)(2,1)S(1)} %get-tuple-element.60.rest_3_), channel_id=1, source_target_pairs={{0,16},{8,24},{16,28},{24,20},{28,12},{20,4},{12,0},{4,8},{1,17},{... | collective-permute-start | bytes 638984 | tf_op jit(solution)/shard_map/ppermute | solution.py:332
  110.3 2.4 %collective-permute-start.5 = (bf16[416,256]{1,0:T(8,128)(2,1)S(1)}, bf16[416,256]{1,0:T(8,128)(2,1)S(1)}, u32[]{:S(2)}, u32[]{:S(2)}) collective-permute-start(bf16[416,256]{1,0:T(8,128)(2,1)S(1)} %get-tuple-element.62.rest_5_), channel_id=1, source_target_pairs={{0,8},{8,16},{16,24},{24,28},{28,20},{20,12},{12,4},{4,0},{1,9},{9... | collective-permute-start | bytes 638984 | tf_op jit(solution)/shard_map/ppermute | solution.py:332
  112.7 17.3 %gather_layer.5 = (bf16[416,256]{1,0:T(8,128)(2,1)S(1)}, bf16[416,256]{1,0:T(8,128)(2,1)S(1)}, bf16[131072,128]{1,0:T(8,128)(2,1)S(1)}) custom-call(s32[16]{0:T(128)S(1)} %fusion.3.turn_ref.source_ref, s32[8,1,16]{2,1,0:T(1,128)S(1)} %bitcast.12, s32[8,1,512]{2,1,0:T(1,128)S(1)} %broadcast_in_dim.60.order_ref, ...), custom_call_target="tpu_custom_call", output_to_operand_aliasing={{2}: (6, {})} | custom-call | bytes 34078720 | tf_op jit(solution)/shard_map/gather_layer/pallas_call | solution.py:168
  130.1 1.5 collective-permute-start.6
  131.5 5.0 %collective-permute-done.6.rest_6_ = bf16[416,256]{1,0:T(8,128)(2,1)S(1)} collective-permute-done((bf16[416,256]{1,0:T(8,128)(2,1)S(1)}, bf16[416,256]{1,0:T(8,128)(2,1)S(1)}, u32[]{:S(2)}, u32[]{:S(2)}) %collective-permute-start.6) | collective-permute-done | bytes 213024 | tf_op jit(solution)/shard_map/ppermute | solution.py:332
  136.5 1.2 copy-done
  137.7 3.1 %upper_layers.1.rest_15_ = bf16[608,256]{1,0:T(8,128)(2,1)S(1)} custom-call(s32[1]{0:T(128)} %dynamic_slice.25.size_ref, s32[16]{0:T(128)S(1)} %fusion.3.turn_ref.source_ref, bf16[8,256,256]{2,1,0:T(8,128)(2,1)S(1)} %copy-done, bf16[2,172,256]{2,1,0:T(8,128)(2,1)S(1)} %bitcast.9, s32[1,416]{1,0:T(1,128)S(1)} %compare_select_fusion.2.row_ref, ...), custom_call_target="tpu_custom_call" | custom-call | tf_op jit(solution)/shard_map/upper_layers/pallas_call | solution.py:252
  140.8 2.1 %collective-permute-start.7 = (bf16[608,256]{1,0:T(8,128)(2,1)S(1)}, bf16[608,256]{1,0:T(8,128)(2,1)S(1)}, u32[]{:S(2)}, u32[]{:S(2)}) collective-permute-start(bf16[608,256]{1,0:T(8,128)(2,1)S(1)} %upper_layers.1.rest_15_), channel_id=1, source_target_pairs={{0,8},{8,16},{16,24},{24,28},{28,20},{20,12},{12,4},{4,0},{1,9},{9... | collective-permute-start | bytes 933896 | tf_op jit(solution)/shard_map/ppermute | solution.py:332
  142.9 0.8 collective-permute-start.11
  143.6 7.5 %collective-permute-done.7.rest_14_ = bf16[608,256]{1,0:T(8,128)(2,1)S(1)} collective-permute-done((bf16[608,256]{1,0:T(8,128)(2,1)S(1)}, bf16[608,256]{1,0:T(8,128)(2,1)S(1)}, u32[]{:S(2)}, u32[]{:S(2)}) %collective-permute-start.7) | collective-permute-done | bytes 311328 | tf_op jit(solution)/shard_map/ppermute | solution.py:332
  151.1 1.7 collective-permute-start.8
  152.8 0.8 collective-permute-start.12
  153.6 7.6 %collective-permute-done.8.rest_12_ = bf16[608,256]{1,0:T(8,128)(2,1)S(1)} collective-permute-done((bf16[608,256]{1,0:T(8,128)(2,1)S(1)}, bf16[608,256]{1,0:T(8,128)(2,1)S(1)}, u32[]{:S(2)}, u32[]{:S(2)}) %collective-permute-start.8) | collective-permute-done | bytes 311328 | tf_op jit(solution)/shard_map/ppermute | solution.py:332
  161.9 1.3 collective-permute-start.13
  163.2 6.8 %collective-permute-done.9.rest_10_ = bf16[608,256]{1,0:T(8,128)(2,1)S(1)} collective-permute-done((bf16[608,256]{1,0:T(8,128)(2,1)S(1)}, bf16[608,256]{1,0:T(8,128)(2,1)S(1)}, u32[]{:S(2)}, u32[]{:S(2)}) %collective-permute-start.9) | collective-permute-done | bytes 311328 | tf_op jit(solution)/shard_map/ppermute | solution.py:332
  170.3 6.6 %collective-permute-done.10.rest_8_ = bf16[608,256]{1,0:T(8,128)(2,1)S(1)} collective-permute-done((bf16[608,256]{1,0:T(8,128)(2,1)S(1)}, bf16[608,256]{1,0:T(8,128)(2,1)S(1)}, u32[]{:S(2)}, u32[]{:S(2)}) %collective-permute-start.10) | collective-permute-done | bytes 311328 | tf_op jit(solution)/shard_map/ppermute | solution.py:332
  176.9 1.5 grad_layer.1
  178.5 2.0 %collective-permute-done.14 = f32[608,256]{1,0:T(8,128)S(1)} collective-permute-done((f32[608,256]{1,0:T(8,128)S(1)}, f32[608,256]{1,0:T(8,128)S(1)}, u32[]{:S(2)}, u32[]{:S(2)}) %collective-permute-start.14) | collective-permute-done | bytes 622624 | tf_op jit(solution)/shard_map/ppermute | solution.py:353
  180.7 9.4 %collective-permute-done.15.other_ref = bf16[608,256]{1,0:T(8,128)(2,1)S(1)} collective-permute-done((bf16[608,256]{1,0:T(8,128)(2,1)S(1)}, bf16[608,256]{1,0:T(8,128)(2,1)S(1)}, u32[]{:S(2)}, u32[]{:S(2)}) %collective-permute-start.15) | collective-permute-done | bytes 311328 | tf_op jit(solution)/shard_map/ppermute | solution.py:357
  190.8 2.0 final_sum.1
  (44 shorter events, 7.1 us)
Async XLA Ops:
  7.2 129.3 %all-gather.2.cloned.1.call-start = ((), (), s32[]{:S(2)}) async-start(), calls=%async_computation | async-start | bytes 1179648 | tf_op jit(solution)/shard_map/all_gather | solution.py:394
  74.5 32.7 %collective-permute-start = (bf16[416,256]{1,0:T(8,128)(2,1)S(1)}, bf16[416,256]{1,0:T(8,128)(2,1)S(1)}, u32[]{:S(2)}, u32[]{:S(2)}) collective-permute-start(bf16[416,256]{1,0:T(8,128)(2,1)S(1)} %get-tuple-element.52.rest_0_), channel_id=1, source_target_pairs={{0,28},{8,20},{16,12},{24,4},{28,0},{20,8},{12,16},{4,24},{1,29},{... | collective-permute-start | bytes 638984 | tf_op jit(solution)/shard_map/ppermute | solution.py:332
  78.2 29.1 %collective-permute-start.1 = (bf16[416,256]{1,0:T(8,128)(2,1)S(1)}, bf16[416,256]{1,0:T(8,128)(2,1)S(1)}, u32[]{:S(2)}, u32[]{:S(2)}) collective-permute-start(bf16[416,256]{1,0:T(8,128)(2,1)S(1)} %get-tuple-element.53.rest_1_), channel_id=1, source_target_pairs={{0,24},{8,28},{16,20},{24,12},{28,4},{20,0},{12,8},{4,16},{1,25},{... | collective-permute-start | bytes 638984 | tf_op jit(solution)/shard_map/ppermute | solution.py:332
  78.2 29.1 %collective-permute-start.2 = (bf16[416,256]{1,0:T(8,128)(2,1)S(1)}, bf16[416,256]{1,0:T(8,128)(2,1)S(1)}, u32[]{:S(2)}, u32[]{:S(2)}) collective-permute-start(bf16[416,256]{1,0:T(8,128)(2,1)S(1)} %get-tuple-element.54.rest_2_), channel_id=1, source_target_pairs={{0,20},{8,12},{16,4},{24,0},{28,8},{20,16},{12,24},{4,28},{1,21},{... | collective-permute-start | bytes 638984 | tf_op jit(solution)/shard_map/ppermute | solution.py:332
  107.3 22.7 %collective-permute-start.3 = (bf16[416,256]{1,0:T(8,128)(2,1)S(1)}, bf16[416,256]{1,0:T(8,128)(2,1)S(1)}, u32[]{:S(2)}, u32[]{:S(2)}) collective-permute-start(bf16[416,256]{1,0:T(8,128)(2,1)S(1)} %get-tuple-element.60.rest_3_), channel_id=1, source_target_pairs={{0,16},{8,24},{16,28},{24,20},{28,12},{20,4},{12,0},{4,8},{1,17},{... | collective-permute-start | bytes 638984 | tf_op jit(solution)/shard_map/ppermute | solution.py:332
  109.7 20.3 %collective-permute-start.4 = (bf16[416,256]{1,0:T(8,128)(2,1)S(1)}, bf16[416,256]{1,0:T(8,128)(2,1)S(1)}, u32[]{:S(2)}, u32[]{:S(2)}) collective-permute-start(bf16[416,256]{1,0:T(8,128)(2,1)S(1)} %get-tuple-element.61.rest_4_), channel_id=1, source_target_pairs={{0,12},{8,4},{16,0},{24,8},{28,16},{20,24},{12,28},{4,20},{1,13},{... | collective-permute-start | bytes 638984 | tf_op jit(solution)/shard_map/ppermute | solution.py:332
  110.3 19.8 %collective-permute-start.5 = (bf16[416,256]{1,0:T(8,128)(2,1)S(1)}, bf16[416,256]{1,0:T(8,128)(2,1)S(1)}, u32[]{:S(2)}, u32[]{:S(2)}) collective-permute-start(bf16[416,256]{1,0:T(8,128)(2,1)S(1)} %get-tuple-element.62.rest_5_), channel_id=1, source_target_pairs={{0,8},{8,16},{16,24},{24,28},{28,20},{20,12},{12,4},{4,0},{1,9},{9... | collective-permute-start | bytes 638984 | tf_op jit(solution)/shard_map/ppermute | solution.py:332
  130.1 6.4 %collective-permute-start.6 = (bf16[416,256]{1,0:T(8,128)(2,1)S(1)}, bf16[416,256]{1,0:T(8,128)(2,1)S(1)}, u32[]{:S(2)}, u32[]{:S(2)}) collective-permute-start(bf16[416,256]{1,0:T(8,128)(2,1)S(1)} %get-tuple-element.66.rest_6_), channel_id=1, source_target_pairs={{0,4},{8,0},{16,8},{24,16},{28,24},{20,28},{12,20},{4,12},{1,5},{9... | collective-permute-start | bytes 638984 | tf_op jit(solution)/shard_map/ppermute | solution.py:332
  136.5 1.2 copy-start
  140.8 10.3 %collective-permute-start.7 = (bf16[608,256]{1,0:T(8,128)(2,1)S(1)}, bf16[608,256]{1,0:T(8,128)(2,1)S(1)}, u32[]{:S(2)}, u32[]{:S(2)}) collective-permute-start(bf16[608,256]{1,0:T(8,128)(2,1)S(1)} %upper_layers.1.rest_15_), channel_id=1, source_target_pairs={{0,8},{8,16},{16,24},{24,28},{28,20},{20,12},{12,4},{4,0},{1,9},{9... | collective-permute-start | bytes 933896 | tf_op jit(solution)/shard_map/ppermute | solution.py:332
  142.9 9.9 %collective-permute-start.11 = (bf16[608,256]{1,0:T(8,128)(2,1)S(1)}, bf16[608,256]{1,0:T(8,128)(2,1)S(1)}, u32[]{:S(2)}, u32[]{:S(2)}) collective-permute-start(bf16[608,256]{1,0:T(8,128)(2,1)S(1)} %upper_layers.1.rest_15_), channel_id=1, source_target_pairs={{0,4},{8,0},{16,8},{24,16},{28,24},{20,28},{12,20},{4,12},{1,5},{9... | collective-permute-start | bytes 933896 | tf_op jit(solution)/shard_map/ppermute | solution.py:332
  151.1 10.1 %collective-permute-start.8 = (bf16[608,256]{1,0:T(8,128)(2,1)S(1)}, bf16[608,256]{1,0:T(8,128)(2,1)S(1)}, u32[]{:S(2)}, u32[]{:S(2)}) collective-permute-start(bf16[608,256]{1,0:T(8,128)(2,1)S(1)} %collective-permute-done.7.rest_14_), channel_id=1, source_target_pairs={{0,8},{8,16},{16,24},{24,28},{28,20},{20,12},{12,4},{4,0},{1,9},{9... | collective-permute-start | bytes 933896 | tf_op jit(solution)/shard_map/ppermute | solution.py:332
  152.8 9.1 %collective-permute-start.12 = (bf16[608,256]{1,0:T(8,128)(2,1)S(1)}, bf16[608,256]{1,0:T(8,128)(2,1)S(1)}, u32[]{:S(2)}, u32[]{:S(2)}) collective-permute-start(bf16[608,256]{1,0:T(8,128)(2,1)S(1)} %collective-permute-done.11.rest_13_), channel_id=1, source_target_pairs={{0,4},{8,0},{16,8},{24,16},{28,24},{20,28},{12,20},{4,12},{1,5},{9... | collective-permute-start | bytes 933896 | tf_op jit(solution)/shard_map/ppermute | solution.py:332
  161.2 8.8 %collective-permute-start.9 = (bf16[608,256]{1,0:T(8,128)(2,1)S(1)}, bf16[608,256]{1,0:T(8,128)(2,1)S(1)}, u32[]{:S(2)}, u32[]{:S(2)}) collective-permute-start(bf16[608,256]{1,0:T(8,128)(2,1)S(1)} %collective-permute-done.8.rest_12_), channel_id=1, source_target_pairs={{0,8},{8,16},{16,24},{24,28},{28,20},{20,12},{12,4},{4,0},{1,9},{9... | collective-permute-start | bytes 933896 | tf_op jit(solution)/shard_map/ppermute | solution.py:332
  161.9 8.4 %collective-permute-start.13 = (bf16[608,256]{1,0:T(8,128)(2,1)S(1)}, bf16[608,256]{1,0:T(8,128)(2,1)S(1)}, u32[]{:S(2)}, u32[]{:S(2)}) collective-permute-start(bf16[608,256]{1,0:T(8,128)(2,1)S(1)} %collective-permute-done.12.rest_11_), channel_id=1, source_target_pairs={{0,4},{8,0},{16,8},{24,16},{28,24},{20,28},{12,20},{4,12},{1,5},{9... | collective-permute-start | bytes 933896 | tf_op jit(solution)/shard_map/ppermute | solution.py:332
  170.0 6.9 %collective-permute-start.10 = (bf16[608,256]{1,0:T(8,128)(2,1)S(1)}, bf16[608,256]{1,0:T(8,128)(2,1)S(1)}, u32[]{:S(2)}, u32[]{:S(2)}) collective-permute-start(bf16[608,256]{1,0:T(8,128)(2,1)S(1)} %collective-permute-done.9.rest_10_), channel_id=1, source_target_pairs={{0,8},{8,16},{16,24},{24,28},{28,20},{20,12},{12,4},{4,0},{1,9},{9... | collective-permute-start | bytes 933896 | tf_op jit(solution)/shard_map/ppermute | solution.py:332
  178.4 2.1 %collective-permute-start.14 = (f32[608,256]{1,0:T(8,128)S(1)}, f32[608,256]{1,0:T(8,128)S(1)}, u32[]{:S(2)}, u32[]{:S(2)}) collective-permute-start(f32[608,256]{1,0:T(8,128)S(1)} %grad_layer.1), channel_id=1, source_target_pairs={{0,1},{1,0},{2,3},{3,2},{4,5},{5,4},{6,7},{7,6},{8,9},{9,8},{10,11... | collective-permute-start | bytes 1867784 | tf_op jit(solution)/shard_map/ppermute | solution.py:353
  180.6 9.5 %copy-start.1 = (bf16[608,256]{1,0:T(8,128)(2,1)}, bf16[608,256]{1,0:T(8,128)(2,1)S(1)}, u32[]{:S(2)}) copy-start(bf16[608,256]{1,0:T(8,128)(2,1)S(1)} %add_convert_fusion.mine_ref) | copy-start | bytes 933892
  180.6 9.5 %collective-permute-start.15 = (bf16[608,256]{1,0:T(8,128)(2,1)S(1)}, bf16[608,256]{1,0:T(8,128)(2,1)S(1)}, u32[]{:S(2)}, u32[]{:S(2)}) collective-permute-start(bf16[608,256]{1,0:T(8,128)(2,1)S(1)} %add_convert_fusion.mine_ref), channel_id=1, source_target_pairs={{0,2},{1,3},{2,0},{3,1},{4,6},{5,7},{6,4},{7,5},{8,10},{9,11},{10,... | collective-permute-start | bytes 933896 | tf_op jit(solution)/shard_map/ppermute | solution.py:357
  190.1 0.7 copy-start.2
Sparse Core Ops, SparseCore 0:
  10.1 42.8 all-gather.1

commit v4 on v3

--- a/solution.py
+++ b/solution.py
@@ -47,15 +47,20 @@
     down = lax.broadcasted_iota(jnp.int32, (BLOCK, BLOCK), 0)
     across = lax.broadcasted_iota(jnp.int32, (BLOCK, BLOCK), 1)
     identity = jnp.where(down == across, 1.0, 0.0).astype(jnp.bfloat16)
-    for part in range(chunk // BLOCK):
-        piece = feats_ref[:, part * BLOCK : (part + 1) * BLOCK]
-        if padded > width:
-            piece = jnp.concatenate([piece, jnp.zeros((padded - width, BLOCK), piece.dtype)], axis=0)
+    filler = jnp.zeros((padded - width, BLOCK), feats_ref.dtype)
+    for part in range(0, chunk // BLOCK, 2):
+        pieces = []
+        for at in (part * BLOCK, (part + 1) * BLOCK):
+            pieces.append(feats_ref[:, at : at + BLOCK])
+            if padded > width:
+                pieces.append(filler)
         turned = lax.dot_general(
-            identity, piece, (((1,), (1,)), ((), ())), preferred_element_type=jnp.float32
-        )
-        start = pl.multiple_of(step * chunk + part * BLOCK, BLOCK)
-        table_ref[pl.ds(start, BLOCK), :] = turned.astype(jnp.bfloat16)
+            identity, jnp.concatenate(pieces, axis=0), (((1,), (1,)), ((), ())),
+            preferred_element_type=jnp.float32,
+        ).astype(jnp.bfloat16)
+        for side in range(2):
+            start = pl.multiple_of(step * chunk + (part + side) * BLOCK, BLOCK)
+            table_ref[pl.ds(start, BLOCK), :] = turned[:, side * padded : (side + 1) * padded]
 
 
 def build_table(node_feats):
@@ -76,39 +81,32 @@
 def gather_kernel(
     fanout, capacity, turn_ref, enough_ref, order_ref, own_ref, near_ref, count_ref, table_ref, *rest
 ):
-    *inputs_refs, _, mask_ref, own_sum_ref, near_sum_ref = rest
+    *inputs_refs, _, own_sum_ref, near_sum_ref = rest
     step = pl.program_id(0)
     width = inputs_refs[0].shape[1] // 2
     padded = table_ref.shape[1]
 
-    @pl.when(step == 0)
-    def _():
-        shape = mask_ref.shape
-        code = lax.broadcasted_iota(jnp.int32, shape, 0)
-        line = lax.broadcasted_iota(jnp.int32, shape, 1)
-        mask_ref[...] = jnp.where(code == line, 1.0, 0.0).astype(jnp.bfloat16)
-
     tiles = table_ref.reshape(table_ref.shape[0] // TILE, TILE, padded)
+    half = TILE // 2
+    low = lax.broadcasted_iota(jnp.int32, (half, padded), 0)
+    high = low + half
 
     def fetch(node):
-        return (tiles[node >> TILE_BITS] * mask_ref[node & (TILE - 1)]).astype(jnp.float32)
-
-    def fold(value):
-        return value[: TILE // 2] + value[TILE // 2 :]
+        tile = tiles[node >> TILE_BITS].astype(jnp.float32)
+        line = jnp.full((half, padded), node, jnp.int32) & (TILE - 1)
+        return jnp.where(line == low, tile[:half], jnp.where(line == high, tile[half:], 0.0))
 
     def gather_rows(slots, first, number):
-        owns, nears = [], []
+        rows = [order_ref[0, 0, first + i] >> 4 for i in range(number)]
+        starts = [row * fanout for row in rows]
+        owns = [fetch(own_ref[0, 0, row]) for row in rows]
+        nears = [fetch(near_ref[0, 0, start]) for start in starts]
+        for slot in range(1, slots):
+            nears = [near + fetch(near_ref[0, 0, start + slot]) for near, start in zip(nears, starts)]
         for i in range(number):
-            row = order_ref[0, 0, first + i] >> 4
-            owns.append(fold(fetch(own_ref[0, 0, row])))
-            totals = [fetch(near_ref[0, 0, row * fanout + slot]) for slot in range(slots)]
-            while len(totals) > 1:
-                totals = [sum(totals[at + 1 : at + 2], totals[at]) for at in range(0, len(totals), 2)]
-            nears.append(fold(totals[0]))
-        for i in range(number):
-            start = pl.multiple_of((first + i) * 8, 8)
-            own_sum_ref[pl.ds(start, 8), :] = owns[i]
-            near_sum_ref[pl.ds(start, 8), :] = nears[i]
+            place = pl.multiple_of((first + i) * half, half)
+            own_sum_ref[pl.ds(place, half), :] = owns[i]
+            near_sum_ref[pl.ds(place, half), :] = nears[i]
 
     begin = 0
     for slots in range(fanout, 0, -1):
@@ -181,7 +179,6 @@
             out_specs=[pl.BlockSpec((capacity, 2 * width), lambda step, turn_ref: (0, 0))] * groups
             + [pl.BlockSpec(memory_space=pltpu.VMEM)],
             scratch_shapes=[
-                pltpu.VMEM((TILE, TILE, padded), jnp.bfloat16),
                 pltpu.VMEM((capacity * 8, padded), jnp.float32),
                 pltpu.VMEM((capacity * 8, padded), jnp.float32),
             ],
@@ -201,7 +198,7 @@
 
 
 def upper_kernel(fanout, size_ref, turn_ref, weights_ref, layer_ref, row_ref, seed_ref, *rest):
-    *inputs_refs, out_ref = rest
+    *inputs_refs, upper_ref, lower_ref = rest
     seed_total = seed_ref.shape[1]
     capacity = inputs_refs[0].shape[0]
     hidden_width = weights_ref.shape[2]
@@ -236,46 +233,56 @@
     spread = spread + lax.dot_general(
         is_near, back_near.astype(jnp.bfloat16), rows, preferred_element_type=jnp.float32
     )
-    out_ref[:capacity] = jnp.where(preact > 0, spread, 0.0).astype(jnp.bfloat16)
-    out_ref[capacity : capacity + seed_total] = seed_hidden
-    out_ref[capacity + seed_total : capacity + 2 * seed_total] = near_mean
-    out_ref[capacity + 2 * seed_total :] = jnp.zeros((seed_total, hidden_width), jnp.bfloat16)
-    out_ref[capacity + 2 * seed_total :, :classes] = dlogits
+    dpreact = jnp.where(preact > 0, spread, 0.0).astype(jnp.bfloat16)
+    split = upper_ref.shape[0]
+    upper_ref[...] = dpreact[:split]
+    lower_ref[: capacity - split] = dpreact[split:]
+    units = [seed_hidden, near_mean, jnp.zeros((seed_total, hidden_width), jnp.bfloat16)]
+    for part, unit in enumerate(units):
+        start = capacity - split + part * seed_total
+        lower_ref[start : start + seed_total] = unit
+    lower_ref[capacity - split + 2 * seed_total :, :classes] = dlogits
 
 
 def upper_layers(inputs, size, turn, weights, layer, row, seeds, fanout):
     seed_total = seeds.shape[1]
     capacity = inputs[0].shape[0]
     hidden_width = weights.shape[2]
+    total = capacity + 3 * seed_total
+    split = round_up(total // 2, 16)
     smem = pl.BlockSpec(memory_space=pltpu.SMEM)
     vmem = pl.BlockSpec(memory_space=pltpu.VMEM)
     return pl.pallas_call(
         functools.partial(upper_kernel, fanout),
         in_specs=[smem] * 2 + [vmem] * (4 + len(inputs)),
-        out_specs=vmem,
-        out_shape=jax.ShapeDtypeStruct((capacity + 3 * seed_total, hidden_width), jnp.bfloat16),
+        out_specs=[vmem] * 2,
+        out_shape=[jax.ShapeDtypeStruct((length, hidden_width), jnp.bfloat16) for length in (split, total - split)],
         compiler_params=pltpu.CompilerParams(vmem_limit_bytes=32 * 2**20),
         name="upper_layers",
     )(size, turn, weights, layer, row, seeds, *inputs)
 
 
 def grad_kernel(seed_total, classes, source_ref, *rest):
-    count = (len(rest) - 2) // 2
-    inputs_refs, sent_refs = rest[:count], rest[count : 2 * count]
-    out_ref, units_ref = rest[2 * count :]
+    count = (len(rest) - 2) // 3
+    inputs_refs, upper_refs, lower_refs = rest[:count], rest[count : 2 * count], rest[2 * count : 3 * count]
+    out_ref, units_ref = rest[3 * count :]
     capacity, double = inputs_refs[0].shape
     hidden_width = out_ref.shape[1]
+    split = upper_refs[0].shape[0]
     rows = (((0,), (0,)), ((), ()))
     first = jnp.zeros((double, hidden_width), jnp.float32)
     for place in range(count):
+        inputs_ref, upper_ref, lower_ref = inputs_refs[place], upper_refs[place], lower_refs[place]
         first = first + lax.dot_general(
-            inputs_refs[place][...], sent_refs[place][:capacity], rows, preferred_element_type=jnp.float32
+            inputs_ref[:split], upper_ref[...], rows, preferred_element_type=jnp.float32
+        )
+        first = first + lax.dot_general(
+            inputs_ref[split:], lower_ref[: capacity - split], rows, preferred_element_type=jnp.float32
         )
         start = pl.multiple_of(source_ref[place] * seed_total, seed_total)
         for part in range(3):
-            units_ref[part, pl.ds(start, seed_total), :] = sent_refs[place][
-                capacity + part * seed_total : capacity + (part + 1) * seed_total
-            ]
+            begin = capacity - split + part * seed_total
+            units_ref[part, pl.ds(start, seed_total), :] = lower_ref[begin : begin + seed_total]
     out_ref[:double] = first
     for layer in range(2):
         second = lax.dot_general(units_ref[2], units_ref[layer], rows, preferred_element_type=jnp.float32)
@@ -283,19 +290,19 @@
         out_ref[start : start + round_up(classes, 8)] = second[: round_up(classes, 8)]
 
 
-def grad_layer(inputs, sent, sources, seed_total, classes):
+def grad_layer(inputs, upper, lower, sources, seed_total, classes):
     capacity, double = inputs[0].shape
-    hidden_width = sent[0].shape[1]
+    hidden_width = upper[0].shape[1]
     vmem = pl.BlockSpec(memory_space=pltpu.VMEM)
     return pl.pallas_call(
         functools.partial(grad_kernel, seed_total, classes),
-        in_specs=[pl.BlockSpec(memory_space=pltpu.SMEM)] + [vmem] * (2 * len(inputs)),
+        in_specs=[pl.BlockSpec(memory_space=pltpu.SMEM)] + [vmem] * (3 * len(inputs)),
         out_specs=vmem,
         out_shape=jax.ShapeDtypeStruct((double + 2 * round_up(classes, 8), hidden_width), jnp.float32),
         scratch_shapes=[pltpu.VMEM((3, len(inputs) * seed_total, hidden_width), jnp.bfloat16)],
         compiler_params=pltpu.CompilerParams(vmem_limit_bytes=40 * 2**20),
         name="grad_layer",
-    )(sources, *inputs, *sent)
+    )(sources, *inputs, *upper, *lower)
 
 
 def final_kernel(mine_ref, other_ref, first_ref, second_ref):
@@ -332,17 +339,17 @@
     return lax.ppermute(array, "feat", [(ring[i], ring[(i + shift) % count]) for i in range(count)])
 
 
-def ring_gather(array, ring):
+def ring_gather(upper, lower, ring):
     count = len(ring)
-    result = [array] + [None] * (count - 1)
-    ahead = behind = array
+    halves = [[half] + [None] * (count - 1) for half in (upper, lower)]
+    moving = [[half, half] for half in (upper, lower)]
     for hop in range(1, count // 2 + 1):
-        behind = send_along(behind, ring, 1)
-        result[count - hop] = behind
-        if 2 * hop < count:
-            ahead = send_along(ahead, ring, -1)
-            result[hop] = ahead
-    return result
+        for half in range(2):
+            for way, sign in enumerate((1, -1)):
+                if 2 * hop < count or half == way:
+                    moving[half][way] = send_along(moving[half][way], ring, sign)
+                    halves[half][-sign * hop % count] = moving[half][way]
+    return halves
 
 
 def group_sum(grads, width, classes):
@@ -399,6 +406,22 @@
         jnp.concatenate([seed_ids, hop1_ids], axis=1)[:, None, :],
         hop2_ids[:, None, :],
     ]
+    node_feats, turn, *lists = lax.optimization_barrier((node_feats, turn, *lists))
+    table = build_table(node_feats)
+    inputs, received, arrived = [], [], []
+    for call in range(CALLS):
+        begin, end = -(-call * count // CALLS), -(-(call + 1) * count // CALLS)
+        *blocks, table = gather_layer(table, turn, begin, end, *lists, slice_width, capacity)
+        if call < CALLS - 1:
+            table, blocks, arrived = lax.optimization_barrier((table, blocks, arrived))
+        else:
+            blocks, arrived, order, hop1_count, label_ids, sizes, second_layer = lax.optimization_barrier(
+                (blocks, arrived, order, hop1_count, label_ids, sizes, second_layer)
+            )
+        inputs += blocks
+        received += arrived
+        arrived = [send_along(block, ring, t) if t else block for t, block in zip(places[begin:end], blocks)]
+    received += arrived
 
     def own(array):
         return lax.dynamic_index_in_dim(array, column_rank, 0, keepdims=False)
@@ -409,23 +432,11 @@
     seeds = jnp.broadcast_to(seeds[:, :, None], (2, seed_total, LANES))
     size = lax.dynamic_slice_in_dim(sizes, column_rank, 1)
     layer = jnp.transpose(second_layer, (0, 2, 1))
-    node_feats, turn, size, layer, row, seeds, *lists = lax.optimization_barrier(
-        (node_feats, turn, size, layer, row, seeds, *lists)
-    )
-    table = build_table(node_feats)
-    inputs, received, arrived = [], [], []
-    for call in range(CALLS):
-        begin, end = -(-call * count // CALLS), -(-(call + 1) * count // CALLS)
-        *blocks, table = gather_layer(table, turn, begin, end, *lists, slice_width, capacity)
-        table, blocks, arrived = lax.optimization_barrier((table, blocks, arrived))
-        inputs += blocks
-        received += arrived
-        arrived = [send_along(block, ring, t) if t else block for t, block in zip(places[begin:end], blocks)]
-    received += arrived
-
-    sent = upper_layers(received, size, turn, weights, layer, row, seeds, fanout)
-    every = ring_gather(sent, ring)
-    grads = grad_layer(inputs, [every[t] for t in places], turn, seed_total, classes)
+    halves = upper_layers(received, size, turn, weights, layer, row, seeds, fanout)
+    upper, lower = ring_gather(*halves, ring)
+    grads = grad_layer(
+        inputs, [upper[t] for t in places], [lower[t] for t in places], turn, seed_total, classes
+    )
     return tuple(group_sum(grads, slice_width, classes))
 
 

time: 199 us -> 166 us (0.83)
  Pallas kernels: 102 us -> 77.5 us
  waiting for transfers between devices: 45.6 us -> 28.1 us
  starting transfers between devices: 22.2 us -> 33 us
    pallas_call x3, Pallas kernels: 71.1 us -> 49.8 us  [gather_layer(): pl.pallas_call(functools.partial(gather_kernel, fanout, capacity), grid_s...]
    ppermute x14 -> x21, waiting for transfers between devices: 33.5 us -> 16 us  [send_along(): lax.ppermute(array, 'feat', [(ring[i], ring[(i + shift) % count]) for i i...]
    ppermute x14 -> x21, starting transfers between devices: 22 us -> 32.8 us  [send_along(): lax.ppermute(array, 'feat', [(ring[i], ring[(i + shift) % count]) for i i...]
    pallas_call x1, Pallas kernels: 24.6 us -> 20.9 us  [build_table(): pl.pallas_call(table_kernel, grid=(nodes // chunk,), in_specs=[pl.BlockSp...]
  transfers between devices with their start and end apart: 17 -> 24, of which waited for: 7 -> 15; matrix products, arithmetic and copies ran while one was open for 7% -> 7% of each run, Pallas kernels for 48% -> 42%
where the time goes in v4:
time: 166 us; the launch traced here: 167 us
  Pallas kernels  77.5 us (47%)
  starting transfers between devices  33 us (20%)
  waiting for transfers between devices  28.1 us (17%)
  between operations  14.3 us (9%)
  other arithmetic  7.49 us (5%)
  local copies, waits for them, and re-layouts  6.33 us (4%)
    pallas_call x3, Pallas kernels, gather_layer(): pl.pallas_call(functools.partial(gather_kernel, fanout, capacity), grid_s...  49.8 us
    ppermute x21, starting transfers between devices, send_along(): lax.ppermute(array, 'feat', [(ring[i], ring[(i + shift) % count]) for i i...  32.8 us
    pallas_call x1, Pallas kernels, build_table(): pl.pallas_call(table_kernel, grid=(nodes // chunk,), in_specs=[pl.BlockSp...  20.9 us
    ppermute x21, waiting for transfers between devices, send_along(): lax.ppermute(array, 'feat', [(ring[i], ring[(i + shift) % count]) for i i...  16 us
    ppermute x1, waiting for transfers between devices, group_sum(): other = lax.ppermute(mine, 'dp', [(i, i ^ stride) for i in range(count)])  9.39 us
  transfers between devices with their start and end apart: 24, of which 15 were waited for; matrix products, arithmetic and copies ran while one was open for 7% of the time, Pallas kernels for 42%

profile of v4, /device:TPU:0, one launch (start us, length us, event | category | flops | bytes accessed | tf_op | source)
XLA Modules:
  0.0 166.7 jit_solution(3484239807729306412)
XLA Ops:
  10.8 2.5 %convert_reduce_fusion = s32[8,704]{1,0:T(8,128)S(1)} fusion(s32[8,704]{1,0:T(8,128)S(1)} %get-tuple-element.86), kind=kLoop, calls=%fused_computation | loop fusion | flops 11889152 | bytes 45056 | tf_op jit(solution)/shard_map/reduce_sum | solution.py:32
  13.3 2.1 %select_reduce_fusion = s32[8,512]{1,0:T(8,128)S(1)} fusion(s32[8,704]{1,0:T(8,128)S(1)} %broadcast_add_fusion, s32[8,704]{1,0:T(8,128)S(1)} %convert_reduce_fusion), kind=kLoop, calls=%fused_computation.1 | loop fusion | flops 8646656 | bytes 61440 | tf_op jit(solution)/shard_map/reduce_sum | solution.py:34
  15.4 1.1 broadcast_in_dim.61.near_ref
  18.3 20.9 %build_table.1.table_ref = bf16[131072,128]{1,0:T(8,128)(2,1)S(1)} custom-call(bf16[128,131072]{1,0:T(8,128)(2,1)} %feats_ref), custom_call_target="tpu_custom_call" | custom-call | tf_op jit(solution)/shard_map/build_table/pallas_call | solution.py:70
  39.3 17.0 %gather_layer.3 = (bf16[416,256]{1,0:T(8,128)(2,1)S(1)}, bf16[416,256]{1,0:T(8,128)(2,1)S(1)}, bf16[416,256]{1,0:T(8,128)(2,1)S(1)}, bf16[131072,128]{1,0:T(8,128)(2,1)S(1)}) custom-call(s32[16]{0:T(128)S(1)} %fusion.3.turn_ref.source_ref, s32[8,1,16]{2,1,0:T(1,128)S(1)} %bitcast.10, ...), custom_call_target="tpu_custom_call", output_to_operand_aliasing={{3}: (6, {})} | custom-call | bytes 51118080 | tf_op jit(solution)/shard_map/gather_layer/pallas_call | solution.py:166
  56.3 8.0 %collective-permute-start = (bf16[416,256]{1,0:T(8,128)(2,1)S(1)}, bf16[416,256]{1,0:T(8,128)(2,1)S(1)}, u32[]{:S(2)}, u32[]{:S(2)}) collective-permute-start(bf16[416,256]{1,0:T(8,128)(2,1)S(1)} %get-tuple-element.55.rest_0_), channel_id=1, source_target_pairs={{0,28},{8,20},{16,12},{24,4},{28,0},{20,8},{12,16},{4,24},{1,29},{... | collective-permute-start | bytes 638984 | tf_op jit(solution)/shard_map/ppermute | solution.py:339
  64.3 3.8 %collective-permute-start.2 = (bf16[416,256]{1,0:T(8,128)(2,1)S(1)}, bf16[416,256]{1,0:T(8,128)(2,1)S(1)}, u32[]{:S(2)}, u32[]{:S(2)}) collective-permute-start(bf16[416,256]{1,0:T(8,128)(2,1)S(1)} %get-tuple-element.57.rest_2_), channel_id=1, source_target_pairs={{0,20},{8,12},{16,4},{24,0},{28,8},{20,16},{12,24},{4,28},{1,21},{... | collective-permute-start | bytes 638984 | tf_op jit(solution)/shard_map/ppermute | solution.py:339
  68.2 19.1 %gather_layer.4 = (bf16[416,256]{1,0:T(8,128)(2,1)S(1)}, bf16[416,256]{1,0:T(8,128)(2,1)S(1)}, bf16[416,256]{1,0:T(8,128)(2,1)S(1)}, bf16[131072,128]{1,0:T(8,128)(2,1)S(1)}) custom-call(s32[16]{0:T(128)S(1)} %fusion.3.turn_ref.source_ref, s32[8,1,16]{2,1,0:T(1,128)S(1)} %bitcast.11, ...), custom_call_target="tpu_custom_call", output_to_operand_aliasing={{3}: (6, {})} | custom-call | bytes 51118080 | tf_op jit(solution)/shard_map/gather_layer/pallas_call | solution.py:166
  87.7 2.9 %collective-permute-start.4 = (bf16[416,256]{1,0:T(8,128)(2,1)S(1)}, bf16[416,256]{1,0:T(8,128)(2,1)S(1)}, u32[]{:S(2)}, u32[]{:S(2)}) collective-permute-start(bf16[416,256]{1,0:T(8,128)(2,1)S(1)} %get-tuple-element.64.rest_4_), channel_id=1, source_target_pairs={{0,12},{8,4},{16,0},{24,8},{28,16},{20,24},{12,28},{4,20},{1,13},{... | collective-permute-start | bytes 638984 | tf_op jit(solution)/shard_map/ppermute | solution.py:339
  90.6 13.7 %gather_layer.5 = (bf16[416,256]{1,0:T(8,128)(2,1)S(1)}, bf16[416,256]{1,0:T(8,128)(2,1)S(1)}, bf16[131072,128]{1,0:T(8,128)(2,1)S(1)}) custom-call(s32[16]{0:T(128)S(1)} %fusion.3.turn_ref.source_ref, s32[8,1,16]{2,1,0:T(1,128)S(1)} %bitcast.12, s32[8,1,512]{2,1,0:T(1,128)S(1)} %broadcast_in_dim.59.order_ref, ...), custom_call_target="tpu_custom_call", output_to_operand_aliasing={{2}: (6, {})} | custom-call | bytes 34078720 | tf_op jit(solution)/shard_map/gather_layer/pallas_call | solution.py:166
  104.3 2.1 %collective-permute-start.6 = (bf16[416,256]{1,0:T(8,128)(2,1)S(1)}, bf16[416,256]{1,0:T(8,128)(2,1)S(1)}, u32[]{:S(2)}, u32[]{:S(2)}) collective-permute-start(bf16[416,256]{1,0:T(8,128)(2,1)S(1)} %get-tuple-element.69.rest_6_), channel_id=1, source_target_pairs={{0,4},{8,0},{16,8},{24,16},{28,24},{20,28},{12,20},{4,12},{1,5},{9... | collective-permute-start | bytes 638984 | tf_op jit(solution)/shard_map/ppermute | solution.py:339
  107.8 3.7 %collective-permute-done.6.rest_6_ = bf16[416,256]{1,0:T(8,128)(2,1)S(1)} collective-permute-done((bf16[416,256]{1,0:T(8,128)(2,1)S(1)}, bf16[416,256]{1,0:T(8,128)(2,1)S(1)}, u32[]{:S(2)}, u32[]{:S(2)}) %collective-permute-start.6) | collective-permute-done | bytes 213024 | tf_op jit(solution)/shard_map/ppermute | solution.py:339
  111.6 1.2 copy-done
  112.8 3.1 %upper_layers.1 = (bf16[304,256]{1,0:T(8,128)(2,1)S(1)}, bf16[304,256]{1,0:T(8,128)(2,1)S(1)}) custom-call(s32[1]{0:T(128)} %dynamic_slice.23.size_ref, s32[16]{0:T(128)S(1)} %fusion.3.turn_ref.source_ref, bf16[8,256,256]{2,1,0:T(8,128)(2,1)S(1)} %copy-done, bf16[2,172,256]{2,1,0:T(8,128)(2,1)S(1)} %bitcast.9, s32[1,416]{1,0:T(1,128)S(1)} %compare_select_fusion.2.row_ref, ...), custom_call_target="tpu_custom_call" | custom-call | tf_op jit(solution)/shard_map/upper_layers/pallas_call | solution.py:255
  115.9 1.1 collective-permute-start.7
  117.1 1.0 collective-permute-start.14
  118.1 2.0 %collective-permute-start.11 = (bf16[304,256]{1,0:T(8,128)(2,1)S(1)}, bf16[304,256]{1,0:T(8,128)(2,1)S(1)}, u32[]{:S(2)}, u32[]{:S(2)}) collective-permute-start(bf16[304,256]{1,0:T(8,128)(2,1)S(1)} %get-tuple-element.82.rest_15_), channel_id=1, source_target_pairs={{0,4},{8,0},{16,8},{24,16},{28,24},{20,28},{12,20},{4,12},{1,5},{9... | collective-permute-start | bytes 466952 | tf_op jit(solution)/shard_map/ppermute | solution.py:339
  120.1 1.5 collective-permute-done.7.rest_14_
  121.6 1.8 %collective-permute-start.8 = (bf16[304,256]{1,0:T(8,128)(2,1)S(1)}, bf16[304,256]{1,0:T(8,128)(2,1)S(1)}, u32[]{:S(2)}, u32[]{:S(2)}) collective-permute-start(bf16[304,256]{1,0:T(8,128)(2,1)S(1)} %collective-permute-done.7.rest_14_), channel_id=1, source_target_pairs={{0,8},{8,16},{16,24},{24,28},{28,20},{20,12},{12,4},{4,0},{1,9},{9... | collective-permute-start | bytes 466952 | tf_op jit(solution)/shard_map/ppermute | solution.py:339
  124.0 1.0 collective-permute-start.15
  125.0 2.3 %collective-permute-done.11.rest_13_ = bf16[304,256]{1,0:T(8,128)(2,1)S(1)} collective-permute-done((bf16[304,256]{1,0:T(8,128)(2,1)S(1)}, bf16[304,256]{1,0:T(8,128)(2,1)S(1)}, u32[]{:S(2)}, u32[]{:S(2)}) %collective-permute-start.11) | collective-permute-done | bytes 155680 | tf_op jit(solution)/shard_map/ppermute | solution.py:339
  127.4 1.0 collective-permute-start.12
  130.5 1.5 collective-permute-start.16
  132.0 2.2 %collective-permute-done.12.rest_11_ = bf16[304,256]{1,0:T(8,128)(2,1)S(1)} collective-permute-done((bf16[304,256]{1,0:T(8,128)(2,1)S(1)}, bf16[304,256]{1,0:T(8,128)(2,1)S(1)}, u32[]{:S(2)}, u32[]{:S(2)}) %collective-permute-start.12) | collective-permute-done | bytes 155680 | tf_op jit(solution)/shard_map/ppermute | solution.py:339
  134.2 1.1 collective-permute-start.13
  137.3 1.3 collective-permute-start.10
  138.5 1.3 collective-permute-start.17
  140.6 2.5 %collective-permute-done.10.rest_8_ = bf16[304,256]{1,0:T(8,128)(2,1)S(1)} collective-permute-done((bf16[304,256]{1,0:T(8,128)(2,1)S(1)}, bf16[304,256]{1,0:T(8,128)(2,1)S(1)}, u32[]{:S(2)}, u32[]{:S(2)}) %collective-permute-start.10) | collective-permute-done | bytes 155680 | tf_op jit(solution)/shard_map/ppermute | solution.py:339
  143.8 1.8 %grad_layer.1 = f32[608,256]{1,0:T(8,128)S(1)} custom-call(s32[16]{0:T(128)S(1)} %fusion.3.turn_ref.source_ref, bf16[416,256]{1,0:T(8,128)(2,1)S(1)} %get-tuple-element.55.rest_0_, bf16[416,256]{1,0:T(8,128)(2,1)S(1)} %get-tuple-element.56.rest_1_, bf16[416,256]{1,0:T(8,128)(2,1)S(1)} %get-tuple-element.57.rest_2_, ...), custom_call_target="tpu_custom_call" | custom-call | tf_op jit(solution)/shard_map/grad_layer/pallas_call | solution.py:297
  145.6 2.0 %collective-permute-done.21 = f32[608,256]{1,0:T(8,128)S(1)} collective-permute-done((f32[608,256]{1,0:T(8,128)S(1)}, f32[608,256]{1,0:T(8,128)S(1)}, u32[]{:S(2)}, u32[]{:S(2)}) %collective-permute-start.21) | collective-permute-done | bytes 622624 | tf_op jit(solution)/shard_map/ppermute | solution.py:360
  147.8 9.4 %collective-permute-done.22.other_ref = bf16[608,256]{1,0:T(8,128)(2,1)S(1)} collective-permute-done((bf16[608,256]{1,0:T(8,128)(2,1)S(1)}, bf16[608,256]{1,0:T(8,128)(2,1)S(1)}, u32[]{:S(2)}, u32[]{:S(2)}) %collective-permute-start.22) | collective-permute-done | bytes 311328 | tf_op jit(solution)/shard_map/ppermute | solution.py:364
  157.9 2.0 %final_sum.1 = (f32[2,128,256]{2,1,0:T(8,128)}, f32[172,2,256]{2,1,0:T(2,128)}) custom-call(bf16[608,256]{1,0:T(8,128)(2,1)} %copy-done.1, bf16[608,256]{1,0:T(8,128)(2,1)} %copy-done.2), custom_call_target="tpu_custom_call" | custom-call | tf_op jit(solution)/shard_map/final_sum/pallas_call | solution.py:320
  (60 shorter events, 14.3 us)
Async XLA Ops:
  7.2 104.4 %all-gather.2.cloned.1.call-start = ((), (), s32[]{:S(2)}) async-start(), calls=%async_computation | async-start | bytes 1179648 | tf_op jit(solution)/shard_map/all_gather | solution.py:401
  56.3 31.0 %collective-permute-start = (bf16[416,256]{1,0:T(8,128)(2,1)S(1)}, bf16[416,256]{1,0:T(8,128)(2,1)S(1)}, u32[]{:S(2)}, u32[]{:S(2)}) collective-permute-start(bf16[416,256]{1,0:T(8,128)(2,1)S(1)} %get-tuple-element.55.rest_0_), channel_id=1, source_target_pairs={{0,28},{8,20},{16,12},{24,4},{28,0},{20,8},{12,16},{4,24},{1,29},{... | collective-permute-start | bytes 638984 | tf_op jit(solution)/shard_map/ppermute | solution.py:339
  64.3 23.3 %collective-permute-start.1 = (bf16[416,256]{1,0:T(8,128)(2,1)S(1)}, bf16[416,256]{1,0:T(8,128)(2,1)S(1)}, u32[]{:S(2)}, u32[]{:S(2)}) collective-permute-start(bf16[416,256]{1,0:T(8,128)(2,1)S(1)} %get-tuple-element.56.rest_1_), channel_id=1, source_target_pairs={{0,24},{8,28},{16,20},{24,12},{28,4},{20,0},{12,8},{4,16},{1,25},{... | collective-permute-start | bytes 638984 | tf_op jit(solution)/shard_map/ppermute | solution.py:339
  64.3 23.3 %collective-permute-start.2 = (bf16[416,256]{1,0:T(8,128)(2,1)S(1)}, bf16[416,256]{1,0:T(8,128)(2,1)S(1)}, u32[]{:S(2)}, u32[]{:S(2)}) collective-permute-start(bf16[416,256]{1,0:T(8,128)(2,1)S(1)} %get-tuple-element.57.rest_2_), channel_id=1, source_target_pairs={{0,20},{8,12},{16,4},{24,0},{28,8},{20,16},{12,24},{4,28},{1,21},{... | collective-permute-start | bytes 638984 | tf_op jit(solution)/shard_map/ppermute | solution.py:339
  87.3 19.2 %copy-start.3 = (bf16[2,256,172]{1,0,2:T(2,128)(2,1)S(1)}, bf16[2,256,172]{1,0,2:T(2,128)(2,1)}, u32[]{:S(2)}) copy-start(bf16[2,256,172]{1,0,2:T(2,128)(2,1)} %param.13) | copy-start | bytes 528388
  87.7 16.6 %collective-permute-start.3 = (bf16[416,256]{1,0:T(8,128)(2,1)S(1)}, bf16[416,256]{1,0:T(8,128)(2,1)S(1)}, u32[]{:S(2)}, u32[]{:S(2)}) collective-permute-start(bf16[416,256]{1,0:T(8,128)(2,1)S(1)} %get-tuple-element.63.rest_3_), channel_id=1, source_target_pairs={{0,16},{8,24},{16,28},{24,20},{28,12},{20,4},{12,0},{4,8},{1,17},{... | collective-permute-start | bytes 638984 | tf_op jit(solution)/shard_map/ppermute | solution.py:339
  87.7 16.6 %collective-permute-start.4 = (bf16[416,256]{1,0:T(8,128)(2,1)S(1)}, bf16[416,256]{1,0:T(8,128)(2,1)S(1)}, u32[]{:S(2)}, u32[]{:S(2)}) collective-permute-start(bf16[416,256]{1,0:T(8,128)(2,1)S(1)} %get-tuple-element.64.rest_4_), channel_id=1, source_target_pairs={{0,12},{8,4},{16,0},{24,8},{28,16},{20,24},{12,28},{4,20},{1,13},{... | collective-permute-start | bytes 638984 | tf_op jit(solution)/shard_map/ppermute | solution.py:339
  90.6 13.7 %collective-permute-start.5 = (bf16[416,256]{1,0:T(8,128)(2,1)S(1)}, bf16[416,256]{1,0:T(8,128)(2,1)S(1)}, u32[]{:S(2)}, u32[]{:S(2)}) collective-permute-start(bf16[416,256]{1,0:T(8,128)(2,1)S(1)} %get-tuple-element.65.rest_5_), channel_id=1, source_target_pairs={{0,8},{8,16},{16,24},{24,28},{28,20},{20,12},{12,4},{4,0},{1,9},{9... | collective-permute-start | bytes 638984 | tf_op jit(solution)/shard_map/ppermute | solution.py:339
  104.3 7.2 %collective-permute-start.6 = (bf16[416,256]{1,0:T(8,128)(2,1)S(1)}, bf16[416,256]{1,0:T(8,128)(2,1)S(1)}, u32[]{:S(2)}, u32[]{:S(2)}) collective-permute-start(bf16[416,256]{1,0:T(8,128)(2,1)S(1)} %get-tuple-element.69.rest_6_), channel_id=1, source_target_pairs={{0,4},{8,0},{16,8},{24,16},{28,24},{20,28},{12,20},{4,12},{1,5},{9... | collective-permute-start | bytes 638984 | tf_op jit(solution)/shard_map/ppermute | solution.py:339
  111.6 1.2 copy-start
  115.9 5.7 %collective-permute-start.7 = (bf16[304,256]{1,0:T(8,128)(2,1)S(1)}, bf16[304,256]{1,0:T(8,128)(2,1)S(1)}, u32[]{:S(2)}, u32[]{:S(2)}) collective-permute-start(bf16[304,256]{1,0:T(8,128)(2,1)S(1)} %get-tuple-element.82.rest_15_), channel_id=1, source_target_pairs={{0,8},{8,16},{16,24},{24,28},{28,20},{20,12},{12,4},{4,0},{1,9},{9... | collective-permute-start | bytes 466952 | tf_op jit(solution)/shard_map/ppermute | solution.py:339
  117.1 7.0 %collective-permute-start.14 = (bf16[304,256]{1,0:T(8,128)(2,1)S(1)}, bf16[304,256]{1,0:T(8,128)(2,1)S(1)}, u32[]{:S(2)}, u32[]{:S(2)}) collective-permute-start(bf16[304,256]{1,0:T(8,128)(2,1)S(1)} %get-tuple-element.83.rest_23_), channel_id=1, source_target_pairs={{0,4},{8,0},{16,8},{24,16},{28,24},{20,28},{12,20},{4,12},{1,5},{9... | collective-permute-start | bytes 466952 | tf_op jit(solution)/shard_map/ppermute | solution.py:339
  118.1 9.3 %collective-permute-start.11 = (bf16[304,256]{1,0:T(8,128)(2,1)S(1)}, bf16[304,256]{1,0:T(8,128)(2,1)S(1)}, u32[]{:S(2)}, u32[]{:S(2)}) collective-permute-start(bf16[304,256]{1,0:T(8,128)(2,1)S(1)} %get-tuple-element.82.rest_15_), channel_id=1, source_target_pairs={{0,4},{8,0},{16,8},{24,16},{28,24},{20,28},{12,20},{4,12},{1,5},{9... | collective-permute-start | bytes 466952 | tf_op jit(solution)/shard_map/ppermute | solution.py:339
  120.0 8.3 %collective-permute-start.18 = (bf16[304,256]{1,0:T(8,128)(2,1)S(1)}, bf16[304,256]{1,0:T(8,128)(2,1)S(1)}, u32[]{:S(2)}, u32[]{:S(2)}) collective-permute-start(bf16[304,256]{1,0:T(8,128)(2,1)S(1)} %get-tuple-element.83.rest_23_), channel_id=1, source_target_pairs={{0,8},{8,16},{16,24},{24,28},{28,20},{20,12},{12,4},{4,0},{1,9},{9... | collective-permute-start | bytes 466952 | tf_op jit(solution)/shard_map/ppermute | solution.py:339
  121.6 7.8 %collective-permute-start.8 = (bf16[304,256]{1,0:T(8,128)(2,1)S(1)}, bf16[304,256]{1,0:T(8,128)(2,1)S(1)}, u32[]{:S(2)}, u32[]{:S(2)}) collective-permute-start(bf16[304,256]{1,0:T(8,128)(2,1)S(1)} %collective-permute-done.7.rest_14_), channel_id=1, source_target_pairs={{0,8},{8,16},{16,24},{24,28},{28,20},{20,12},{12,4},{4,0},{1,9},{9... | collective-permute-start | bytes 466952 | tf_op jit(solution)/shard_map/ppermute | solution.py:339
  124.0 6.5 %collective-permute-start.15 = (bf16[304,256]{1,0:T(8,128)(2,1)S(1)}, bf16[304,256]{1,0:T(8,128)(2,1)S(1)}, u32[]{:S(2)}, u32[]{:S(2)}) collective-permute-start(bf16[304,256]{1,0:T(8,128)(2,1)S(1)} %collective-permute-done.14.rest_21_), channel_id=1, source_target_pairs={{0,4},{8,0},{16,8},{24,16},{28,24},{20,28},{12,20},{4,12},{1,5},{9... | collective-permute-start | bytes 466952 | tf_op jit(solution)/shard_map/ppermute | solution.py:339
  127.4 6.9 %collective-permute-start.12 = (bf16[304,256]{1,0:T(8,128)(2,1)S(1)}, bf16[304,256]{1,0:T(8,128)(2,1)S(1)}, u32[]{:S(2)}, u32[]{:S(2)}) collective-permute-start(bf16[304,256]{1,0:T(8,128)(2,1)S(1)} %collective-permute-done.11.rest_13_), channel_id=1, source_target_pairs={{0,4},{8,0},{16,8},{24,16},{28,24},{20,28},{12,20},{4,12},{1,5},{9... | collective-permute-start | bytes 466952 | tf_op jit(solution)/shard_map/ppermute | solution.py:339
  128.4 7.0 %collective-permute-start.19 = (bf16[304,256]{1,0:T(8,128)(2,1)S(1)}, bf16[304,256]{1,0:T(8,128)(2,1)S(1)}, u32[]{:S(2)}, u32[]{:S(2)}) collective-permute-start(bf16[304,256]{1,0:T(8,128)(2,1)S(1)} %collective-permute-done.18.rest_22_), channel_id=1, source_target_pairs={{0,8},{8,16},{16,24},{24,28},{28,20},{20,12},{12,4},{4,0},{1,9},{9... | collective-permute-start | bytes 466952 | tf_op jit(solution)/shard_map/ppermute | solution.py:339
  129.5 7.8 %collective-permute-start.9 = (bf16[304,256]{1,0:T(8,128)(2,1)S(1)}, bf16[304,256]{1,0:T(8,128)(2,1)S(1)}, u32[]{:S(2)}, u32[]{:S(2)}) collective-permute-start(bf16[304,256]{1,0:T(8,128)(2,1)S(1)} %collective-permute-done.8.rest_12_), channel_id=1, source_target_pairs={{0,8},{8,16},{16,24},{24,28},{28,20},{20,12},{12,4},{4,0},{1,9},{9... | collective-permute-start | bytes 466952 | tf_op jit(solution)/shard_map/ppermute | solution.py:339
  130.5 8.0 %collective-permute-start.16 = (bf16[304,256]{1,0:T(8,128)(2,1)S(1)}, bf16[304,256]{1,0:T(8,128)(2,1)S(1)}, u32[]{:S(2)}, u32[]{:S(2)}) collective-permute-start(bf16[304,256]{1,0:T(8,128)(2,1)S(1)} %collective-permute-done.15.rest_19_), channel_id=1, source_target_pairs={{0,4},{8,0},{16,8},{24,16},{28,24},{20,28},{12,20},{4,12},{1,5},{9... | collective-permute-start | bytes 466952 | tf_op jit(solution)/shard_map/ppermute | solution.py:339
  134.2 6.0 %collective-permute-start.13 = (bf16[304,256]{1,0:T(8,128)(2,1)S(1)}, bf16[304,256]{1,0:T(8,128)(2,1)S(1)}, u32[]{:S(2)}, u32[]{:S(2)}) collective-permute-start(bf16[304,256]{1,0:T(8,128)(2,1)S(1)} %collective-permute-done.12.rest_11_), channel_id=1, source_target_pairs={{0,4},{8,0},{16,8},{24,16},{28,24},{20,28},{12,20},{4,12},{1,5},{9... | collective-permute-start | bytes 466952 | tf_op jit(solution)/shard_map/ppermute | solution.py:339
  135.3 5.2 %collective-permute-start.20 = (bf16[304,256]{1,0:T(8,128)(2,1)S(1)}, bf16[304,256]{1,0:T(8,128)(2,1)S(1)}, u32[]{:S(2)}, u32[]{:S(2)}) collective-permute-start(bf16[304,256]{1,0:T(8,128)(2,1)S(1)} %collective-permute-done.19.rest_20_), channel_id=1, source_target_pairs={{0,8},{8,16},{16,24},{24,28},{28,20},{20,12},{12,4},{4,0},{1,9},{9... | collective-permute-start | bytes 466952 | tf_op jit(solution)/shard_map/ppermute | solution.py:339
  137.3 5.8 %collective-permute-start.10 = (bf16[304,256]{1,0:T(8,128)(2,1)S(1)}, bf16[304,256]{1,0:T(8,128)(2,1)S(1)}, u32[]{:S(2)}, u32[]{:S(2)}) collective-permute-start(bf16[304,256]{1,0:T(8,128)(2,1)S(1)} %collective-permute-done.9.rest_10_), channel_id=1, source_target_pairs={{0,8},{8,16},{16,24},{24,28},{28,20},{20,12},{12,4},{4,0},{1,9},{9... | collective-permute-start | bytes 466952 | tf_op jit(solution)/shard_map/ppermute | solution.py:339
  138.5 5.2 %collective-permute-start.17 = (bf16[304,256]{1,0:T(8,128)(2,1)S(1)}, bf16[304,256]{1,0:T(8,128)(2,1)S(1)}, u32[]{:S(2)}, u32[]{:S(2)}) collective-permute-start(bf16[304,256]{1,0:T(8,128)(2,1)S(1)} %collective-permute-done.16.rest_17_), channel_id=1, source_target_pairs={{0,4},{8,0},{16,8},{24,16},{28,24},{20,28},{12,20},{4,12},{1,5},{9... | collective-permute-start | bytes 466952 | tf_op jit(solution)/shard_map/ppermute | solution.py:339
  145.5 2.1 %collective-permute-start.21 = (f32[608,256]{1,0:T(8,128)S(1)}, f32[608,256]{1,0:T(8,128)S(1)}, u32[]{:S(2)}, u32[]{:S(2)}) collective-permute-start(f32[608,256]{1,0:T(8,128)S(1)} %grad_layer.1), channel_id=1, source_target_pairs={{0,1},{1,0},{2,3},{3,2},{4,5},{5,4},{6,7},{7,6},{8,9},{9,8},{10,11... | collective-permute-start | bytes 1867784 | tf_op jit(solution)/shard_map/ppermute | solution.py:360
  147.7 9.5 %copy-start.1 = (bf16[608,256]{1,0:T(8,128)(2,1)}, bf16[608,256]{1,0:T(8,128)(2,1)S(1)}, u32[]{:S(2)}) copy-start(bf16[608,256]{1,0:T(8,128)(2,1)S(1)} %add_convert_fusion.mine_ref) | copy-start | bytes 933892
  147.8 9.5 %collective-permute-start.22 = (bf16[608,256]{1,0:T(8,128)(2,1)S(1)}, bf16[608,256]{1,0:T(8,128)(2,1)S(1)}, u32[]{:S(2)}, u32[]{:S(2)}) collective-permute-start(bf16[608,256]{1,0:T(8,128)(2,1)S(1)} %add_convert_fusion.mine_ref), channel_id=1, source_target_pairs={{0,2},{1,3},{2,0},{3,1},{4,6},{5,7},{6,4},{7,5},{8,10},{9,11},{10,... | collective-permute-start | bytes 933896 | tf_op jit(solution)/shard_map/ppermute | solution.py:364
  157.2 0.7 copy-start.2
Sparse Core Ops, SparseCore 0:
  10.1 42.8 all-gather.1

commit v5 on v4

--- a/solution.py
+++ b/solution.py
@@ -10,7 +10,7 @@
 LANES = 128
 TILE = 16
 TILE_BITS = 4
-UNROLL = 4
+UNROLL = TILE // 4
 CALLS = 3
 BLOCK = 256
 
@@ -54,10 +54,13 @@
             pieces.append(feats_ref[:, at : at + BLOCK])
             if padded > width:
                 pieces.append(filler)
-        turned = lax.dot_general(
-            identity, jnp.concatenate(pieces, axis=0), (((1,), (1,)), ((), ())),
-            preferred_element_type=jnp.float32,
-        ).astype(jnp.bfloat16)
+        both = jnp.concatenate(pieces, axis=0)
+        if part % 4:
+            turned = jnp.transpose(both)
+        else:
+            turned = lax.dot_general(
+                identity, both, (((1,), (1,)), ((), ())), preferred_element_type=jnp.float32
+            ).astype(jnp.bfloat16)
         for side in range(2):
             start = pl.multiple_of(step * chunk + (part + side) * BLOCK, BLOCK)
             table_ref[pl.ds(start, BLOCK), :] = turned[:, side * padded : (side + 1) * padded]
@@ -96,6 +99,17 @@
         line = jnp.full((half, padded), node, jnp.int32) & (TILE - 1)
         return jnp.where(line == low, tile[:half], jnp.where(line == high, tile[half:], 0.0))
 
+    def add_lines(values):
+        step = 1
+        while step < half:
+            chosen = (low & step) == 0
+            values = [
+                jnp.where(chosen, one, two) + pltpu.roll(jnp.where(chosen, two, one), half - step, 0)
+                for one, two in zip(values[::2], values[1::2])
+            ]
+            step *= 2
+        return values[0]
+
     def gather_rows(slots, first, number):
         rows = [order_ref[0, 0, first + i] >> 4 for i in range(number)]
         starts = [row * fanout for row in rows]
@@ -103,10 +117,10 @@
         nears = [fetch(near_ref[0, 0, start]) for start in starts]
         for slot in range(1, slots):
             nears = [near + fetch(near_ref[0, 0, start + slot]) for near, start in zip(nears, starts)]
-        for i in range(number):
-            place = pl.multiple_of((first + i) * half, half)
-            own_sum_ref[pl.ds(place, half), :] = owns[i]
-            near_sum_ref[pl.ds(place, half), :] = nears[i]
+        empty = [jnp.zeros((half, padded), jnp.float32)] * (UNROLL - number)
+        totals = add_lines(owns + empty + nears + empty)
+        own_sum_ref[pl.ds(first, number), :] = totals[:number]
+        near_sum_ref[pl.ds(first, number), :] = totals[UNROLL : UNROLL + number]
 
     begin = 0
     for slots in range(fanout, 0, -1):
@@ -126,22 +140,14 @@
         begin = end
 
     def clear(at, carry):
-        start = pl.multiple_of(at * 8, 8)
-        own_sum_ref[pl.ds(start, 8), :] = jnp.zeros((8, padded), jnp.float32)
-        near_sum_ref[pl.ds(start, 8), :] = jnp.zeros((8, padded), jnp.float32)
+        own_sum_ref[pl.ds(at, 1), :] = jnp.zeros((1, padded), jnp.float32)
+        near_sum_ref[pl.ds(at, 1), :] = jnp.zeros((1, padded), jnp.float32)
         return carry
 
     lax.fori_loop(begin, capacity, clear, 0)
-
-    def collect(ref):
-        total = ref[pl.ds(0, capacity, stride=8), :]
-        for line in range(1, 8):
-            total = total + ref[pl.ds(line, capacity, stride=8), :]
-        return total
-
     counts = jnp.transpose(jnp.broadcast_to(count_ref[0], (padded, count_ref.shape[2])))[:capacity]
-    own = collect(own_sum_ref).astype(jnp.bfloat16)[:, :width]
-    near = (collect(near_sum_ref) / counts).astype(jnp.bfloat16)[:, :width]
+    own = own_sum_ref[...].astype(jnp.bfloat16)[:, :width]
+    near = (near_sum_ref[...] / counts).astype(jnp.bfloat16)[:, :width]
     both = jnp.concatenate([own, near], axis=1)
     for place, inputs_ref in enumerate(inputs_refs):
 
@@ -179,8 +185,8 @@
             out_specs=[pl.BlockSpec((capacity, 2 * width), lambda step, turn_ref: (0, 0))] * groups
             + [pl.BlockSpec(memory_space=pltpu.VMEM)],
             scratch_shapes=[
-                pltpu.VMEM((capacity * 8, padded), jnp.float32),
-                pltpu.VMEM((capacity * 8, padded), jnp.float32),
+                pltpu.VMEM((capacity, padded), jnp.float32),
+                pltpu.VMEM((capacity, padded), jnp.float32),
             ],
         ),
         out_shape=[jax.ShapeDtypeStruct((capacity, 2 * width), jnp.bfloat16)] * groups

time: 166 us -> 167 us (level)
  waiting for transfers between devices: 28.1 us -> 30.2 us
  Pallas kernels: 77.5 us -> 75.4 us
    ppermute x1, starting transfers between devices: 0.07 us -> 3.91 us  [group_sum(): other = lax.ppermute(mine, 'dp', [(i, i ^ stride) for i in range(count)])]
    ppermute x21, waiting for transfers between devices: 16 us -> 19.8 us  [send_along(): lax.ppermute(array, 'feat', [(ring[i], ring[(i + shift) % count]) for i i...]
    ppermute x21, starting transfers between devices: 32.8 us -> 29 us  [send_along(): lax.ppermute(array, 'feat', [(ring[i], ring[(i + shift) % count]) for i i...]
    ppermute x1, waiting for transfers between devices: 9.39 us -> 7.66 us  [group_sum(): other = lax.ppermute(mine, 'dp', [(i, i ^ stride) for i in range(count)])]
  transfers between devices with their start and end apart: 24 -> 24, of which waited for: 15 -> 10; matrix products, arithmetic and copies ran while one was open for 7% -> 7% of each run, Pallas kernels for 42% -> 41%
where the time goes in v5:
time: 167 us
  Pallas kernels  75.4 us (45%)
  starting transfers between devices  33 us (20%)
  waiting for transfers between devices  30.2 us (18%)
  between operations  14.3 us (9%)
  other arithmetic  7.49 us (4%)
  local copies, waits for them, and re-layouts  6.33 us (4%)
    pallas_call x3, Pallas kernels, gather_layer(): pl.pallas_call(functools.partial(gather_kernel, fanout, capacity), grid_s...  48.8 us
    ppermute x21, starting transfers between devices, send_along(): lax.ppermute(array, 'feat', [(ring[i], ring[(i + shift) % count]) for i i...  29 us
    pallas_call x1, Pallas kernels, build_table(): pl.pallas_call(table_kernel, grid=(nodes // chunk,), in_specs=[pl.BlockSp...  19.9 us
    ppermute x21, waiting for transfers between devices, send_along(): lax.ppermute(array, 'feat', [(ring[i], ring[(i + shift) % count]) for i i...  19.8 us
    ppermute x1, waiting for transfers between devices, group_sum(): other = lax.ppermute(mine, 'dp', [(i, i ^ stride) for i in range(count)])  7.66 us
    ppermute x1, starting transfers between devices, group_sum(): other = lax.ppermute(mine, 'dp', [(i, i ^ stride) for i in range(count)])  3.91 us
  transfers between devices with their start and end apart: 24, of which 10 were waited for; matrix products, arithmetic and copies ran while one was open for 7% of the time, Pallas kernels for 41%

profile of v5, /device:TPU:0, one launch (start us, length us, event | category | flops | bytes accessed | tf_op | source)
XLA Modules:
  0.0 166.8 jit_solution(228728315577118135)
XLA Ops:
  10.8 2.5 %convert_reduce_fusion = s32[8,704]{1,0:T(8,128)S(1)} fusion(s32[8,704]{1,0:T(8,128)S(1)} %get-tuple-element.86), kind=kLoop, calls=%fused_computation | loop fusion | flops 11889152 | bytes 45056 | tf_op jit(solution)/shard_map/reduce_sum | solution.py:32
  13.3 2.1 %select_reduce_fusion = s32[8,512]{1,0:T(8,128)S(1)} fusion(s32[8,704]{1,0:T(8,128)S(1)} %broadcast_add_fusion, s32[8,704]{1,0:T(8,128)S(1)} %convert_reduce_fusion), kind=kLoop, calls=%fused_computation.1 | loop fusion | flops 8646656 | bytes 61440 | tf_op jit(solution)/shard_map/reduce_sum | solution.py:34
  15.4 1.1 broadcast_in_dim.61.near_ref
  18.3 19.9 %build_table.1.table_ref = bf16[131072,128]{1,0:T(8,128)(2,1)S(1)} custom-call(bf16[128,131072]{1,0:T(8,128)(2,1)} %feats_ref), custom_call_target="tpu_custom_call" | custom-call | tf_op jit(solution)/shard_map/build_table/pallas_call | solution.py:73
  38.2 20.1 %gather_layer.3 = (bf16[416,256]{1,0:T(8,128)(2,1)S(1)}, bf16[416,256]{1,0:T(8,128)(2,1)S(1)}, bf16[416,256]{1,0:T(8,128)(2,1)S(1)}, bf16[131072,128]{1,0:T(8,128)(2,1)S(1)}) custom-call(s32[16]{0:T(128)S(1)} %fusion.3.turn_ref.source_ref, s32[8,1,16]{2,1,0:T(1,128)S(1)} %bitcast.10, ...), custom_call_target="tpu_custom_call", output_to_operand_aliasing={{3}: (6, {})} | custom-call | bytes 51118080 | tf_op jit(solution)/shard_map/gather_layer/pallas_call | solution.py:172
  58.3 2.5 %collective-permute-start = (bf16[416,256]{1,0:T(8,128)(2,1)S(1)}, bf16[416,256]{1,0:T(8,128)(2,1)S(1)}, u32[]{:S(2)}, u32[]{:S(2)}) collective-permute-start(bf16[416,256]{1,0:T(8,128)(2,1)S(1)} %get-tuple-element.55.rest_0_), channel_id=1, source_target_pairs={{0,28},{8,20},{16,12},{24,4},{28,0},{20,8},{12,16},{4,24},{1,29},{... | collective-permute-start | bytes 638984 | tf_op jit(solution)/shard_map/ppermute | solution.py:345
  60.8 3.6 %collective-permute-start.1 = (bf16[416,256]{1,0:T(8,128)(2,1)S(1)}, bf16[416,256]{1,0:T(8,128)(2,1)S(1)}, u32[]{:S(2)}, u32[]{:S(2)}) collective-permute-start(bf16[416,256]{1,0:T(8,128)(2,1)S(1)} %get-tuple-element.56.rest_1_), channel_id=1, source_target_pairs={{0,24},{8,28},{16,20},{24,12},{28,4},{20,0},{12,8},{4,16},{1,25},{... | collective-permute-start | bytes 638984 | tf_op jit(solution)/shard_map/ppermute | solution.py:345
  64.6 16.7 %gather_layer.4 = (bf16[416,256]{1,0:T(8,128)(2,1)S(1)}, bf16[416,256]{1,0:T(8,128)(2,1)S(1)}, bf16[416,256]{1,0:T(8,128)(2,1)S(1)}, bf16[131072,128]{1,0:T(8,128)(2,1)S(1)}) custom-call(s32[16]{0:T(128)S(1)} %fusion.3.turn_ref.source_ref, s32[8,1,16]{2,1,0:T(1,128)S(1)} %bitcast.11, ...), custom_call_target="tpu_custom_call", output_to_operand_aliasing={{3}: (6, {})} | custom-call | bytes 51118080 | tf_op jit(solution)/shard_map/gather_layer/pallas_call | solution.py:172
  81.4 4.7 %collective-permute-done.1.rest_1_ = bf16[416,256]{1,0:T(8,128)(2,1)S(1)} collective-permute-done((bf16[416,256]{1,0:T(8,128)(2,1)S(1)}, bf16[416,256]{1,0:T(8,128)(2,1)S(1)}, u32[]{:S(2)}, u32[]{:S(2)}) %collective-permute-start.1) | collective-permute-done | bytes 213024 | tf_op jit(solution)/shard_map/ppermute | solution.py:345
  86.1 2.9 %collective-permute-start.4 = (bf16[416,256]{1,0:T(8,128)(2,1)S(1)}, bf16[416,256]{1,0:T(8,128)(2,1)S(1)}, u32[]{:S(2)}, u32[]{:S(2)}) collective-permute-start(bf16[416,256]{1,0:T(8,128)(2,1)S(1)} %get-tuple-element.64.rest_4_), channel_id=1, source_target_pairs={{0,12},{8,4},{16,0},{24,8},{28,16},{20,24},{12,28},{4,20},{1,13},{... | collective-permute-start | bytes 638984 | tf_op jit(solution)/shard_map/ppermute | solution.py:345
  89.1 12.0 %gather_layer.5 = (bf16[416,256]{1,0:T(8,128)(2,1)S(1)}, bf16[416,256]{1,0:T(8,128)(2,1)S(1)}, bf16[131072,128]{1,0:T(8,128)(2,1)S(1)}) custom-call(s32[16]{0:T(128)S(1)} %fusion.3.turn_ref.source_ref, s32[8,1,16]{2,1,0:T(1,128)S(1)} %bitcast.12, s32[8,1,512]{2,1,0:T(1,128)S(1)} %broadcast_in_dim.59.order_ref, ...), custom_call_target="tpu_custom_call", output_to_operand_aliasing={{2}: (6, {})} | custom-call | bytes 34078720 | tf_op jit(solution)/shard_map/gather_layer/pallas_call | solution.py:172
  101.1 3.2 %collective-permute-start.6 = (bf16[416,256]{1,0:T(8,128)(2,1)S(1)}, bf16[416,256]{1,0:T(8,128)(2,1)S(1)}, u32[]{:S(2)}, u32[]{:S(2)}) collective-permute-start(bf16[416,256]{1,0:T(8,128)(2,1)S(1)} %get-tuple-element.69.rest_6_), channel_id=1, source_target_pairs={{0,4},{8,0},{16,8},{24,16},{28,24},{20,28},{12,20},{4,12},{1,5},{9... | collective-permute-start | bytes 638984 | tf_op jit(solution)/shard_map/ppermute | solution.py:345
  105.7 3.5 %collective-permute-done.6.rest_6_ = bf16[416,256]{1,0:T(8,128)(2,1)S(1)} collective-permute-done((bf16[416,256]{1,0:T(8,128)(2,1)S(1)}, bf16[416,256]{1,0:T(8,128)(2,1)S(1)}, u32[]{:S(2)}, u32[]{:S(2)}) %collective-permute-start.6) | collective-permute-done | bytes 213024 | tf_op jit(solution)/shard_map/ppermute | solution.py:345
  109.3 1.2 copy-done
  110.5 3.1 %upper_layers.1 = (bf16[304,256]{1,0:T(8,128)(2,1)S(1)}, bf16[304,256]{1,0:T(8,128)(2,1)S(1)}) custom-call(s32[1]{0:T(128)} %dynamic_slice.23.size_ref, s32[16]{0:T(128)S(1)} %fusion.3.turn_ref.source_ref, bf16[8,256,256]{2,1,0:T(8,128)(2,1)S(1)} %copy-done, bf16[2,172,256]{2,1,0:T(8,128)(2,1)S(1)} %bitcast.9, s32[1,416]{1,0:T(1,128)S(1)} %compare_select_fusion.2.row_ref, ...), custom_call_target="tpu_custom_call" | custom-call | tf_op jit(solution)/shard_map/upper_layers/pallas_call | solution.py:261
  113.6 1.8 %collective-permute-start.7 = (bf16[304,256]{1,0:T(8,128)(2,1)S(1)}, bf16[304,256]{1,0:T(8,128)(2,1)S(1)}, u32[]{:S(2)}, u32[]{:S(2)}) collective-permute-start(bf16[304,256]{1,0:T(8,128)(2,1)S(1)} %get-tuple-element.82.rest_15_), channel_id=1, source_target_pairs={{0,8},{8,16},{16,24},{24,28},{28,20},{20,12},{12,4},{4,0},{1,9},{9... | collective-permute-start | bytes 466952 | tf_op jit(solution)/shard_map/ppermute | solution.py:345
  116.2 2.0 %collective-permute-start.11 = (bf16[304,256]{1,0:T(8,128)(2,1)S(1)}, bf16[304,256]{1,0:T(8,128)(2,1)S(1)}, u32[]{:S(2)}, u32[]{:S(2)}) collective-permute-start(bf16[304,256]{1,0:T(8,128)(2,1)S(1)} %get-tuple-element.82.rest_15_), channel_id=1, source_target_pairs={{0,4},{8,0},{16,8},{24,16},{28,24},{20,28},{12,20},{4,12},{1,5},{9... | collective-permute-start | bytes 466952 | tf_op jit(solution)/shard_map/ppermute | solution.py:345
  118.2 1.8 %collective-permute-done.7.rest_14_ = bf16[304,256]{1,0:T(8,128)(2,1)S(1)} collective-permute-done((bf16[304,256]{1,0:T(8,128)(2,1)S(1)}, bf16[304,256]{1,0:T(8,128)(2,1)S(1)}, u32[]{:S(2)}, u32[]{:S(2)}) %collective-permute-start.7) | collective-permute-done | bytes 155680 | tf_op jit(solution)/shard_map/ppermute | solution.py:345
  120.0 2.2 %collective-permute-start.8 = (bf16[304,256]{1,0:T(8,128)(2,1)S(1)}, bf16[304,256]{1,0:T(8,128)(2,1)S(1)}, u32[]{:S(2)}, u32[]{:S(2)}) collective-permute-start(bf16[304,256]{1,0:T(8,128)(2,1)S(1)} %collective-permute-done.7.rest_14_), channel_id=1, source_target_pairs={{0,8},{8,16},{16,24},{24,28},{28,20},{20,12},{12,4},{4,0},{1,9},{9... | collective-permute-start | bytes 466952 | tf_op jit(solution)/shard_map/ppermute | solution.py:345
  123.1 2.5 %collective-permute-done.11.rest_13_ = bf16[304,256]{1,0:T(8,128)(2,1)S(1)} collective-permute-done((bf16[304,256]{1,0:T(8,128)(2,1)S(1)}, bf16[304,256]{1,0:T(8,128)(2,1)S(1)}, u32[]{:S(2)}, u32[]{:S(2)}) %collective-permute-start.11) | collective-permute-done | bytes 155680 | tf_op jit(solution)/shard_map/ppermute | solution.py:345
  126.3 1.4 collective-permute-start.19
  127.7 1.8 %collective-permute-start.9 = (bf16[304,256]{1,0:T(8,128)(2,1)S(1)}, bf16[304,256]{1,0:T(8,128)(2,1)S(1)}, u32[]{:S(2)}, u32[]{:S(2)}) collective-permute-start(bf16[304,256]{1,0:T(8,128)(2,1)S(1)} %collective-permute-done.8.rest_12_), channel_id=1, source_target_pairs={{0,8},{8,16},{16,24},{24,28},{28,20},{20,12},{12,4},{4,0},{1,9},{9... | collective-permute-start | bytes 466952 | tf_op jit(solution)/shard_map/ppermute | solution.py:345
  129.9 2.7 %collective-permute-done.12.rest_11_ = bf16[304,256]{1,0:T(8,128)(2,1)S(1)} collective-permute-done((bf16[304,256]{1,0:T(8,128)(2,1)S(1)}, bf16[304,256]{1,0:T(8,128)(2,1)S(1)}, u32[]{:S(2)}, u32[]{:S(2)}) %collective-permute-start.12) | collective-permute-done | bytes 155680 | tf_op jit(solution)/shard_map/ppermute | solution.py:345
  133.2 1.4 collective-permute-start.20
  134.6 1.8 %collective-permute-start.10 = (bf16[304,256]{1,0:T(8,128)(2,1)S(1)}, bf16[304,256]{1,0:T(8,128)(2,1)S(1)}, u32[]{:S(2)}, u32[]{:S(2)}) collective-permute-start(bf16[304,256]{1,0:T(8,128)(2,1)S(1)} %collective-permute-done.9.rest_10_), channel_id=1, source_target_pairs={{0,8},{8,16},{16,24},{24,28},{28,20},{20,12},{12,4},{4,0},{1,9},{9... | collective-permute-start | bytes 466952 | tf_op jit(solution)/shard_map/ppermute | solution.py:345
  137.2 2.4 %collective-permute-done.13.rest_9_ = bf16[304,256]{1,0:T(8,128)(2,1)S(1)} collective-permute-done((bf16[304,256]{1,0:T(8,128)(2,1)S(1)}, bf16[304,256]{1,0:T(8,128)(2,1)S(1)}, u32[]{:S(2)}, u32[]{:S(2)}) %collective-permute-start.13) | collective-permute-done | bytes 155680 | tf_op jit(solution)/shard_map/ppermute | solution.py:345
  140.4 1.3 collective-permute-done.17.rest_16_
  141.7 1.8 %grad_layer.1 = f32[608,256]{1,0:T(8,128)S(1)} custom-call(s32[16]{0:T(128)S(1)} %fusion.3.turn_ref.source_ref, bf16[416,256]{1,0:T(8,128)(2,1)S(1)} %get-tuple-element.55.rest_0_, bf16[416,256]{1,0:T(8,128)(2,1)S(1)} %get-tuple-element.56.rest_1_, bf16[416,256]{1,0:T(8,128)(2,1)S(1)} %get-tuple-element.57.rest_2_, ...), custom_call_target="tpu_custom_call" | custom-call | tf_op jit(solution)/shard_map/grad_layer/pallas_call | solution.py:303
  143.5 2.0 %collective-permute-done.21 = f32[608,256]{1,0:T(8,128)S(1)} collective-permute-done((f32[608,256]{1,0:T(8,128)S(1)}, f32[608,256]{1,0:T(8,128)S(1)}, u32[]{:S(2)}, u32[]{:S(2)}) %collective-permute-start.21) | collective-permute-done | bytes 622624 | tf_op jit(solution)/shard_map/ppermute | solution.py:366
  145.7 3.9 %collective-permute-start.22 = (bf16[608,256]{1,0:T(8,128)(2,1)S(1)}, bf16[608,256]{1,0:T(8,128)(2,1)S(1)}, u32[]{:S(2)}, u32[]{:S(2)}) collective-permute-start(bf16[608,256]{1,0:T(8,128)(2,1)S(1)} %add_convert_fusion.mine_ref), channel_id=1, source_target_pairs={{0,2},{1,3},{2,0},{3,1},{4,6},{5,7},{6,4},{7,5},{8,10},{9,11},{10,... | collective-permute-start | bytes 933896 | tf_op jit(solution)/shard_map/ppermute | solution.py:370
  149.6 7.7 %collective-permute-done.22.other_ref = bf16[608,256]{1,0:T(8,128)(2,1)S(1)} collective-permute-done((bf16[608,256]{1,0:T(8,128)(2,1)S(1)}, bf16[608,256]{1,0:T(8,128)(2,1)S(1)}, u32[]{:S(2)}, u32[]{:S(2)}) %collective-permute-start.22) | collective-permute-done | bytes 311328 | tf_op jit(solution)/shard_map/ppermute | solution.py:370
  158.0 2.0 %final_sum.1 = (f32[2,128,256]{2,1,0:T(8,128)}, f32[172,2,256]{2,1,0:T(2,128)}) custom-call(bf16[608,256]{1,0:T(8,128)(2,1)} %copy-done.1, bf16[608,256]{1,0:T(8,128)(2,1)} %copy-done.2), custom_call_target="tpu_custom_call" | custom-call | tf_op jit(solution)/shard_map/final_sum/pallas_call | solution.py:326
  (60 shorter events, 12.9 us)
Async XLA Ops:
  7.2 102.0 %all-gather.2.cloned.1.call-start = ((), (), s32[]{:S(2)}) async-start(), calls=%async_computation | async-start | bytes 1179648 | tf_op jit(solution)/shard_map/all_gather | solution.py:407
  58.3 23.0 %collective-permute-start = (bf16[416,256]{1,0:T(8,128)(2,1)S(1)}, bf16[416,256]{1,0:T(8,128)(2,1)S(1)}, u32[]{:S(2)}, u32[]{:S(2)}) collective-permute-start(bf16[416,256]{1,0:T(8,128)(2,1)S(1)} %get-tuple-element.55.rest_0_), channel_id=1, source_target_pairs={{0,28},{8,20},{16,12},{24,4},{28,0},{20,8},{12,16},{4,24},{1,29},{... | collective-permute-start | bytes 638984 | tf_op jit(solution)/shard_map/ppermute | solution.py:345
  60.8 25.3 %collective-permute-start.1 = (bf16[416,256]{1,0:T(8,128)(2,1)S(1)}, bf16[416,256]{1,0:T(8,128)(2,1)S(1)}, u32[]{:S(2)}, u32[]{:S(2)}) collective-permute-start(bf16[416,256]{1,0:T(8,128)(2,1)S(1)} %get-tuple-element.56.rest_1_), channel_id=1, source_target_pairs={{0,24},{8,28},{16,20},{24,12},{28,4},{20,0},{12,8},{4,16},{1,25},{... | collective-permute-start | bytes 638984 | tf_op jit(solution)/shard_map/ppermute | solution.py:345
  64.5 21.7 %collective-permute-start.2 = (bf16[416,256]{1,0:T(8,128)(2,1)S(1)}, bf16[416,256]{1,0:T(8,128)(2,1)S(1)}, u32[]{:S(2)}, u32[]{:S(2)}) collective-permute-start(bf16[416,256]{1,0:T(8,128)(2,1)S(1)} %get-tuple-element.57.rest_2_), channel_id=1, source_target_pairs={{0,20},{8,12},{16,4},{24,0},{28,8},{20,16},{12,24},{4,28},{1,21},{... | collective-permute-start | bytes 638984 | tf_op jit(solution)/shard_map/ppermute | solution.py:345
  81.4 22.9 %copy-start.3 = (bf16[2,256,172]{1,0,2:T(2,128)(2,1)S(1)}, bf16[2,256,172]{1,0,2:T(2,128)(2,1)}, u32[]{:S(2)}) copy-start(bf16[2,256,172]{1,0,2:T(2,128)(2,1)} %param.13) | copy-start | bytes 528388
  86.1 14.9 %collective-permute-start.3 = (bf16[416,256]{1,0:T(8,128)(2,1)S(1)}, bf16[416,256]{1,0:T(8,128)(2,1)S(1)}, u32[]{:S(2)}, u32[]{:S(2)}) collective-permute-start(bf16[416,256]{1,0:T(8,128)(2,1)S(1)} %get-tuple-element.63.rest_3_), channel_id=1, source_target_pairs={{0,16},{8,24},{16,28},{24,20},{28,12},{20,4},{12,0},{4,8},{1,17},{... | collective-permute-start | bytes 638984 | tf_op jit(solution)/shard_map/ppermute | solution.py:345
  86.1 14.9 %collective-permute-start.4 = (bf16[416,256]{1,0:T(8,128)(2,1)S(1)}, bf16[416,256]{1,0:T(8,128)(2,1)S(1)}, u32[]{:S(2)}, u32[]{:S(2)}) collective-permute-start(bf16[416,256]{1,0:T(8,128)(2,1)S(1)} %get-tuple-element.64.rest_4_), channel_id=1, source_target_pairs={{0,12},{8,4},{16,0},{24,8},{28,16},{20,24},{12,28},{4,20},{1,13},{... | collective-permute-start | bytes 638984 | tf_op jit(solution)/shard_map/ppermute | solution.py:345
  89.1 12.0 %collective-permute-start.5 = (bf16[416,256]{1,0:T(8,128)(2,1)S(1)}, bf16[416,256]{1,0:T(8,128)(2,1)S(1)}, u32[]{:S(2)}, u32[]{:S(2)}) collective-permute-start(bf16[416,256]{1,0:T(8,128)(2,1)S(1)} %get-tuple-element.65.rest_5_), channel_id=1, source_target_pairs={{0,8},{8,16},{16,24},{24,28},{28,20},{20,12},{12,4},{4,0},{1,9},{9... | collective-permute-start | bytes 638984 | tf_op jit(solution)/shard_map/ppermute | solution.py:345
  101.1 8.1 %collective-permute-start.6 = (bf16[416,256]{1,0:T(8,128)(2,1)S(1)}, bf16[416,256]{1,0:T(8,128)(2,1)S(1)}, u32[]{:S(2)}, u32[]{:S(2)}) collective-permute-start(bf16[416,256]{1,0:T(8,128)(2,1)S(1)} %get-tuple-element.69.rest_6_), channel_id=1, source_target_pairs={{0,4},{8,0},{16,8},{24,16},{28,24},{20,28},{12,20},{4,12},{1,5},{9... | collective-permute-start | bytes 638984 | tf_op jit(solution)/shard_map/ppermute | solution.py:345
  109.2 1.2 copy-start
  113.6 6.5 %collective-permute-start.7 = (bf16[304,256]{1,0:T(8,128)(2,1)S(1)}, bf16[304,256]{1,0:T(8,128)(2,1)S(1)}, u32[]{:S(2)}, u32[]{:S(2)}) collective-permute-start(bf16[304,256]{1,0:T(8,128)(2,1)S(1)} %get-tuple-element.82.rest_15_), channel_id=1, source_target_pairs={{0,8},{8,16},{16,24},{24,28},{28,20},{20,12},{12,4},{4,0},{1,9},{9... | collective-permute-start | bytes 466952 | tf_op jit(solution)/shard_map/ppermute | solution.py:345
  115.4 6.9 %collective-permute-start.14 = (bf16[304,256]{1,0:T(8,128)(2,1)S(1)}, bf16[304,256]{1,0:T(8,128)(2,1)S(1)}, u32[]{:S(2)}, u32[]{:S(2)}) collective-permute-start(bf16[304,256]{1,0:T(8,128)(2,1)S(1)} %get-tuple-element.83.rest_23_), channel_id=1, source_target_pairs={{0,4},{8,0},{16,8},{24,16},{28,24},{20,28},{12,20},{4,12},{1,5},{9... | collective-permute-start | bytes 466952 | tf_op jit(solution)/shard_map/ppermute | solution.py:345
  116.2 9.5 %collective-permute-start.11 = (bf16[304,256]{1,0:T(8,128)(2,1)S(1)}, bf16[304,256]{1,0:T(8,128)(2,1)S(1)}, u32[]{:S(2)}, u32[]{:S(2)}) collective-permute-start(bf16[304,256]{1,0:T(8,128)(2,1)S(1)} %get-tuple-element.82.rest_15_), channel_id=1, source_target_pairs={{0,4},{8,0},{16,8},{24,16},{28,24},{20,28},{12,20},{4,12},{1,5},{9... | collective-permute-start | bytes 466952 | tf_op jit(solution)/shard_map/ppermute | solution.py:345
  118.1 8.1 %collective-permute-start.18 = (bf16[304,256]{1,0:T(8,128)(2,1)S(1)}, bf16[304,256]{1,0:T(8,128)(2,1)S(1)}, u32[]{:S(2)}, u32[]{:S(2)}) collective-permute-start(bf16[304,256]{1,0:T(8,128)(2,1)S(1)} %get-tuple-element.83.rest_23_), channel_id=1, source_target_pairs={{0,8},{8,16},{16,24},{24,28},{28,20},{20,12},{12,4},{4,0},{1,9},{9... | collective-permute-start | bytes 466952 | tf_op jit(solution)/shard_map/ppermute | solution.py:345
  120.0 7.6 %collective-permute-start.8 = (bf16[304,256]{1,0:T(8,128)(2,1)S(1)}, bf16[304,256]{1,0:T(8,128)(2,1)S(1)}, u32[]{:S(2)}, u32[]{:S(2)}) collective-permute-start(bf16[304,256]{1,0:T(8,128)(2,1)S(1)} %collective-permute-done.7.rest_14_), channel_id=1, source_target_pairs={{0,8},{8,16},{16,24},{24,28},{28,20},{20,12},{12,4},{4,0},{1,9},{9... | collective-permute-start | bytes 466952 | tf_op jit(solution)/shard_map/ppermute | solution.py:345
  122.3 7.2 %collective-permute-start.15 = (bf16[304,256]{1,0:T(8,128)(2,1)S(1)}, bf16[304,256]{1,0:T(8,128)(2,1)S(1)}, u32[]{:S(2)}, u32[]{:S(2)}) collective-permute-start(bf16[304,256]{1,0:T(8,128)(2,1)S(1)} %collective-permute-done.14.rest_21_), channel_id=1, source_target_pairs={{0,4},{8,0},{16,8},{24,16},{28,24},{20,28},{12,20},{4,12},{1,5},{9... | collective-permute-start | bytes 466952 | tf_op jit(solution)/shard_map/ppermute | solution.py:345
  125.6 7.0 %collective-permute-start.12 = (bf16[304,256]{1,0:T(8,128)(2,1)S(1)}, bf16[304,256]{1,0:T(8,128)(2,1)S(1)}, u32[]{:S(2)}, u32[]{:S(2)}) collective-permute-start(bf16[304,256]{1,0:T(8,128)(2,1)S(1)} %collective-permute-done.11.rest_13_), channel_id=1, source_target_pairs={{0,4},{8,0},{16,8},{24,16},{28,24},{20,28},{12,20},{4,12},{1,5},{9... | collective-permute-start | bytes 466952 | tf_op jit(solution)/shard_map/ppermute | solution.py:345
  126.3 7.0 %collective-permute-start.19 = (bf16[304,256]{1,0:T(8,128)(2,1)S(1)}, bf16[304,256]{1,0:T(8,128)(2,1)S(1)}, u32[]{:S(2)}, u32[]{:S(2)}) collective-permute-start(bf16[304,256]{1,0:T(8,128)(2,1)S(1)} %collective-permute-done.18.rest_22_), channel_id=1, source_target_pairs={{0,8},{8,16},{16,24},{24,28},{28,20},{20,12},{12,4},{4,0},{1,9},{9... | collective-permute-start | bytes 466952 | tf_op jit(solution)/shard_map/ppermute | solution.py:345
  127.7 7.0 %collective-permute-start.9 = (bf16[304,256]{1,0:T(8,128)(2,1)S(1)}, bf16[304,256]{1,0:T(8,128)(2,1)S(1)}, u32[]{:S(2)}, u32[]{:S(2)}) collective-permute-start(bf16[304,256]{1,0:T(8,128)(2,1)S(1)} %collective-permute-done.8.rest_12_), channel_id=1, source_target_pairs={{0,8},{8,16},{16,24},{24,28},{28,20},{20,12},{12,4},{4,0},{1,9},{9... | collective-permute-start | bytes 466952 | tf_op jit(solution)/shard_map/ppermute | solution.py:345
  129.5 7.0 %collective-permute-start.16 = (bf16[304,256]{1,0:T(8,128)(2,1)S(1)}, bf16[304,256]{1,0:T(8,128)(2,1)S(1)}, u32[]{:S(2)}, u32[]{:S(2)}) collective-permute-start(bf16[304,256]{1,0:T(8,128)(2,1)S(1)} %collective-permute-done.15.rest_19_), channel_id=1, source_target_pairs={{0,4},{8,0},{16,8},{24,16},{28,24},{20,28},{12,20},{4,12},{1,5},{9... | collective-permute-start | bytes 466952 | tf_op jit(solution)/shard_map/ppermute | solution.py:345
  132.6 7.0 %collective-permute-start.13 = (bf16[304,256]{1,0:T(8,128)(2,1)S(1)}, bf16[304,256]{1,0:T(8,128)(2,1)S(1)}, u32[]{:S(2)}, u32[]{:S(2)}) collective-permute-start(bf16[304,256]{1,0:T(8,128)(2,1)S(1)} %collective-permute-done.12.rest_11_), channel_id=1, source_target_pairs={{0,4},{8,0},{16,8},{24,16},{28,24},{20,28},{12,20},{4,12},{1,5},{9... | collective-permute-start | bytes 466952 | tf_op jit(solution)/shard_map/ppermute | solution.py:345
  133.2 6.3 %collective-permute-start.20 = (bf16[304,256]{1,0:T(8,128)(2,1)S(1)}, bf16[304,256]{1,0:T(8,128)(2,1)S(1)}, u32[]{:S(2)}, u32[]{:S(2)}) collective-permute-start(bf16[304,256]{1,0:T(8,128)(2,1)S(1)} %collective-permute-done.19.rest_20_), channel_id=1, source_target_pairs={{0,8},{8,16},{16,24},{24,28},{28,20},{20,12},{12,4},{4,0},{1,9},{9... | collective-permute-start | bytes 466952 | tf_op jit(solution)/shard_map/ppermute | solution.py:345
  134.6 5.8 %collective-permute-start.10 = (bf16[304,256]{1,0:T(8,128)(2,1)S(1)}, bf16[304,256]{1,0:T(8,128)(2,1)S(1)}, u32[]{:S(2)}, u32[]{:S(2)}) collective-permute-start(bf16[304,256]{1,0:T(8,128)(2,1)S(1)} %collective-permute-done.9.rest_10_), channel_id=1, source_target_pairs={{0,8},{8,16},{16,24},{24,28},{28,20},{20,12},{12,4},{4,0},{1,9},{9... | collective-permute-start | bytes 466952 | tf_op jit(solution)/shard_map/ppermute | solution.py:345
  136.5 5.2 %collective-permute-start.17 = (bf16[304,256]{1,0:T(8,128)(2,1)S(1)}, bf16[304,256]{1,0:T(8,128)(2,1)S(1)}, u32[]{:S(2)}, u32[]{:S(2)}) collective-permute-start(bf16[304,256]{1,0:T(8,128)(2,1)S(1)} %collective-permute-done.16.rest_17_), channel_id=1, source_target_pairs={{0,4},{8,0},{16,8},{24,16},{28,24},{20,28},{12,20},{4,12},{1,5},{9... | collective-permute-start | bytes 466952 | tf_op jit(solution)/shard_map/ppermute | solution.py:345
  143.5 2.1 %collective-permute-start.21 = (f32[608,256]{1,0:T(8,128)S(1)}, f32[608,256]{1,0:T(8,128)S(1)}, u32[]{:S(2)}, u32[]{:S(2)}) collective-permute-start(f32[608,256]{1,0:T(8,128)S(1)} %grad_layer.1), channel_id=1, source_target_pairs={{0,1},{1,0},{2,3},{3,2},{4,5},{5,4},{6,7},{7,6},{8,9},{9,8},{10,11... | collective-permute-start | bytes 1867784 | tf_op jit(solution)/shard_map/ppermute | solution.py:366
  145.7 11.6 %copy-start.1 = (bf16[608,256]{1,0:T(8,128)(2,1)}, bf16[608,256]{1,0:T(8,128)(2,1)S(1)}, u32[]{:S(2)}) copy-start(bf16[608,256]{1,0:T(8,128)(2,1)S(1)} %add_convert_fusion.mine_ref) | copy-start | bytes 933892
  145.7 11.6 %collective-permute-start.22 = (bf16[608,256]{1,0:T(8,128)(2,1)S(1)}, bf16[608,256]{1,0:T(8,128)(2,1)S(1)}, u32[]{:S(2)}, u32[]{:S(2)}) collective-permute-start(bf16[608,256]{1,0:T(8,128)(2,1)S(1)} %add_convert_fusion.mine_ref), channel_id=1, source_target_pairs={{0,2},{1,3},{2,0},{3,1},{4,6},{5,7},{6,4},{7,5},{8,10},{9,11},{10,... | collective-permute-start | bytes 933896 | tf_op jit(solution)/shard_map/ppermute | solution.py:370
  157.3 0.7 copy-start.2
Sparse Core Ops, SparseCore 0:
  10.1 42.8 all-gather.1

commit v6 on v5

--- a/solution.py
+++ b/solution.py
@@ -10,7 +10,6 @@
 LANES = 128
 TILE = 16
 TILE_BITS = 4
-UNROLL = TILE // 4
 CALLS = 3
 BLOCK = 256
 
@@ -40,18 +39,20 @@
     return order, enough
 
 
-def table_kernel(feats_ref, table_ref):
+def table_kernel(*refs):
+    *feats_refs, table_ref = refs
     step = pl.program_id(0)
-    width, chunk = feats_ref.shape
+    chunk = feats_refs[0].shape[1]
+    width = sum(ref.shape[0] for ref in feats_refs)
     padded = table_ref.shape[1]
     down = lax.broadcasted_iota(jnp.int32, (BLOCK, BLOCK), 0)
     across = lax.broadcasted_iota(jnp.int32, (BLOCK, BLOCK), 1)
     identity = jnp.where(down == across, 1.0, 0.0).astype(jnp.bfloat16)
-    filler = jnp.zeros((padded - width, BLOCK), feats_ref.dtype)
+    filler = jnp.zeros((padded - width, BLOCK), jnp.bfloat16)
     for part in range(0, chunk // BLOCK, 2):
         pieces = []
         for at in (part * BLOCK, (part + 1) * BLOCK):
-            pieces.append(feats_ref[:, at : at + BLOCK])
+            pieces += [feats_ref[:, at : at + BLOCK] for feats_ref in feats_refs]
             if padded > width:
                 pieces.append(filler)
         both = jnp.concatenate(pieces, axis=0)
@@ -70,15 +71,16 @@
     width, nodes = node_feats.shape
     padded = max(width, LANES)
     chunk = min(nodes, 8192)
+    streams = max(1, width // 32)
     return pl.pallas_call(
         table_kernel,
         grid=(nodes // chunk,),
-        in_specs=[pl.BlockSpec((width, chunk), lambda step: (0, step))],
+        in_specs=[pl.BlockSpec((width // streams, chunk), lambda step, at=at: (at, step)) for at in range(streams)],
         out_specs=pl.BlockSpec(memory_space=pltpu.VMEM),
         out_shape=pltpu.VMEM((nodes, padded), jnp.bfloat16),
         compiler_params=pltpu.CompilerParams(vmem_limit_bytes=8 * 2**20),
         name="build_table",
-    )(node_feats)
+    )(*[node_feats] * streams)
 
 
 def gather_kernel(
@@ -94,9 +96,12 @@
     low = lax.broadcasted_iota(jnp.int32, (half, padded), 0)
     high = low + half
 
-    def fetch(node):
+    def fetch(node, wanted=None):
         tile = tiles[node >> TILE_BITS].astype(jnp.float32)
-        line = jnp.full((half, padded), node, jnp.int32) & (TILE - 1)
+        if wanted is None:
+            line = jnp.full((half, padded), node, jnp.int32) & (TILE - 1)
+        else:
+            line = jnp.full((half, padded), jnp.where(wanted, node & (TILE - 1), TILE), jnp.int32)
         return jnp.where(line == low, tile[:half], jnp.where(line == high, tile[half:], 0.0))
 
     def add_lines(values):
@@ -110,41 +115,39 @@
             step *= 2
         return values[0]
 
-    def gather_rows(slots, first, number):
-        rows = [order_ref[0, 0, first + i] >> 4 for i in range(number)]
+    def gather_rows(slots, exact, number, carry):
+        first = pl.multiple_of(number * half, half)
+        entries = [order_ref[0, 0, first + i] for i in range(half)]
+        rows = [entry >> 4 for entry in entries]
         starts = [row * fanout for row in rows]
-        owns = [fetch(own_ref[0, 0, row]) for row in rows]
-        nears = [fetch(near_ref[0, 0, start]) for start in starts]
+
+        def near(i, slot):
+            node = near_ref[0, 0, starts[i] + slot]
+            return fetch(node) if exact else fetch(node, slot < (entries[i] & 15))
+
+        own_sum_ref[pl.ds(first, half), :] = add_lines([fetch(own_ref[0, 0, row]) for row in rows])
+        nears = [near(i, 0) for i in range(half)]
         for slot in range(1, slots):
-            nears = [near + fetch(near_ref[0, 0, start + slot]) for near, start in zip(nears, starts)]
-        empty = [jnp.zeros((half, padded), jnp.float32)] * (UNROLL - number)
-        totals = add_lines(owns + empty + nears + empty)
-        own_sum_ref[pl.ds(first, number), :] = totals[:number]
-        near_sum_ref[pl.ds(first, number), :] = totals[UNROLL : UNROLL + number]
-
-    begin = 0
+            nears = [nears[i] + near(i, slot) for i in range(half)]
+        near_sum_ref[pl.ds(first, half), :] = add_lines(nears)
+        return carry
+
+    start = 0
     for slots in range(fanout, 0, -1):
         end = enough_ref[0, 0, slots]
-        whole = end - begin >= UNROLL
-
-        def chunk_of(number, carry, slots=slots, begin=begin, end=end):
-            gather_rows(slots, jnp.minimum(begin + number * UNROLL, end - UNROLL), UNROLL)
-            return carry
-
-        def one_of(at, carry, slots=slots):
-            gather_rows(slots, at, 1)
-            return carry
-
-        lax.fori_loop(0, jnp.where(whole, lax.div(end - begin + UNROLL - 1, UNROLL), 0), chunk_of, 0)
-        lax.fori_loop(begin, jnp.where(whole, begin, end), one_of, 0)
-        begin = end
-
-    def clear(at, carry):
-        own_sum_ref[pl.ds(at, 1), :] = jnp.zeros((1, padded), jnp.float32)
-        near_sum_ref[pl.ds(at, 1), :] = jnp.zeros((1, padded), jnp.float32)
+        whole = jnp.maximum(lax.div(end, half), start)
+        stop = lax.div(end + half - 1, half)
+        lax.fori_loop(start, whole, functools.partial(gather_rows, slots, True), 0)
+        lax.fori_loop(whole, stop, functools.partial(gather_rows, slots, False), 0)
+        start = stop
+
+    def clear(number, carry):
+        first = pl.multiple_of(number * half, half)
+        own_sum_ref[pl.ds(first, half), :] = jnp.zeros((half, padded), jnp.float32)
+        near_sum_ref[pl.ds(first, half), :] = jnp.zeros((half, padded), jnp.float32)
         return carry
 
-    lax.fori_loop(begin, capacity, clear, 0)
+    lax.fori_loop(start, capacity // half, clear, 0)
     counts = jnp.transpose(jnp.broadcast_to(count_ref[0], (padded, count_ref.shape[2])))[:capacity]
     own = own_sum_ref[...].astype(jnp.bfloat16)[:, :width]
     near = (near_sum_ref[...] / counts).astype(jnp.bfloat16)[:, :width]

time: 167 us -> 161 us (0.964)
  Pallas kernels: 75.4 us -> 70.6 us
  waiting for transfers between devices: 30.2 us -> 28.2 us
    pallas_call x3, Pallas kernels: 48.8 us -> 44.6 us  [gather_layer(): pl.pallas_call(functools.partial(gather_kernel, fanout, capacity), grid_s...]
    ppermute x21, waiting for transfers between devices: 19.8 us -> 17.8 us  [send_along(): lax.ppermute(array, 'feat', [(ring[i], ring[(i + shift) % count]) for i i...]
  transfers between devices with their start and end apart: 24 -> 24, of which waited for: 10 -> 14; matrix products, arithmetic and copies ran while one was open for 7% -> 7% of each run, Pallas kernels for 41% -> 40%
where the time goes in v6:
time: 161 us
  Pallas kernels  70.6 us (44%)
  starting transfers between devices  33.9 us (21%)
  waiting for transfers between devices  28.2 us (18%)
  between operations  14.3 us (9%)
  other arithmetic  7.49 us (5%)
  local copies, waits for them, and re-layouts  6.33 us (4%)
    pallas_call x3, Pallas kernels, gather_layer(): pl.pallas_call(functools.partial(gather_kernel, fanout, capacity), grid_s...  44.6 us
    ppermute x21, starting transfers between devices, send_along(): lax.ppermute(array, 'feat', [(ring[i], ring[(i + shift) % count]) for i i...  29.8 us
    pallas_call x1, Pallas kernels, build_table(): pl.pallas_call(table_kernel, grid=(nodes // chunk,), in_specs=[pl.BlockSp...  19.2 us
    ppermute x21, waiting for transfers between devices, send_along(): lax.ppermute(array, 'feat', [(ring[i], ring[(i + shift) % count]) for i i...  17.8 us
    ppermute x1, waiting for transfers between devices, group_sum(): other = lax.ppermute(mine, 'dp', [(i, i ^ stride) for i in range(count)])  7.66 us
    ppermute x1, starting transfers between devices, group_sum(): other = lax.ppermute(mine, 'dp', [(i, i ^ stride) for i in range(count)])  3.99 us
  transfers between devices with their start and end apart: 24, of which 14 were waited for; matrix products, arithmetic and copies ran while one was open for 7% of the time, Pallas kernels for 40%

profile of v6, /device:TPU:0, one launch (start us, length us, event | category | flops | bytes accessed | tf_op | source)
XLA Modules:
  0.0 160.8 jit_solution(8199451708416733856)
XLA Ops:
  10.8 2.5 %convert_reduce_fusion = s32[8,704]{1,0:T(8,128)S(1)} fusion(s32[8,704]{1,0:T(8,128)S(1)} %get-tuple-element.86), kind=kLoop, calls=%fused_computation | loop fusion | flops 11889152 | bytes 45056 | tf_op jit(solution)/shard_map/reduce_sum | solution.py:31
  13.3 2.1 %select_reduce_fusion = s32[8,512]{1,0:T(8,128)S(1)} fusion(s32[8,704]{1,0:T(8,128)S(1)} %broadcast_add_fusion, s32[8,704]{1,0:T(8,128)S(1)} %convert_reduce_fusion), kind=kLoop, calls=%fused_computation.1 | loop fusion | flops 8646656 | bytes 61440 | tf_op jit(solution)/shard_map/reduce_sum | solution.py:33
  15.4 1.1 broadcast_in_dim.61.near_ref
  18.3 19.2 %build_table.1.table_ref = bf16[131072,128]{1,0:T(8,128)(2,1)S(1)} custom-call(bf16[128,131072]{1,0:T(8,128)(2,1)} %refs_3_, bf16[128,131072]{1,0:T(8,128)(2,1)} %refs_3_, bf16[128,131072]{1,0:T(8,128)(2,1)} %refs_3_, bf16[128,131072]{1,0:T(8,128)(2,1)} %refs_3_), custom_call_target="tpu_custom_call" | custom-call | tf_op jit(solution)/shard_map/build_table/pallas_call | solution.py:75
  37.6 18.7 %gather_layer.3 = (bf16[416,256]{1,0:T(8,128)(2,1)S(1)}, bf16[416,256]{1,0:T(8,128)(2,1)S(1)}, bf16[416,256]{1,0:T(8,128)(2,1)S(1)}, bf16[131072,128]{1,0:T(8,128)(2,1)S(1)}) custom-call(s32[16]{0:T(128)S(1)} %fusion.3.turn_ref.source_ref, s32[8,1,16]{2,1,0:T(1,128)S(1)} %bitcast.10, ...), custom_call_target="tpu_custom_call", output_to_operand_aliasing={{3}: (6, {})} | custom-call | bytes 51118080 | tf_op jit(solution)/shard_map/gather_layer/pallas_call | solution.py:175
  56.5 6.3 %collective-permute-start.1 = (bf16[416,256]{1,0:T(8,128)(2,1)S(1)}, bf16[416,256]{1,0:T(8,128)(2,1)S(1)}, u32[]{:S(2)}, u32[]{:S(2)}) collective-permute-start(bf16[416,256]{1,0:T(8,128)(2,1)S(1)} %get-tuple-element.56.rest_1_), channel_id=1, source_target_pairs={{0,24},{8,28},{16,20},{24,12},{28,4},{20,0},{12,8},{4,16},{1,25},{... | collective-permute-start | bytes 638984 | tf_op jit(solution)/shard_map/ppermute | solution.py:348
  62.8 18.0 %gather_layer.4 = (bf16[416,256]{1,0:T(8,128)(2,1)S(1)}, bf16[416,256]{1,0:T(8,128)(2,1)S(1)}, bf16[416,256]{1,0:T(8,128)(2,1)S(1)}, bf16[131072,128]{1,0:T(8,128)(2,1)S(1)}) custom-call(s32[16]{0:T(128)S(1)} %fusion.3.turn_ref.source_ref, s32[8,1,16]{2,1,0:T(1,128)S(1)} %bitcast.11, ...), custom_call_target="tpu_custom_call", output_to_operand_aliasing={{3}: (6, {})} | custom-call | bytes 51118080 | tf_op jit(solution)/shard_map/gather_layer/pallas_call | solution.py:175
  81.3 2.9 %collective-permute-start.4 = (bf16[416,256]{1,0:T(8,128)(2,1)S(1)}, bf16[416,256]{1,0:T(8,128)(2,1)S(1)}, u32[]{:S(2)}, u32[]{:S(2)}) collective-permute-start(bf16[416,256]{1,0:T(8,128)(2,1)S(1)} %get-tuple-element.64.rest_4_), channel_id=1, source_target_pairs={{0,12},{8,4},{16,0},{24,8},{28,16},{20,24},{12,28},{4,20},{1,13},{... | collective-permute-start | bytes 638984 | tf_op jit(solution)/shard_map/ppermute | solution.py:348
  84.2 1.1 collective-permute-start.5
  85.3 7.8 %gather_layer.5 = (bf16[416,256]{1,0:T(8,128)(2,1)S(1)}, bf16[416,256]{1,0:T(8,128)(2,1)S(1)}, bf16[131072,128]{1,0:T(8,128)(2,1)S(1)}) custom-call(s32[16]{0:T(128)S(1)} %fusion.3.turn_ref.source_ref, s32[8,1,16]{2,1,0:T(1,128)S(1)} %bitcast.12, s32[8,1,512]{2,1,0:T(1,128)S(1)} %broadcast_in_dim.59.order_ref, ...), custom_call_target="tpu_custom_call", output_to_operand_aliasing={{2}: (6, {})} | custom-call | bytes 34078720 | tf_op jit(solution)/shard_map/gather_layer/pallas_call | solution.py:175
  93.1 1.1 collective-permute-done.3.rest_3_
  94.3 2.9 %collective-permute-start.6 = (bf16[416,256]{1,0:T(8,128)(2,1)S(1)}, bf16[416,256]{1,0:T(8,128)(2,1)S(1)}, u32[]{:S(2)}, u32[]{:S(2)}) collective-permute-start(bf16[416,256]{1,0:T(8,128)(2,1)S(1)} %get-tuple-element.69.rest_6_), channel_id=1, source_target_pairs={{0,4},{8,0},{16,8},{24,16},{28,24},{20,28},{12,20},{4,12},{1,5},{9... | collective-permute-start | bytes 638984 | tf_op jit(solution)/shard_map/ppermute | solution.py:348
  98.5 2.9 %collective-permute-done.6.rest_6_ = bf16[416,256]{1,0:T(8,128)(2,1)S(1)} collective-permute-done((bf16[416,256]{1,0:T(8,128)(2,1)S(1)}, bf16[416,256]{1,0:T(8,128)(2,1)S(1)}, u32[]{:S(2)}, u32[]{:S(2)}) %collective-permute-start.6) | collective-permute-done | bytes 213024 | tf_op jit(solution)/shard_map/ppermute | solution.py:348
  101.4 1.2 copy-done
  102.7 3.1 %upper_layers.1 = (bf16[304,256]{1,0:T(8,128)(2,1)S(1)}, bf16[304,256]{1,0:T(8,128)(2,1)S(1)}) custom-call(s32[1]{0:T(128)} %dynamic_slice.23.size_ref, s32[16]{0:T(128)S(1)} %fusion.3.turn_ref.source_ref, bf16[8,256,256]{2,1,0:T(8,128)(2,1)S(1)} %copy-done, bf16[2,172,256]{2,1,0:T(8,128)(2,1)S(1)} %bitcast.9, s32[1,416]{1,0:T(1,128)S(1)} %compare_select_fusion.2.row_ref, ...), custom_call_target="tpu_custom_call" | custom-call | tf_op jit(solution)/shard_map/upper_layers/pallas_call | solution.py:264
  105.8 3.9 %collective-permute-start.7 = (bf16[304,256]{1,0:T(8,128)(2,1)S(1)}, bf16[304,256]{1,0:T(8,128)(2,1)S(1)}, u32[]{:S(2)}, u32[]{:S(2)}) collective-permute-start(bf16[304,256]{1,0:T(8,128)(2,1)S(1)} %get-tuple-element.82.rest_15_), channel_id=1, source_target_pairs={{0,8},{8,16},{16,24},{24,28},{28,20},{20,12},{12,4},{4,0},{1,9},{9... | collective-permute-start | bytes 466952 | tf_op jit(solution)/shard_map/ppermute | solution.py:348
  109.6 1.4 collective-permute-start.11
  111.7 1.7 %collective-permute-done.7.rest_14_ = bf16[304,256]{1,0:T(8,128)(2,1)S(1)} collective-permute-done((bf16[304,256]{1,0:T(8,128)(2,1)S(1)}, bf16[304,256]{1,0:T(8,128)(2,1)S(1)}, u32[]{:S(2)}, u32[]{:S(2)}) %collective-permute-start.7) | collective-permute-done | bytes 155680 | tf_op jit(solution)/shard_map/ppermute | solution.py:348
  113.3 2.4 %collective-permute-start.8 = (bf16[304,256]{1,0:T(8,128)(2,1)S(1)}, bf16[304,256]{1,0:T(8,128)(2,1)S(1)}, u32[]{:S(2)}, u32[]{:S(2)}) collective-permute-start(bf16[304,256]{1,0:T(8,128)(2,1)S(1)} %collective-permute-done.7.rest_14_), channel_id=1, source_target_pairs={{0,8},{8,16},{16,24},{24,28},{28,20},{20,12},{12,4},{4,0},{1,9},{9... | collective-permute-start | bytes 466952 | tf_op jit(solution)/shard_map/ppermute | solution.py:348
  116.5 3.3 %collective-permute-done.11.rest_13_ = bf16[304,256]{1,0:T(8,128)(2,1)S(1)} collective-permute-done((bf16[304,256]{1,0:T(8,128)(2,1)S(1)}, bf16[304,256]{1,0:T(8,128)(2,1)S(1)}, u32[]{:S(2)}, u32[]{:S(2)}) %collective-permute-start.11) | collective-permute-done | bytes 155680 | tf_op jit(solution)/shard_map/ppermute | solution.py:348
  119.8 2.0 %collective-permute-start.19 = (bf16[304,256]{1,0:T(8,128)(2,1)S(1)}, bf16[304,256]{1,0:T(8,128)(2,1)S(1)}, u32[]{:S(2)}, u32[]{:S(2)}) collective-permute-start(bf16[304,256]{1,0:T(8,128)(2,1)S(1)} %collective-permute-done.18.rest_22_), channel_id=1, source_target_pairs={{0,8},{8,16},{16,24},{24,28},{28,20},{20,12},{12,4},{4,0},{1,9},{9... | collective-permute-start | bytes 466952 | tf_op jit(solution)/shard_map/ppermute | solution.py:348
  121.8 1.9 %collective-permute-start.9 = (bf16[304,256]{1,0:T(8,128)(2,1)S(1)}, bf16[304,256]{1,0:T(8,128)(2,1)S(1)}, u32[]{:S(2)}, u32[]{:S(2)}) collective-permute-start(bf16[304,256]{1,0:T(8,128)(2,1)S(1)} %collective-permute-done.8.rest_12_), channel_id=1, source_target_pairs={{0,8},{8,16},{16,24},{24,28},{28,20},{20,12},{12,4},{4,0},{1,9},{9... | collective-permute-start | bytes 466952 | tf_op jit(solution)/shard_map/ppermute | solution.py:348
  123.9 2.7 %collective-permute-done.12.rest_11_ = bf16[304,256]{1,0:T(8,128)(2,1)S(1)} collective-permute-done((bf16[304,256]{1,0:T(8,128)(2,1)S(1)}, bf16[304,256]{1,0:T(8,128)(2,1)S(1)}, u32[]{:S(2)}, u32[]{:S(2)}) %collective-permute-start.12) | collective-permute-done | bytes 155680 | tf_op jit(solution)/shard_map/ppermute | solution.py:348
  126.8 1.8 %collective-permute-start.20 = (bf16[304,256]{1,0:T(8,128)(2,1)S(1)}, bf16[304,256]{1,0:T(8,128)(2,1)S(1)}, u32[]{:S(2)}, u32[]{:S(2)}) collective-permute-start(bf16[304,256]{1,0:T(8,128)(2,1)S(1)} %collective-permute-done.19.rest_20_), channel_id=1, source_target_pairs={{0,8},{8,16},{16,24},{24,28},{28,20},{20,12},{12,4},{4,0},{1,9},{9... | collective-permute-start | bytes 466952 | tf_op jit(solution)/shard_map/ppermute | solution.py:348
  128.9 1.4 collective-permute-start.10
  132.0 2.2 %collective-permute-done.10.rest_8_ = bf16[304,256]{1,0:T(8,128)(2,1)S(1)} collective-permute-done((bf16[304,256]{1,0:T(8,128)(2,1)S(1)}, bf16[304,256]{1,0:T(8,128)(2,1)S(1)}, u32[]{:S(2)}, u32[]{:S(2)}) %collective-permute-start.10) | collective-permute-done | bytes 155680 | tf_op jit(solution)/shard_map/ppermute | solution.py:348
  134.2 1.4 collective-permute-done.17.rest_16_
  135.6 1.8 %grad_layer.1 = f32[608,256]{1,0:T(8,128)S(1)} custom-call(s32[16]{0:T(128)S(1)} %fusion.3.turn_ref.source_ref, bf16[416,256]{1,0:T(8,128)(2,1)S(1)} %get-tuple-element.55.rest_0_, bf16[416,256]{1,0:T(8,128)(2,1)S(1)} %get-tuple-element.56.rest_1_, bf16[416,256]{1,0:T(8,128)(2,1)S(1)} %get-tuple-element.57.rest_2_, ...), custom_call_target="tpu_custom_call" | custom-call | tf_op jit(solution)/shard_map/grad_layer/pallas_call | solution.py:306
  137.4 2.0 %collective-permute-done.21 = f32[608,256]{1,0:T(8,128)S(1)} collective-permute-done((f32[608,256]{1,0:T(8,128)S(1)}, f32[608,256]{1,0:T(8,128)S(1)}, u32[]{:S(2)}, u32[]{:S(2)}) %collective-permute-start.21) | collective-permute-done | bytes 622624 | tf_op jit(solution)/shard_map/ppermute | solution.py:369
  139.6 4.0 %collective-permute-start.22 = (bf16[608,256]{1,0:T(8,128)(2,1)S(1)}, bf16[608,256]{1,0:T(8,128)(2,1)S(1)}, u32[]{:S(2)}, u32[]{:S(2)}) collective-permute-start(bf16[608,256]{1,0:T(8,128)(2,1)S(1)} %add_convert_fusion.mine_ref), channel_id=1, source_target_pairs={{0,2},{1,3},{2,0},{3,1},{4,6},{5,7},{6,4},{7,5},{8,10},{9,11},{10,... | collective-permute-start | bytes 933896 | tf_op jit(solution)/shard_map/ppermute | solution.py:373
  143.6 7.7 %collective-permute-done.22.other_ref = bf16[608,256]{1,0:T(8,128)(2,1)S(1)} collective-permute-done((bf16[608,256]{1,0:T(8,128)(2,1)S(1)}, bf16[608,256]{1,0:T(8,128)(2,1)S(1)}, u32[]{:S(2)}, u32[]{:S(2)}) %collective-permute-start.22) | collective-permute-done | bytes 311328 | tf_op jit(solution)/shard_map/ppermute | solution.py:373
  152.0 2.0 %final_sum.1 = (f32[2,128,256]{2,1,0:T(8,128)}, f32[172,2,256]{2,1,0:T(2,128)}) custom-call(bf16[608,256]{1,0:T(8,128)(2,1)} %copy-done.1, bf16[608,256]{1,0:T(8,128)(2,1)} %copy-done.2), custom_call_target="tpu_custom_call" | custom-call | tf_op jit(solution)/shard_map/final_sum/pallas_call | solution.py:329
  (60 shorter events, 12.1 us)
Async XLA Ops:
  7.2 94.2 %all-gather.2.cloned.1.call-start = ((), (), s32[]{:S(2)}) async-start(), calls=%async_computation | async-start | bytes 1179648 | tf_op jit(solution)/shard_map/all_gather | solution.py:410
  56.3 24.5 %collective-permute-start = (bf16[416,256]{1,0:T(8,128)(2,1)S(1)}, bf16[416,256]{1,0:T(8,128)(2,1)S(1)}, u32[]{:S(2)}, u32[]{:S(2)}) collective-permute-start(bf16[416,256]{1,0:T(8,128)(2,1)S(1)} %get-tuple-element.55.rest_0_), channel_id=1, source_target_pairs={{0,28},{8,20},{16,12},{24,4},{28,0},{20,8},{12,16},{4,24},{1,29},{... | collective-permute-start | bytes 638984 | tf_op jit(solution)/shard_map/ppermute | solution.py:348
  56.5 24.7 %collective-permute-start.1 = (bf16[416,256]{1,0:T(8,128)(2,1)S(1)}, bf16[416,256]{1,0:T(8,128)(2,1)S(1)}, u32[]{:S(2)}, u32[]{:S(2)}) collective-permute-start(bf16[416,256]{1,0:T(8,128)(2,1)S(1)} %get-tuple-element.56.rest_1_), channel_id=1, source_target_pairs={{0,24},{8,28},{16,20},{24,12},{28,4},{20,0},{12,8},{4,16},{1,25},{... | collective-permute-start | bytes 638984 | tf_op jit(solution)/shard_map/ppermute | solution.py:348
  62.8 18.4 %collective-permute-start.2 = (bf16[416,256]{1,0:T(8,128)(2,1)S(1)}, bf16[416,256]{1,0:T(8,128)(2,1)S(1)}, u32[]{:S(2)}, u32[]{:S(2)}) collective-permute-start(bf16[416,256]{1,0:T(8,128)(2,1)S(1)} %get-tuple-element.57.rest_2_), channel_id=1, source_target_pairs={{0,20},{8,12},{16,4},{24,0},{28,8},{20,16},{12,24},{4,28},{1,21},{... | collective-permute-start | bytes 638984 | tf_op jit(solution)/shard_map/ppermute | solution.py:348
  80.8 16.3 %copy-start.3 = (bf16[2,256,172]{1,0,2:T(2,128)(2,1)S(1)}, bf16[2,256,172]{1,0,2:T(2,128)(2,1)}, u32[]{:S(2)}) copy-start(bf16[2,256,172]{1,0,2:T(2,128)(2,1)} %param.13) | copy-start | bytes 528388
  81.2 13.0 %collective-permute-start.3 = (bf16[416,256]{1,0:T(8,128)(2,1)S(1)}, bf16[416,256]{1,0:T(8,128)(2,1)S(1)}, u32[]{:S(2)}, u32[]{:S(2)}) collective-permute-start(bf16[416,256]{1,0:T(8,128)(2,1)S(1)} %get-tuple-element.63.rest_3_), channel_id=1, source_target_pairs={{0,16},{8,24},{16,28},{24,20},{28,12},{20,4},{12,0},{4,8},{1,17},{... | collective-permute-start | bytes 638984 | tf_op jit(solution)/shard_map/ppermute | solution.py:348
  81.3 13.0 %collective-permute-start.4 = (bf16[416,256]{1,0:T(8,128)(2,1)S(1)}, bf16[416,256]{1,0:T(8,128)(2,1)S(1)}, u32[]{:S(2)}, u32[]{:S(2)}) collective-permute-start(bf16[416,256]{1,0:T(8,128)(2,1)S(1)} %get-tuple-element.64.rest_4_), channel_id=1, source_target_pairs={{0,12},{8,4},{16,0},{24,8},{28,16},{20,24},{12,28},{4,20},{1,13},{... | collective-permute-start | bytes 638984 | tf_op jit(solution)/shard_map/ppermute | solution.py:348
  84.2 10.1 %collective-permute-start.5 = (bf16[416,256]{1,0:T(8,128)(2,1)S(1)}, bf16[416,256]{1,0:T(8,128)(2,1)S(1)}, u32[]{:S(2)}, u32[]{:S(2)}) collective-permute-start(bf16[416,256]{1,0:T(8,128)(2,1)S(1)} %get-tuple-element.65.rest_5_), channel_id=1, source_target_pairs={{0,8},{8,16},{16,24},{24,28},{28,20},{20,12},{12,4},{4,0},{1,9},{9... | collective-permute-start | bytes 638984 | tf_op jit(solution)/shard_map/ppermute | solution.py:348
  94.3 7.1 %collective-permute-start.6 = (bf16[416,256]{1,0:T(8,128)(2,1)S(1)}, bf16[416,256]{1,0:T(8,128)(2,1)S(1)}, u32[]{:S(2)}, u32[]{:S(2)}) collective-permute-start(bf16[416,256]{1,0:T(8,128)(2,1)S(1)} %get-tuple-element.69.rest_6_), channel_id=1, source_target_pairs={{0,4},{8,0},{16,8},{24,16},{28,24},{20,28},{12,20},{4,12},{1,5},{9... | collective-permute-start | bytes 638984 | tf_op jit(solution)/shard_map/ppermute | solution.py:348
  101.4 1.2 copy-start
  105.8 7.6 %collective-permute-start.7 = (bf16[304,256]{1,0:T(8,128)(2,1)S(1)}, bf16[304,256]{1,0:T(8,128)(2,1)S(1)}, u32[]{:S(2)}, u32[]{:S(2)}) collective-permute-start(bf16[304,256]{1,0:T(8,128)(2,1)S(1)} %get-tuple-element.82.rest_15_), channel_id=1, source_target_pairs={{0,8},{8,16},{16,24},{24,28},{28,20},{20,12},{12,4},{4,0},{1,9},{9... | collective-permute-start | bytes 466952 | tf_op jit(solution)/shard_map/ppermute | solution.py:348
  109.6 6.9 %collective-permute-start.14 = (bf16[304,256]{1,0:T(8,128)(2,1)S(1)}, bf16[304,256]{1,0:T(8,128)(2,1)S(1)}, u32[]{:S(2)}, u32[]{:S(2)}) collective-permute-start(bf16[304,256]{1,0:T(8,128)(2,1)S(1)} %get-tuple-element.83.rest_23_), channel_id=1, source_target_pairs={{0,4},{8,0},{16,8},{24,16},{28,24},{20,28},{12,20},{4,12},{1,5},{9... | collective-permute-start | bytes 466952 | tf_op jit(solution)/shard_map/ppermute | solution.py:348
  109.6 10.2 %collective-permute-start.11 = (bf16[304,256]{1,0:T(8,128)(2,1)S(1)}, bf16[304,256]{1,0:T(8,128)(2,1)S(1)}, u32[]{:S(2)}, u32[]{:S(2)}) collective-permute-start(bf16[304,256]{1,0:T(8,128)(2,1)S(1)} %get-tuple-element.82.rest_15_), channel_id=1, source_target_pairs={{0,4},{8,0},{16,8},{24,16},{28,24},{20,28},{12,20},{4,12},{1,5},{9... | collective-permute-start | bytes 466952 | tf_op jit(solution)/shard_map/ppermute | solution.py:348
  111.0 8.8 %collective-permute-start.18 = (bf16[304,256]{1,0:T(8,128)(2,1)S(1)}, bf16[304,256]{1,0:T(8,128)(2,1)S(1)}, u32[]{:S(2)}, u32[]{:S(2)}) collective-permute-start(bf16[304,256]{1,0:T(8,128)(2,1)S(1)} %get-tuple-element.83.rest_23_), channel_id=1, source_target_pairs={{0,8},{8,16},{16,24},{24,28},{28,20},{20,12},{12,4},{4,0},{1,9},{9... | collective-permute-start | bytes 466952 | tf_op jit(solution)/shard_map/ppermute | solution.py:348
  113.3 8.5 %collective-permute-start.8 = (bf16[304,256]{1,0:T(8,128)(2,1)S(1)}, bf16[304,256]{1,0:T(8,128)(2,1)S(1)}, u32[]{:S(2)}, u32[]{:S(2)}) collective-permute-start(bf16[304,256]{1,0:T(8,128)(2,1)S(1)} %collective-permute-done.7.rest_14_), channel_id=1, source_target_pairs={{0,8},{8,16},{16,24},{24,28},{28,20},{20,12},{12,4},{4,0},{1,9},{9... | collective-permute-start | bytes 466952 | tf_op jit(solution)/shard_map/ppermute | solution.py:348
  116.5 7.3 %collective-permute-start.15 = (bf16[304,256]{1,0:T(8,128)(2,1)S(1)}, bf16[304,256]{1,0:T(8,128)(2,1)S(1)}, u32[]{:S(2)}, u32[]{:S(2)}) collective-permute-start(bf16[304,256]{1,0:T(8,128)(2,1)S(1)} %collective-permute-done.14.rest_21_), channel_id=1, source_target_pairs={{0,4},{8,0},{16,8},{24,16},{28,24},{20,28},{12,20},{4,12},{1,5},{9... | collective-permute-start | bytes 466952 | tf_op jit(solution)/shard_map/ppermute | solution.py:348
  119.8 6.8 %collective-permute-start.12 = (bf16[304,256]{1,0:T(8,128)(2,1)S(1)}, bf16[304,256]{1,0:T(8,128)(2,1)S(1)}, u32[]{:S(2)}, u32[]{:S(2)}) collective-permute-start(bf16[304,256]{1,0:T(8,128)(2,1)S(1)} %collective-permute-done.11.rest_13_), channel_id=1, source_target_pairs={{0,4},{8,0},{16,8},{24,16},{28,24},{20,28},{12,20},{4,12},{1,5},{9... | collective-permute-start | bytes 466952 | tf_op jit(solution)/shard_map/ppermute | solution.py:348
  119.8 7.0 %collective-permute-start.19 = (bf16[304,256]{1,0:T(8,128)(2,1)S(1)}, bf16[304,256]{1,0:T(8,128)(2,1)S(1)}, u32[]{:S(2)}, u32[]{:S(2)}) collective-permute-start(bf16[304,256]{1,0:T(8,128)(2,1)S(1)} %collective-permute-done.18.rest_22_), channel_id=1, source_target_pairs={{0,8},{8,16},{16,24},{24,28},{28,20},{20,12},{12,4},{4,0},{1,9},{9... | collective-permute-start | bytes 466952 | tf_op jit(solution)/shard_map/ppermute | solution.py:348
  121.8 7.1 %collective-permute-start.9 = (bf16[304,256]{1,0:T(8,128)(2,1)S(1)}, bf16[304,256]{1,0:T(8,128)(2,1)S(1)}, u32[]{:S(2)}, u32[]{:S(2)}) collective-permute-start(bf16[304,256]{1,0:T(8,128)(2,1)S(1)} %collective-permute-done.8.rest_12_), channel_id=1, source_target_pairs={{0,8},{8,16},{16,24},{24,28},{28,20},{20,12},{12,4},{4,0},{1,9},{9... | collective-permute-start | bytes 466952 | tf_op jit(solution)/shard_map/ppermute | solution.py:348
  123.8 6.6 %collective-permute-start.16 = (bf16[304,256]{1,0:T(8,128)(2,1)S(1)}, bf16[304,256]{1,0:T(8,128)(2,1)S(1)}, u32[]{:S(2)}, u32[]{:S(2)}) collective-permute-start(bf16[304,256]{1,0:T(8,128)(2,1)S(1)} %collective-permute-done.15.rest_19_), channel_id=1, source_target_pairs={{0,4},{8,0},{16,8},{24,16},{28,24},{20,28},{12,20},{4,12},{1,5},{9... | collective-permute-start | bytes 466952 | tf_op jit(solution)/shard_map/ppermute | solution.py:348
  126.6 5.2 %collective-permute-start.13 = (bf16[304,256]{1,0:T(8,128)(2,1)S(1)}, bf16[304,256]{1,0:T(8,128)(2,1)S(1)}, u32[]{:S(2)}, u32[]{:S(2)}) collective-permute-start(bf16[304,256]{1,0:T(8,128)(2,1)S(1)} %collective-permute-done.12.rest_11_), channel_id=1, source_target_pairs={{0,4},{8,0},{16,8},{24,16},{28,24},{20,28},{12,20},{4,12},{1,5},{9... | collective-permute-start | bytes 466952 | tf_op jit(solution)/shard_map/ppermute | solution.py:348
  126.8 5.2 %collective-permute-start.20 = (bf16[304,256]{1,0:T(8,128)(2,1)S(1)}, bf16[304,256]{1,0:T(8,128)(2,1)S(1)}, u32[]{:S(2)}, u32[]{:S(2)}) collective-permute-start(bf16[304,256]{1,0:T(8,128)(2,1)S(1)} %collective-permute-done.19.rest_20_), channel_id=1, source_target_pairs={{0,8},{8,16},{16,24},{24,28},{28,20},{20,12},{12,4},{4,0},{1,9},{9... | collective-permute-start | bytes 466952 | tf_op jit(solution)/shard_map/ppermute | solution.py:348
  128.9 5.2 %collective-permute-start.10 = (bf16[304,256]{1,0:T(8,128)(2,1)S(1)}, bf16[304,256]{1,0:T(8,128)(2,1)S(1)}, u32[]{:S(2)}, u32[]{:S(2)}) collective-permute-start(bf16[304,256]{1,0:T(8,128)(2,1)S(1)} %collective-permute-done.9.rest_10_), channel_id=1, source_target_pairs={{0,8},{8,16},{16,24},{24,28},{28,20},{20,12},{12,4},{4,0},{1,9},{9... | collective-permute-start | bytes 466952 | tf_op jit(solution)/shard_map/ppermute | solution.py:348
  130.4 5.2 %collective-permute-start.17 = (bf16[304,256]{1,0:T(8,128)(2,1)S(1)}, bf16[304,256]{1,0:T(8,128)(2,1)S(1)}, u32[]{:S(2)}, u32[]{:S(2)}) collective-permute-start(bf16[304,256]{1,0:T(8,128)(2,1)S(1)} %collective-permute-done.16.rest_17_), channel_id=1, source_target_pairs={{0,4},{8,0},{16,8},{24,16},{28,24},{20,28},{12,20},{4,12},{1,5},{9... | collective-permute-start | bytes 466952 | tf_op jit(solution)/shard_map/ppermute | solution.py:348
  137.4 2.1 %collective-permute-start.21 = (f32[608,256]{1,0:T(8,128)S(1)}, f32[608,256]{1,0:T(8,128)S(1)}, u32[]{:S(2)}, u32[]{:S(2)}) collective-permute-start(f32[608,256]{1,0:T(8,128)S(1)} %grad_layer.1), channel_id=1, source_target_pairs={{0,1},{1,0},{2,3},{3,2},{4,5},{5,4},{6,7},{7,6},{8,9},{9,8},{10,11... | collective-permute-start | bytes 1867784 | tf_op jit(solution)/shard_map/ppermute | solution.py:369
  139.6 11.7 %copy-start.1 = (bf16[608,256]{1,0:T(8,128)(2,1)}, bf16[608,256]{1,0:T(8,128)(2,1)S(1)}, u32[]{:S(2)}) copy-start(bf16[608,256]{1,0:T(8,128)(2,1)S(1)} %add_convert_fusion.mine_ref) | copy-start | bytes 933892
  139.6 11.7 %collective-permute-start.22 = (bf16[608,256]{1,0:T(8,128)(2,1)S(1)}, bf16[608,256]{1,0:T(8,128)(2,1)S(1)}, u32[]{:S(2)}, u32[]{:S(2)}) collective-permute-start(bf16[608,256]{1,0:T(8,128)(2,1)S(1)} %add_convert_fusion.mine_ref), channel_id=1, source_target_pairs={{0,2},{1,3},{2,0},{3,1},{4,6},{5,7},{6,4},{7,5},{8,10},{9,11},{10,... | collective-permute-start | bytes 933896 | tf_op jit(solution)/shard_map/ppermute | solution.py:373
  151.2 0.7 copy-start.2
Sparse Core Ops, SparseCore 0:
  10.1 42.8 all-gather.1

commit v7 on v6

--- a/solution.py
+++ b/solution.py
@@ -18,29 +18,55 @@
     return (value + step - 1) // step * step
 
 
-def plan_rows(hop1_count, hop2_count, sizes, kept):
-    groups, seed_total = hop1_count.shape
-    row_total = hop2_count.shape[1]
-    fanout = (row_total - seed_total) // seed_total
-    live = jnp.arange(seed_total)[None, :] < sizes[:, None]
-    near = jnp.arange(fanout)[None, None, :] < jnp.where(live, hop1_count, 0)[:, :, None]
-    used = jnp.concatenate([live, near.reshape(groups, -1)], axis=1)
-    count = jnp.where(used, hop2_count, 0)
-    row = jnp.arange(row_total)[None, :]
-    mixed = count * row_total + (row_total - 1 - row)
-    place = jnp.sum((mixed[:, None, :] > mixed[:, :, None]).astype(jnp.int32), axis=2)
-    packed = row * 16 + count
-    order = jnp.sum(
-        jnp.where(place[:, None, :] == jnp.arange(kept)[None, :, None], packed[:, None, :], 0), axis=2
+def plan_rows(seed_total, fanout, size, hop1_row, hop2_row, lower_ref, equal_ref):
+    row_total = hop2_row.shape[1]
+    kept = round_up(capacity_of(seed_total, row_total), LANES)
+
+    def flags(condition):
+        return jnp.where(condition, 1.0, 0.0).astype(jnp.bfloat16)
+
+    def iota(shape, dim):
+        return lax.broadcasted_iota(jnp.int32, shape, dim)
+
+    def product(one, two):
+        return jnp.dot(one, two, preferred_element_type=jnp.float32)
+
+    def spread(row):
+        return jnp.broadcast_to(row, (row_total, row.shape[1]))
+
+    ones = jnp.ones((row_total, LANES), jnp.bfloat16)
+    count = product(equal_ref[...] * spread(hop2_row.astype(jnp.float32).astype(jnp.bfloat16)), ones)
+    shape = (row_total, seed_total)
+    seed, row = iota(shape, 1), iota(shape, 0)
+    first = seed_total + seed * fanout
+    live = seed < size
+    last = first + jnp.where(live, spread(hop1_row), 0)
+    used = ((row >= first) & (row < last)) | ((row == seed) & live)
+    key = count * product(flags(used), ones[:seed_total])
+    rank = iota(key.shape, 1).astype(jnp.float32)
+    mine = key == rank
+    before = product(lower_ref[...], flags(mine))
+    above = product(jnp.ones((16, row_total), jnp.bfloat16), flags(key > rank))
+    enough = product(jnp.ones((16, row_total), jnp.bfloat16), flags(key >= rank))
+    place = jnp.sum(jnp.where(mine, before + spread(above[:1]), 0.0), axis=1, keepdims=True)
+    there = jnp.broadcast_to(place, (row_total, kept)) == iota((row_total, kept), 1).astype(jnp.float32)
+    number = iota((16, row_total), 1)
+    high = product((number >> 5).astype(jnp.float32).astype(jnp.bfloat16), flags(there))
+    low = product((number & 31).astype(jnp.float32).astype(jnp.bfloat16), flags(there))
+    held = product(
+        jnp.ones((16, row_total), jnp.bfloat16),
+        jnp.where(there, jnp.broadcast_to(key[:, :1], there.shape), 0.0).astype(jnp.bfloat16),
     )
-    enough = jnp.sum(
-        (count[:, None, :] >= jnp.arange(16)[None, :, None]).astype(jnp.int32), axis=2
-    )
-    return order, enough
-
-
-def table_kernel(*refs):
-    *feats_refs, table_ref = refs
+    order = (high * 32 + low) * 16 + held
+    return order[:1].astype(jnp.int32), jnp.maximum(held[:1], 1.0), enough[:1].astype(jnp.int32)
+
+
+def capacity_of(seed_total, row_total):
+    return round_up(seed_total + row_total // 2, 16)
+
+
+def table_kernel(steps, seed_total, fanout, turn_ref, size_ref, hop1_ref, hop2_ref, *refs):
+    *feats_refs, table_ref, order_ref, count_ref, enough_ref, lower_ref, equal_ref = refs
     step = pl.program_id(0)
     chunk = feats_refs[0].shape[1]
     width = sum(ref.shape[0] for ref in feats_refs)
@@ -49,38 +75,75 @@
     across = lax.broadcasted_iota(jnp.int32, (BLOCK, BLOCK), 1)
     identity = jnp.where(down == across, 1.0, 0.0).astype(jnp.bfloat16)
     filler = jnp.zeros((padded - width, BLOCK), jnp.bfloat16)
-    for part in range(0, chunk // BLOCK, 2):
-        pieces = []
-        for at in (part * BLOCK, (part + 1) * BLOCK):
-            pieces += [feats_ref[:, at : at + BLOCK] for feats_ref in feats_refs]
-            if padded > width:
-                pieces.append(filler)
-        both = jnp.concatenate(pieces, axis=0)
-        if part % 4:
-            turned = jnp.transpose(both)
-        else:
-            turned = lax.dot_general(
-                identity, both, (((1,), (1,)), ((), ())), preferred_element_type=jnp.float32
-            ).astype(jnp.bfloat16)
-        for side in range(2):
-            start = pl.multiple_of(step * chunk + (part + side) * BLOCK, BLOCK)
-            table_ref[pl.ds(start, BLOCK), :] = turned[:, side * padded : (side + 1) * padded]
-
-
-def build_table(node_feats):
+
+    def turn_features():
+        for part in range(0, chunk // BLOCK, 2):
+            pieces = []
+            for at in (part * BLOCK, (part + 1) * BLOCK):
+                pieces += [feats_ref[:, at : at + BLOCK] for feats_ref in feats_refs]
+                if padded > width:
+                    pieces.append(filler)
+            both = jnp.concatenate(pieces, axis=0)
+            if part % 4:
+                turned = jnp.transpose(both)
+            else:
+                turned = lax.dot_general(
+                    identity, both, (((1,), (1,)), ((), ())), preferred_element_type=jnp.float32
+                ).astype(jnp.bfloat16)
+            for side in range(2):
+                start = pl.multiple_of(step * chunk + (part + side) * BLOCK, BLOCK)
+                table_ref[pl.ds(start, BLOCK), :] = turned[:, side * padded : (side + 1) * padded]
+
+    @pl.when(step == 0)
+    def _():
+        shape = lower_ref.shape
+        below = lax.broadcasted_iota(jnp.int32, shape, 1) - lax.broadcasted_iota(jnp.int32, shape, 0)
+        lower_ref[...] = jnp.where(below < 0, 1.0, 0.0).astype(jnp.bfloat16)
+        equal_ref[...] = jnp.where(below == 0, 1.0, 0.0).astype(jnp.bfloat16)
+
+    @pl.when(lax.rem(step, steps) == 0)
+    def _():
+        size = size_ref[turn_ref[0] + lax.div(step, steps)]
+        order_ref[0], count_ref[0], enough_ref[0] = plan_rows(
+            seed_total, fanout, size, hop1_ref[0], hop2_ref[0], lower_ref, equal_ref
+        )
+        turn_features()
+
+    @pl.when(lax.rem(step, steps) != 0)
+    def _():
+        turn_features()
+
+
+def build_table(node_feats, turn, batch_sizes, hop1_count, hop2_count, fanout):
     width, nodes = node_feats.shape
+    groups, seed_total = hop1_count.shape
+    row_total = hop2_count.shape[1]
+    kept = round_up(capacity_of(seed_total, row_total), LANES)
     padded = max(width, LANES)
-    chunk = min(nodes, 8192)
+    steps = 2 if groups < 16 else 1
+    chunk = nodes // (groups * steps)
     streams = max(1, width // 32)
+    smem = pl.BlockSpec(memory_space=pltpu.SMEM)
+
+    def per_group(length):
+        return pl.BlockSpec((1, 1, length), lambda step: (lax.div(step, steps), 0, 0))
+
     return pl.pallas_call(
-        table_kernel,
-        grid=(nodes // chunk,),
-        in_specs=[pl.BlockSpec((width // streams, chunk), lambda step, at=at: (at, step)) for at in range(streams)],
-        out_specs=pl.BlockSpec(memory_space=pltpu.VMEM),
-        out_shape=pltpu.VMEM((nodes, padded), jnp.bfloat16),
-        compiler_params=pltpu.CompilerParams(vmem_limit_bytes=8 * 2**20),
+        functools.partial(table_kernel, steps, seed_total, fanout),
+        grid=(groups * steps,),
+        in_specs=[smem, smem, per_group(seed_total), per_group(row_total)]
+        + [pl.BlockSpec((width // streams, chunk), lambda step, at=at: (at, step)) for at in range(streams)],
+        out_specs=[pl.BlockSpec(memory_space=pltpu.VMEM), per_group(kept), per_group(kept), per_group(LANES)],
+        out_shape=[
+            pltpu.VMEM((nodes, padded), jnp.bfloat16),
+            pltpu.HBM((groups, 1, kept), jnp.int32),
+            pltpu.HBM((groups, 1, kept), jnp.float32),
+            pltpu.HBM((groups, 1, LANES), jnp.int32),
+        ],
+        scratch_shapes=[pltpu.VMEM((row_total, row_total), jnp.bfloat16)] * 2,
+        compiler_params=pltpu.CompilerParams(vmem_limit_bytes=12 * 2**20),
         name="build_table",
-    )(*[node_feats] * streams)
+    )(turn, batch_sizes, hop1_count[:, None, :], hop2_count[:, None, :], *[node_feats] * streams)
 
 
 def gather_kernel(
@@ -167,7 +230,7 @@
     fanout = near_ids.shape[2] // row_total
 
     def group_of(step, turn_ref):
-        return (turn_ref[begin + step], 0, 0)
+        return (turn_ref[2 + begin + step], 0, 0)
 
     def per_group(length):
         return pl.BlockSpec((1, 1, length), group_of, memory_space=pltpu.SMEM)
@@ -178,7 +241,7 @@
             num_scalar_prefetch=1,
             grid=(groups,),
             in_specs=[
-                per_group(16),
+                per_group(LANES),
                 per_group(kept),
                 per_group(row_total),
                 per_group(row_total * fanout),
@@ -212,7 +275,7 @@
     capacity = inputs_refs[0].shape[0]
     hidden_width = weights_ref.shape[2]
     classes = layer_ref.shape[1]
-    size = size_ref[0]
+    size = size_ref[turn_ref[1]]
     seed = lax.broadcasted_iota(jnp.int32, (seed_total, capacity), 0)
     row = jnp.broadcast_to(row_ref[...], (seed_total, capacity))
     first = seed_total + seed * fanout
@@ -220,7 +283,7 @@
     is_near = jnp.where((row >= first) & (row < first + fanout), 1.0, 0.0).astype(jnp.bfloat16)
     preact = jnp.zeros((capacity, hidden_width), jnp.float32)
     for place, inputs_ref in enumerate(inputs_refs):
-        source = turn_ref[len(inputs_refs) + place]
+        source = turn_ref[2 + len(inputs_refs) + place]
         preact = preact + jnp.dot(inputs_ref[...], weights_ref[source], preferred_element_type=jnp.float32)
     hidden = jnp.maximum(preact, 0.0).astype(jnp.bfloat16)
     counts = seed_ref[0][:, :1].astype(jnp.float32)
@@ -253,7 +316,7 @@
     lower_ref[capacity - split + 2 * seed_total :, :classes] = dlogits
 
 
-def upper_layers(inputs, size, turn, weights, layer, row, seeds, fanout):
+def upper_layers(inputs, sizes, turn, weights, layer, row, seeds, fanout):
     seed_total = seeds.shape[1]
     capacity = inputs[0].shape[0]
     hidden_width = weights.shape[2]
@@ -268,7 +331,7 @@
         out_shape=[jax.ShapeDtypeStruct((length, hidden_width), jnp.bfloat16) for length in (split, total - split)],
         compiler_params=pltpu.CompilerParams(vmem_limit_bytes=32 * 2**20),
         name="upper_layers",
-    )(size, turn, weights, layer, row, seeds, *inputs)
+    )(sizes, turn, weights, layer, row, seeds, *inputs)
 
 
 def grad_kernel(seed_total, classes, source_ref, *rest):
@@ -288,7 +351,7 @@
         first = first + lax.dot_general(
             inputs_ref[split:], lower_ref[: capacity - split], rows, preferred_element_type=jnp.float32
         )
-        start = pl.multiple_of(source_ref[place] * seed_total, seed_total)
+        start = pl.multiple_of(source_ref[2 + place] * seed_total, seed_total)
         for part in range(3):
             begin = capacity - split + part * seed_total
             units_ref[part, pl.ds(start, seed_total), :] = lower_ref[begin : begin + seed_total]
@@ -328,6 +391,7 @@
     hidden_width = mine.shape[1]
     first, second = pl.pallas_call(
         final_kernel,
+        in_specs=[pl.BlockSpec(memory_space=pltpu.VMEM)] * 2,
         out_shape=[
             jax.ShapeDtypeStruct((2, width, hidden_width), jnp.float32),
             jax.ShapeDtypeStruct((classes, 2, hidden_width), jnp.float32),
@@ -394,12 +458,9 @@
     slice_width = node_feats.shape[0]
     hidden_width = first_layer.shape[2]
     classes = second_layer.shape[2]
-    capacity = round_up(seed_total + row_total // 2, 16)
-    kept = round_up(capacity, LANES)
+    capacity = capacity_of(seed_total, row_total)
     column_rank = lax.axis_index("feat")
     group_start = lax.axis_index("dp") * groups
-    sizes = lax.dynamic_slice_in_dim(batch_sizes, group_start, groups)
-    order, enough = plan_rows(hop1_count, hop2_count, sizes, kept)
     count = lax.axis_size("feat")
     ring = ring_of(count)
     places = sorted(range(count), key=lambda t: -min(t, count - t))
@@ -407,16 +468,12 @@
         [ring[(ring.index(i) + sign * t) % count] for sign in (1, -1) for t in places] for i in range(count)
     ]
     turn = lax.dynamic_index_in_dim(jnp.array(turns, jnp.int32), column_rank, 0, keepdims=False)
+    turn = jnp.concatenate([jnp.stack([group_start, group_start + column_rank]), turn])
     weights = lax.all_gather(first_layer.reshape(2 * slice_width, hidden_width), "feat", axis=0)
-    lists = [
-        enough[:, None, :],
-        order[:, None, :],
-        jnp.maximum(order % 16, 1).astype(jnp.float32)[:, None, :],
-        jnp.concatenate([seed_ids, hop1_ids], axis=1)[:, None, :],
-        hop2_ids[:, None, :],
-    ]
+    lists = [jnp.concatenate([seed_ids, hop1_ids], axis=1)[:, None, :], hop2_ids[:, None, :]]
     node_feats, turn, *lists = lax.optimization_barrier((node_feats, turn, *lists))
-    table = build_table(node_feats)
+    table, order, counts, enough = build_table(node_feats, turn, batch_sizes, hop1_count, hop2_count, fanout)
+    lists = [enough, order, counts, *lists]
     inputs, received, arrived = [], [], []
     for call in range(CALLS):
         begin, end = -(-call * count // CALLS), -(-(call + 1) * count // CALLS)
@@ -424,8 +481,8 @@
         if call < CALLS - 1:
             table, blocks, arrived = lax.optimization_barrier((table, blocks, arrived))
         else:
-            blocks, arrived, order, hop1_count, label_ids, sizes, second_layer = lax.optimization_barrier(
-                (blocks, arrived, order, hop1_count, label_ids, sizes, second_layer)
+            blocks, arrived, order, hop1_count, label_ids, second_layer, weights = lax.optimization_barrier(
+                (blocks, arrived, order, hop1_count, label_ids, second_layer, weights)
             )
         inputs += blocks
         received += arrived
@@ -435,13 +492,12 @@
     def own(array):
         return lax.dynamic_index_in_dim(array, column_rank, 0, keepdims=False)
 
-    own_order = own(order)[None, :capacity]
+    own_order = own(order)[:, :capacity]
     row = jnp.where(own_order % 16 > 0, own_order // 16, -1)
     seeds = jnp.stack([own(hop1_count), own(label_ids)])
     seeds = jnp.broadcast_to(seeds[:, :, None], (2, seed_total, LANES))
-    size = lax.dynamic_slice_in_dim(sizes, column_rank, 1)
     layer = jnp.transpose(second_layer, (0, 2, 1))
-    halves = upper_layers(received, size, turn, weights, layer, row, seeds, fanout)
+    halves = upper_layers(received, batch_sizes, turn, weights, layer, row, seeds, fanout)
     upper, lower = ring_gather(*halves, ring)
     grads = grad_layer(
         inputs, [upper[t] for t in places], [lower[t] for t in places], turn, seed_total, classes

time: 161 us -> 172 us (1.068)
  Pallas kernels: 70.6 us -> 83.3 us
  other arithmetic: 7.49 us -> 1.01 us
  local copies, waits for them, and re-layouts: 6.33 us -> 9.49 us
    pallas_call x2, Pallas kernels: 21.2 us -> 35.9 us  [the longest x1 33.9 us: build_table(): pl.pallas_call(functools.partial(table_kernel, steps, seed_total, fanout)...]
    reduce_sum x3 -> x0, other arithmetic: 4.82 us -> none  [the longest x1 2.46 us: plan_rows(): jnp.sum((mixed[:, None, :] > mixed[:, :, None]).astype(jnp.int32), axis=2)]
    unnamed x8 -> x22, local copies, waits for them, and re-layouts: 1.95 us -> 5.43 us
    ppermute x21, starting transfers between devices: 29.8 us -> 32.5 us  [send_along(): lax.ppermute(array, 'feat', [(ring[i], ring[(i + shift) % count]) for i i...]
    ppermute x1, starting transfers between devices: 3.99 us -> 1.24 us  [group_sum(): other = lax.ppermute(mine, 'dp', [(i, i ^ stride) for i in range(count)])]
  transfers between devices with their start and end apart: 24 -> 24, of which waited for: 14 -> 13; matrix products, arithmetic and copies ran while one was open for 7% -> 3% of each run, Pallas kernels for 40% -> 45%
where the time goes in v7:
time: 172 us; the launch traced here: 171 us
  Pallas kernels  83.3 us (48%)
  starting transfers between devices  33.9 us (20%)
  waiting for transfers between devices  29.3 us (17%)
  between operations  14.2 us (8%)
  local copies, waits for them, and re-layouts  9.49 us (6%)
    pallas_call x3, Pallas kernels, gather_layer(): pl.pallas_call(functools.partial(gather_kernel, fanout, capacity), grid_s...  43.2 us
    pallas_call x1, Pallas kernels, build_table(): pl.pallas_call(functools.partial(table_kernel, steps, seed_total, fanout)...  33.9 us
    ppermute x21, starting transfers between devices, send_along(): lax.ppermute(array, 'feat', [(ring[i], ring[(i + shift) % count]) for i i...  32.5 us
    ppermute x21, waiting for transfers between devices, send_along(): lax.ppermute(array, 'feat', [(ring[i], ring[(i + shift) % count]) for i i...  18.3 us
    ppermute x1, waiting for transfers between devices, group_sum(): other = lax.ppermute(mine, 'dp', [(i, i ^ stride) for i in range(count)])  8.23 us
    unnamed x22, local copies, waits for them, and re-layouts  5.43 us
  transfers between devices with their start and end apart: 24, of which 13 were waited for; matrix products, arithmetic and copies ran while one was open for 3% of the time, Pallas kernels for 45%

profile of v7, /device:TPU:0, one launch (start us, length us, event | category | flops | bytes accessed | tf_op | source)
XLA Modules:
  0.0 171.2 jit_solution(1942858954171993233)
XLA Ops:
  7.9 1.1 broadcast_in_dim.21.near_ref
  12.7 33.9 %build_table.1 = (bf16[131072,128]{1,0:T(8,128)(2,1)S(1)}, s32[8,1,512]{2,1,0:T(1,128)}, f32[8,1,512]{2,1,0:T(1,128)}, s32[8,1,128]{2,1,0:T(1,128)}) custom-call(s32[18]{0:T(128)S(1)} %pad_add_fusion.2.turn_ref.source_ref, s32[32]{0:T(128)S(1)} %copy-done.6, s32[8,1,64]{2,1,0:T(1,128)S(1)} %bitcast.13, s32[8,1,704]{2,1,0:T(1,128)S(1)} %broadcast_in_dim.23.hop2_ref, ...), custom_call_target="tpu_custom_call" | custom-call | tf_op jit(solution)/shard_map/build_table/pallas_call | solution.py:131
  48.7 14.4 %gather_layer.3 = (bf16[416,256]{1,0:T(8,128)(2,1)S(1)}, bf16[416,256]{1,0:T(8,128)(2,1)S(1)}, bf16[416,256]{1,0:T(8,128)(2,1)S(1)}, bf16[131072,128]{1,0:T(8,128)(2,1)S(1)}) custom-call(s32[18]{0:T(128)S(1)} %pad_add_fusion.2.turn_ref.source_ref, s32[8,1,128]{2,1,0:T(1,128)S(1)} %copy-done.3, ...), custom_call_target="tpu_custom_call", output_to_operand_aliasing={{3}: (6, {})} | custom-call | bytes 51118080 | tf_op jit(solution)/shard_map/gather_layer/pallas_call | solution.py:238
  63.2 7.2 %collective-permute-start = (bf16[416,256]{1,0:T(8,128)(2,1)S(1)}, bf16[416,256]{1,0:T(8,128)(2,1)S(1)}, u32[]{:S(2)}, u32[]{:S(2)}) collective-permute-start(bf16[416,256]{1,0:T(8,128)(2,1)S(1)} %get-tuple-element.57.rest_0_), channel_id=1, source_target_pairs={{0,28},{8,20},{16,12},{24,4},{28,0},{20,8},{12,16},{4,24},{1,29},{... | collective-permute-start | bytes 638984 | tf_op jit(solution)/shard_map/ppermute | solution.py:412
  70.4 1.1 collective-permute-start.1
  71.5 2.7 %collective-permute-start.2 = (bf16[416,256]{1,0:T(8,128)(2,1)S(1)}, bf16[416,256]{1,0:T(8,128)(2,1)S(1)}, u32[]{:S(2)}, u32[]{:S(2)}) collective-permute-start(bf16[416,256]{1,0:T(8,128)(2,1)S(1)} %get-tuple-element.59.rest_2_), channel_id=1, source_target_pairs={{0,20},{8,12},{16,4},{24,0},{28,8},{20,16},{12,24},{4,28},{1,21},{... | collective-permute-start | bytes 638984 | tf_op jit(solution)/shard_map/ppermute | solution.py:412
  74.2 17.3 %gather_layer.4 = (bf16[416,256]{1,0:T(8,128)(2,1)S(1)}, bf16[416,256]{1,0:T(8,128)(2,1)S(1)}, bf16[416,256]{1,0:T(8,128)(2,1)S(1)}, bf16[131072,128]{1,0:T(8,128)(2,1)S(1)}) custom-call(s32[18]{0:T(128)S(1)} %pad_add_fusion.2.turn_ref.source_ref, s32[8,1,128]{2,1,0:T(1,128)S(1)} %copy-done.3, ...), custom_call_target="tpu_custom_call", output_to_operand_aliasing={{3}: (6, {})} | custom-call | bytes 51118080 | tf_op jit(solution)/shard_map/gather_layer/pallas_call | solution.py:238
  91.5 2.1 %collective-permute-done.1.rest_1_ = bf16[416,256]{1,0:T(8,128)(2,1)S(1)} collective-permute-done((bf16[416,256]{1,0:T(8,128)(2,1)S(1)}, bf16[416,256]{1,0:T(8,128)(2,1)S(1)}, u32[]{:S(2)}, u32[]{:S(2)}) %collective-permute-start.1) | collective-permute-done | bytes 213024 | tf_op jit(solution)/shard_map/ppermute | solution.py:412
  93.6 2.9 %collective-permute-start.4 = (bf16[416,256]{1,0:T(8,128)(2,1)S(1)}, bf16[416,256]{1,0:T(8,128)(2,1)S(1)}, u32[]{:S(2)}, u32[]{:S(2)}) collective-permute-start(bf16[416,256]{1,0:T(8,128)(2,1)S(1)} %get-tuple-element.66.rest_4_), channel_id=1, source_target_pairs={{0,12},{8,4},{16,0},{24,8},{28,16},{20,24},{12,28},{4,20},{1,13},{... | collective-permute-start | bytes 638984 | tf_op jit(solution)/shard_map/ppermute | solution.py:412
  97.0 11.5 %gather_layer.5 = (bf16[416,256]{1,0:T(8,128)(2,1)S(1)}, bf16[416,256]{1,0:T(8,128)(2,1)S(1)}, bf16[131072,128]{1,0:T(8,128)(2,1)S(1)}) custom-call(s32[18]{0:T(128)S(1)} %pad_add_fusion.2.turn_ref.source_ref, s32[8,1,128]{2,1,0:T(1,128)S(1)} %copy-done.4, s32[8,1,512]{2,1,0:T(1,128)S(1)} %copy-done.1, ...), custom_call_target="tpu_custom_call", output_to_operand_aliasing={{2}: (6, {})} | custom-call | bytes 34078720 | tf_op jit(solution)/shard_map/gather_layer/pallas_call | solution.py:238
  108.6 3.2 %collective-permute-start.6 = (bf16[416,256]{1,0:T(8,128)(2,1)S(1)}, bf16[416,256]{1,0:T(8,128)(2,1)S(1)}, u32[]{:S(2)}, u32[]{:S(2)}) collective-permute-start(bf16[416,256]{1,0:T(8,128)(2,1)S(1)} %get-tuple-element.71.rest_6_), channel_id=1, source_target_pairs={{0,4},{8,0},{16,8},{24,16},{28,24},{20,28},{12,20},{4,12},{1,5},{9... | collective-permute-start | bytes 638984 | tf_op jit(solution)/shard_map/ppermute | solution.py:412
  113.3 2.2 %collective-permute-done.6.rest_6_ = bf16[416,256]{1,0:T(8,128)(2,1)S(1)} collective-permute-done((bf16[416,256]{1,0:T(8,128)(2,1)S(1)}, bf16[416,256]{1,0:T(8,128)(2,1)S(1)}, u32[]{:S(2)}, u32[]{:S(2)}) %collective-permute-start.6) | collective-permute-done | bytes 213024 | tf_op jit(solution)/shard_map/ppermute | solution.py:412
  115.5 1.2 copy-done
  116.7 2.4 %upper_layers.1 = (bf16[304,256]{1,0:T(8,128)(2,1)S(1)}, bf16[304,256]{1,0:T(8,128)(2,1)S(1)}) custom-call(s32[32]{0:T(128)S(1)} %copy-done.7, s32[18]{0:T(128)S(1)} %pad_add_fusion.2.turn_ref.source_ref, bf16[8,256,256]{2,1,0:T(8,128)(2,1)S(1)} %copy-done, bf16[2,172,256]{2,1,0:T(8,128)(2,1)S(1)} %bitcast.12, s32[1,416]{1,0:T(1,128)S(1)} %compare_select_fusion.row_ref, ...), custom_call_target="tpu_custom_call" | custom-call | tf_op jit(solution)/shard_map/upper_layers/pallas_call | solution.py:327
  119.2 1.9 %collective-permute-start.7 = (bf16[304,256]{1,0:T(8,128)(2,1)S(1)}, bf16[304,256]{1,0:T(8,128)(2,1)S(1)}, u32[]{:S(2)}, u32[]{:S(2)}) collective-permute-start(bf16[304,256]{1,0:T(8,128)(2,1)S(1)} %get-tuple-element.84.rest_15_), channel_id=1, source_target_pairs={{0,8},{8,16},{16,24},{24,28},{28,20},{20,12},{12,4},{4,0},{1,9},{9... | collective-permute-start | bytes 466952 | tf_op jit(solution)/shard_map/ppermute | solution.py:412
  121.8 2.0 %collective-permute-start.11 = (bf16[304,256]{1,0:T(8,128)(2,1)S(1)}, bf16[304,256]{1,0:T(8,128)(2,1)S(1)}, u32[]{:S(2)}, u32[]{:S(2)}) collective-permute-start(bf16[304,256]{1,0:T(8,128)(2,1)S(1)} %get-tuple-element.84.rest_15_), channel_id=1, source_target_pairs={{0,4},{8,0},{16,8},{24,16},{28,24},{20,28},{12,20},{4,12},{1,5},{9... | collective-permute-start | bytes 466952 | tf_op jit(solution)/shard_map/ppermute | solution.py:412
  123.8 2.5 %collective-permute-done.7.rest_14_ = bf16[304,256]{1,0:T(8,128)(2,1)S(1)} collective-permute-done((bf16[304,256]{1,0:T(8,128)(2,1)S(1)}, bf16[304,256]{1,0:T(8,128)(2,1)S(1)}, u32[]{:S(2)}, u32[]{:S(2)}) %collective-permute-start.7) | collective-permute-done | bytes 155680 | tf_op jit(solution)/shard_map/ppermute | solution.py:412
  126.3 1.7 collective-permute-start.8
  128.6 2.5 %collective-permute-done.11.rest_13_ = bf16[304,256]{1,0:T(8,128)(2,1)S(1)} collective-permute-done((bf16[304,256]{1,0:T(8,128)(2,1)S(1)}, bf16[304,256]{1,0:T(8,128)(2,1)S(1)}, u32[]{:S(2)}, u32[]{:S(2)}) %collective-permute-start.11) | collective-permute-done | bytes 155680 | tf_op jit(solution)/shard_map/ppermute | solution.py:412
  131.4 1.7 %collective-permute-start.19 = (bf16[304,256]{1,0:T(8,128)(2,1)S(1)}, bf16[304,256]{1,0:T(8,128)(2,1)S(1)}, u32[]{:S(2)}, u32[]{:S(2)}) collective-permute-start(bf16[304,256]{1,0:T(8,128)(2,1)S(1)} %collective-permute-done.18.rest_22_), channel_id=1, source_target_pairs={{0,8},{8,16},{16,24},{24,28},{28,20},{20,12},{12,4},{4,0},{1,9},{9... | collective-permute-start | bytes 466952 | tf_op jit(solution)/shard_map/ppermute | solution.py:412
  133.8 1.1 collective-permute-start.9
  135.0 0.9 collective-permute-start.16
  135.9 2.5 %collective-permute-done.12.rest_11_ = bf16[304,256]{1,0:T(8,128)(2,1)S(1)} collective-permute-done((bf16[304,256]{1,0:T(8,128)(2,1)S(1)}, bf16[304,256]{1,0:T(8,128)(2,1)S(1)}, u32[]{:S(2)}, u32[]{:S(2)}) %collective-permute-start.12) | collective-permute-done | bytes 155680 | tf_op jit(solution)/shard_map/ppermute | solution.py:412
  138.4 2.0 %collective-permute-start.20 = (bf16[304,256]{1,0:T(8,128)(2,1)S(1)}, bf16[304,256]{1,0:T(8,128)(2,1)S(1)}, u32[]{:S(2)}, u32[]{:S(2)}) collective-permute-start(bf16[304,256]{1,0:T(8,128)(2,1)S(1)} %collective-permute-done.19.rest_20_), channel_id=1, source_target_pairs={{0,8},{8,16},{16,24},{24,28},{28,20},{20,12},{12,4},{4,0},{1,9},{9... | collective-permute-start | bytes 466952 | tf_op jit(solution)/shard_map/ppermute | solution.py:412
  141.2 1.7 %collective-permute-start.10 = (bf16[304,256]{1,0:T(8,128)(2,1)S(1)}, bf16[304,256]{1,0:T(8,128)(2,1)S(1)}, u32[]{:S(2)}, u32[]{:S(2)}) collective-permute-start(bf16[304,256]{1,0:T(8,128)(2,1)S(1)} %collective-permute-done.9.rest_10_), channel_id=1, source_target_pairs={{0,8},{8,16},{16,24},{24,28},{28,20},{20,12},{12,4},{4,0},{1,9},{9... | collective-permute-start | bytes 466952 | tf_op jit(solution)/shard_map/ppermute | solution.py:412
  143.9 2.5 %collective-permute-done.10.rest_8_ = bf16[304,256]{1,0:T(8,128)(2,1)S(1)} collective-permute-done((bf16[304,256]{1,0:T(8,128)(2,1)S(1)}, bf16[304,256]{1,0:T(8,128)(2,1)S(1)}, u32[]{:S(2)}, u32[]{:S(2)}) %collective-permute-start.10) | collective-permute-done | bytes 155680 | tf_op jit(solution)/shard_map/ppermute | solution.py:412
  146.4 1.7 %collective-permute-done.17.rest_16_ = bf16[304,256]{1,0:T(8,128)(2,1)S(1)} collective-permute-done((bf16[304,256]{1,0:T(8,128)(2,1)S(1)}, bf16[304,256]{1,0:T(8,128)(2,1)S(1)}, u32[]{:S(2)}, u32[]{:S(2)}) %collective-permute-start.17) | collective-permute-done | bytes 155680 | tf_op jit(solution)/shard_map/ppermute | solution.py:412
  148.2 1.8 %grad_layer.1 = f32[608,256]{1,0:T(8,128)S(1)} custom-call(s32[18]{0:T(128)S(1)} %pad_add_fusion.2.turn_ref.source_ref, bf16[416,256]{1,0:T(8,128)(2,1)S(1)} %get-tuple-element.57.rest_0_, bf16[416,256]{1,0:T(8,128)(2,1)S(1)} %get-tuple-element.58.rest_1_, bf16[416,256]{1,0:T(8,128)(2,1)S(1)} %get-tuple-element.59.rest_2_, ...), custom_call_target="tpu_custom_call" | custom-call | tf_op jit(solution)/shard_map/grad_layer/pallas_call | solution.py:369
  150.0 2.0 %collective-permute-done.21 = f32[608,256]{1,0:T(8,128)S(1)} collective-permute-done((f32[608,256]{1,0:T(8,128)S(1)}, f32[608,256]{1,0:T(8,128)S(1)}, u32[]{:S(2)}, u32[]{:S(2)}) %collective-permute-start.21) | collective-permute-done | bytes 622624 | tf_op jit(solution)/shard_map/ppermute | solution.py:433
  152.2 1.2 collective-permute-start.22
  153.4 8.2 %collective-permute-done.22.other_ref = bf16[608,256]{1,0:T(8,128)(2,1)S(1)} collective-permute-done((bf16[608,256]{1,0:T(8,128)(2,1)S(1)}, bf16[608,256]{1,0:T(8,128)(2,1)S(1)}, u32[]{:S(2)}, u32[]{:S(2)}) %collective-permute-start.22) | collective-permute-done | bytes 311328 | tf_op jit(solution)/shard_map/ppermute | solution.py:437
  162.4 2.0 %final_sum.1 = (f32[2,128,256]{2,1,0:T(8,128)}, f32[172,2,256]{2,1,0:T(2,128)}) custom-call(bf16[608,256]{1,0:T(8,128)(2,1)} %copy-done.8, bf16[608,256]{1,0:T(8,128)(2,1)} %copy-done.9), custom_call_target="tpu_custom_call" | custom-call | tf_op jit(solution)/shard_map/final_sum/pallas_call | solution.py:392
  (59 shorter events, 13.7 us)
Async XLA Ops:
  7.2 101.4 %all-gather.2.cloned.1.call-start = ((), (), s32[]{:S(2)}) async-start(), calls=%async_computation | async-start | bytes 1179648 | tf_op jit(solution)/shard_map/all_gather | solution.py:472
  46.6 0.7 copy-start.1
  47.3 0.7 copy-start.2
  48.7 48.3 %copy-start.4 = (s32[8,1,128]{2,1,0:T(1,128)S(1)}, s32[8,1,128]{2,1,0:T(1,128)}, u32[]{:S(2)}) copy-start(s32[8,1,128]{2,1,0:T(1,128)} %get-tuple-element.47.enough_ref) | copy-start | bytes 12292
  63.2 48.6 %copy-start.10 = (bf16[2,256,172]{1,0,2:T(2,128)(2,1)S(1)}, bf16[2,256,172]{1,0,2:T(2,128)(2,1)}, u32[]{:S(2)}) copy-start(bf16[2,256,172]{1,0,2:T(2,128)(2,1)} %param.13) | copy-start | bytes 528388
  63.2 52.3 %copy-start.7 = (s32[32]{0:T(128)S(1)}, s32[32]{0:T(128)}, u32[]{:S(2)}) copy-start(s32[32]{0:T(128)} %size_ref.3) | copy-start | bytes 388
  63.2 28.3 %collective-permute-start = (bf16[416,256]{1,0:T(8,128)(2,1)S(1)}, bf16[416,256]{1,0:T(8,128)(2,1)S(1)}, u32[]{:S(2)}, u32[]{:S(2)}) collective-permute-start(bf16[416,256]{1,0:T(8,128)(2,1)S(1)} %get-tuple-element.57.rest_0_), channel_id=1, source_target_pairs={{0,28},{8,20},{16,12},{24,4},{28,0},{20,8},{12,16},{4,24},{1,29},{... | collective-permute-start | bytes 638984 | tf_op jit(solution)/shard_map/ppermute | solution.py:412
  70.4 23.2 %collective-permute-start.1 = (bf16[416,256]{1,0:T(8,128)(2,1)S(1)}, bf16[416,256]{1,0:T(8,128)(2,1)S(1)}, u32[]{:S(2)}, u32[]{:S(2)}) collective-permute-start(bf16[416,256]{1,0:T(8,128)(2,1)S(1)} %get-tuple-element.58.rest_1_), channel_id=1, source_target_pairs={{0,24},{8,28},{16,20},{24,12},{28,4},{20,0},{12,8},{4,16},{1,25},{... | collective-permute-start | bytes 638984 | tf_op jit(solution)/shard_map/ppermute | solution.py:412
  71.5 22.1 %collective-permute-start.2 = (bf16[416,256]{1,0:T(8,128)(2,1)S(1)}, bf16[416,256]{1,0:T(8,128)(2,1)S(1)}, u32[]{:S(2)}, u32[]{:S(2)}) collective-permute-start(bf16[416,256]{1,0:T(8,128)(2,1)S(1)} %get-tuple-element.59.rest_2_), channel_id=1, source_target_pairs={{0,20},{8,12},{16,4},{24,0},{28,8},{20,16},{12,24},{4,28},{1,21},{... | collective-permute-start | bytes 638984 | tf_op jit(solution)/shard_map/ppermute | solution.py:412
  93.6 14.9 %collective-permute-start.3 = (bf16[416,256]{1,0:T(8,128)(2,1)S(1)}, bf16[416,256]{1,0:T(8,128)(2,1)S(1)}, u32[]{:S(2)}, u32[]{:S(2)}) collective-permute-start(bf16[416,256]{1,0:T(8,128)(2,1)S(1)} %get-tuple-element.65.rest_3_), channel_id=1, source_target_pairs={{0,16},{8,24},{16,28},{24,20},{28,12},{20,4},{12,0},{4,8},{1,17},{... | collective-permute-start | bytes 638984 | tf_op jit(solution)/shard_map/ppermute | solution.py:412
  93.6 14.9 %collective-permute-start.4 = (bf16[416,256]{1,0:T(8,128)(2,1)S(1)}, bf16[416,256]{1,0:T(8,128)(2,1)S(1)}, u32[]{:S(2)}, u32[]{:S(2)}) collective-permute-start(bf16[416,256]{1,0:T(8,128)(2,1)S(1)} %get-tuple-element.66.rest_4_), channel_id=1, source_target_pairs={{0,12},{8,4},{16,0},{24,8},{28,16},{20,24},{12,28},{4,20},{1,13},{... | collective-permute-start | bytes 638984 | tf_op jit(solution)/shard_map/ppermute | solution.py:412
  96.6 12.0 %collective-permute-start.5 = (bf16[416,256]{1,0:T(8,128)(2,1)S(1)}, bf16[416,256]{1,0:T(8,128)(2,1)S(1)}, u32[]{:S(2)}, u32[]{:S(2)}) collective-permute-start(bf16[416,256]{1,0:T(8,128)(2,1)S(1)} %get-tuple-element.67.rest_5_), channel_id=1, source_target_pairs={{0,8},{8,16},{16,24},{24,28},{28,20},{20,12},{12,4},{4,0},{1,9},{9... | collective-permute-start | bytes 638984 | tf_op jit(solution)/shard_map/ppermute | solution.py:412
  108.6 6.8 %collective-permute-start.6 = (bf16[416,256]{1,0:T(8,128)(2,1)S(1)}, bf16[416,256]{1,0:T(8,128)(2,1)S(1)}, u32[]{:S(2)}, u32[]{:S(2)}) collective-permute-start(bf16[416,256]{1,0:T(8,128)(2,1)S(1)} %get-tuple-element.71.rest_6_), channel_id=1, source_target_pairs={{0,4},{8,0},{16,8},{24,16},{28,24},{20,28},{12,20},{4,12},{1,5},{9... | collective-permute-start | bytes 638984 | tf_op jit(solution)/shard_map/ppermute | solution.py:412
  115.5 1.2 copy-start
  119.2 7.2 %collective-permute-start.7 = (bf16[304,256]{1,0:T(8,128)(2,1)S(1)}, bf16[304,256]{1,0:T(8,128)(2,1)S(1)}, u32[]{:S(2)}, u32[]{:S(2)}) collective-permute-start(bf16[304,256]{1,0:T(8,128)(2,1)S(1)} %get-tuple-element.84.rest_15_), channel_id=1, source_target_pairs={{0,8},{8,16},{16,24},{24,28},{28,20},{20,12},{12,4},{4,0},{1,9},{9... | collective-permute-start | bytes 466952 | tf_op jit(solution)/shard_map/ppermute | solution.py:412
  121.1 7.0 %collective-permute-start.14 = (bf16[304,256]{1,0:T(8,128)(2,1)S(1)}, bf16[304,256]{1,0:T(8,128)(2,1)S(1)}, u32[]{:S(2)}, u32[]{:S(2)}) collective-permute-start(bf16[304,256]{1,0:T(8,128)(2,1)S(1)} %get-tuple-element.85.rest_23_), channel_id=1, source_target_pairs={{0,4},{8,0},{16,8},{24,16},{28,24},{20,28},{12,20},{4,12},{1,5},{9... | collective-permute-start | bytes 466952 | tf_op jit(solution)/shard_map/ppermute | solution.py:412
  121.8 9.3 %collective-permute-start.11 = (bf16[304,256]{1,0:T(8,128)(2,1)S(1)}, bf16[304,256]{1,0:T(8,128)(2,1)S(1)}, u32[]{:S(2)}, u32[]{:S(2)}) collective-permute-start(bf16[304,256]{1,0:T(8,128)(2,1)S(1)} %get-tuple-element.84.rest_15_), channel_id=1, source_target_pairs={{0,4},{8,0},{16,8},{24,16},{28,24},{20,28},{12,20},{4,12},{1,5},{9... | collective-permute-start | bytes 466952 | tf_op jit(solution)/shard_map/ppermute | solution.py:412
  123.8 7.7 %collective-permute-start.18 = (bf16[304,256]{1,0:T(8,128)(2,1)S(1)}, bf16[304,256]{1,0:T(8,128)(2,1)S(1)}, u32[]{:S(2)}, u32[]{:S(2)}) collective-permute-start(bf16[304,256]{1,0:T(8,128)(2,1)S(1)} %get-tuple-element.85.rest_23_), channel_id=1, source_target_pairs={{0,8},{8,16},{16,24},{24,28},{28,20},{20,12},{12,4},{4,0},{1,9},{9... | collective-permute-start | bytes 466952 | tf_op jit(solution)/shard_map/ppermute | solution.py:412
  126.3 7.5 %collective-permute-start.8 = (bf16[304,256]{1,0:T(8,128)(2,1)S(1)}, bf16[304,256]{1,0:T(8,128)(2,1)S(1)}, u32[]{:S(2)}, u32[]{:S(2)}) collective-permute-start(bf16[304,256]{1,0:T(8,128)(2,1)S(1)} %collective-permute-done.7.rest_14_), channel_id=1, source_target_pairs={{0,8},{8,16},{16,24},{24,28},{28,20},{20,12},{12,4},{4,0},{1,9},{9... | collective-permute-start | bytes 466952 | tf_op jit(solution)/shard_map/ppermute | solution.py:412
  128.0 7.0 %collective-permute-start.15 = (bf16[304,256]{1,0:T(8,128)(2,1)S(1)}, bf16[304,256]{1,0:T(8,128)(2,1)S(1)}, u32[]{:S(2)}, u32[]{:S(2)}) collective-permute-start(bf16[304,256]{1,0:T(8,128)(2,1)S(1)} %collective-permute-done.14.rest_21_), channel_id=1, source_target_pairs={{0,4},{8,0},{16,8},{24,16},{28,24},{20,28},{12,20},{4,12},{1,5},{9... | collective-permute-start | bytes 466952 | tf_op jit(solution)/shard_map/ppermute | solution.py:412
  131.1 7.2 %collective-permute-start.12 = (bf16[304,256]{1,0:T(8,128)(2,1)S(1)}, bf16[304,256]{1,0:T(8,128)(2,1)S(1)}, u32[]{:S(2)}, u32[]{:S(2)}) collective-permute-start(bf16[304,256]{1,0:T(8,128)(2,1)S(1)} %collective-permute-done.11.rest_13_), channel_id=1, source_target_pairs={{0,4},{8,0},{16,8},{24,16},{28,24},{20,28},{12,20},{4,12},{1,5},{9... | collective-permute-start | bytes 466952 | tf_op jit(solution)/shard_map/ppermute | solution.py:412
  131.4 6.9 %collective-permute-start.19 = (bf16[304,256]{1,0:T(8,128)(2,1)S(1)}, bf16[304,256]{1,0:T(8,128)(2,1)S(1)}, u32[]{:S(2)}, u32[]{:S(2)}) collective-permute-start(bf16[304,256]{1,0:T(8,128)(2,1)S(1)} %collective-permute-done.18.rest_22_), channel_id=1, source_target_pairs={{0,8},{8,16},{16,24},{24,28},{28,20},{20,12},{12,4},{4,0},{1,9},{9... | collective-permute-start | bytes 466952 | tf_op jit(solution)/shard_map/ppermute | solution.py:412
  133.8 7.3 %collective-permute-start.9 = (bf16[304,256]{1,0:T(8,128)(2,1)S(1)}, bf16[304,256]{1,0:T(8,128)(2,1)S(1)}, u32[]{:S(2)}, u32[]{:S(2)}) collective-permute-start(bf16[304,256]{1,0:T(8,128)(2,1)S(1)} %collective-permute-done.8.rest_12_), channel_id=1, source_target_pairs={{0,8},{8,16},{16,24},{24,28},{28,20},{20,12},{12,4},{4,0},{1,9},{9... | collective-permute-start | bytes 466952 | tf_op jit(solution)/shard_map/ppermute | solution.py:412
  135.0 7.9 %collective-permute-start.16 = (bf16[304,256]{1,0:T(8,128)(2,1)S(1)}, bf16[304,256]{1,0:T(8,128)(2,1)S(1)}, u32[]{:S(2)}, u32[]{:S(2)}) collective-permute-start(bf16[304,256]{1,0:T(8,128)(2,1)S(1)} %collective-permute-done.15.rest_19_), channel_id=1, source_target_pairs={{0,4},{8,0},{16,8},{24,16},{28,24},{20,28},{12,20},{4,12},{1,5},{9... | collective-permute-start | bytes 466952 | tf_op jit(solution)/shard_map/ppermute | solution.py:412
  138.3 5.6 %collective-permute-start.13 = (bf16[304,256]{1,0:T(8,128)(2,1)S(1)}, bf16[304,256]{1,0:T(8,128)(2,1)S(1)}, u32[]{:S(2)}, u32[]{:S(2)}) collective-permute-start(bf16[304,256]{1,0:T(8,128)(2,1)S(1)} %collective-permute-done.12.rest_11_), channel_id=1, source_target_pairs={{0,4},{8,0},{16,8},{24,16},{28,24},{20,28},{12,20},{4,12},{1,5},{9... | collective-permute-start | bytes 466952 | tf_op jit(solution)/shard_map/ppermute | solution.py:412
  138.4 5.6 %collective-permute-start.20 = (bf16[304,256]{1,0:T(8,128)(2,1)S(1)}, bf16[304,256]{1,0:T(8,128)(2,1)S(1)}, u32[]{:S(2)}, u32[]{:S(2)}) collective-permute-start(bf16[304,256]{1,0:T(8,128)(2,1)S(1)} %collective-permute-done.19.rest_20_), channel_id=1, source_target_pairs={{0,8},{8,16},{16,24},{24,28},{28,20},{20,12},{12,4},{4,0},{1,9},{9... | collective-permute-start | bytes 466952 | tf_op jit(solution)/shard_map/ppermute | solution.py:412
  141.2 5.2 %collective-permute-start.10 = (bf16[304,256]{1,0:T(8,128)(2,1)S(1)}, bf16[304,256]{1,0:T(8,128)(2,1)S(1)}, u32[]{:S(2)}, u32[]{:S(2)}) collective-permute-start(bf16[304,256]{1,0:T(8,128)(2,1)S(1)} %collective-permute-done.9.rest_10_), channel_id=1, source_target_pairs={{0,8},{8,16},{16,24},{24,28},{28,20},{20,12},{12,4},{4,0},{1,9},{9... | collective-permute-start | bytes 466952 | tf_op jit(solution)/shard_map/ppermute | solution.py:412
  142.9 5.2 %collective-permute-start.17 = (bf16[304,256]{1,0:T(8,128)(2,1)S(1)}, bf16[304,256]{1,0:T(8,128)(2,1)S(1)}, u32[]{:S(2)}, u32[]{:S(2)}) collective-permute-start(bf16[304,256]{1,0:T(8,128)(2,1)S(1)} %collective-permute-done.16.rest_17_), channel_id=1, source_target_pairs={{0,4},{8,0},{16,8},{24,16},{28,24},{20,28},{12,20},{4,12},{1,5},{9... | collective-permute-start | bytes 466952 | tf_op jit(solution)/shard_map/ppermute | solution.py:412
  149.9 2.1 %collective-permute-start.21 = (f32[608,256]{1,0:T(8,128)S(1)}, f32[608,256]{1,0:T(8,128)S(1)}, u32[]{:S(2)}, u32[]{:S(2)}) collective-permute-start(f32[608,256]{1,0:T(8,128)S(1)} %grad_layer.1), channel_id=1, source_target_pairs={{0,1},{1,0},{2,3},{3,2},{4,5},{5,4},{6,7},{7,6},{8,9},{9,8},{10,11... | collective-permute-start | bytes 1867784 | tf_op jit(solution)/shard_map/ppermute | solution.py:433
  152.1 9.5 %copy-start.8 = (bf16[608,256]{1,0:T(8,128)(2,1)}, bf16[608,256]{1,0:T(8,128)(2,1)S(1)}, u32[]{:S(2)}) copy-start(bf16[608,256]{1,0:T(8,128)(2,1)S(1)} %add_convert_fusion.mine_ref) | copy-start | bytes 933892
  152.2 9.5 %collective-permute-start.22 = (bf16[608,256]{1,0:T(8,128)(2,1)S(1)}, bf16[608,256]{1,0:T(8,128)(2,1)S(1)}, u32[]{:S(2)}, u32[]{:S(2)}) collective-permute-start(bf16[608,256]{1,0:T(8,128)(2,1)S(1)} %add_convert_fusion.mine_ref), channel_id=1, source_target_pairs={{0,2},{1,3},{2,0},{3,1},{4,6},{5,7},{6,4},{7,5},{8,10},{9,11},{10,... | collective-permute-start | bytes 933896 | tf_op jit(solution)/shard_map/ppermute | solution.py:437
  161.6 0.7 copy-start.9
  (3 other events, 2.0 us)
Sparse Core Ops, SparseCore 0:
  10.1 42.9 all-gather.1

commit v8 on v6

--- a/solution.py
+++ b/solution.py
@@ -93,43 +93,42 @@
 
     tiles = table_ref.reshape(table_ref.shape[0] // TILE, TILE, padded)
     half = TILE // 2
-    low = lax.broadcasted_iota(jnp.int32, (half, padded), 0)
-    high = low + half
-
-    def fetch(node, wanted=None):
-        tile = tiles[node >> TILE_BITS].astype(jnp.float32)
+    span = half * TILE
+    line = lax.broadcasted_iota(jnp.int32, (half, span), 0)
+    place = lax.broadcasted_iota(jnp.int32, (half, span), 1)
+    choice = jnp.where(line == (place >> TILE_BITS), place & (TILE - 1), -1)
+
+    def picks(nodes, wanted=None):
+        if wanted is not None:
+            nodes = [jnp.where(want, node & (TILE - 1), TILE) for node, want in zip(nodes, wanted)]
+        value = jnp.full((half, span), nodes[0], jnp.int32)
+        for i in range(1, half):
+            value = jnp.where(line == i, nodes[i], value)
         if wanted is None:
-            line = jnp.full((half, padded), node, jnp.int32) & (TILE - 1)
-        else:
-            line = jnp.full((half, padded), jnp.where(wanted, node & (TILE - 1), TILE), jnp.int32)
-        return jnp.where(line == low, tile[:half], jnp.where(line == high, tile[half:], 0.0))
-
-    def add_lines(values):
-        step = 1
-        while step < half:
-            chosen = (low & step) == 0
-            values = [
-                jnp.where(chosen, one, two) + pltpu.roll(jnp.where(chosen, two, one), half - step, 0)
-                for one, two in zip(values[::2], values[1::2])
-            ]
-            step *= 2
-        return values[0]
+            value = value & (TILE - 1)
+        return jnp.where(value == choice, 1.0, 0.0).astype(jnp.bfloat16)
+
+    def fetch(lists, wanted=None):
+        left = [picks(nodes, wanted[at] if wanted else None) for at, nodes in enumerate(lists)]
+        right = [tiles[node >> TILE_BITS] for nodes in lists for node in nodes]
+        return jnp.dot(
+            jnp.concatenate(left, axis=1), jnp.concatenate(right, axis=0), preferred_element_type=jnp.float32
+        )
 
     def gather_rows(slots, exact, number, carry):
         first = pl.multiple_of(number * half, half)
         entries = [order_ref[0, 0, first + i] for i in range(half)]
         rows = [entry >> 4 for entry in entries]
         starts = [row * fanout for row in rows]
-
-        def near(i, slot):
-            node = near_ref[0, 0, starts[i] + slot]
-            return fetch(node) if exact else fetch(node, slot < (entries[i] & 15))
-
-        own_sum_ref[pl.ds(first, half), :] = add_lines([fetch(own_ref[0, 0, row]) for row in rows])
-        nears = [near(i, 0) for i in range(half)]
-        for slot in range(1, slots):
-            nears = [nears[i] + near(i, slot) for i in range(half)]
-        near_sum_ref[pl.ds(first, half), :] = add_lines(nears)
+        own_sum_ref[pl.ds(first, half), :] = fetch([[own_ref[0, 0, row] for row in rows]])
+        total = None
+        for slot in range(0, slots, 2):
+            pair = range(slot, min(slot + 2, slots))
+            lists = [[near_ref[0, 0, start + at] for start in starts] for at in pair]
+            wanted = None if exact else [[at < (entry & 15) for entry in entries] for at in pair]
+            part = fetch(lists, wanted)
+            total = part if total is None else total + part
+        near_sum_ref[pl.ds(first, half), :] = total
         return carry
 
     start = 0

time: 161 us -> 196 us (1.22); the launches traced: 161 us -> 192 us
  Pallas kernels: 70.6 us -> 90.3 us
  starting transfers between devices: 33.9 us -> 49.1 us
  waiting for transfers between devices: 28.2 us -> 24.5 us
    pallas_call x3, Pallas kernels: 44.6 us -> 64.2 us  [gather_layer(): pl.pallas_call(functools.partial(gather_kernel, fanout, capacity), grid_s...]
    ppermute x21, starting transfers between devices: 29.8 us -> 37.1 us  [send_along(): lax.ppermute(array, 'feat', [(ring[i], ring[(i + shift) % count]) for i i...]
    ppermute x1, starting transfers between devices: 0.07 us -> 5.29 us  [group_sum(): lax.ppermute(mine, 'dp', [(i, i ^ stride) for i in range(count)])]
    ppermute x21, waiting for transfers between devices: 17.8 us -> 14.4 us  [send_along(): lax.ppermute(array, 'feat', [(ring[i], ring[(i + shift) % count]) for i i...]
    ppermute x1, starting transfers between devices: 3.99 us -> 6.62 us  [group_sum(): other = lax.ppermute(mine, 'dp', [(i, i ^ stride) for i in range(count)])]
  transfers between devices with their start and end apart: 24 -> 24, of which waited for: 14 -> 12; matrix products, arithmetic and copies ran while one was open for 7% -> 6% of each run, Pallas kernels for 40% -> 43%
where the time goes in v8:
time: 196 us; the launch traced here: 192 us
  Pallas kernels  90.3 us (46%)
  starting transfers between devices  49.1 us (25%)
  waiting for transfers between devices  24.5 us (12%)
  between operations  14.3 us (7%)
  other arithmetic  7.49 us (4%)
  local copies, waits for them, and re-layouts  6.33 us (3%)
    pallas_call x3, Pallas kernels, gather_layer(): pl.pallas_call(functools.partial(gather_kernel, fanout, capacity), grid_s...  64.2 us
    ppermute x21, starting transfers between devices, send_along(): lax.ppermute(array, 'feat', [(ring[i], ring[(i + shift) % count]) for i i...  37.1 us
    pallas_call x1, Pallas kernels, build_table(): pl.pallas_call(table_kernel, grid=(nodes // chunk,), in_specs=[pl.BlockSp...  19.2 us
    ppermute x21, waiting for transfers between devices, send_along(): lax.ppermute(array, 'feat', [(ring[i], ring[(i + shift) % count]) for i i...  14.4 us
    ppermute x1, waiting for transfers between devices, group_sum(): other = lax.ppermute(mine, 'dp', [(i, i ^ stride) for i in range(count)])  7.79 us
    ppermute x1, starting transfers between devices, group_sum(): other = lax.ppermute(mine, 'dp', [(i, i ^ stride) for i in range(count)])  6.62 us
    ppermute x1, starting transfers between devices, group_sum(): lax.ppermute(mine, 'dp', [(i, i ^ stride) for i in range(count)])  5.29 us
  transfers between devices with their start and end apart: 24, of which 12 were waited for; matrix products, arithmetic and copies ran while one was open for 6% of the time, Pallas kernels for 43%

profile of v8, /device:TPU:0, one launch (start us, length us, event | category | flops | bytes accessed | tf_op | source)
XLA Modules:
  0.0 192.0 jit_solution(5058073596818134167)
XLA Ops:
  10.8 2.5 %convert_reduce_fusion = s32[8,704]{1,0:T(8,128)S(1)} fusion(s32[8,704]{1,0:T(8,128)S(1)} %get-tuple-element.86), kind=kLoop, calls=%fused_computation | loop fusion | flops 11889152 | bytes 45056 | tf_op jit(solution)/shard_map/reduce_sum | solution.py:31
  13.3 2.1 %select_reduce_fusion = s32[8,512]{1,0:T(8,128)S(1)} fusion(s32[8,704]{1,0:T(8,128)S(1)} %broadcast_add_fusion, s32[8,704]{1,0:T(8,128)S(1)} %convert_reduce_fusion), kind=kLoop, calls=%fused_computation.1 | loop fusion | flops 8646656 | bytes 61440 | tf_op jit(solution)/shard_map/reduce_sum | solution.py:33
  15.4 1.1 broadcast_in_dim.61.near_ref
  18.3 19.2 %build_table.1.table_ref = bf16[131072,128]{1,0:T(8,128)(2,1)S(1)} custom-call(bf16[128,131072]{1,0:T(8,128)(2,1)} %refs_3_, bf16[128,131072]{1,0:T(8,128)(2,1)} %refs_3_, bf16[128,131072]{1,0:T(8,128)(2,1)} %refs_3_, bf16[128,131072]{1,0:T(8,128)(2,1)} %refs_3_), custom_call_target="tpu_custom_call" | custom-call | tf_op jit(solution)/shard_map/build_table/pallas_call | solution.py:75
  37.6 22.2 %gather_layer.3 = (bf16[416,256]{1,0:T(8,128)(2,1)S(1)}, bf16[416,256]{1,0:T(8,128)(2,1)S(1)}, bf16[416,256]{1,0:T(8,128)(2,1)S(1)}, bf16[131072,128]{1,0:T(8,128)(2,1)S(1)}) custom-call(s32[16]{0:T(128)S(1)} %fusion.3.turn_ref.source_ref, s32[8,1,16]{2,1,0:T(1,128)S(1)} %bitcast.10, ...), custom_call_target="tpu_custom_call", output_to_operand_aliasing={{3}: (6, {})} | custom-call | bytes 51118080 | tf_op jit(solution)/shard_map/gather_layer/pallas_call | solution.py:174
  59.8 10.0 %collective-permute-start = (bf16[416,256]{1,0:T(8,128)(2,1)S(1)}, bf16[416,256]{1,0:T(8,128)(2,1)S(1)}, u32[]{:S(2)}, u32[]{:S(2)}) collective-permute-start(bf16[416,256]{1,0:T(8,128)(2,1)S(1)} %get-tuple-element.55.rest_0_), channel_id=1, source_target_pairs={{0,28},{8,20},{16,12},{24,4},{28,0},{20,8},{12,16},{4,24},{1,29},{... | collective-permute-start | bytes 638984 | tf_op jit(solution)/shard_map/ppermute | solution.py:347
  69.8 3.8 %collective-permute-start.2 = (bf16[416,256]{1,0:T(8,128)(2,1)S(1)}, bf16[416,256]{1,0:T(8,128)(2,1)S(1)}, u32[]{:S(2)}, u32[]{:S(2)}) collective-permute-start(bf16[416,256]{1,0:T(8,128)(2,1)S(1)} %get-tuple-element.57.rest_2_), channel_id=1, source_target_pairs={{0,20},{8,12},{16,4},{24,0},{28,8},{20,16},{12,24},{4,28},{1,21},{... | collective-permute-start | bytes 638984 | tf_op jit(solution)/shard_map/ppermute | solution.py:347
  73.6 26.1 %gather_layer.4 = (bf16[416,256]{1,0:T(8,128)(2,1)S(1)}, bf16[416,256]{1,0:T(8,128)(2,1)S(1)}, bf16[416,256]{1,0:T(8,128)(2,1)S(1)}, bf16[131072,128]{1,0:T(8,128)(2,1)S(1)}) custom-call(s32[16]{0:T(128)S(1)} %fusion.3.turn_ref.source_ref, s32[8,1,16]{2,1,0:T(1,128)S(1)} %bitcast.11, ...), custom_call_target="tpu_custom_call", output_to_operand_aliasing={{3}: (6, {})} | custom-call | bytes 51118080 | tf_op jit(solution)/shard_map/gather_layer/pallas_call | solution.py:174
  99.9 2.9 %collective-permute-start.4 = (bf16[416,256]{1,0:T(8,128)(2,1)S(1)}, bf16[416,256]{1,0:T(8,128)(2,1)S(1)}, u32[]{:S(2)}, u32[]{:S(2)}) collective-permute-start(bf16[416,256]{1,0:T(8,128)(2,1)S(1)} %get-tuple-element.64.rest_4_), channel_id=1, source_target_pairs={{0,12},{8,4},{16,0},{24,8},{28,16},{20,24},{12,28},{4,20},{1,13},{... | collective-permute-start | bytes 638984 | tf_op jit(solution)/shard_map/ppermute | solution.py:347
  102.8 15.9 %gather_layer.5 = (bf16[416,256]{1,0:T(8,128)(2,1)S(1)}, bf16[416,256]{1,0:T(8,128)(2,1)S(1)}, bf16[131072,128]{1,0:T(8,128)(2,1)S(1)}) custom-call(s32[16]{0:T(128)S(1)} %fusion.3.turn_ref.source_ref, s32[8,1,16]{2,1,0:T(1,128)S(1)} %bitcast.12, s32[8,1,512]{2,1,0:T(1,128)S(1)} %broadcast_in_dim.59.order_ref, ...), custom_call_target="tpu_custom_call", output_to_operand_aliasing={{2}: (6, {})} | custom-call | bytes 34078720 | tf_op jit(solution)/shard_map/gather_layer/pallas_call | solution.py:174
  118.7 5.8 %collective-permute-start.6 = (bf16[416,256]{1,0:T(8,128)(2,1)S(1)}, bf16[416,256]{1,0:T(8,128)(2,1)S(1)}, u32[]{:S(2)}, u32[]{:S(2)}) collective-permute-start(bf16[416,256]{1,0:T(8,128)(2,1)S(1)} %get-tuple-element.69.rest_6_), channel_id=1, source_target_pairs={{0,4},{8,0},{16,8},{24,16},{28,24},{20,28},{12,20},{4,12},{1,5},{9... | collective-permute-start | bytes 638984 | tf_op jit(solution)/shard_map/ppermute | solution.py:347
  125.8 2.0 %collective-permute-done.6.rest_6_ = bf16[416,256]{1,0:T(8,128)(2,1)S(1)} collective-permute-done((bf16[416,256]{1,0:T(8,128)(2,1)S(1)}, bf16[416,256]{1,0:T(8,128)(2,1)S(1)}, u32[]{:S(2)}, u32[]{:S(2)}) %collective-permute-start.6) | collective-permute-done | bytes 213024 | tf_op jit(solution)/shard_map/ppermute | solution.py:347
  127.9 1.2 copy-done
  129.1 3.1 %upper_layers.1 = (bf16[304,256]{1,0:T(8,128)(2,1)S(1)}, bf16[304,256]{1,0:T(8,128)(2,1)S(1)}) custom-call(s32[1]{0:T(128)} %dynamic_slice.23.size_ref, s32[16]{0:T(128)S(1)} %fusion.3.turn_ref.source_ref, bf16[8,256,256]{2,1,0:T(8,128)(2,1)S(1)} %copy-done, bf16[2,172,256]{2,1,0:T(8,128)(2,1)S(1)} %bitcast.9, s32[1,416]{1,0:T(1,128)S(1)} %compare_select_fusion.2.row_ref, ...), custom_call_target="tpu_custom_call" | custom-call | tf_op jit(solution)/shard_map/upper_layers/pallas_call | solution.py:263
  132.3 2.5 %collective-permute-start.14 = (bf16[304,256]{1,0:T(8,128)(2,1)S(1)}, bf16[304,256]{1,0:T(8,128)(2,1)S(1)}, u32[]{:S(2)}, u32[]{:S(2)}) collective-permute-start(bf16[304,256]{1,0:T(8,128)(2,1)S(1)} %get-tuple-element.83.rest_23_), channel_id=1, source_target_pairs={{0,4},{8,0},{16,8},{24,16},{28,24},{20,28},{12,20},{4,12},{1,5},{9... | collective-permute-start | bytes 466952 | tf_op jit(solution)/shard_map/ppermute | solution.py:347
  134.8 2.0 %collective-permute-start.11 = (bf16[304,256]{1,0:T(8,128)(2,1)S(1)}, bf16[304,256]{1,0:T(8,128)(2,1)S(1)}, u32[]{:S(2)}, u32[]{:S(2)}) collective-permute-start(bf16[304,256]{1,0:T(8,128)(2,1)S(1)} %get-tuple-element.82.rest_15_), channel_id=1, source_target_pairs={{0,4},{8,0},{16,8},{24,16},{28,24},{20,28},{12,20},{4,12},{1,5},{9... | collective-permute-start | bytes 466952 | tf_op jit(solution)/shard_map/ppermute | solution.py:347
  136.8 1.1 collective-permute-done.7.rest_14_
  138.8 1.2 collective-permute-start.15
  140.4 1.5 collective-permute-start.12
  142.5 1.2 collective-permute-done.8.rest_12_
  144.0 2.2 %collective-permute-start.16 = (bf16[304,256]{1,0:T(8,128)(2,1)S(1)}, bf16[304,256]{1,0:T(8,128)(2,1)S(1)}, u32[]{:S(2)}, u32[]{:S(2)}) collective-permute-start(bf16[304,256]{1,0:T(8,128)(2,1)S(1)} %collective-permute-done.15.rest_19_), channel_id=1, source_target_pairs={{0,4},{8,0},{16,8},{24,16},{28,24},{20,28},{12,20},{4,12},{1,5},{9... | collective-permute-start | bytes 466952 | tf_op jit(solution)/shard_map/ppermute | solution.py:347
  146.2 2.0 %collective-permute-start.13 = (bf16[304,256]{1,0:T(8,128)(2,1)S(1)}, bf16[304,256]{1,0:T(8,128)(2,1)S(1)}, u32[]{:S(2)}, u32[]{:S(2)}) collective-permute-start(bf16[304,256]{1,0:T(8,128)(2,1)S(1)} %collective-permute-done.12.rest_11_), channel_id=1, source_target_pairs={{0,4},{8,0},{16,8},{24,16},{28,24},{20,28},{12,20},{4,12},{1,5},{9... | collective-permute-start | bytes 466952 | tf_op jit(solution)/shard_map/ppermute | solution.py:347
  149.4 2.9 %collective-permute-done.9.rest_10_ = bf16[304,256]{1,0:T(8,128)(2,1)S(1)} collective-permute-done((bf16[304,256]{1,0:T(8,128)(2,1)S(1)}, bf16[304,256]{1,0:T(8,128)(2,1)S(1)}, u32[]{:S(2)}, u32[]{:S(2)}) %collective-permute-start.9) | collective-permute-done | bytes 155680 | tf_op jit(solution)/shard_map/ppermute | solution.py:347
  152.7 1.5 collective-permute-start.17
  154.3 1.6 collective-permute-done.20.rest_18_
  155.9 3.3 %collective-permute-done.10.rest_8_ = bf16[304,256]{1,0:T(8,128)(2,1)S(1)} collective-permute-done((bf16[304,256]{1,0:T(8,128)(2,1)S(1)}, bf16[304,256]{1,0:T(8,128)(2,1)S(1)}, u32[]{:S(2)}, u32[]{:S(2)}) %collective-permute-start.10) | collective-permute-done | bytes 155680 | tf_op jit(solution)/shard_map/ppermute | solution.py:347
  159.2 1.8 grad_layer.1
  161.0 5.3 %collective-permute-start.21 = (f32[608,256]{1,0:T(8,128)S(1)}, f32[608,256]{1,0:T(8,128)S(1)}, u32[]{:S(2)}, u32[]{:S(2)}) collective-permute-start(f32[608,256]{1,0:T(8,128)S(1)} %grad_layer.1), channel_id=1, source_target_pairs={{0,1},{1,0},{2,3},{3,2},{4,5},{5,4},{6,7},{7,6},{8,9},{9,8},{10,11... | collective-permute-start | bytes 1867784 | tf_op jit(solution)/shard_map/ppermute | solution.py:368
  166.3 1.7 collective-permute-done.21
  168.0 6.6 %collective-permute-start.22 = (bf16[608,256]{1,0:T(8,128)(2,1)S(1)}, bf16[608,256]{1,0:T(8,128)(2,1)S(1)}, u32[]{:S(2)}, u32[]{:S(2)}) collective-permute-start(bf16[608,256]{1,0:T(8,128)(2,1)S(1)} %add_convert_fusion.mine_ref), channel_id=1, source_target_pairs={{0,2},{1,3},{2,0},{3,1},{4,6},{5,7},{6,4},{7,5},{8,10},{9,11},{10,... | collective-permute-start | bytes 933896 | tf_op jit(solution)/shard_map/ppermute | solution.py:372
  174.7 7.8 %collective-permute-done.22.other_ref = bf16[608,256]{1,0:T(8,128)(2,1)S(1)} collective-permute-done((bf16[608,256]{1,0:T(8,128)(2,1)S(1)}, bf16[608,256]{1,0:T(8,128)(2,1)S(1)}, u32[]{:S(2)}, u32[]{:S(2)}) %collective-permute-start.22) | collective-permute-done | bytes 311328 | tf_op jit(solution)/shard_map/ppermute | solution.py:372
  183.2 2.0 %final_sum.1 = (f32[2,128,256]{2,1,0:T(8,128)}, f32[172,2,256]{2,1,0:T(2,128)}) custom-call(bf16[608,256]{1,0:T(8,128)(2,1)} %copy-done.1, bf16[608,256]{1,0:T(8,128)(2,1)} %copy-done.2), custom_call_target="tpu_custom_call" | custom-call | tf_op jit(solution)/shard_map/final_sum/pallas_call | solution.py:328
  (60 shorter events, 11.6 us)
Async XLA Ops:
  7.2 120.6 %all-gather.2.cloned.1.call-start = ((), (), s32[]{:S(2)}) async-start(), calls=%async_computation | async-start | bytes 1179648 | tf_op jit(solution)/shard_map/all_gather | solution.py:409
  59.8 40.0 %collective-permute-start = (bf16[416,256]{1,0:T(8,128)(2,1)S(1)}, bf16[416,256]{1,0:T(8,128)(2,1)S(1)}, u32[]{:S(2)}, u32[]{:S(2)}) collective-permute-start(bf16[416,256]{1,0:T(8,128)(2,1)S(1)} %get-tuple-element.55.rest_0_), channel_id=1, source_target_pairs={{0,28},{8,20},{16,12},{24,4},{28,0},{20,8},{12,16},{4,24},{1,29},{... | collective-permute-start | bytes 638984 | tf_op jit(solution)/shard_map/ppermute | solution.py:347
  69.8 30.0 %collective-permute-start.1 = (bf16[416,256]{1,0:T(8,128)(2,1)S(1)}, bf16[416,256]{1,0:T(8,128)(2,1)S(1)}, u32[]{:S(2)}, u32[]{:S(2)}) collective-permute-start(bf16[416,256]{1,0:T(8,128)(2,1)S(1)} %get-tuple-element.56.rest_1_), channel_id=1, source_target_pairs={{0,24},{8,28},{16,20},{24,12},{28,4},{20,0},{12,8},{4,16},{1,25},{... | collective-permute-start | bytes 638984 | tf_op jit(solution)/shard_map/ppermute | solution.py:347
  69.8 30.0 %collective-permute-start.2 = (bf16[416,256]{1,0:T(8,128)(2,1)S(1)}, bf16[416,256]{1,0:T(8,128)(2,1)S(1)}, u32[]{:S(2)}, u32[]{:S(2)}) collective-permute-start(bf16[416,256]{1,0:T(8,128)(2,1)S(1)} %get-tuple-element.57.rest_2_), channel_id=1, source_target_pairs={{0,20},{8,12},{16,4},{24,0},{28,8},{20,16},{12,24},{4,28},{1,21},{... | collective-permute-start | bytes 638984 | tf_op jit(solution)/shard_map/ppermute | solution.py:347
  99.8 24.7 %copy-start.3 = (bf16[2,256,172]{1,0,2:T(2,128)(2,1)S(1)}, bf16[2,256,172]{1,0,2:T(2,128)(2,1)}, u32[]{:S(2)}) copy-start(bf16[2,256,172]{1,0,2:T(2,128)(2,1)} %param.13) | copy-start | bytes 528388
  99.8 18.8 %collective-permute-start.3 = (bf16[416,256]{1,0:T(8,128)(2,1)S(1)}, bf16[416,256]{1,0:T(8,128)(2,1)S(1)}, u32[]{:S(2)}, u32[]{:S(2)}) collective-permute-start(bf16[416,256]{1,0:T(8,128)(2,1)S(1)} %get-tuple-element.63.rest_3_), channel_id=1, source_target_pairs={{0,16},{8,24},{16,28},{24,20},{28,12},{20,4},{12,0},{4,8},{1,17},{... | collective-permute-start | bytes 638984 | tf_op jit(solution)/shard_map/ppermute | solution.py:347
  99.9 18.8 %collective-permute-start.4 = (bf16[416,256]{1,0:T(8,128)(2,1)S(1)}, bf16[416,256]{1,0:T(8,128)(2,1)S(1)}, u32[]{:S(2)}, u32[]{:S(2)}) collective-permute-start(bf16[416,256]{1,0:T(8,128)(2,1)S(1)} %get-tuple-element.64.rest_4_), channel_id=1, source_target_pairs={{0,12},{8,4},{16,0},{24,8},{28,16},{20,24},{12,28},{4,20},{1,13},{... | collective-permute-start | bytes 638984 | tf_op jit(solution)/shard_map/ppermute | solution.py:347
  102.8 15.9 %collective-permute-start.5 = (bf16[416,256]{1,0:T(8,128)(2,1)S(1)}, bf16[416,256]{1,0:T(8,128)(2,1)S(1)}, u32[]{:S(2)}, u32[]{:S(2)}) collective-permute-start(bf16[416,256]{1,0:T(8,128)(2,1)S(1)} %get-tuple-element.65.rest_5_), channel_id=1, source_target_pairs={{0,8},{8,16},{16,24},{24,28},{28,20},{20,12},{12,4},{4,0},{1,9},{9... | collective-permute-start | bytes 638984 | tf_op jit(solution)/shard_map/ppermute | solution.py:347
  118.7 9.1 %collective-permute-start.6 = (bf16[416,256]{1,0:T(8,128)(2,1)S(1)}, bf16[416,256]{1,0:T(8,128)(2,1)S(1)}, u32[]{:S(2)}, u32[]{:S(2)}) collective-permute-start(bf16[416,256]{1,0:T(8,128)(2,1)S(1)} %get-tuple-element.69.rest_6_), channel_id=1, source_target_pairs={{0,4},{8,0},{16,8},{24,16},{28,24},{20,28},{12,20},{4,12},{1,5},{9... | collective-permute-start | bytes 638984 | tf_op jit(solution)/shard_map/ppermute | solution.py:347
  127.9 1.2 copy-start
  132.2 5.7 %collective-permute-start.7 = (bf16[304,256]{1,0:T(8,128)(2,1)S(1)}, bf16[304,256]{1,0:T(8,128)(2,1)S(1)}, u32[]{:S(2)}, u32[]{:S(2)}) collective-permute-start(bf16[304,256]{1,0:T(8,128)(2,1)S(1)} %get-tuple-element.82.rest_15_), channel_id=1, source_target_pairs={{0,8},{8,16},{16,24},{24,28},{28,20},{20,12},{12,4},{4,0},{1,9},{9... | collective-permute-start | bytes 466952 | tf_op jit(solution)/shard_map/ppermute | solution.py:347
  132.3 6.5 %collective-permute-start.14 = (bf16[304,256]{1,0:T(8,128)(2,1)S(1)}, bf16[304,256]{1,0:T(8,128)(2,1)S(1)}, u32[]{:S(2)}, u32[]{:S(2)}) collective-permute-start(bf16[304,256]{1,0:T(8,128)(2,1)S(1)} %get-tuple-element.83.rest_23_), channel_id=1, source_target_pairs={{0,4},{8,0},{16,8},{24,16},{28,24},{20,28},{12,20},{4,12},{1,5},{9... | collective-permute-start | bytes 466952 | tf_op jit(solution)/shard_map/ppermute | solution.py:347
  134.8 5.7 %collective-permute-start.11 = (bf16[304,256]{1,0:T(8,128)(2,1)S(1)}, bf16[304,256]{1,0:T(8,128)(2,1)S(1)}, u32[]{:S(2)}, u32[]{:S(2)}) collective-permute-start(bf16[304,256]{1,0:T(8,128)(2,1)S(1)} %get-tuple-element.82.rest_15_), channel_id=1, source_target_pairs={{0,4},{8,0},{16,8},{24,16},{28,24},{20,28},{12,20},{4,12},{1,5},{9... | collective-permute-start | bytes 466952 | tf_op jit(solution)/shard_map/ppermute | solution.py:347
  136.8 5.2 %collective-permute-start.18 = (bf16[304,256]{1,0:T(8,128)(2,1)S(1)}, bf16[304,256]{1,0:T(8,128)(2,1)S(1)}, u32[]{:S(2)}, u32[]{:S(2)}) collective-permute-start(bf16[304,256]{1,0:T(8,128)(2,1)S(1)} %get-tuple-element.83.rest_23_), channel_id=1, source_target_pairs={{0,8},{8,16},{16,24},{24,28},{28,20},{20,12},{12,4},{4,0},{1,9},{9... | collective-permute-start | bytes 466952 | tf_op jit(solution)/shard_map/ppermute | solution.py:347
  137.9 5.7 %collective-permute-start.8 = (bf16[304,256]{1,0:T(8,128)(2,1)S(1)}, bf16[304,256]{1,0:T(8,128)(2,1)S(1)}, u32[]{:S(2)}, u32[]{:S(2)}) collective-permute-start(bf16[304,256]{1,0:T(8,128)(2,1)S(1)} %collective-permute-done.7.rest_14_), channel_id=1, source_target_pairs={{0,8},{8,16},{16,24},{24,28},{28,20},{20,12},{12,4},{4,0},{1,9},{9... | collective-permute-start | bytes 466952 | tf_op jit(solution)/shard_map/ppermute | solution.py:347
  138.8 5.2 %collective-permute-start.15 = (bf16[304,256]{1,0:T(8,128)(2,1)S(1)}, bf16[304,256]{1,0:T(8,128)(2,1)S(1)}, u32[]{:S(2)}, u32[]{:S(2)}) collective-permute-start(bf16[304,256]{1,0:T(8,128)(2,1)S(1)} %collective-permute-done.14.rest_21_), channel_id=1, source_target_pairs={{0,4},{8,0},{16,8},{24,16},{28,24},{20,28},{12,20},{4,12},{1,5},{9... | collective-permute-start | bytes 466952 | tf_op jit(solution)/shard_map/ppermute | solution.py:347
  140.4 5.7 %collective-permute-start.12 = (bf16[304,256]{1,0:T(8,128)(2,1)S(1)}, bf16[304,256]{1,0:T(8,128)(2,1)S(1)}, u32[]{:S(2)}, u32[]{:S(2)}) collective-permute-start(bf16[304,256]{1,0:T(8,128)(2,1)S(1)} %collective-permute-done.11.rest_13_), channel_id=1, source_target_pairs={{0,4},{8,0},{16,8},{24,16},{28,24},{20,28},{12,20},{4,12},{1,5},{9... | collective-permute-start | bytes 466952 | tf_op jit(solution)/shard_map/ppermute | solution.py:347
  142.0 6.9 %collective-permute-start.19 = (bf16[304,256]{1,0:T(8,128)(2,1)S(1)}, bf16[304,256]{1,0:T(8,128)(2,1)S(1)}, u32[]{:S(2)}, u32[]{:S(2)}) collective-permute-start(bf16[304,256]{1,0:T(8,128)(2,1)S(1)} %collective-permute-done.18.rest_22_), channel_id=1, source_target_pairs={{0,8},{8,16},{16,24},{24,28},{28,20},{20,12},{12,4},{4,0},{1,9},{9... | collective-permute-start | bytes 466952 | tf_op jit(solution)/shard_map/ppermute | solution.py:347
  143.7 8.6 %collective-permute-start.9 = (bf16[304,256]{1,0:T(8,128)(2,1)S(1)}, bf16[304,256]{1,0:T(8,128)(2,1)S(1)}, u32[]{:S(2)}, u32[]{:S(2)}) collective-permute-start(bf16[304,256]{1,0:T(8,128)(2,1)S(1)} %collective-permute-done.8.rest_12_), channel_id=1, source_target_pairs={{0,8},{8,16},{16,24},{24,28},{28,20},{20,12},{12,4},{4,0},{1,9},{9... | collective-permute-start | bytes 466952 | tf_op jit(solution)/shard_map/ppermute | solution.py:347
  144.0 8.7 %collective-permute-start.16 = (bf16[304,256]{1,0:T(8,128)(2,1)S(1)}, bf16[304,256]{1,0:T(8,128)(2,1)S(1)}, u32[]{:S(2)}, u32[]{:S(2)}) collective-permute-start(bf16[304,256]{1,0:T(8,128)(2,1)S(1)} %collective-permute-done.15.rest_19_), channel_id=1, source_target_pairs={{0,4},{8,0},{16,8},{24,16},{28,24},{20,28},{12,20},{4,12},{1,5},{9... | collective-permute-start | bytes 466952 | tf_op jit(solution)/shard_map/ppermute | solution.py:347
  146.2 8.1 %collective-permute-start.13 = (bf16[304,256]{1,0:T(8,128)(2,1)S(1)}, bf16[304,256]{1,0:T(8,128)(2,1)S(1)}, u32[]{:S(2)}, u32[]{:S(2)}) collective-permute-start(bf16[304,256]{1,0:T(8,128)(2,1)S(1)} %collective-permute-done.12.rest_11_), channel_id=1, source_target_pairs={{0,4},{8,0},{16,8},{24,16},{28,24},{20,28},{12,20},{4,12},{1,5},{9... | collective-permute-start | bytes 466952 | tf_op jit(solution)/shard_map/ppermute | solution.py:347
  148.9 7.0 %collective-permute-start.20 = (bf16[304,256]{1,0:T(8,128)(2,1)S(1)}, bf16[304,256]{1,0:T(8,128)(2,1)S(1)}, u32[]{:S(2)}, u32[]{:S(2)}) collective-permute-start(bf16[304,256]{1,0:T(8,128)(2,1)S(1)} %collective-permute-done.19.rest_20_), channel_id=1, source_target_pairs={{0,8},{8,16},{16,24},{24,28},{28,20},{20,12},{12,4},{4,0},{1,9},{9... | collective-permute-start | bytes 466952 | tf_op jit(solution)/shard_map/ppermute | solution.py:347
  152.2 7.0 %collective-permute-start.10 = (bf16[304,256]{1,0:T(8,128)(2,1)S(1)}, bf16[304,256]{1,0:T(8,128)(2,1)S(1)}, u32[]{:S(2)}, u32[]{:S(2)}) collective-permute-start(bf16[304,256]{1,0:T(8,128)(2,1)S(1)} %collective-permute-done.9.rest_10_), channel_id=1, source_target_pairs={{0,8},{8,16},{16,24},{24,28},{28,20},{20,12},{12,4},{4,0},{1,9},{9... | collective-permute-start | bytes 466952 | tf_op jit(solution)/shard_map/ppermute | solution.py:347
  152.7 6.5 %collective-permute-start.17 = (bf16[304,256]{1,0:T(8,128)(2,1)S(1)}, bf16[304,256]{1,0:T(8,128)(2,1)S(1)}, u32[]{:S(2)}, u32[]{:S(2)}) collective-permute-start(bf16[304,256]{1,0:T(8,128)(2,1)S(1)} %collective-permute-done.16.rest_17_), channel_id=1, source_target_pairs={{0,4},{8,0},{16,8},{24,16},{28,24},{20,28},{12,20},{4,12},{1,5},{9... | collective-permute-start | bytes 466952 | tf_op jit(solution)/shard_map/ppermute | solution.py:347
  161.0 7.0 %collective-permute-start.21 = (f32[608,256]{1,0:T(8,128)S(1)}, f32[608,256]{1,0:T(8,128)S(1)}, u32[]{:S(2)}, u32[]{:S(2)}) collective-permute-start(f32[608,256]{1,0:T(8,128)S(1)} %grad_layer.1), channel_id=1, source_target_pairs={{0,1},{1,0},{2,3},{3,2},{4,5},{5,4},{6,7},{7,6},{8,9},{9,8},{10,11... | collective-permute-start | bytes 1867784 | tf_op jit(solution)/shard_map/ppermute | solution.py:368
  168.0 14.4 %copy-start.1 = (bf16[608,256]{1,0:T(8,128)(2,1)}, bf16[608,256]{1,0:T(8,128)(2,1)S(1)}, u32[]{:S(2)}) copy-start(bf16[608,256]{1,0:T(8,128)(2,1)S(1)} %add_convert_fusion.mine_ref) | copy-start | bytes 933892
  168.0 14.4 %collective-permute-start.22 = (bf16[608,256]{1,0:T(8,128)(2,1)S(1)}, bf16[608,256]{1,0:T(8,128)(2,1)S(1)}, u32[]{:S(2)}, u32[]{:S(2)}) collective-permute-start(bf16[608,256]{1,0:T(8,128)(2,1)S(1)} %add_convert_fusion.mine_ref), channel_id=1, source_target_pairs={{0,2},{1,3},{2,0},{3,1},{4,6},{5,7},{6,4},{7,5},{8,10},{9,11},{10,... | collective-permute-start | bytes 933896 | tf_op jit(solution)/shard_map/ppermute | solution.py:372
  182.5 0.7 copy-start.2
Sparse Core Ops, SparseCore 0:
  10.1 42.7 all-gather.1

commit v9 on v6

--- a/solution.py
+++ b/solution.py
@@ -272,26 +272,27 @@
 
 
 def grad_kernel(seed_total, classes, source_ref, *rest):
-    count = (len(rest) - 2) // 3
+    count = (len(rest) - 3) // 3
     inputs_refs, upper_refs, lower_refs = rest[:count], rest[count : 2 * count], rest[2 * count : 3 * count]
-    out_ref, units_ref = rest[3 * count :]
+    out_ref, dpreact_ref, units_ref = rest[3 * count :]
     capacity, double = inputs_refs[0].shape
     hidden_width = out_ref.shape[1]
     split = upper_refs[0].shape[0]
     rows = (((0,), (0,)), ((), ()))
-    first = jnp.zeros((double, hidden_width), jnp.float32)
     for place in range(count):
-        inputs_ref, upper_ref, lower_ref = inputs_refs[place], upper_refs[place], lower_refs[place]
-        first = first + lax.dot_general(
-            inputs_ref[:split], upper_ref[...], rows, preferred_element_type=jnp.float32
-        )
-        first = first + lax.dot_general(
-            inputs_ref[split:], lower_ref[: capacity - split], rows, preferred_element_type=jnp.float32
-        )
-        start = pl.multiple_of(source_ref[place] * seed_total, seed_total)
+        source = source_ref[2 * count + place]
+        upper_ref, lower_ref = upper_refs[place], lower_refs[place]
+        dpreact_ref[source, :split] = upper_ref[...]
+        dpreact_ref[source, split:] = lower_ref[: capacity - split]
+        start = pl.multiple_of(source * seed_total, seed_total)
         for part in range(3):
             begin = capacity - split + part * seed_total
             units_ref[part, pl.ds(start, seed_total), :] = lower_ref[begin : begin + seed_total]
+    first = jnp.zeros((double, hidden_width), jnp.float32)
+    for place, inputs_ref in enumerate(inputs_refs):
+        first = first + lax.dot_general(
+            inputs_ref[...], dpreact_ref[source_ref[place]], rows, preferred_element_type=jnp.float32
+        )
     out_ref[:double] = first
     for layer in range(2):
         second = lax.dot_general(units_ref[2], units_ref[layer], rows, preferred_element_type=jnp.float32)
@@ -308,7 +309,10 @@
         in_specs=[pl.BlockSpec(memory_space=pltpu.SMEM)] + [vmem] * (3 * len(inputs)),
         out_specs=vmem,
         out_shape=jax.ShapeDtypeStruct((double + 2 * round_up(classes, 8), hidden_width), jnp.float32),
-        scratch_shapes=[pltpu.VMEM((3, len(inputs) * seed_total, hidden_width), jnp.bfloat16)],
+        scratch_shapes=[
+            pltpu.VMEM((len(inputs), capacity, hidden_width), jnp.bfloat16),
+            pltpu.VMEM((3, len(inputs) * seed_total, hidden_width), jnp.bfloat16),
+        ],
         compiler_params=pltpu.CompilerParams(vmem_limit_bytes=40 * 2**20),
         name="grad_layer",
     )(sources, *inputs, *upper, *lower)
@@ -346,6 +350,18 @@
 def send_along(array, ring, shift):
     count = len(ring)
     return lax.ppermute(array, "feat", [(ring[i], ring[(i + shift) % count]) for i in range(count)])
+
+
+def partner(device, number, count):
+    return device ^ number if count & (count - 1) == 0 else (device + number) % count
+
+
+def sender(device, number, count):
+    return next(i for i in range(count) if partner(i, number, count) == device)
+
+
+def exchange(array, number, count):
+    return lax.ppermute(array, "feat", [(i, partner(i, number, count)) for i in range(count)])
 
 
 def ring_gather(upper, lower, ring):
@@ -402,9 +418,15 @@
     order, enough = plan_rows(hop1_count, hop2_count, sizes, kept)
     count = lax.axis_size("feat")
     ring = ring_of(count)
-    places = sorted(range(count), key=lambda t: -min(t, count - t))
+    places = list(range(count))[::-1]
+    if count & (count - 1) == 0:
+        half = count // 2
+        places = [t for t in places if t >= half][::-1] + [t for t in places if t < half]
     turns = [
-        [ring[(ring.index(i) + sign * t) % count] for sign in (1, -1) for t in places] for i in range(count)
+        [partner(i, t, count) for t in places]
+        + [sender(i, t, count) for t in places]
+        + [ring[(ring.index(i) + t) % count] for t in range(count)]
+        for i in range(count)
     ]
     turn = lax.dynamic_index_in_dim(jnp.array(turns, jnp.int32), column_rank, 0, keepdims=False)
     weights = lax.all_gather(first_layer.reshape(2 * slice_width, hidden_width), "feat", axis=0)
@@ -429,7 +451,7 @@
             )
         inputs += blocks
         received += arrived
-        arrived = [send_along(block, ring, t) if t else block for t, block in zip(places[begin:end], blocks)]
+        arrived = [exchange(block, t, count) if t else block for t, block in zip(places[begin:end], blocks)]
     received += arrived
 
     def own(array):
@@ -443,9 +465,7 @@
     layer = jnp.transpose(second_layer, (0, 2, 1))
     halves = upper_layers(received, size, turn, weights, layer, row, seeds, fanout)
     upper, lower = ring_gather(*halves, ring)
-    grads = grad_layer(
-        inputs, [upper[t] for t in places], [lower[t] for t in places], turn, seed_total, classes
-    )
+    grads = grad_layer(inputs, upper, lower, turn, seed_total, classes)
     return tuple(group_sum(grads, slice_width, classes))
 
 

time: 161 us -> 165 us (1.025)
  waiting for transfers between devices: 28.2 us -> 41 us
  Pallas kernels: 70.6 us -> 63.2 us
  starting transfers between devices: 33.9 us -> 31.9 us
    ppermute x0 -> x7, waiting for transfers between devices: none -> 17.3 us  [exchange(): lax.ppermute(array, 'feat', [(i, partner(i, number, count)) for i in rang...]
    ppermute x0 -> x7, starting transfers between devices: none -> 14.7 us  [exchange(): lax.ppermute(array, 'feat', [(i, partner(i, number, count)) for i in rang...]
    ppermute x21 -> x14, starting transfers between devices: 29.8 us -> 17 us  [send_along(): lax.ppermute(array, 'feat', [(ring[i], ring[(i + shift) % count]) for i i...]
    pallas_call x3, Pallas kernels: 44.6 us -> 37.3 us  [gather_layer(): pl.pallas_call(functools.partial(gather_kernel, fanout, capacity), grid_s...]
    ppermute x21 -> x14, waiting for transfers between devices: 17.8 us -> 11.7 us  [send_along(): lax.ppermute(array, 'feat', [(ring[i], ring[(i + shift) % count]) for i i...]
    ppermute x1, starting transfers between devices: 3.99 us -> 0.07 us  [group_sum(): other = lax.ppermute(mine, 'dp', [(i, i ^ stride) for i in range(count)])]
    ppermute x1, waiting for transfers between devices: 7.66 us -> 9.39 us  [group_sum(): other = lax.ppermute(mine, 'dp', [(i, i ^ stride) for i in range(count)])]
  transfers between devices with their start and end apart: 24 -> 24, of which waited for: 14 -> 14; matrix products, arithmetic and copies ran while one was open for 7% -> 7% of each run, Pallas kernels for 40% -> 34%
where the time goes in v9:
time: 165 us; the launch traced here: 164 us
  Pallas kernels  63.2 us (38%)
  waiting for transfers between devices  41 us (25%)
  starting transfers between devices  31.9 us (19%)
  between operations  14.3 us (9%)
  other arithmetic  7.49 us (5%)
  local copies, waits for them, and re-layouts  6.33 us (4%)
    pallas_call x3, Pallas kernels, gather_layer(): pl.pallas_call(functools.partial(gather_kernel, fanout, capacity), grid_s...  37.3 us
    pallas_call x1, Pallas kernels, build_table(): pl.pallas_call(table_kernel, grid=(nodes // chunk,), in_specs=[pl.BlockSp...  19.2 us
    ppermute x7, waiting for transfers between devices, exchange(): lax.ppermute(array, 'feat', [(i, partner(i, number, count)) for i in rang...  17.3 us
    ppermute x14, starting transfers between devices, send_along(): lax.ppermute(array, 'feat', [(ring[i], ring[(i + shift) % count]) for i i...  17 us
    ppermute x7, starting transfers between devices, exchange(): lax.ppermute(array, 'feat', [(i, partner(i, number, count)) for i in rang...  14.7 us
    ppermute x14, waiting for transfers between devices, send_along(): lax.ppermute(array, 'feat', [(ring[i], ring[(i + shift) % count]) for i i...  11.7 us
    ppermute x1, waiting for transfers between devices, group_sum(): other = lax.ppermute(mine, 'dp', [(i, i ^ stride) for i in range(count)])  9.39 us
  transfers between devices with their start and end apart: 24, of which 14 were waited for; matrix products, arithmetic and copies ran while one was open for 7% of the time, Pallas kernels for 34%

profile of v9, /device:TPU:0, one launch (start us, length us, event | category | flops | bytes accessed | tf_op | source)
XLA Modules:
  0.0 164.2 jit_solution(10468597590871212976)
XLA Ops:
  10.8 2.5 %convert_reduce_fusion = s32[8,704]{1,0:T(8,128)S(1)} fusion(s32[8,704]{1,0:T(8,128)S(1)} %get-tuple-element.86), kind=kLoop, calls=%fused_computation | loop fusion | flops 11889152 | bytes 45056 | tf_op jit(solution)/shard_map/reduce_sum | solution.py:31
  13.3 2.1 %select_reduce_fusion = s32[8,512]{1,0:T(8,128)S(1)} fusion(s32[8,704]{1,0:T(8,128)S(1)} %broadcast_add_fusion, s32[8,704]{1,0:T(8,128)S(1)} %convert_reduce_fusion), kind=kLoop, calls=%fused_computation.1 | loop fusion | flops 8646656 | bytes 61440 | tf_op jit(solution)/shard_map/reduce_sum | solution.py:33
  18.3 19.2 %build_table.1.table_ref = bf16[131072,128]{1,0:T(8,128)(2,1)S(1)} custom-call(bf16[128,131072]{1,0:T(8,128)(2,1)} %refs_3_, bf16[128,131072]{1,0:T(8,128)(2,1)} %refs_3_, bf16[128,131072]{1,0:T(8,128)(2,1)} %refs_3_, bf16[128,131072]{1,0:T(8,128)(2,1)} %refs_3_), custom_call_target="tpu_custom_call" | custom-call | tf_op jit(solution)/shard_map/build_table/pallas_call | solution.py:75
  37.6 16.1 %gather_layer.3 = (bf16[416,256]{1,0:T(8,128)(2,1)S(1)}, bf16[416,256]{1,0:T(8,128)(2,1)S(1)}, bf16[416,256]{1,0:T(8,128)(2,1)S(1)}, bf16[131072,128]{1,0:T(8,128)(2,1)S(1)}) custom-call(s32[24]{0:T(128)S(1)} %fusion.3.turn_ref.source_ref, s32[8,1,16]{2,1,0:T(1,128)S(1)} %bitcast.10, ...), custom_call_target="tpu_custom_call", output_to_operand_aliasing={{3}: (6, {})} | custom-call | bytes 51118080 | tf_op jit(solution)/shard_map/gather_layer/pallas_call | solution.py:175
  53.7 2.1 %collective-permute-start = (bf16[416,256]{1,0:T(8,128)(2,1)S(1)}, bf16[416,256]{1,0:T(8,128)(2,1)S(1)}, u32[]{:S(2)}, u32[]{:S(2)}) collective-permute-start(bf16[416,256]{1,0:T(8,128)(2,1)S(1)} %get-tuple-element.55.rest_0_), channel_id=1, source_target_pairs={{0,16},{4,20},{8,24},{12,28},{16,0},{20,4},{24,8},{28,12},{1,17},{... | collective-permute-start | bytes 638984 | tf_op jit(solution)/shard_map/ppermute | solution.py:364
  55.8 2.2 %collective-permute-start.1 = (bf16[416,256]{1,0:T(8,128)(2,1)S(1)}, bf16[416,256]{1,0:T(8,128)(2,1)S(1)}, u32[]{:S(2)}, u32[]{:S(2)}) collective-permute-start(bf16[416,256]{1,0:T(8,128)(2,1)S(1)} %get-tuple-element.56.rest_1_), channel_id=1, source_target_pairs={{0,20},{4,16},{8,28},{12,24},{16,4},{20,0},{24,12},{28,8},{1,21},{... | collective-permute-start | bytes 638984 | tf_op jit(solution)/shard_map/ppermute | solution.py:364
  58.0 2.5 %collective-permute-start.2 = (bf16[416,256]{1,0:T(8,128)(2,1)S(1)}, bf16[416,256]{1,0:T(8,128)(2,1)S(1)}, u32[]{:S(2)}, u32[]{:S(2)}) collective-permute-start(bf16[416,256]{1,0:T(8,128)(2,1)S(1)} %get-tuple-element.57.rest_2_), channel_id=1, source_target_pairs={{0,24},{4,28},{8,16},{12,20},{16,8},{20,12},{24,0},{28,4},{1,25},{... | collective-permute-start | bytes 638984 | tf_op jit(solution)/shard_map/ppermute | solution.py:364
  60.4 13.0 %gather_layer.4 = (bf16[416,256]{1,0:T(8,128)(2,1)S(1)}, bf16[416,256]{1,0:T(8,128)(2,1)S(1)}, bf16[416,256]{1,0:T(8,128)(2,1)S(1)}, bf16[131072,128]{1,0:T(8,128)(2,1)S(1)}) custom-call(s32[24]{0:T(128)S(1)} %fusion.3.turn_ref.source_ref, s32[8,1,16]{2,1,0:T(1,128)S(1)} %bitcast.11, ...), custom_call_target="tpu_custom_call", output_to_operand_aliasing={{3}: (6, {})} | custom-call | bytes 51118080 | tf_op jit(solution)/shard_map/gather_layer/pallas_call | solution.py:175
  73.4 7.6 %collective-permute-done.1.rest_1_ = bf16[416,256]{1,0:T(8,128)(2,1)S(1)} collective-permute-done((bf16[416,256]{1,0:T(8,128)(2,1)S(1)}, bf16[416,256]{1,0:T(8,128)(2,1)S(1)}, u32[]{:S(2)}, u32[]{:S(2)}) %collective-permute-start.1) | collective-permute-done | bytes 213024 | tf_op jit(solution)/shard_map/ppermute | solution.py:364
  81.1 3.7 %collective-permute-start.3 = (bf16[416,256]{1,0:T(8,128)(2,1)S(1)}, bf16[416,256]{1,0:T(8,128)(2,1)S(1)}, u32[]{:S(2)}, u32[]{:S(2)}) collective-permute-start(bf16[416,256]{1,0:T(8,128)(2,1)S(1)} %get-tuple-element.63.rest_3_), channel_id=1, source_target_pairs={{0,28},{4,24},{8,20},{12,16},{16,12},{20,8},{24,4},{28,0},{1,29},{... | collective-permute-start | bytes 638984 | tf_op jit(solution)/shard_map/ppermute | solution.py:364
  84.8 4.2 %collective-permute-start.4 = (bf16[416,256]{1,0:T(8,128)(2,1)S(1)}, bf16[416,256]{1,0:T(8,128)(2,1)S(1)}, u32[]{:S(2)}, u32[]{:S(2)}) collective-permute-start(bf16[416,256]{1,0:T(8,128)(2,1)S(1)} %get-tuple-element.64.rest_4_), channel_id=1, source_target_pairs={{0,12},{4,8},{8,4},{12,0},{16,28},{20,24},{24,20},{28,16},{1,13},{... | collective-permute-start | bytes 638984 | tf_op jit(solution)/shard_map/ppermute | solution.py:364
  89.0 8.3 %gather_layer.5 = (bf16[416,256]{1,0:T(8,128)(2,1)S(1)}, bf16[416,256]{1,0:T(8,128)(2,1)S(1)}, bf16[131072,128]{1,0:T(8,128)(2,1)S(1)}) custom-call(s32[24]{0:T(128)S(1)} %fusion.3.turn_ref.source_ref, s32[8,1,16]{2,1,0:T(1,128)S(1)} %bitcast.12, s32[8,1,512]{2,1,0:T(1,128)S(1)} %broadcast_in_dim.59.order_ref, ...), custom_call_target="tpu_custom_call", output_to_operand_aliasing={{2}: (6, {})} | custom-call | bytes 34078720 | tf_op jit(solution)/shard_map/gather_layer/pallas_call | solution.py:175
  97.7 4.0 %collective-permute-done.5.rest_5_ = bf16[416,256]{1,0:T(8,128)(2,1)S(1)} collective-permute-done((bf16[416,256]{1,0:T(8,128)(2,1)S(1)}, bf16[416,256]{1,0:T(8,128)(2,1)S(1)}, u32[]{:S(2)}, u32[]{:S(2)}) %collective-permute-start.5) | collective-permute-done | bytes 213024 | tf_op jit(solution)/shard_map/ppermute | solution.py:364
  103.0 5.3 %collective-permute-done.6.rest_6_ = bf16[416,256]{1,0:T(8,128)(2,1)S(1)} collective-permute-done((bf16[416,256]{1,0:T(8,128)(2,1)S(1)}, bf16[416,256]{1,0:T(8,128)(2,1)S(1)}, u32[]{:S(2)}, u32[]{:S(2)}) %collective-permute-start.6) | collective-permute-done | bytes 213024 | tf_op jit(solution)/shard_map/ppermute | solution.py:364
  108.4 1.2 copy-done
  109.6 3.1 %upper_layers.1 = (bf16[304,256]{1,0:T(8,128)(2,1)S(1)}, bf16[304,256]{1,0:T(8,128)(2,1)S(1)}) custom-call(s32[1]{0:T(128)} %dynamic_slice.23.size_ref, s32[24]{0:T(128)S(1)} %fusion.3.turn_ref.source_ref, bf16[8,256,256]{2,1,0:T(8,128)(2,1)S(1)} %copy-done, bf16[2,172,256]{2,1,0:T(8,128)(2,1)S(1)} %bitcast.9, s32[1,416]{1,0:T(1,128)S(1)} %compare_select_fusion.2.row_ref, ...), custom_call_target="tpu_custom_call" | custom-call | tf_op jit(solution)/shard_map/upper_layers/pallas_call | solution.py:264
  112.7 2.5 %collective-permute-start.10 = (bf16[304,256]{1,0:T(8,128)(2,1)S(1)}, bf16[304,256]{1,0:T(8,128)(2,1)S(1)}, u32[]{:S(2)}, u32[]{:S(2)}) collective-permute-start(bf16[304,256]{1,0:T(8,128)(2,1)S(1)} %get-tuple-element.82.rest_8_), channel_id=1, source_target_pairs={{0,8},{8,16},{16,24},{24,28},{28,20},{20,12},{12,4},{4,0},{1,9},{9... | collective-permute-start | bytes 466952 | tf_op jit(solution)/shard_map/ppermute | solution.py:352
  115.3 2.0 %collective-permute-start.18 = (bf16[304,256]{1,0:T(8,128)(2,1)S(1)}, bf16[304,256]{1,0:T(8,128)(2,1)S(1)}, u32[]{:S(2)}, u32[]{:S(2)}) collective-permute-start(bf16[304,256]{1,0:T(8,128)(2,1)S(1)} %get-tuple-element.83.rest_16_), channel_id=1, source_target_pairs={{0,8},{8,16},{16,24},{24,28},{28,20},{20,12},{12,4},{4,0},{1,9},{9... | collective-permute-start | bytes 466952 | tf_op jit(solution)/shard_map/ppermute | solution.py:352
  117.3 2.5 %collective-permute-done.10.rest_15_ = bf16[304,256]{1,0:T(8,128)(2,1)S(1)} collective-permute-done((bf16[304,256]{1,0:T(8,128)(2,1)S(1)}, bf16[304,256]{1,0:T(8,128)(2,1)S(1)}, u32[]{:S(2)}, u32[]{:S(2)}) %collective-permute-start.10) | collective-permute-done | bytes 155680 | tf_op jit(solution)/shard_map/ppermute | solution.py:352
  119.7 2.5 %collective-permute-start.11 = (bf16[304,256]{1,0:T(8,128)(2,1)S(1)}, bf16[304,256]{1,0:T(8,128)(2,1)S(1)}, u32[]{:S(2)}, u32[]{:S(2)}) collective-permute-start(bf16[304,256]{1,0:T(8,128)(2,1)S(1)} %collective-permute-done.10.rest_15_), channel_id=1, source_target_pairs={{0,8},{8,16},{16,24},{24,28},{28,20},{20,12},{12,4},{4,0},{1,9},{9... | collective-permute-start | bytes 466952 | tf_op jit(solution)/shard_map/ppermute | solution.py:352
  123.1 2.5 %collective-permute-start.19 = (bf16[304,256]{1,0:T(8,128)(2,1)S(1)}, bf16[304,256]{1,0:T(8,128)(2,1)S(1)}, u32[]{:S(2)}, u32[]{:S(2)}) collective-permute-start(bf16[304,256]{1,0:T(8,128)(2,1)S(1)} %collective-permute-done.18.rest_23_), channel_id=1, source_target_pairs={{0,8},{8,16},{16,24},{24,28},{28,20},{20,12},{12,4},{4,0},{1,9},{9... | collective-permute-start | bytes 466952 | tf_op jit(solution)/shard_map/ppermute | solution.py:352
  125.6 1.1 collective-permute-done.11.rest_14_
  126.7 2.5 %collective-permute-start.12 = (bf16[304,256]{1,0:T(8,128)(2,1)S(1)}, bf16[304,256]{1,0:T(8,128)(2,1)S(1)}, u32[]{:S(2)}, u32[]{:S(2)}) collective-permute-start(bf16[304,256]{1,0:T(8,128)(2,1)S(1)} %collective-permute-done.11.rest_14_), channel_id=1, source_target_pairs={{0,8},{8,16},{16,24},{24,28},{28,20},{20,12},{12,4},{4,0},{1,9},{9... | collective-permute-start | bytes 466952 | tf_op jit(solution)/shard_map/ppermute | solution.py:352
  130.0 2.5 %collective-permute-start.20 = (bf16[304,256]{1,0:T(8,128)(2,1)S(1)}, bf16[304,256]{1,0:T(8,128)(2,1)S(1)}, u32[]{:S(2)}, u32[]{:S(2)}) collective-permute-start(bf16[304,256]{1,0:T(8,128)(2,1)S(1)} %collective-permute-done.19.rest_22_), channel_id=1, source_target_pairs={{0,8},{8,16},{16,24},{24,28},{28,20},{20,12},{12,4},{4,0},{1,9},{9... | collective-permute-start | bytes 466952 | tf_op jit(solution)/shard_map/ppermute | solution.py:352
  132.5 1.1 collective-permute-done.12.rest_13_
  133.7 2.5 %collective-permute-start.13 = (bf16[304,256]{1,0:T(8,128)(2,1)S(1)}, bf16[304,256]{1,0:T(8,128)(2,1)S(1)}, u32[]{:S(2)}, u32[]{:S(2)}) collective-permute-start(bf16[304,256]{1,0:T(8,128)(2,1)S(1)} %collective-permute-done.12.rest_13_), channel_id=1, source_target_pairs={{0,8},{8,16},{16,24},{24,28},{28,20},{20,12},{12,4},{4,0},{1,9},{9... | collective-permute-start | bytes 466952 | tf_op jit(solution)/shard_map/ppermute | solution.py:352
  136.2 1.7 %collective-permute-done.9.rest_11_ = bf16[304,256]{1,0:T(8,128)(2,1)S(1)} collective-permute-done((bf16[304,256]{1,0:T(8,128)(2,1)S(1)}, bf16[304,256]{1,0:T(8,128)(2,1)S(1)}, u32[]{:S(2)}, u32[]{:S(2)}) %collective-permute-start.9) | collective-permute-done | bytes 155680 | tf_op jit(solution)/shard_map/ppermute | solution.py:352
  138.9 2.5 %collective-permute-done.17.rest_20_ = bf16[304,256]{1,0:T(8,128)(2,1)S(1)} collective-permute-done((bf16[304,256]{1,0:T(8,128)(2,1)S(1)}, bf16[304,256]{1,0:T(8,128)(2,1)S(1)}, u32[]{:S(2)}, u32[]{:S(2)}) %collective-permute-start.17) | collective-permute-done | bytes 155680 | tf_op jit(solution)/shard_map/ppermute | solution.py:352
  141.4 1.5 grad_layer.1
  143.0 2.0 %collective-permute-done.21 = f32[608,256]{1,0:T(8,128)S(1)} collective-permute-done((f32[608,256]{1,0:T(8,128)S(1)}, f32[608,256]{1,0:T(8,128)S(1)}, u32[]{:S(2)}, u32[]{:S(2)}) %collective-permute-start.21) | collective-permute-done | bytes 622624 | tf_op jit(solution)/shard_map/ppermute | solution.py:385
  145.2 9.4 %collective-permute-done.22.other_ref = bf16[608,256]{1,0:T(8,128)(2,1)S(1)} collective-permute-done((bf16[608,256]{1,0:T(8,128)(2,1)S(1)}, bf16[608,256]{1,0:T(8,128)(2,1)S(1)}, u32[]{:S(2)}, u32[]{:S(2)}) %collective-permute-start.22) | collective-permute-done | bytes 311328 | tf_op jit(solution)/shard_map/ppermute | solution.py:389
  155.3 2.0 %final_sum.1 = (f32[2,128,256]{2,1,0:T(8,128)}, f32[172,2,256]{2,1,0:T(2,128)}) custom-call(bf16[608,256]{1,0:T(8,128)(2,1)} %copy-done.1, bf16[608,256]{1,0:T(8,128)(2,1)} %copy-done.2), custom_call_target="tpu_custom_call" | custom-call | tf_op jit(solution)/shard_map/final_sum/pallas_call | solution.py:333
  (60 shorter events, 12.1 us)
Async XLA Ops:
  7.2 101.2 %all-gather.2.cloned.1.call-start = ((), (), s32[]{:S(2)}) async-start(), calls=%async_computation | async-start | bytes 1179648 | tf_op jit(solution)/shard_map/all_gather | solution.py:432
  53.7 19.8 %collective-permute-start = (bf16[416,256]{1,0:T(8,128)(2,1)S(1)}, bf16[416,256]{1,0:T(8,128)(2,1)S(1)}, u32[]{:S(2)}, u32[]{:S(2)}) collective-permute-start(bf16[416,256]{1,0:T(8,128)(2,1)S(1)} %get-tuple-element.55.rest_0_), channel_id=1, source_target_pairs={{0,16},{4,20},{8,24},{12,28},{16,0},{20,4},{24,8},{28,12},{1,17},{... | collective-permute-start | bytes 638984 | tf_op jit(solution)/shard_map/ppermute | solution.py:364
  55.8 25.3 %collective-permute-start.1 = (bf16[416,256]{1,0:T(8,128)(2,1)S(1)}, bf16[416,256]{1,0:T(8,128)(2,1)S(1)}, u32[]{:S(2)}, u32[]{:S(2)}) collective-permute-start(bf16[416,256]{1,0:T(8,128)(2,1)S(1)} %get-tuple-element.56.rest_1_), channel_id=1, source_target_pairs={{0,20},{4,16},{8,28},{12,24},{16,4},{20,0},{24,12},{28,8},{1,21},{... | collective-permute-start | bytes 638984 | tf_op jit(solution)/shard_map/ppermute | solution.py:364
  58.0 23.1 %collective-permute-start.2 = (bf16[416,256]{1,0:T(8,128)(2,1)S(1)}, bf16[416,256]{1,0:T(8,128)(2,1)S(1)}, u32[]{:S(2)}, u32[]{:S(2)}) collective-permute-start(bf16[416,256]{1,0:T(8,128)(2,1)S(1)} %get-tuple-element.57.rest_2_), channel_id=1, source_target_pairs={{0,24},{4,28},{8,16},{12,20},{16,8},{20,12},{24,0},{28,4},{1,25},{... | collective-permute-start | bytes 638984 | tf_op jit(solution)/shard_map/ppermute | solution.py:364
  73.4 28.2 %copy-start.3 = (bf16[2,256,172]{1,0,2:T(2,128)(2,1)S(1)}, bf16[2,256,172]{1,0,2:T(2,128)(2,1)}, u32[]{:S(2)}) copy-start(bf16[2,256,172]{1,0,2:T(2,128)(2,1)} %param.13) | copy-start | bytes 528388
  81.1 16.2 %collective-permute-start.3 = (bf16[416,256]{1,0:T(8,128)(2,1)S(1)}, bf16[416,256]{1,0:T(8,128)(2,1)S(1)}, u32[]{:S(2)}, u32[]{:S(2)}) collective-permute-start(bf16[416,256]{1,0:T(8,128)(2,1)S(1)} %get-tuple-element.63.rest_3_), channel_id=1, source_target_pairs={{0,28},{4,24},{8,20},{12,16},{16,12},{20,8},{24,4},{28,0},{1,29},{... | collective-permute-start | bytes 638984 | tf_op jit(solution)/shard_map/ppermute | solution.py:364
  84.8 12.9 %collective-permute-start.4 = (bf16[416,256]{1,0:T(8,128)(2,1)S(1)}, bf16[416,256]{1,0:T(8,128)(2,1)S(1)}, u32[]{:S(2)}, u32[]{:S(2)}) collective-permute-start(bf16[416,256]{1,0:T(8,128)(2,1)S(1)} %get-tuple-element.64.rest_4_), channel_id=1, source_target_pairs={{0,12},{4,8},{8,4},{12,0},{16,28},{20,24},{24,20},{28,16},{1,13},{... | collective-permute-start | bytes 638984 | tf_op jit(solution)/shard_map/ppermute | solution.py:364
  89.0 12.7 %collective-permute-start.5 = (bf16[416,256]{1,0:T(8,128)(2,1)S(1)}, bf16[416,256]{1,0:T(8,128)(2,1)S(1)}, u32[]{:S(2)}, u32[]{:S(2)}) collective-permute-start(bf16[416,256]{1,0:T(8,128)(2,1)S(1)} %get-tuple-element.65.rest_5_), channel_id=1, source_target_pairs={{0,8},{4,12},{8,0},{12,4},{16,24},{20,28},{24,16},{28,20},{1,9},{5... | collective-permute-start | bytes 638984 | tf_op jit(solution)/shard_map/ppermute | solution.py:364
  101.6 6.7 %collective-permute-start.6 = (bf16[416,256]{1,0:T(8,128)(2,1)S(1)}, bf16[416,256]{1,0:T(8,128)(2,1)S(1)}, u32[]{:S(2)}, u32[]{:S(2)}) collective-permute-start(bf16[416,256]{1,0:T(8,128)(2,1)S(1)} %get-tuple-element.69.rest_6_), channel_id=1, source_target_pairs={{0,4},{4,0},{8,12},{12,8},{16,20},{20,16},{24,28},{28,24},{1,5},{5... | collective-permute-start | bytes 638984 | tf_op jit(solution)/shard_map/ppermute | solution.py:364
  108.4 1.2 copy-start
  112.7 7.0 %collective-permute-start.10 = (bf16[304,256]{1,0:T(8,128)(2,1)S(1)}, bf16[304,256]{1,0:T(8,128)(2,1)S(1)}, u32[]{:S(2)}, u32[]{:S(2)}) collective-permute-start(bf16[304,256]{1,0:T(8,128)(2,1)S(1)} %get-tuple-element.82.rest_8_), channel_id=1, source_target_pairs={{0,8},{8,16},{16,24},{24,28},{28,20},{20,12},{12,4},{4,0},{1,9},{9... | collective-permute-start | bytes 466952 | tf_op jit(solution)/shard_map/ppermute | solution.py:352
  115.3 7.0 %collective-permute-start.14 = (bf16[304,256]{1,0:T(8,128)(2,1)S(1)}, bf16[304,256]{1,0:T(8,128)(2,1)S(1)}, u32[]{:S(2)}, u32[]{:S(2)}) collective-permute-start(bf16[304,256]{1,0:T(8,128)(2,1)S(1)} %get-tuple-element.83.rest_16_), channel_id=1, source_target_pairs={{0,4},{8,0},{16,8},{24,16},{28,24},{20,28},{12,20},{4,12},{1,5},{9... | collective-permute-start | bytes 466952 | tf_op jit(solution)/shard_map/ppermute | solution.py:352
  115.3 7.8 %collective-permute-start.18 = (bf16[304,256]{1,0:T(8,128)(2,1)S(1)}, bf16[304,256]{1,0:T(8,128)(2,1)S(1)}, u32[]{:S(2)}, u32[]{:S(2)}) collective-permute-start(bf16[304,256]{1,0:T(8,128)(2,1)S(1)} %get-tuple-element.83.rest_16_), channel_id=1, source_target_pairs={{0,8},{8,16},{16,24},{24,28},{28,20},{20,12},{12,4},{4,0},{1,9},{9... | collective-permute-start | bytes 466952 | tf_op jit(solution)/shard_map/ppermute | solution.py:352
  117.3 8.3 %collective-permute-start.7 = (bf16[304,256]{1,0:T(8,128)(2,1)S(1)}, bf16[304,256]{1,0:T(8,128)(2,1)S(1)}, u32[]{:S(2)}, u32[]{:S(2)}) collective-permute-start(bf16[304,256]{1,0:T(8,128)(2,1)S(1)} %get-tuple-element.82.rest_8_), channel_id=1, source_target_pairs={{0,4},{8,0},{16,8},{24,16},{28,24},{20,28},{12,20},{4,12},{1,5},{9... | collective-permute-start | bytes 466952 | tf_op jit(solution)/shard_map/ppermute | solution.py:352
  119.7 7.0 %collective-permute-start.11 = (bf16[304,256]{1,0:T(8,128)(2,1)S(1)}, bf16[304,256]{1,0:T(8,128)(2,1)S(1)}, u32[]{:S(2)}, u32[]{:S(2)}) collective-permute-start(bf16[304,256]{1,0:T(8,128)(2,1)S(1)} %collective-permute-done.10.rest_15_), channel_id=1, source_target_pairs={{0,8},{8,16},{16,24},{24,28},{28,20},{20,12},{12,4},{4,0},{1,9},{9... | collective-permute-start | bytes 466952 | tf_op jit(solution)/shard_map/ppermute | solution.py:352
  122.2 7.0 %collective-permute-start.15 = (bf16[304,256]{1,0:T(8,128)(2,1)S(1)}, bf16[304,256]{1,0:T(8,128)(2,1)S(1)}, u32[]{:S(2)}, u32[]{:S(2)}) collective-permute-start(bf16[304,256]{1,0:T(8,128)(2,1)S(1)} %collective-permute-done.14.rest_17_), channel_id=1, source_target_pairs={{0,4},{8,0},{16,8},{24,16},{28,24},{20,28},{12,20},{4,12},{1,5},{9... | collective-permute-start | bytes 466952 | tf_op jit(solution)/shard_map/ppermute | solution.py:352
  123.1 7.0 %collective-permute-start.19 = (bf16[304,256]{1,0:T(8,128)(2,1)S(1)}, bf16[304,256]{1,0:T(8,128)(2,1)S(1)}, u32[]{:S(2)}, u32[]{:S(2)}) collective-permute-start(bf16[304,256]{1,0:T(8,128)(2,1)S(1)} %collective-permute-done.18.rest_23_), channel_id=1, source_target_pairs={{0,8},{8,16},{16,24},{24,28},{28,20},{20,12},{12,4},{4,0},{1,9},{9... | collective-permute-start | bytes 466952 | tf_op jit(solution)/shard_map/ppermute | solution.py:352
  125.6 7.0 %collective-permute-start.8 = (bf16[304,256]{1,0:T(8,128)(2,1)S(1)}, bf16[304,256]{1,0:T(8,128)(2,1)S(1)}, u32[]{:S(2)}, u32[]{:S(2)}) collective-permute-start(bf16[304,256]{1,0:T(8,128)(2,1)S(1)} %collective-permute-done.7.rest_9_), channel_id=1, source_target_pairs={{0,4},{8,0},{16,8},{24,16},{28,24},{20,28},{12,20},{4,12},{1,5},{9... | collective-permute-start | bytes 466952 | tf_op jit(solution)/shard_map/ppermute | solution.py:352
  126.7 7.0 %collective-permute-start.12 = (bf16[304,256]{1,0:T(8,128)(2,1)S(1)}, bf16[304,256]{1,0:T(8,128)(2,1)S(1)}, u32[]{:S(2)}, u32[]{:S(2)}) collective-permute-start(bf16[304,256]{1,0:T(8,128)(2,1)S(1)} %collective-permute-done.11.rest_14_), channel_id=1, source_target_pairs={{0,8},{8,16},{16,24},{24,28},{28,20},{20,12},{12,4},{4,0},{1,9},{9... | collective-permute-start | bytes 466952 | tf_op jit(solution)/shard_map/ppermute | solution.py:352
  129.2 7.0 %collective-permute-start.16 = (bf16[304,256]{1,0:T(8,128)(2,1)S(1)}, bf16[304,256]{1,0:T(8,128)(2,1)S(1)}, u32[]{:S(2)}, u32[]{:S(2)}) collective-permute-start(bf16[304,256]{1,0:T(8,128)(2,1)S(1)} %collective-permute-done.15.rest_18_), channel_id=1, source_target_pairs={{0,4},{8,0},{16,8},{24,16},{28,24},{20,28},{12,20},{4,12},{1,5},{9... | collective-permute-start | bytes 466952 | tf_op jit(solution)/shard_map/ppermute | solution.py:352
  130.0 6.1 %collective-permute-start.20 = (bf16[304,256]{1,0:T(8,128)(2,1)S(1)}, bf16[304,256]{1,0:T(8,128)(2,1)S(1)}, u32[]{:S(2)}, u32[]{:S(2)}) collective-permute-start(bf16[304,256]{1,0:T(8,128)(2,1)S(1)} %collective-permute-done.19.rest_22_), channel_id=1, source_target_pairs={{0,8},{8,16},{16,24},{24,28},{28,20},{20,12},{12,4},{4,0},{1,9},{9... | collective-permute-start | bytes 466952 | tf_op jit(solution)/shard_map/ppermute | solution.py:352
  132.5 5.3 %collective-permute-start.9 = (bf16[304,256]{1,0:T(8,128)(2,1)S(1)}, bf16[304,256]{1,0:T(8,128)(2,1)S(1)}, u32[]{:S(2)}, u32[]{:S(2)}) collective-permute-start(bf16[304,256]{1,0:T(8,128)(2,1)S(1)} %collective-permute-done.8.rest_10_), channel_id=1, source_target_pairs={{0,4},{8,0},{16,8},{24,16},{28,24},{20,28},{12,20},{4,12},{1,5},{9... | collective-permute-start | bytes 466952 | tf_op jit(solution)/shard_map/ppermute | solution.py:352
  133.7 5.2 %collective-permute-start.13 = (bf16[304,256]{1,0:T(8,128)(2,1)S(1)}, bf16[304,256]{1,0:T(8,128)(2,1)S(1)}, u32[]{:S(2)}, u32[]{:S(2)}) collective-permute-start(bf16[304,256]{1,0:T(8,128)(2,1)S(1)} %collective-permute-done.12.rest_13_), channel_id=1, source_target_pairs={{0,8},{8,16},{16,24},{24,28},{28,20},{20,12},{12,4},{4,0},{1,9},{9... | collective-permute-start | bytes 466952 | tf_op jit(solution)/shard_map/ppermute | solution.py:352
  136.2 5.2 %collective-permute-start.17 = (bf16[304,256]{1,0:T(8,128)(2,1)S(1)}, bf16[304,256]{1,0:T(8,128)(2,1)S(1)}, u32[]{:S(2)}, u32[]{:S(2)}) collective-permute-start(bf16[304,256]{1,0:T(8,128)(2,1)S(1)} %collective-permute-done.16.rest_19_), channel_id=1, source_target_pairs={{0,4},{8,0},{16,8},{24,16},{28,24},{20,28},{12,20},{4,12},{1,5},{9... | collective-permute-start | bytes 466952 | tf_op jit(solution)/shard_map/ppermute | solution.py:352
  142.9 2.1 %collective-permute-start.21 = (f32[608,256]{1,0:T(8,128)S(1)}, f32[608,256]{1,0:T(8,128)S(1)}, u32[]{:S(2)}, u32[]{:S(2)}) collective-permute-start(f32[608,256]{1,0:T(8,128)S(1)} %grad_layer.1), channel_id=1, source_target_pairs={{0,1},{1,0},{2,3},{3,2},{4,5},{5,4},{6,7},{7,6},{8,9},{9,8},{10,11... | collective-permute-start | bytes 1867784 | tf_op jit(solution)/shard_map/ppermute | solution.py:385
  145.1 9.5 %copy-start.1 = (bf16[608,256]{1,0:T(8,128)(2,1)}, bf16[608,256]{1,0:T(8,128)(2,1)S(1)}, u32[]{:S(2)}) copy-start(bf16[608,256]{1,0:T(8,128)(2,1)S(1)} %add_convert_fusion.mine_ref) | copy-start | bytes 933892
  145.2 9.5 %collective-permute-start.22 = (bf16[608,256]{1,0:T(8,128)(2,1)S(1)}, bf16[608,256]{1,0:T(8,128)(2,1)S(1)}, u32[]{:S(2)}, u32[]{:S(2)}) collective-permute-start(bf16[608,256]{1,0:T(8,128)(2,1)S(1)} %add_convert_fusion.mine_ref), channel_id=1, source_target_pairs={{0,2},{1,3},{2,0},{3,1},{4,6},{5,7},{6,4},{7,5},{8,10},{9,11},{10,... | collective-permute-start | bytes 933896 | tf_op jit(solution)/shard_map/ppermute | solution.py:389
  154.6 0.7 copy-start.2
Sparse Core Ops, SparseCore 0:
  10.1 42.8 all-gather.1

commit v10 on v9

--- a/solution.py
+++ b/solution.py
@@ -419,9 +419,10 @@
     count = lax.axis_size("feat")
     ring = ring_of(count)
     places = list(range(count))[::-1]
-    if count & (count - 1) == 0:
-        half = count // 2
-        places = [t for t in places if t >= half][::-1] + [t for t in places if t < half]
+    if count > 2 and count & (count - 1) == 0:
+        far, near = range(count // 2, count), range(count // 2 - 1, 1, -1)
+        mixed = [((at + 0.5) / len(part), t) for part in (far, near) for at, t in enumerate(part)]
+        places = [t for _, t in sorted(mixed)] + [1, 0]
     turns = [
         [partner(i, t, count) for t in places]
         + [sender(i, t, count) for t in places]

time: 165 us -> 162 us (0.982)
  waiting for transfers between devices: 41 us -> 29.6 us
  starting transfers between devices: 31.9 us -> 36.6 us
  Pallas kernels: 63.2 us -> 67.2 us
    ppermute x7, waiting for transfers between devices: 17.3 us -> 5.81 us  [exchange(): lax.ppermute(array, 'feat', [(i, partner(i, number, count)) for i in rang...]
    pallas_call x3, Pallas kernels: 37.3 us -> 41.4 us  [gather_layer(): pl.pallas_call(functools.partial(gather_kernel, fanout, capacity), grid_s...]
    ppermute x7, starting transfers between devices: 14.7 us -> 17.7 us  [exchange(): lax.ppermute(array, 'feat', [(i, partner(i, number, count)) for i in rang...]
    ppermute x14, starting transfers between devices: 17 us -> 18.8 us  [send_along(): lax.ppermute(array, 'feat', [(ring[i], ring[(i + shift) % count]) for i i...]
  transfers between devices with their start and end apart: 24 -> 24, of which waited for: 14 -> 14; matrix products, arithmetic and copies ran while one was open for 7% -> 7% of each run, Pallas kernels for 34% -> 38%
where the time goes in v10:
time: 162 us; the launch traced here: 161 us
  Pallas kernels  67.2 us (41%)
  starting transfers between devices  36.6 us (23%)
  waiting for transfers between devices  29.6 us (18%)
  between operations  14.3 us (9%)
  other arithmetic  7.49 us (5%)
  local copies, waits for them, and re-layouts  6.33 us (4%)
    pallas_call x3, Pallas kernels, gather_layer(): pl.pallas_call(functools.partial(gather_kernel, fanout, capacity), grid_s...  41.4 us
    pallas_call x1, Pallas kernels, build_table(): pl.pallas_call(table_kernel, grid=(nodes // chunk,), in_specs=[pl.BlockSp...  19.2 us
    ppermute x14, starting transfers between devices, send_along(): lax.ppermute(array, 'feat', [(ring[i], ring[(i + shift) % count]) for i i...  18.8 us
    ppermute x7, starting transfers between devices, exchange(): lax.ppermute(array, 'feat', [(i, partner(i, number, count)) for i in rang...  17.7 us
    ppermute x14, waiting for transfers between devices, send_along(): lax.ppermute(array, 'feat', [(ring[i], ring[(i + shift) % count]) for i i...  11.7 us
    ppermute x1, waiting for transfers between devices, group_sum(): other = lax.ppermute(mine, 'dp', [(i, i ^ stride) for i in range(count)])  9.39 us
    ppermute x7, waiting for transfers between devices, exchange(): lax.ppermute(array, 'feat', [(i, partner(i, number, count)) for i in rang...  5.81 us
  transfers between devices with their start and end apart: 24, of which 14 were waited for; matrix products, arithmetic and copies ran while one was open for 7% of the time, Pallas kernels for 38%

profile of v10, /device:TPU:0, one launch (start us, length us, event | category | flops | bytes accessed | tf_op | source)
XLA Modules:
  0.0 161.5 jit_solution(18040259241025744837)
XLA Ops:
  10.8 2.5 %convert_reduce_fusion = s32[8,704]{1,0:T(8,128)S(1)} fusion(s32[8,704]{1,0:T(8,128)S(1)} %get-tuple-element.86), kind=kLoop, calls=%fused_computation | loop fusion | flops 11889152 | bytes 45056 | tf_op jit(solution)/shard_map/reduce_sum | solution.py:31
  13.3 2.1 %select_reduce_fusion = s32[8,512]{1,0:T(8,128)S(1)} fusion(s32[8,704]{1,0:T(8,128)S(1)} %broadcast_add_fusion, s32[8,704]{1,0:T(8,128)S(1)} %convert_reduce_fusion), kind=kLoop, calls=%fused_computation.1 | loop fusion | flops 8646656 | bytes 61440 | tf_op jit(solution)/shard_map/reduce_sum | solution.py:33
  15.4 1.1 broadcast_in_dim.61.near_ref
  18.3 19.2 %build_table.1.table_ref = bf16[131072,128]{1,0:T(8,128)(2,1)S(1)} custom-call(bf16[128,131072]{1,0:T(8,128)(2,1)} %refs_3_, bf16[128,131072]{1,0:T(8,128)(2,1)} %refs_3_, bf16[128,131072]{1,0:T(8,128)(2,1)} %refs_3_, bf16[128,131072]{1,0:T(8,128)(2,1)} %refs_3_), custom_call_target="tpu_custom_call" | custom-call | tf_op jit(solution)/shard_map/build_table/pallas_call | solution.py:75
  37.6 15.2 %gather_layer.3 = (bf16[416,256]{1,0:T(8,128)(2,1)S(1)}, bf16[416,256]{1,0:T(8,128)(2,1)S(1)}, bf16[416,256]{1,0:T(8,128)(2,1)S(1)}, bf16[131072,128]{1,0:T(8,128)(2,1)S(1)}) custom-call(s32[24]{0:T(128)S(1)} %fusion.3.turn_ref.source_ref, s32[8,1,16]{2,1,0:T(1,128)S(1)} %bitcast.10, ...), custom_call_target="tpu_custom_call", output_to_operand_aliasing={{3}: (6, {})} | custom-call | bytes 51118080 | tf_op jit(solution)/shard_map/gather_layer/pallas_call | solution.py:175
  52.8 7.5 %collective-permute-start = (bf16[416,256]{1,0:T(8,128)(2,1)S(1)}, bf16[416,256]{1,0:T(8,128)(2,1)S(1)}, u32[]{:S(2)}, u32[]{:S(2)}) collective-permute-start(bf16[416,256]{1,0:T(8,128)(2,1)S(1)} %get-tuple-element.55.rest_0_), channel_id=1, source_target_pairs={{0,16},{4,20},{8,24},{12,28},{16,0},{20,4},{24,8},{28,12},{1,17},{... | collective-permute-start | bytes 638984 | tf_op jit(solution)/shard_map/ppermute | solution.py:364
  60.6 13.4 %gather_layer.4 = (bf16[416,256]{1,0:T(8,128)(2,1)S(1)}, bf16[416,256]{1,0:T(8,128)(2,1)S(1)}, bf16[416,256]{1,0:T(8,128)(2,1)S(1)}, bf16[131072,128]{1,0:T(8,128)(2,1)S(1)}) custom-call(s32[24]{0:T(128)S(1)} %fusion.3.turn_ref.source_ref, s32[8,1,16]{2,1,0:T(1,128)S(1)} %bitcast.11, ...), custom_call_target="tpu_custom_call", output_to_operand_aliasing={{3}: (6, {})} | custom-call | bytes 51118080 | tf_op jit(solution)/shard_map/gather_layer/pallas_call | solution.py:175
  74.1 2.5 %collective-permute-done.2.rest_2_ = bf16[416,256]{1,0:T(8,128)(2,1)S(1)} collective-permute-done((bf16[416,256]{1,0:T(8,128)(2,1)S(1)}, bf16[416,256]{1,0:T(8,128)(2,1)S(1)}, u32[]{:S(2)}, u32[]{:S(2)}) %collective-permute-start.2) | collective-permute-done | bytes 213024 | tf_op jit(solution)/shard_map/ppermute | solution.py:364
  76.6 7.5 %collective-permute-start.3 = (bf16[416,256]{1,0:T(8,128)(2,1)S(1)}, bf16[416,256]{1,0:T(8,128)(2,1)S(1)}, u32[]{:S(2)}, u32[]{:S(2)}) collective-permute-start(bf16[416,256]{1,0:T(8,128)(2,1)S(1)} %get-tuple-element.63.rest_3_), channel_id=1, source_target_pairs={{0,24},{4,28},{8,16},{12,20},{16,8},{20,12},{24,0},{28,4},{1,25},{... | collective-permute-start | bytes 638984 | tf_op jit(solution)/shard_map/ppermute | solution.py:364
  84.1 12.8 %gather_layer.5 = (bf16[416,256]{1,0:T(8,128)(2,1)S(1)}, bf16[416,256]{1,0:T(8,128)(2,1)S(1)}, bf16[131072,128]{1,0:T(8,128)(2,1)S(1)}) custom-call(s32[24]{0:T(128)S(1)} %fusion.3.turn_ref.source_ref, s32[8,1,16]{2,1,0:T(1,128)S(1)} %bitcast.12, s32[8,1,512]{2,1,0:T(1,128)S(1)} %broadcast_in_dim.59.order_ref, ...), custom_call_target="tpu_custom_call", output_to_operand_aliasing={{2}: (6, {})} | custom-call | bytes 34078720 | tf_op jit(solution)/shard_map/gather_layer/pallas_call | solution.py:175
  97.4 2.3 %collective-permute-start.6 = (bf16[416,256]{1,0:T(8,128)(2,1)S(1)}, bf16[416,256]{1,0:T(8,128)(2,1)S(1)}, u32[]{:S(2)}, u32[]{:S(2)}) collective-permute-start(bf16[416,256]{1,0:T(8,128)(2,1)S(1)} %get-tuple-element.69.rest_6_), channel_id=1, source_target_pairs={{0,4},{4,0},{8,12},{12,8},{16,20},{20,16},{24,28},{28,24},{1,5},{5... | collective-permute-start | bytes 638984 | tf_op jit(solution)/shard_map/ppermute | solution.py:364
  101.0 2.8 %collective-permute-done.6.rest_6_ = bf16[416,256]{1,0:T(8,128)(2,1)S(1)} collective-permute-done((bf16[416,256]{1,0:T(8,128)(2,1)S(1)}, bf16[416,256]{1,0:T(8,128)(2,1)S(1)}, u32[]{:S(2)}, u32[]{:S(2)}) %collective-permute-start.6) | collective-permute-done | bytes 213024 | tf_op jit(solution)/shard_map/ppermute | solution.py:364
  103.9 1.2 copy-done
  105.1 3.1 %upper_layers.1 = (bf16[304,256]{1,0:T(8,128)(2,1)S(1)}, bf16[304,256]{1,0:T(8,128)(2,1)S(1)}) custom-call(s32[1]{0:T(128)} %dynamic_slice.23.size_ref, s32[24]{0:T(128)S(1)} %fusion.3.turn_ref.source_ref, bf16[8,256,256]{2,1,0:T(8,128)(2,1)S(1)} %copy-done, bf16[2,172,256]{2,1,0:T(8,128)(2,1)S(1)} %bitcast.9, s32[1,416]{1,0:T(1,128)S(1)} %compare_select_fusion.2.row_ref, ...), custom_call_target="tpu_custom_call" | custom-call | tf_op jit(solution)/shard_map/upper_layers/pallas_call | solution.py:264
  108.2 4.4 %collective-permute-start.10 = (bf16[304,256]{1,0:T(8,128)(2,1)S(1)}, bf16[304,256]{1,0:T(8,128)(2,1)S(1)}, u32[]{:S(2)}, u32[]{:S(2)}) collective-permute-start(bf16[304,256]{1,0:T(8,128)(2,1)S(1)} %get-tuple-element.82.rest_8_), channel_id=1, source_target_pairs={{0,8},{8,16},{16,24},{24,28},{28,20},{20,12},{12,4},{4,0},{1,9},{9... | collective-permute-start | bytes 466952 | tf_op jit(solution)/shard_map/ppermute | solution.py:352
  112.6 2.0 %collective-permute-start.18 = (bf16[304,256]{1,0:T(8,128)(2,1)S(1)}, bf16[304,256]{1,0:T(8,128)(2,1)S(1)}, u32[]{:S(2)}, u32[]{:S(2)}) collective-permute-start(bf16[304,256]{1,0:T(8,128)(2,1)S(1)} %get-tuple-element.83.rest_16_), channel_id=1, source_target_pairs={{0,8},{8,16},{16,24},{24,28},{28,20},{20,12},{12,4},{4,0},{1,9},{9... | collective-permute-start | bytes 466952 | tf_op jit(solution)/shard_map/ppermute | solution.py:352
  114.6 2.5 %collective-permute-done.10.rest_15_ = bf16[304,256]{1,0:T(8,128)(2,1)S(1)} collective-permute-done((bf16[304,256]{1,0:T(8,128)(2,1)S(1)}, bf16[304,256]{1,0:T(8,128)(2,1)S(1)}, u32[]{:S(2)}, u32[]{:S(2)}) %collective-permute-start.10) | collective-permute-done | bytes 155680 | tf_op jit(solution)/shard_map/ppermute | solution.py:352
  117.1 2.5 %collective-permute-start.11 = (bf16[304,256]{1,0:T(8,128)(2,1)S(1)}, bf16[304,256]{1,0:T(8,128)(2,1)S(1)}, u32[]{:S(2)}, u32[]{:S(2)}) collective-permute-start(bf16[304,256]{1,0:T(8,128)(2,1)S(1)} %collective-permute-done.10.rest_15_), channel_id=1, source_target_pairs={{0,8},{8,16},{16,24},{24,28},{28,20},{20,12},{12,4},{4,0},{1,9},{9... | collective-permute-start | bytes 466952 | tf_op jit(solution)/shard_map/ppermute | solution.py:352
  119.6 0.8 collective-permute-done.18.rest_23_
  120.4 2.5 %collective-permute-start.19 = (bf16[304,256]{1,0:T(8,128)(2,1)S(1)}, bf16[304,256]{1,0:T(8,128)(2,1)S(1)}, u32[]{:S(2)}, u32[]{:S(2)}) collective-permute-start(bf16[304,256]{1,0:T(8,128)(2,1)S(1)} %collective-permute-done.18.rest_23_), channel_id=1, source_target_pairs={{0,8},{8,16},{16,24},{24,28},{28,20},{20,12},{12,4},{4,0},{1,9},{9... | collective-permute-start | bytes 466952 | tf_op jit(solution)/shard_map/ppermute | solution.py:352
  122.9 1.1 collective-permute-done.11.rest_14_
  124.0 2.5 %collective-permute-start.12 = (bf16[304,256]{1,0:T(8,128)(2,1)S(1)}, bf16[304,256]{1,0:T(8,128)(2,1)S(1)}, u32[]{:S(2)}, u32[]{:S(2)}) collective-permute-start(bf16[304,256]{1,0:T(8,128)(2,1)S(1)} %collective-permute-done.11.rest_14_), channel_id=1, source_target_pairs={{0,8},{8,16},{16,24},{24,28},{28,20},{20,12},{12,4},{4,0},{1,9},{9... | collective-permute-start | bytes 466952 | tf_op jit(solution)/shard_map/ppermute | solution.py:352
  126.5 0.8 collective-permute-done.19.rest_22_
  127.4 2.5 %collective-permute-start.20 = (bf16[304,256]{1,0:T(8,128)(2,1)S(1)}, bf16[304,256]{1,0:T(8,128)(2,1)S(1)}, u32[]{:S(2)}, u32[]{:S(2)}) collective-permute-start(bf16[304,256]{1,0:T(8,128)(2,1)S(1)} %collective-permute-done.19.rest_22_), channel_id=1, source_target_pairs={{0,8},{8,16},{16,24},{24,28},{28,20},{20,12},{12,4},{4,0},{1,9},{9... | collective-permute-start | bytes 466952 | tf_op jit(solution)/shard_map/ppermute | solution.py:352
  129.9 1.1 collective-permute-done.12.rest_13_
  131.0 2.5 %collective-permute-start.13 = (bf16[304,256]{1,0:T(8,128)(2,1)S(1)}, bf16[304,256]{1,0:T(8,128)(2,1)S(1)}, u32[]{:S(2)}, u32[]{:S(2)}) collective-permute-start(bf16[304,256]{1,0:T(8,128)(2,1)S(1)} %collective-permute-done.12.rest_13_), channel_id=1, source_target_pairs={{0,8},{8,16},{16,24},{24,28},{28,20},{20,12},{12,4},{4,0},{1,9},{9... | collective-permute-start | bytes 466952 | tf_op jit(solution)/shard_map/ppermute | solution.py:352
  133.7 2.2 %collective-permute-done.9.rest_11_ = bf16[304,256]{1,0:T(8,128)(2,1)S(1)} collective-permute-done((bf16[304,256]{1,0:T(8,128)(2,1)S(1)}, bf16[304,256]{1,0:T(8,128)(2,1)S(1)}, u32[]{:S(2)}, u32[]{:S(2)}) %collective-permute-start.9) | collective-permute-done | bytes 155680 | tf_op jit(solution)/shard_map/ppermute | solution.py:352
  136.2 2.5 %collective-permute-done.17.rest_20_ = bf16[304,256]{1,0:T(8,128)(2,1)S(1)} collective-permute-done((bf16[304,256]{1,0:T(8,128)(2,1)S(1)}, bf16[304,256]{1,0:T(8,128)(2,1)S(1)}, u32[]{:S(2)}, u32[]{:S(2)}) %collective-permute-start.17) | collective-permute-done | bytes 155680 | tf_op jit(solution)/shard_map/ppermute | solution.py:352
  138.7 1.5 grad_layer.1
  140.3 2.0 %collective-permute-done.21 = f32[608,256]{1,0:T(8,128)S(1)} collective-permute-done((f32[608,256]{1,0:T(8,128)S(1)}, f32[608,256]{1,0:T(8,128)S(1)}, u32[]{:S(2)}, u32[]{:S(2)}) %collective-permute-start.21) | collective-permute-done | bytes 622624 | tf_op jit(solution)/shard_map/ppermute | solution.py:385
  142.6 9.4 %collective-permute-done.22.other_ref = bf16[608,256]{1,0:T(8,128)(2,1)S(1)} collective-permute-done((bf16[608,256]{1,0:T(8,128)(2,1)S(1)}, bf16[608,256]{1,0:T(8,128)(2,1)S(1)}, u32[]{:S(2)}, u32[]{:S(2)}) %collective-permute-start.22) | collective-permute-done | bytes 311328 | tf_op jit(solution)/shard_map/ppermute | solution.py:389
  152.7 2.0 %final_sum.1 = (f32[2,128,256]{2,1,0:T(8,128)}, f32[172,2,256]{2,1,0:T(2,128)}) custom-call(bf16[608,256]{1,0:T(8,128)(2,1)} %copy-done.1, bf16[608,256]{1,0:T(8,128)(2,1)} %copy-done.2), custom_call_target="tpu_custom_call" | custom-call | tf_op jit(solution)/shard_map/final_sum/pallas_call | solution.py:333
  (60 shorter events, 9.3 us)
Async XLA Ops:
  7.2 96.7 %all-gather.2.cloned.1.call-start = ((), (), s32[]{:S(2)}) async-start(), calls=%async_computation | async-start | bytes 1179648 | tf_op jit(solution)/shard_map/all_gather | solution.py:433
  52.8 21.3 %collective-permute-start = (bf16[416,256]{1,0:T(8,128)(2,1)S(1)}, bf16[416,256]{1,0:T(8,128)(2,1)S(1)}, u32[]{:S(2)}, u32[]{:S(2)}) collective-permute-start(bf16[416,256]{1,0:T(8,128)(2,1)S(1)} %get-tuple-element.55.rest_0_), channel_id=1, source_target_pairs={{0,16},{4,20},{8,24},{12,28},{16,0},{20,4},{24,8},{28,12},{1,17},{... | collective-permute-start | bytes 638984 | tf_op jit(solution)/shard_map/ppermute | solution.py:364
  60.3 13.8 %collective-permute-start.1 = (bf16[416,256]{1,0:T(8,128)(2,1)S(1)}, bf16[416,256]{1,0:T(8,128)(2,1)S(1)}, u32[]{:S(2)}, u32[]{:S(2)}) collective-permute-start(bf16[416,256]{1,0:T(8,128)(2,1)S(1)} %get-tuple-element.56.rest_1_), channel_id=1, source_target_pairs={{0,12},{4,8},{8,4},{12,0},{16,28},{20,24},{24,20},{28,16},{1,13},{... | collective-permute-start | bytes 638984 | tf_op jit(solution)/shard_map/ppermute | solution.py:364
  60.6 16.0 %collective-permute-start.2 = (bf16[416,256]{1,0:T(8,128)(2,1)S(1)}, bf16[416,256]{1,0:T(8,128)(2,1)S(1)}, u32[]{:S(2)}, u32[]{:S(2)}) collective-permute-start(bf16[416,256]{1,0:T(8,128)(2,1)S(1)} %get-tuple-element.57.rest_2_), channel_id=1, source_target_pairs={{0,20},{4,16},{8,28},{12,24},{16,4},{20,0},{24,12},{28,8},{1,21},{... | collective-permute-start | bytes 638984 | tf_op jit(solution)/shard_map/ppermute | solution.py:364
  74.1 25.6 %copy-start.3 = (bf16[2,256,172]{1,0,2:T(2,128)(2,1)S(1)}, bf16[2,256,172]{1,0,2:T(2,128)(2,1)}, u32[]{:S(2)}) copy-start(bf16[2,256,172]{1,0,2:T(2,128)(2,1)} %param.13) | copy-start | bytes 528388
  76.6 20.3 %collective-permute-start.3 = (bf16[416,256]{1,0:T(8,128)(2,1)S(1)}, bf16[416,256]{1,0:T(8,128)(2,1)S(1)}, u32[]{:S(2)}, u32[]{:S(2)}) collective-permute-start(bf16[416,256]{1,0:T(8,128)(2,1)S(1)} %get-tuple-element.63.rest_3_), channel_id=1, source_target_pairs={{0,24},{4,28},{8,16},{12,20},{16,8},{20,12},{24,0},{28,4},{1,25},{... | collective-permute-start | bytes 638984 | tf_op jit(solution)/shard_map/ppermute | solution.py:364
  84.1 12.8 %collective-permute-start.4 = (bf16[416,256]{1,0:T(8,128)(2,1)S(1)}, bf16[416,256]{1,0:T(8,128)(2,1)S(1)}, u32[]{:S(2)}, u32[]{:S(2)}) collective-permute-start(bf16[416,256]{1,0:T(8,128)(2,1)S(1)} %get-tuple-element.64.rest_4_), channel_id=1, source_target_pairs={{0,8},{4,12},{8,0},{12,4},{16,24},{20,28},{24,16},{28,20},{1,9},{5... | collective-permute-start | bytes 638984 | tf_op jit(solution)/shard_map/ppermute | solution.py:364
  84.1 13.3 %collective-permute-start.5 = (bf16[416,256]{1,0:T(8,128)(2,1)S(1)}, bf16[416,256]{1,0:T(8,128)(2,1)S(1)}, u32[]{:S(2)}, u32[]{:S(2)}) collective-permute-start(bf16[416,256]{1,0:T(8,128)(2,1)S(1)} %get-tuple-element.65.rest_5_), channel_id=1, source_target_pairs={{0,28},{4,24},{8,20},{12,16},{16,12},{20,8},{24,4},{28,0},{1,29},{... | collective-permute-start | bytes 638984 | tf_op jit(solution)/shard_map/ppermute | solution.py:364
  97.4 6.4 %collective-permute-start.6 = (bf16[416,256]{1,0:T(8,128)(2,1)S(1)}, bf16[416,256]{1,0:T(8,128)(2,1)S(1)}, u32[]{:S(2)}, u32[]{:S(2)}) collective-permute-start(bf16[416,256]{1,0:T(8,128)(2,1)S(1)} %get-tuple-element.69.rest_6_), channel_id=1, source_target_pairs={{0,4},{4,0},{8,12},{12,8},{16,20},{20,16},{24,28},{28,24},{1,5},{5... | collective-permute-start | bytes 638984 | tf_op jit(solution)/shard_map/ppermute | solution.py:364
  103.9 1.2 copy-start
  108.2 8.8 %collective-permute-start.10 = (bf16[304,256]{1,0:T(8,128)(2,1)S(1)}, bf16[304,256]{1,0:T(8,128)(2,1)S(1)}, u32[]{:S(2)}, u32[]{:S(2)}) collective-permute-start(bf16[304,256]{1,0:T(8,128)(2,1)S(1)} %get-tuple-element.82.rest_8_), channel_id=1, source_target_pairs={{0,8},{8,16},{16,24},{24,28},{28,20},{20,12},{12,4},{4,0},{1,9},{9... | collective-permute-start | bytes 466952 | tf_op jit(solution)/shard_map/ppermute | solution.py:352
  112.6 7.0 %collective-permute-start.14 = (bf16[304,256]{1,0:T(8,128)(2,1)S(1)}, bf16[304,256]{1,0:T(8,128)(2,1)S(1)}, u32[]{:S(2)}, u32[]{:S(2)}) collective-permute-start(bf16[304,256]{1,0:T(8,128)(2,1)S(1)} %get-tuple-element.83.rest_16_), channel_id=1, source_target_pairs={{0,4},{8,0},{16,8},{24,16},{28,24},{20,28},{12,20},{4,12},{1,5},{9... | collective-permute-start | bytes 466952 | tf_op jit(solution)/shard_map/ppermute | solution.py:352
  112.6 7.8 %collective-permute-start.18 = (bf16[304,256]{1,0:T(8,128)(2,1)S(1)}, bf16[304,256]{1,0:T(8,128)(2,1)S(1)}, u32[]{:S(2)}, u32[]{:S(2)}) collective-permute-start(bf16[304,256]{1,0:T(8,128)(2,1)S(1)} %get-tuple-element.83.rest_16_), channel_id=1, source_target_pairs={{0,8},{8,16},{16,24},{24,28},{28,20},{20,12},{12,4},{4,0},{1,9},{9... | collective-permute-start | bytes 466952 | tf_op jit(solution)/shard_map/ppermute | solution.py:352
  114.6 8.3 %collective-permute-start.7 = (bf16[304,256]{1,0:T(8,128)(2,1)S(1)}, bf16[304,256]{1,0:T(8,128)(2,1)S(1)}, u32[]{:S(2)}, u32[]{:S(2)}) collective-permute-start(bf16[304,256]{1,0:T(8,128)(2,1)S(1)} %get-tuple-element.82.rest_8_), channel_id=1, source_target_pairs={{0,4},{8,0},{16,8},{24,16},{28,24},{20,28},{12,20},{4,12},{1,5},{9... | collective-permute-start | bytes 466952 | tf_op jit(solution)/shard_map/ppermute | solution.py:352
  117.1 7.0 %collective-permute-start.11 = (bf16[304,256]{1,0:T(8,128)(2,1)S(1)}, bf16[304,256]{1,0:T(8,128)(2,1)S(1)}, u32[]{:S(2)}, u32[]{:S(2)}) collective-permute-start(bf16[304,256]{1,0:T(8,128)(2,1)S(1)} %collective-permute-done.10.rest_15_), channel_id=1, source_target_pairs={{0,8},{8,16},{16,24},{24,28},{28,20},{20,12},{12,4},{4,0},{1,9},{9... | collective-permute-start | bytes 466952 | tf_op jit(solution)/shard_map/ppermute | solution.py:352
  119.6 7.0 %collective-permute-start.15 = (bf16[304,256]{1,0:T(8,128)(2,1)S(1)}, bf16[304,256]{1,0:T(8,128)(2,1)S(1)}, u32[]{:S(2)}, u32[]{:S(2)}) collective-permute-start(bf16[304,256]{1,0:T(8,128)(2,1)S(1)} %collective-permute-done.14.rest_17_), channel_id=1, source_target_pairs={{0,4},{8,0},{16,8},{24,16},{28,24},{20,28},{12,20},{4,12},{1,5},{9... | collective-permute-start | bytes 466952 | tf_op jit(solution)/shard_map/ppermute | solution.py:352
  120.4 7.0 %collective-permute-start.19 = (bf16[304,256]{1,0:T(8,128)(2,1)S(1)}, bf16[304,256]{1,0:T(8,128)(2,1)S(1)}, u32[]{:S(2)}, u32[]{:S(2)}) collective-permute-start(bf16[304,256]{1,0:T(8,128)(2,1)S(1)} %collective-permute-done.18.rest_23_), channel_id=1, source_target_pairs={{0,8},{8,16},{16,24},{24,28},{28,20},{20,12},{12,4},{4,0},{1,9},{9... | collective-permute-start | bytes 466952 | tf_op jit(solution)/shard_map/ppermute | solution.py:352
  122.9 7.0 %collective-permute-start.8 = (bf16[304,256]{1,0:T(8,128)(2,1)S(1)}, bf16[304,256]{1,0:T(8,128)(2,1)S(1)}, u32[]{:S(2)}, u32[]{:S(2)}) collective-permute-start(bf16[304,256]{1,0:T(8,128)(2,1)S(1)} %collective-permute-done.7.rest_9_), channel_id=1, source_target_pairs={{0,4},{8,0},{16,8},{24,16},{28,24},{20,28},{12,20},{4,12},{1,5},{9... | collective-permute-start | bytes 466952 | tf_op jit(solution)/shard_map/ppermute | solution.py:352
  124.0 7.0 %collective-permute-start.12 = (bf16[304,256]{1,0:T(8,128)(2,1)S(1)}, bf16[304,256]{1,0:T(8,128)(2,1)S(1)}, u32[]{:S(2)}, u32[]{:S(2)}) collective-permute-start(bf16[304,256]{1,0:T(8,128)(2,1)S(1)} %collective-permute-done.11.rest_14_), channel_id=1, source_target_pairs={{0,8},{8,16},{16,24},{24,28},{28,20},{20,12},{12,4},{4,0},{1,9},{9... | collective-permute-start | bytes 466952 | tf_op jit(solution)/shard_map/ppermute | solution.py:352
  126.5 7.0 %collective-permute-start.16 = (bf16[304,256]{1,0:T(8,128)(2,1)S(1)}, bf16[304,256]{1,0:T(8,128)(2,1)S(1)}, u32[]{:S(2)}, u32[]{:S(2)}) collective-permute-start(bf16[304,256]{1,0:T(8,128)(2,1)S(1)} %collective-permute-done.15.rest_18_), channel_id=1, source_target_pairs={{0,4},{8,0},{16,8},{24,16},{28,24},{20,28},{12,20},{4,12},{1,5},{9... | collective-permute-start | bytes 466952 | tf_op jit(solution)/shard_map/ppermute | solution.py:352
  127.4 6.4 %collective-permute-start.20 = (bf16[304,256]{1,0:T(8,128)(2,1)S(1)}, bf16[304,256]{1,0:T(8,128)(2,1)S(1)}, u32[]{:S(2)}, u32[]{:S(2)}) collective-permute-start(bf16[304,256]{1,0:T(8,128)(2,1)S(1)} %collective-permute-done.19.rest_22_), channel_id=1, source_target_pairs={{0,8},{8,16},{16,24},{24,28},{28,20},{20,12},{12,4},{4,0},{1,9},{9... | collective-permute-start | bytes 466952 | tf_op jit(solution)/shard_map/ppermute | solution.py:352
  129.9 6.0 %collective-permute-start.9 = (bf16[304,256]{1,0:T(8,128)(2,1)S(1)}, bf16[304,256]{1,0:T(8,128)(2,1)S(1)}, u32[]{:S(2)}, u32[]{:S(2)}) collective-permute-start(bf16[304,256]{1,0:T(8,128)(2,1)S(1)} %collective-permute-done.8.rest_10_), channel_id=1, source_target_pairs={{0,4},{8,0},{16,8},{24,16},{28,24},{20,28},{12,20},{4,12},{1,5},{9... | collective-permute-start | bytes 466952 | tf_op jit(solution)/shard_map/ppermute | solution.py:352
  131.0 5.2 %collective-permute-start.13 = (bf16[304,256]{1,0:T(8,128)(2,1)S(1)}, bf16[304,256]{1,0:T(8,128)(2,1)S(1)}, u32[]{:S(2)}, u32[]{:S(2)}) collective-permute-start(bf16[304,256]{1,0:T(8,128)(2,1)S(1)} %collective-permute-done.12.rest_13_), channel_id=1, source_target_pairs={{0,8},{8,16},{16,24},{24,28},{28,20},{20,12},{12,4},{4,0},{1,9},{9... | collective-permute-start | bytes 466952 | tf_op jit(solution)/shard_map/ppermute | solution.py:352
  133.5 5.2 %collective-permute-start.17 = (bf16[304,256]{1,0:T(8,128)(2,1)S(1)}, bf16[304,256]{1,0:T(8,128)(2,1)S(1)}, u32[]{:S(2)}, u32[]{:S(2)}) collective-permute-start(bf16[304,256]{1,0:T(8,128)(2,1)S(1)} %collective-permute-done.16.rest_19_), channel_id=1, source_target_pairs={{0,4},{8,0},{16,8},{24,16},{28,24},{20,28},{12,20},{4,12},{1,5},{9... | collective-permute-start | bytes 466952 | tf_op jit(solution)/shard_map/ppermute | solution.py:352
  140.3 2.1 %collective-permute-start.21 = (f32[608,256]{1,0:T(8,128)S(1)}, f32[608,256]{1,0:T(8,128)S(1)}, u32[]{:S(2)}, u32[]{:S(2)}) collective-permute-start(f32[608,256]{1,0:T(8,128)S(1)} %grad_layer.1), channel_id=1, source_target_pairs={{0,1},{1,0},{2,3},{3,2},{4,5},{5,4},{6,7},{7,6},{8,9},{9,8},{10,11... | collective-permute-start | bytes 1867784 | tf_op jit(solution)/shard_map/ppermute | solution.py:385
  142.5 9.5 %copy-start.1 = (bf16[608,256]{1,0:T(8,128)(2,1)}, bf16[608,256]{1,0:T(8,128)(2,1)S(1)}, u32[]{:S(2)}) copy-start(bf16[608,256]{1,0:T(8,128)(2,1)S(1)} %add_convert_fusion.mine_ref) | copy-start | bytes 933892
  142.5 9.5 %collective-permute-start.22 = (bf16[608,256]{1,0:T(8,128)(2,1)S(1)}, bf16[608,256]{1,0:T(8,128)(2,1)S(1)}, u32[]{:S(2)}, u32[]{:S(2)}) collective-permute-start(bf16[608,256]{1,0:T(8,128)(2,1)S(1)} %add_convert_fusion.mine_ref), channel_id=1, source_target_pairs={{0,2},{1,3},{2,0},{3,1},{4,6},{5,7},{6,4},{7,5},{8,10},{9,11},{10,... | collective-permute-start | bytes 933896 | tf_op jit(solution)/shard_map/ppermute | solution.py:389
  152.0 0.7 copy-start.2
Sparse Core Ops, SparseCore 0:
  10.1 42.8 all-gather.1

commit v11 on v10

--- a/solution.py
+++ b/solution.py
@@ -447,9 +447,12 @@
         if call < CALLS - 1:
             table, blocks, arrived = lax.optimization_barrier((table, blocks, arrived))
         else:
-            blocks, arrived, order, hop1_count, label_ids, sizes, second_layer = lax.optimization_barrier(
-                (blocks, arrived, order, hop1_count, label_ids, sizes, second_layer)
+            blocks, arrived, order, hop1_count, label_ids, sizes, second_layer, weights = (
+                lax.optimization_barrier(
+                    (blocks, arrived, order, hop1_count, label_ids, sizes, second_layer, weights)
+                )
             )
+            weights = jnp.where(turn[0] >= 0, weights, jnp.zeros_like(weights))
         inputs += blocks
         received += arrived
         arrived = [exchange(block, t, count) if t else block for t, block in zip(places[begin:end], blocks)]

time: 162 us -> 160 us (0.988)
  Pallas kernels: 67.2 us -> 70.1 us
  waiting for transfers between devices: 29.6 us -> 27.1 us
    pallas_call x3, Pallas kernels: 41.4 us -> 44.3 us  [gather_layer(): pl.pallas_call(functools.partial(gather_kernel, fanout, capacity), grid_s...]
    ppermute x7, starting transfers between devices: 17.7 us -> 14.9 us  [exchange(): lax.ppermute(array, 'feat', [(i, partner(i, number, count)) for i in rang...]
    ppermute x7, waiting for transfers between devices: 5.81 us -> 3.3 us  [exchange(): lax.ppermute(array, 'feat', [(i, partner(i, number, count)) for i in rang...]
    ppermute x14, starting transfers between devices: 18.8 us -> 20.4 us  [send_along(): lax.ppermute(array, 'feat', [(ring[i], ring[(i + shift) % count]) for i i...]
  transfers between devices with their start and end apart: 24 -> 24, of which waited for: 14 -> 12; matrix products, arithmetic and copies ran while one was open for 7% -> 8% of each run, Pallas kernels for 38% -> 39%
where the time goes in v11:
time: 160 us; the launch traced here: 161 us
  Pallas kernels  70.1 us (44%)
  starting transfers between devices  35.5 us (22%)
  waiting for transfers between devices  27.1 us (17%)
  between operations  14.3 us (9%)
  other arithmetic  8.8 us (6%)
  local copies, waits for them, and re-layouts  5.1 us (3%)
    pallas_call x3, Pallas kernels, gather_layer(): pl.pallas_call(functools.partial(gather_kernel, fanout, capacity), grid_s...  44.3 us
    ppermute x14, starting transfers between devices, send_along(): lax.ppermute(array, 'feat', [(ring[i], ring[(i + shift) % count]) for i i...  20.4 us
    pallas_call x1, Pallas kernels, build_table(): pl.pallas_call(table_kernel, grid=(nodes // chunk,), in_specs=[pl.BlockSp...  19.2 us
    ppermute x7, starting transfers between devices, exchange(): lax.ppermute(array, 'feat', [(i, partner(i, number, count)) for i in rang...  14.9 us
    ppermute x14, waiting for transfers between devices, send_along(): lax.ppermute(array, 'feat', [(ring[i], ring[(i + shift) % count]) for i i...  11.7 us
    ppermute x1, waiting for transfers between devices, group_sum(): other = lax.ppermute(mine, 'dp', [(i, i ^ stride) for i in range(count)])  9.39 us
    ppermute x7, waiting for transfers between devices, exchange(): lax.ppermute(array, 'feat', [(i, partner(i, number, count)) for i in rang...  3.3 us
  transfers between devices with their start and end apart: 24, of which 12 were waited for; matrix products, arithmetic and copies ran while one was open for 8% of the time, Pallas kernels for 39%

profile of v11, /device:TPU:0, one launch (start us, length us, event | category | flops | bytes accessed | tf_op | source)
XLA Modules:
  0.0 160.9 jit_solution(16497144856096840654)
XLA Ops:
  10.8 2.5 %convert_reduce_fusion = s32[8,704]{1,0:T(8,128)S(1)} fusion(s32[8,704]{1,0:T(8,128)S(1)} %get-tuple-element.88), kind=kLoop, calls=%fused_computation | loop fusion | flops 11889152 | bytes 45056 | tf_op jit(solution)/shard_map/reduce_sum | solution.py:31
  13.3 2.1 %select_reduce_fusion = s32[8,512]{1,0:T(8,128)S(1)} fusion(s32[8,704]{1,0:T(8,128)S(1)} %broadcast_add_fusion, s32[8,704]{1,0:T(8,128)S(1)} %convert_reduce_fusion), kind=kLoop, calls=%fused_computation.1 | loop fusion | flops 8646656 | bytes 61440 | tf_op jit(solution)/shard_map/reduce_sum | solution.py:33
  15.4 1.1 broadcast_in_dim.64.near_ref
  18.4 19.2 %build_table.1.table_ref = bf16[131072,128]{1,0:T(8,128)(2,1)S(1)} custom-call(bf16[128,131072]{1,0:T(8,128)(2,1)} %refs_3_, bf16[128,131072]{1,0:T(8,128)(2,1)} %refs_3_, bf16[128,131072]{1,0:T(8,128)(2,1)} %refs_3_, bf16[128,131072]{1,0:T(8,128)(2,1)} %refs_3_), custom_call_target="tpu_custom_call" | custom-call | tf_op jit(solution)/shard_map/build_table/pallas_call | solution.py:75
  37.6 17.5 %gather_layer.3 = (bf16[416,256]{1,0:T(8,128)(2,1)S(1)}, bf16[416,256]{1,0:T(8,128)(2,1)S(1)}, bf16[416,256]{1,0:T(8,128)(2,1)S(1)}, bf16[131072,128]{1,0:T(8,128)(2,1)S(1)}) custom-call(s32[24]{0:T(128)S(1)} %fusion.3.turn_ref.source_ref, s32[8,1,16]{2,1,0:T(1,128)S(1)} %bitcast.12, ...), custom_call_target="tpu_custom_call", output_to_operand_aliasing={{3}: (6, {})} | custom-call | bytes 51118080 | tf_op jit(solution)/shard_map/gather_layer/pallas_call | solution.py:175
  55.6 7.5 %collective-permute-start.1 = (bf16[416,256]{1,0:T(8,128)(2,1)S(1)}, bf16[416,256]{1,0:T(8,128)(2,1)S(1)}, u32[]{:S(2)}, u32[]{:S(2)}) collective-permute-start(bf16[416,256]{1,0:T(8,128)(2,1)S(1)} %get-tuple-element.57.rest_1_), channel_id=1, source_target_pairs={{0,12},{4,8},{8,4},{12,0},{16,28},{20,24},{24,20},{28,16},{1,13},{... | collective-permute-start | bytes 638984 | tf_op jit(solution)/shard_map/ppermute | solution.py:364
  63.1 17.4 %gather_layer.4 = (bf16[416,256]{1,0:T(8,128)(2,1)S(1)}, bf16[416,256]{1,0:T(8,128)(2,1)S(1)}, bf16[416,256]{1,0:T(8,128)(2,1)S(1)}, bf16[131072,128]{1,0:T(8,128)(2,1)S(1)}) custom-call(s32[24]{0:T(128)S(1)} %fusion.3.turn_ref.source_ref, s32[8,1,16]{2,1,0:T(1,128)S(1)} %bitcast.13, ...), custom_call_target="tpu_custom_call", output_to_operand_aliasing={{3}: (6, {})} | custom-call | bytes 51118080 | tf_op jit(solution)/shard_map/gather_layer/pallas_call | solution.py:175
  80.8 3.4 %collective-permute-start.4 = (bf16[416,256]{1,0:T(8,128)(2,1)S(1)}, bf16[416,256]{1,0:T(8,128)(2,1)S(1)}, u32[]{:S(2)}, u32[]{:S(2)}) collective-permute-start(bf16[416,256]{1,0:T(8,128)(2,1)S(1)} %get-tuple-element.65.rest_4_), channel_id=1, source_target_pairs={{0,8},{4,12},{8,0},{12,4},{16,24},{20,28},{24,16},{28,20},{1,9},{5... | collective-permute-start | bytes 638984 | tf_op jit(solution)/shard_map/ppermute | solution.py:364
  84.2 1.7 %collective-permute-start.5 = (bf16[416,256]{1,0:T(8,128)(2,1)S(1)}, bf16[416,256]{1,0:T(8,128)(2,1)S(1)}, u32[]{:S(2)}, u32[]{:S(2)}) collective-permute-start(bf16[416,256]{1,0:T(8,128)(2,1)S(1)} %get-tuple-element.66.rest_5_), channel_id=1, source_target_pairs={{0,28},{4,24},{8,20},{12,16},{16,12},{20,8},{24,4},{28,0},{1,29},{... | collective-permute-start | bytes 638984 | tf_op jit(solution)/shard_map/ppermute | solution.py:364
  85.9 9.4 %gather_layer.5 = (bf16[416,256]{1,0:T(8,128)(2,1)S(1)}, bf16[416,256]{1,0:T(8,128)(2,1)S(1)}, bf16[131072,128]{1,0:T(8,128)(2,1)S(1)}) custom-call(s32[24]{0:T(128)S(1)} %fusion.3.turn_ref.source_ref, s32[8,1,16]{2,1,0:T(1,128)S(1)} %bitcast.14, s32[8,1,512]{2,1,0:T(1,128)S(1)} %broadcast_in_dim.62.order_ref, ...), custom_call_target="tpu_custom_call", output_to_operand_aliasing={{2}: (6, {})} | custom-call | bytes 34078720 | tf_op jit(solution)/shard_map/gather_layer/pallas_call | solution.py:175
  95.3 1.7 %collective-permute-done.5.rest_5_ = bf16[416,256]{1,0:T(8,128)(2,1)S(1)} collective-permute-done((bf16[416,256]{1,0:T(8,128)(2,1)S(1)}, bf16[416,256]{1,0:T(8,128)(2,1)S(1)}, u32[]{:S(2)}, u32[]{:S(2)}) %collective-permute-start.5) | collective-permute-done | bytes 213024 | tf_op jit(solution)/shard_map/ppermute | solution.py:364
  97.0 1.6 collective-permute-start.6
  99.9 1.3 broadcast_select_fusion.weights_ref
  101.2 1.6 collective-permute-done.6.rest_6_
  102.9 3.1 %upper_layers.1 = (bf16[304,256]{1,0:T(8,128)(2,1)S(1)}, bf16[304,256]{1,0:T(8,128)(2,1)S(1)}) custom-call(s32[1]{0:T(128)} %dynamic_slice.23.size_ref, s32[24]{0:T(128)S(1)} %fusion.3.turn_ref.source_ref, bf16[8,256,256]{2,1,0:T(8,128)(2,1)S(1)} %broadcast_select_fusion.weights_ref, bf16[2,172,256]{2,1,0:T(8,128)(2,1)S(1)} %bitcast.11, ...), custom_call_target="tpu_custom_call" | custom-call | tf_op jit(solution)/shard_map/upper_layers/pallas_call | solution.py:264
  106.0 6.0 %collective-permute-start.10 = (bf16[304,256]{1,0:T(8,128)(2,1)S(1)}, bf16[304,256]{1,0:T(8,128)(2,1)S(1)}, u32[]{:S(2)}, u32[]{:S(2)}) collective-permute-start(bf16[304,256]{1,0:T(8,128)(2,1)S(1)} %get-tuple-element.84.rest_8_), channel_id=1, source_target_pairs={{0,8},{8,16},{16,24},{24,28},{28,20},{20,12},{12,4},{4,0},{1,9},{9... | collective-permute-start | bytes 466952 | tf_op jit(solution)/shard_map/ppermute | solution.py:352
  112.0 2.0 %collective-permute-start.18 = (bf16[304,256]{1,0:T(8,128)(2,1)S(1)}, bf16[304,256]{1,0:T(8,128)(2,1)S(1)}, u32[]{:S(2)}, u32[]{:S(2)}) collective-permute-start(bf16[304,256]{1,0:T(8,128)(2,1)S(1)} %get-tuple-element.85.rest_16_), channel_id=1, source_target_pairs={{0,8},{8,16},{16,24},{24,28},{28,20},{20,12},{12,4},{4,0},{1,9},{9... | collective-permute-start | bytes 466952 | tf_op jit(solution)/shard_map/ppermute | solution.py:352
  114.0 2.5 %collective-permute-done.10.rest_15_ = bf16[304,256]{1,0:T(8,128)(2,1)S(1)} collective-permute-done((bf16[304,256]{1,0:T(8,128)(2,1)S(1)}, bf16[304,256]{1,0:T(8,128)(2,1)S(1)}, u32[]{:S(2)}, u32[]{:S(2)}) %collective-permute-start.10) | collective-permute-done | bytes 155680 | tf_op jit(solution)/shard_map/ppermute | solution.py:352
  116.5 2.5 %collective-permute-start.11 = (bf16[304,256]{1,0:T(8,128)(2,1)S(1)}, bf16[304,256]{1,0:T(8,128)(2,1)S(1)}, u32[]{:S(2)}, u32[]{:S(2)}) collective-permute-start(bf16[304,256]{1,0:T(8,128)(2,1)S(1)} %collective-permute-done.10.rest_15_), channel_id=1, source_target_pairs={{0,8},{8,16},{16,24},{24,28},{28,20},{20,12},{12,4},{4,0},{1,9},{9... | collective-permute-start | bytes 466952 | tf_op jit(solution)/shard_map/ppermute | solution.py:352
  119.8 2.5 %collective-permute-start.19 = (bf16[304,256]{1,0:T(8,128)(2,1)S(1)}, bf16[304,256]{1,0:T(8,128)(2,1)S(1)}, u32[]{:S(2)}, u32[]{:S(2)}) collective-permute-start(bf16[304,256]{1,0:T(8,128)(2,1)S(1)} %collective-permute-done.18.rest_23_), channel_id=1, source_target_pairs={{0,8},{8,16},{16,24},{24,28},{28,20},{20,12},{12,4},{4,0},{1,9},{9... | collective-permute-start | bytes 466952 | tf_op jit(solution)/shard_map/ppermute | solution.py:352
  122.3 1.1 collective-permute-done.11.rest_14_
  123.4 2.5 %collective-permute-start.12 = (bf16[304,256]{1,0:T(8,128)(2,1)S(1)}, bf16[304,256]{1,0:T(8,128)(2,1)S(1)}, u32[]{:S(2)}, u32[]{:S(2)}) collective-permute-start(bf16[304,256]{1,0:T(8,128)(2,1)S(1)} %collective-permute-done.11.rest_14_), channel_id=1, source_target_pairs={{0,8},{8,16},{16,24},{24,28},{28,20},{20,12},{12,4},{4,0},{1,9},{9... | collective-permute-start | bytes 466952 | tf_op jit(solution)/shard_map/ppermute | solution.py:352
  126.8 2.5 %collective-permute-start.20 = (bf16[304,256]{1,0:T(8,128)(2,1)S(1)}, bf16[304,256]{1,0:T(8,128)(2,1)S(1)}, u32[]{:S(2)}, u32[]{:S(2)}) collective-permute-start(bf16[304,256]{1,0:T(8,128)(2,1)S(1)} %collective-permute-done.19.rest_22_), channel_id=1, source_target_pairs={{0,8},{8,16},{16,24},{24,28},{28,20},{20,12},{12,4},{4,0},{1,9},{9... | collective-permute-start | bytes 466952 | tf_op jit(solution)/shard_map/ppermute | solution.py:352
  129.2 1.1 collective-permute-done.12.rest_13_
  130.4 2.5 %collective-permute-start.13 = (bf16[304,256]{1,0:T(8,128)(2,1)S(1)}, bf16[304,256]{1,0:T(8,128)(2,1)S(1)}, u32[]{:S(2)}, u32[]{:S(2)}) collective-permute-start(bf16[304,256]{1,0:T(8,128)(2,1)S(1)} %collective-permute-done.12.rest_13_), channel_id=1, source_target_pairs={{0,8},{8,16},{16,24},{24,28},{28,20},{20,12},{12,4},{4,0},{1,9},{9... | collective-permute-start | bytes 466952 | tf_op jit(solution)/shard_map/ppermute | solution.py:352
  132.9 1.7 %collective-permute-done.9.rest_11_ = bf16[304,256]{1,0:T(8,128)(2,1)S(1)} collective-permute-done((bf16[304,256]{1,0:T(8,128)(2,1)S(1)}, bf16[304,256]{1,0:T(8,128)(2,1)S(1)}, u32[]{:S(2)}, u32[]{:S(2)}) %collective-permute-start.9) | collective-permute-done | bytes 155680 | tf_op jit(solution)/shard_map/ppermute | solution.py:352
  134.6 1.0 collective-permute-done.13.rest_12_
  135.6 2.5 %collective-permute-done.17.rest_20_ = bf16[304,256]{1,0:T(8,128)(2,1)S(1)} collective-permute-done((bf16[304,256]{1,0:T(8,128)(2,1)S(1)}, bf16[304,256]{1,0:T(8,128)(2,1)S(1)}, u32[]{:S(2)}, u32[]{:S(2)}) %collective-permute-start.17) | collective-permute-done | bytes 155680 | tf_op jit(solution)/shard_map/ppermute | solution.py:352
  138.1 1.5 grad_layer.1
  139.7 2.0 %collective-permute-done.21 = f32[608,256]{1,0:T(8,128)S(1)} collective-permute-done((f32[608,256]{1,0:T(8,128)S(1)}, f32[608,256]{1,0:T(8,128)S(1)}, u32[]{:S(2)}, u32[]{:S(2)}) %collective-permute-start.21) | collective-permute-done | bytes 622624 | tf_op jit(solution)/shard_map/ppermute | solution.py:385
  141.9 9.4 %collective-permute-done.22.other_ref = bf16[608,256]{1,0:T(8,128)(2,1)S(1)} collective-permute-done((bf16[608,256]{1,0:T(8,128)(2,1)S(1)}, bf16[608,256]{1,0:T(8,128)(2,1)S(1)}, u32[]{:S(2)}, u32[]{:S(2)}) %collective-permute-start.22) | collective-permute-done | bytes 311328 | tf_op jit(solution)/shard_map/ppermute | solution.py:389
  152.0 2.0 %final_sum.1 = (f32[2,128,256]{2,1,0:T(8,128)}, f32[172,2,256]{2,1,0:T(2,128)}) custom-call(bf16[608,256]{1,0:T(8,128)(2,1)} %copy-done, bf16[608,256]{1,0:T(8,128)(2,1)} %copy-done.1), custom_call_target="tpu_custom_call" | custom-call | tf_op jit(solution)/shard_map/final_sum/pallas_call | solution.py:333
  (59 shorter events, 10.2 us)
Async XLA Ops:
  7.2 89.8 %all-gather.2.cloned.1.call-start = ((), (), s32[]{:S(2)}) async-start(), calls=%async_computation | async-start | bytes 1179648 | tf_op jit(solution)/shard_map/all_gather | solution.py:433
  55.1 25.4 %collective-permute-start = (bf16[416,256]{1,0:T(8,128)(2,1)S(1)}, bf16[416,256]{1,0:T(8,128)(2,1)S(1)}, u32[]{:S(2)}, u32[]{:S(2)}) collective-permute-start(bf16[416,256]{1,0:T(8,128)(2,1)S(1)} %get-tuple-element.56.rest_0_), channel_id=1, source_target_pairs={{0,16},{4,20},{8,24},{12,28},{16,0},{20,4},{24,8},{28,12},{1,17},{... | collective-permute-start | bytes 638984 | tf_op jit(solution)/shard_map/ppermute | solution.py:364
  55.6 24.9 %collective-permute-start.1 = (bf16[416,256]{1,0:T(8,128)(2,1)S(1)}, bf16[416,256]{1,0:T(8,128)(2,1)S(1)}, u32[]{:S(2)}, u32[]{:S(2)}) collective-permute-start(bf16[416,256]{1,0:T(8,128)(2,1)S(1)} %get-tuple-element.57.rest_1_), channel_id=1, source_target_pairs={{0,12},{4,8},{8,4},{12,0},{16,28},{20,24},{24,20},{28,16},{1,13},{... | collective-permute-start | bytes 638984 | tf_op jit(solution)/shard_map/ppermute | solution.py:364
  63.1 17.4 %collective-permute-start.2 = (bf16[416,256]{1,0:T(8,128)(2,1)S(1)}, bf16[416,256]{1,0:T(8,128)(2,1)S(1)}, u32[]{:S(2)}, u32[]{:S(2)}) collective-permute-start(bf16[416,256]{1,0:T(8,128)(2,1)S(1)} %get-tuple-element.58.rest_2_), channel_id=1, source_target_pairs={{0,20},{4,16},{8,28},{12,24},{16,4},{20,0},{24,12},{28,8},{1,21},{... | collective-permute-start | bytes 638984 | tf_op jit(solution)/shard_map/ppermute | solution.py:364
  80.5 18.1 %copy-start.2 = (bf16[2,256,172]{1,0,2:T(2,128)(2,1)S(1)}, bf16[2,256,172]{1,0,2:T(2,128)(2,1)}, u32[]{:S(2)}) copy-start(bf16[2,256,172]{1,0,2:T(2,128)(2,1)} %param.13) | copy-start | bytes 528388
  80.5 14.8 %collective-permute-start.3 = (bf16[416,256]{1,0:T(8,128)(2,1)S(1)}, bf16[416,256]{1,0:T(8,128)(2,1)S(1)}, u32[]{:S(2)}, u32[]{:S(2)}) collective-permute-start(bf16[416,256]{1,0:T(8,128)(2,1)S(1)} %get-tuple-element.64.rest_3_), channel_id=1, source_target_pairs={{0,24},{4,28},{8,16},{12,20},{16,8},{20,12},{24,0},{28,4},{1,25},{... | collective-permute-start | bytes 638984 | tf_op jit(solution)/shard_map/ppermute | solution.py:364
  80.8 14.5 %collective-permute-start.4 = (bf16[416,256]{1,0:T(8,128)(2,1)S(1)}, bf16[416,256]{1,0:T(8,128)(2,1)S(1)}, u32[]{:S(2)}, u32[]{:S(2)}) collective-permute-start(bf16[416,256]{1,0:T(8,128)(2,1)S(1)} %get-tuple-element.65.rest_4_), channel_id=1, source_target_pairs={{0,8},{4,12},{8,0},{12,4},{16,24},{20,28},{24,16},{28,20},{1,9},{5... | collective-permute-start | bytes 638984 | tf_op jit(solution)/shard_map/ppermute | solution.py:364
  84.2 12.8 %collective-permute-start.5 = (bf16[416,256]{1,0:T(8,128)(2,1)S(1)}, bf16[416,256]{1,0:T(8,128)(2,1)S(1)}, u32[]{:S(2)}, u32[]{:S(2)}) collective-permute-start(bf16[416,256]{1,0:T(8,128)(2,1)S(1)} %get-tuple-element.66.rest_5_), channel_id=1, source_target_pairs={{0,28},{4,24},{8,20},{12,16},{16,12},{20,8},{24,4},{28,0},{1,29},{... | collective-permute-start | bytes 638984 | tf_op jit(solution)/shard_map/ppermute | solution.py:364
  97.0 5.8 %collective-permute-start.6 = (bf16[416,256]{1,0:T(8,128)(2,1)S(1)}, bf16[416,256]{1,0:T(8,128)(2,1)S(1)}, u32[]{:S(2)}, u32[]{:S(2)}) collective-permute-start(bf16[416,256]{1,0:T(8,128)(2,1)S(1)} %get-tuple-element.70.rest_6_), channel_id=1, source_target_pairs={{0,4},{4,0},{8,12},{12,8},{16,20},{20,16},{24,28},{28,24},{1,5},{5... | collective-permute-start | bytes 638984 | tf_op jit(solution)/shard_map/ppermute | solution.py:364
  106.0 10.5 %collective-permute-start.10 = (bf16[304,256]{1,0:T(8,128)(2,1)S(1)}, bf16[304,256]{1,0:T(8,128)(2,1)S(1)}, u32[]{:S(2)}, u32[]{:S(2)}) collective-permute-start(bf16[304,256]{1,0:T(8,128)(2,1)S(1)} %get-tuple-element.84.rest_8_), channel_id=1, source_target_pairs={{0,8},{8,16},{16,24},{24,28},{28,20},{20,12},{12,4},{4,0},{1,9},{9... | collective-permute-start | bytes 466952 | tf_op jit(solution)/shard_map/ppermute | solution.py:352
  112.0 7.0 %collective-permute-start.14 = (bf16[304,256]{1,0:T(8,128)(2,1)S(1)}, bf16[304,256]{1,0:T(8,128)(2,1)S(1)}, u32[]{:S(2)}, u32[]{:S(2)}) collective-permute-start(bf16[304,256]{1,0:T(8,128)(2,1)S(1)} %get-tuple-element.85.rest_16_), channel_id=1, source_target_pairs={{0,4},{8,0},{16,8},{24,16},{28,24},{20,28},{12,20},{4,12},{1,5},{9... | collective-permute-start | bytes 466952 | tf_op jit(solution)/shard_map/ppermute | solution.py:352
  112.0 7.8 %collective-permute-start.18 = (bf16[304,256]{1,0:T(8,128)(2,1)S(1)}, bf16[304,256]{1,0:T(8,128)(2,1)S(1)}, u32[]{:S(2)}, u32[]{:S(2)}) collective-permute-start(bf16[304,256]{1,0:T(8,128)(2,1)S(1)} %get-tuple-element.85.rest_16_), channel_id=1, source_target_pairs={{0,8},{8,16},{16,24},{24,28},{28,20},{20,12},{12,4},{4,0},{1,9},{9... | collective-permute-start | bytes 466952 | tf_op jit(solution)/shard_map/ppermute | solution.py:352
  114.0 8.3 %collective-permute-start.7 = (bf16[304,256]{1,0:T(8,128)(2,1)S(1)}, bf16[304,256]{1,0:T(8,128)(2,1)S(1)}, u32[]{:S(2)}, u32[]{:S(2)}) collective-permute-start(bf16[304,256]{1,0:T(8,128)(2,1)S(1)} %get-tuple-element.84.rest_8_), channel_id=1, source_target_pairs={{0,4},{8,0},{16,8},{24,16},{28,24},{20,28},{12,20},{4,12},{1,5},{9... | collective-permute-start | bytes 466952 | tf_op jit(solution)/shard_map/ppermute | solution.py:352
  116.5 7.0 %collective-permute-start.11 = (bf16[304,256]{1,0:T(8,128)(2,1)S(1)}, bf16[304,256]{1,0:T(8,128)(2,1)S(1)}, u32[]{:S(2)}, u32[]{:S(2)}) collective-permute-start(bf16[304,256]{1,0:T(8,128)(2,1)S(1)} %collective-permute-done.10.rest_15_), channel_id=1, source_target_pairs={{0,8},{8,16},{16,24},{24,28},{28,20},{20,12},{12,4},{4,0},{1,9},{9... | collective-permute-start | bytes 466952 | tf_op jit(solution)/shard_map/ppermute | solution.py:352
  118.9 7.0 %collective-permute-start.15 = (bf16[304,256]{1,0:T(8,128)(2,1)S(1)}, bf16[304,256]{1,0:T(8,128)(2,1)S(1)}, u32[]{:S(2)}, u32[]{:S(2)}) collective-permute-start(bf16[304,256]{1,0:T(8,128)(2,1)S(1)} %collective-permute-done.14.rest_17_), channel_id=1, source_target_pairs={{0,4},{8,0},{16,8},{24,16},{28,24},{20,28},{12,20},{4,12},{1,5},{9... | collective-permute-start | bytes 466952 | tf_op jit(solution)/shard_map/ppermute | solution.py:352
  119.8 7.0 %collective-permute-start.19 = (bf16[304,256]{1,0:T(8,128)(2,1)S(1)}, bf16[304,256]{1,0:T(8,128)(2,1)S(1)}, u32[]{:S(2)}, u32[]{:S(2)}) collective-permute-start(bf16[304,256]{1,0:T(8,128)(2,1)S(1)} %collective-permute-done.18.rest_23_), channel_id=1, source_target_pairs={{0,8},{8,16},{16,24},{24,28},{28,20},{20,12},{12,4},{4,0},{1,9},{9... | collective-permute-start | bytes 466952 | tf_op jit(solution)/shard_map/ppermute | solution.py:352
  122.3 7.0 %collective-permute-start.8 = (bf16[304,256]{1,0:T(8,128)(2,1)S(1)}, bf16[304,256]{1,0:T(8,128)(2,1)S(1)}, u32[]{:S(2)}, u32[]{:S(2)}) collective-permute-start(bf16[304,256]{1,0:T(8,128)(2,1)S(1)} %collective-permute-done.7.rest_9_), channel_id=1, source_target_pairs={{0,4},{8,0},{16,8},{24,16},{28,24},{20,28},{12,20},{4,12},{1,5},{9... | collective-permute-start | bytes 466952 | tf_op jit(solution)/shard_map/ppermute | solution.py:352
  123.4 7.0 %collective-permute-start.12 = (bf16[304,256]{1,0:T(8,128)(2,1)S(1)}, bf16[304,256]{1,0:T(8,128)(2,1)S(1)}, u32[]{:S(2)}, u32[]{:S(2)}) collective-permute-start(bf16[304,256]{1,0:T(8,128)(2,1)S(1)} %collective-permute-done.11.rest_14_), channel_id=1, source_target_pairs={{0,8},{8,16},{16,24},{24,28},{28,20},{20,12},{12,4},{4,0},{1,9},{9... | collective-permute-start | bytes 466952 | tf_op jit(solution)/shard_map/ppermute | solution.py:352
  125.9 7.0 %collective-permute-start.16 = (bf16[304,256]{1,0:T(8,128)(2,1)S(1)}, bf16[304,256]{1,0:T(8,128)(2,1)S(1)}, u32[]{:S(2)}, u32[]{:S(2)}) collective-permute-start(bf16[304,256]{1,0:T(8,128)(2,1)S(1)} %collective-permute-done.15.rest_18_), channel_id=1, source_target_pairs={{0,4},{8,0},{16,8},{24,16},{28,24},{20,28},{12,20},{4,12},{1,5},{9... | collective-permute-start | bytes 466952 | tf_op jit(solution)/shard_map/ppermute | solution.py:352
  126.8 6.1 %collective-permute-start.20 = (bf16[304,256]{1,0:T(8,128)(2,1)S(1)}, bf16[304,256]{1,0:T(8,128)(2,1)S(1)}, u32[]{:S(2)}, u32[]{:S(2)}) collective-permute-start(bf16[304,256]{1,0:T(8,128)(2,1)S(1)} %collective-permute-done.19.rest_22_), channel_id=1, source_target_pairs={{0,8},{8,16},{16,24},{24,28},{28,20},{20,12},{12,4},{4,0},{1,9},{9... | collective-permute-start | bytes 466952 | tf_op jit(solution)/shard_map/ppermute | solution.py:352
  129.2 5.4 %collective-permute-start.9 = (bf16[304,256]{1,0:T(8,128)(2,1)S(1)}, bf16[304,256]{1,0:T(8,128)(2,1)S(1)}, u32[]{:S(2)}, u32[]{:S(2)}) collective-permute-start(bf16[304,256]{1,0:T(8,128)(2,1)S(1)} %collective-permute-done.8.rest_10_), channel_id=1, source_target_pairs={{0,4},{8,0},{16,8},{24,16},{28,24},{20,28},{12,20},{4,12},{1,5},{9... | collective-permute-start | bytes 466952 | tf_op jit(solution)/shard_map/ppermute | solution.py:352
  130.4 5.2 %collective-permute-start.13 = (bf16[304,256]{1,0:T(8,128)(2,1)S(1)}, bf16[304,256]{1,0:T(8,128)(2,1)S(1)}, u32[]{:S(2)}, u32[]{:S(2)}) collective-permute-start(bf16[304,256]{1,0:T(8,128)(2,1)S(1)} %collective-permute-done.12.rest_13_), channel_id=1, source_target_pairs={{0,8},{8,16},{16,24},{24,28},{28,20},{20,12},{12,4},{4,0},{1,9},{9... | collective-permute-start | bytes 466952 | tf_op jit(solution)/shard_map/ppermute | solution.py:352
  132.9 5.2 %collective-permute-start.17 = (bf16[304,256]{1,0:T(8,128)(2,1)S(1)}, bf16[304,256]{1,0:T(8,128)(2,1)S(1)}, u32[]{:S(2)}, u32[]{:S(2)}) collective-permute-start(bf16[304,256]{1,0:T(8,128)(2,1)S(1)} %collective-permute-done.16.rest_19_), channel_id=1, source_target_pairs={{0,4},{8,0},{16,8},{24,16},{28,24},{20,28},{12,20},{4,12},{1,5},{9... | collective-permute-start | bytes 466952 | tf_op jit(solution)/shard_map/ppermute | solution.py:352
  139.6 2.1 %collective-permute-start.21 = (f32[608,256]{1,0:T(8,128)S(1)}, f32[608,256]{1,0:T(8,128)S(1)}, u32[]{:S(2)}, u32[]{:S(2)}) collective-permute-start(f32[608,256]{1,0:T(8,128)S(1)} %grad_layer.1), channel_id=1, source_target_pairs={{0,1},{1,0},{2,3},{3,2},{4,5},{5,4},{6,7},{7,6},{8,9},{9,8},{10,11... | collective-permute-start | bytes 1867784 | tf_op jit(solution)/shard_map/ppermute | solution.py:385
  141.9 9.5 %copy-start = (bf16[608,256]{1,0:T(8,128)(2,1)}, bf16[608,256]{1,0:T(8,128)(2,1)S(1)}, u32[]{:S(2)}) copy-start(bf16[608,256]{1,0:T(8,128)(2,1)S(1)} %add_convert_fusion.mine_ref) | copy-start | bytes 933892
  141.9 9.5 %collective-permute-start.22 = (bf16[608,256]{1,0:T(8,128)(2,1)S(1)}, bf16[608,256]{1,0:T(8,128)(2,1)S(1)}, u32[]{:S(2)}, u32[]{:S(2)}) collective-permute-start(bf16[608,256]{1,0:T(8,128)(2,1)S(1)} %add_convert_fusion.mine_ref), channel_id=1, source_target_pairs={{0,2},{1,3},{2,0},{3,1},{4,6},{5,7},{6,4},{7,5},{8,10},{9,11},{10,... | collective-permute-start | bytes 933896 | tf_op jit(solution)/shard_map/ppermute | solution.py:389
  151.3 0.7 copy-start.1
Sparse Core Ops, SparseCore 0:
  10.1 42.8 all-gather.1
